TPU v7x, 32 devices: a whole 2x2x4 slice. The times are simulated.
32 devices in a mesh: parts: 2 (over y), row: 4 (over z), col: 4 (over x, core).
Axes of the slice: x: 2, y: 2, z: 4, core: 2. Of those that a mesh axis runs over, the one named last changes fastest.
Arguments:
- tokens: bfloat16 [3072, 4096], P(('parts', 'row'), 'col'), parts along dimension 0, may hold values from -6 to 6
- gate_weight: bfloat16 [4096, 14336], P('row', 'col'), may hold values from -0.09375 to 0.09375
- up_weight: bfloat16 [4096, 14336], P('row', 'col'), may hold values from -0.09375 to 0.09375
Outputs:
- hidden: bfloat16 [3072, 14336], P(('parts', 'row'), 'col'), parts along dimension 0
There are 2 independent parts, one for each index of `parts`. A program takes and returns all parts, laid end to end along the dimension named above; an argument that names none is the same for every part. Nothing has to cross between parts.
All inputs are finite; a program needn't handle non-finite values.
Results may differ from a plain program's by a relative error of at most 0.001.
Values may be sent and summed in bfloat16 or wider, within the bound.
No kernel may reach another device: no remote copies, remote signals or barrier semaphores. Data moves between devices by JAX's collectives and lax.ppermute only.
A program may use at most 192 MiB of HBM per device.

v0:
```python
import jax
import jax.numpy as jnp
from jax import lax
from jax.sharding import PartitionSpec as P


def on_device(tokens, gate_weight, up_weight):
    whole = lax.all_gather(tokens, "col", axis=1, tiled=True)

    def part_product(piece):
        return jnp.dot(whole, piece, preferred_element_type=jnp.float32)

    def add_one(piece):
        return part_product(piece)

    gate = add_one(lax.all_gather(gate_weight, "row", axis=0, tiled=True))
    up = add_one(lax.all_gather(up_weight, "row", axis=0, tiled=True))
    return (jax.nn.silu(gate) * up).astype(jnp.bfloat16)


def solution(mesh):
    placed = (P(("parts", "row"), "col"), P("row", "col"), P("row", "col"))
    return jax.shard_map(
        on_device, mesh=mesh, in_specs=placed, out_specs=P(("parts", "row"), "col"), check_vma=False
    )
```

profile of v0, /device:TPU:12, one launch (start us, length us, event | category | flops | bytes accessed | tf_op | source)
XLA Modules:
  0.0 1049.3 jit_solution(1281028460049977952)
XLA Ops:
  6.5 0.0 all-gather.4.cloned.1.call-start
  6.5 0.7 all-gather.4.cloned.1.call-update
  7.3 0.0 all-gather.6.cloned.1.call-start
  7.3 0.7 all-gather.6.cloned.1.call-update
  8.0 0.0 all-gather.8.cloned.1.call-start
  8.1 0.7 all-gather.8.cloned.1.call-update
  8.7 29.9 %all-gather.4.cloned.1.call-done = bf16[384,4096]{1,0:T(8,128)(2,1)} async-done(((bf16[384,1024]{1,0:T(8,128)(2,1)}), bf16[384,4096]{1,0:T(8,128)(2,1)}) %all-gather.4.cloned.1.call-update) | async-done | bytes 3145744 | tf_op jit(solution)/shard_map/all_gather | solution.py:8
  38.6 0.0 copy-start
  38.6 492.0 %all-gather.6.cloned.1.call-done = bf16[4096,3584]{1,0:T(8,128)(2,1)} async-done(((bf16[1024,3584]{1,0:T(8,128)(2,1)}), bf16[4096,3584]{1,0:T(8,128)(2,1)}) %all-gather.6.cloned.1.call-update) | async-done | bytes 29360144 | tf_op jit(solution)/shard_map/all_gather | solution.py:16
  530.6 19.3 %fusion.1 = f32[384,3584]{1,0:T(8,128)} fusion(bf16[384,4096]{1,0:T(8,128)(2,1)} %all-gather.4.cloned.1.call-done, bf16[4096,3584]{1,0:T(8,128)(2,1)} %all-gather.6.cloned.1.call-done), kind=kOutput, calls=%fused_computation.2 | convolution fusion | flops 11274289152 | bytes 38010880 | tf_op jit(solution)/shard_map/dot_general | solution.py:11
  549.9 473.6 %all-gather.8.cloned.1.call-done = bf16[4096,3584]{1,0:T(8,128)(2,1)} async-done(((bf16[1024,3584]{1,0:T(8,128)(2,1)}), bf16[4096,3584]{1,0:T(8,128)(2,1)}) %all-gather.8.cloned.1.call-update) | async-done | bytes 29360144 | tf_op jit(solution)/shard_map/all_gather | solution.py:17
  1023.5 0.0 copy-done
  1023.5 19.2 %fusion = bf16[384,3584]{1,0:T(8,128)(2,1)} fusion(bf16[384,4096]{1,0:T(8,128)(2,1)S(1)} %copy-done, bf16[4096,3584]{1,0:T(8,128)(2,1)} %all-gather.8.cloned.1.call-done, f32[384,3584]{1,0:T(8,128)} %fusion.1), kind=kOutput, calls=%fused_computation.1 | convolution fusion | flops 11282546688 | bytes 40763392 | tf_op jit(solution)/shard_map/dot_general | solution.py:11
Async XLA Ops:
  6.5 32.1 %all-gather.4.cloned.1.call-start = ((), (), s32[]{:S(2)}) async-start(), calls=%async_computation | async-start | bytes 3932160 | tf_op jit(solution)/shard_map/all_gather | solution.py:8
  7.3 523.3 %all-gather.6.cloned.1.call-start = ((), (), s32[]{:S(2)}) async-start(), calls=%async_computation.1 | async-start | bytes 36700160 | tf_op jit(solution)/shard_map/all_gather | solution.py:16
  8.0 1015.5 %all-gather.8.cloned.1.call-start = ((), (), s32[]{:S(2)}) async-start(), calls=%async_computation.2 | async-start | bytes 36700160 | tf_op jit(solution)/shard_map/all_gather | solution.py:17
  38.6 985.0 %copy-start = (bf16[384,4096]{1,0:T(8,128)(2,1)S(1)}, bf16[384,4096]{1,0:T(8,128)(2,1)}, u32[]{:S(2)}) copy-start(bf16[384,4096]{1,0:T(8,128)(2,1)} %all-gather.4.cloned.1.call-done) | copy-start | bytes 9437188
Sparse Core Ops, SparseCore 0:
  8.9 29.6 all-gather.3
  40.2 490.3 all-gather.5
  532.2 491.3 all-gather.7
where the time goes:
time: 1050 us
  waiting for transfers between devices  998 us (95%)
  matrix products  38.6 us (4%)
  between operations  13.1 us (1%)
    all_gather x1, waiting for transfers between devices, on_device(): gate = add_one(lax.all_gather(gate_weight, 'row', axis=0, tiled=True))  492 us
    all_gather x1, waiting for transfers between devices, on_device(): up = add_one(lax.all_gather(up_weight, 'row', axis=0, tiled=True))  474 us
    dot_general x2, matrix products, part_product(): return jnp.dot(whole, piece, preferred_element_type=jnp.float32)  38.6 us
    all_gather x1, waiting for transfers between devices, on_device(): whole = lax.all_gather(tokens, 'col', axis=1, tiled=True)  29.9 us
  transfers between devices with their start and end apart: 3, of which 3 were waited for; matrix products, arithmetic and copies ran while one was open for 2% of the time, Pallas kernels for 0%

commit v1 on v0

v1 whole, which is shorter than its diff:
```python
import jax
import jax.numpy as jnp
from jax import lax
from jax.sharding import PartitionSpec as P

CHUNKS = 1


def cut(width, pieces):
    unit = 128 if width % 128 == 0 else width
    units = width // unit
    pieces = min(pieces, units)
    edges = [unit * (units * i // pieces) for i in range(pieces + 1)]
    return list(zip(edges[:-1], edges[1:]))


def on_device(tokens, gate_weight, up_weight):
    rows = lax.axis_size("row")
    parts = lax.axis_size("parts")
    z = lax.axis_index("row")
    y = lax.axis_index("parts")
    mine, ff = tokens.shape[0], gate_weight.shape[1]
    depth = gate_weight.shape[0]
    share = depth // parts
    width = ff // rows

    whole = lax.all_gather(lax.all_gather(tokens, "row", axis=0, tiled=True), "col", axis=1, tiled=True)

    def rotated(value, shift):
        return lax.ppermute(value, "row", [(i, (i + shift) % rows) for i in range(rows)])

    hidden = jnp.zeros((mine, ff), jnp.bfloat16)
    for low, high in cut(width, CHUNKS):
        wide = high - low
        gate = up = 0.0
        for shift in range(rows):
            to, came = (z + shift) % rows, (z - shift) % rows
            if shift == 0:
                both = [lax.dynamic_slice(w, (0, z * width + low), (depth, wide)) for w in (gate_weight, up_weight)]
            else:
                sent = jnp.stack([
                    lax.dynamic_slice(w, (y * share, to * width + low), (share, wide))
                    for w in (gate_weight, up_weight)
                ])
                both = lax.all_gather(rotated(sent, shift), "parts", axis=1, tiled=True)
            features = lax.dynamic_slice(whole, (0, came * depth), (whole.shape[0], depth))
            gate += jnp.dot(features, both[0], preferred_element_type=jnp.float32)
            up += jnp.dot(features, both[1], preferred_element_type=jnp.float32)
        done = (jax.nn.silu(gate) * up).astype(jnp.bfloat16)
        for shift in range(rows):
            to, came = (z + shift) % rows, (z - shift) % rows
            block = lax.dynamic_slice(done, (to * mine, 0), (mine, wide))
            if shift:
                block = rotated(block, shift)
            hidden = lax.dynamic_update_slice(hidden, block, (0, came * width + low))
    return hidden


def solution(mesh):
    placed = (P(("parts", "row"), "col"), P("row", "col"), P("row", "col"))
    return jax.shard_map(
        on_device, mesh=mesh, in_specs=placed, out_specs=P(("parts", "row"), "col"), check_vma=False
    )
```

time: 1050 us -> 413 us (0.39)
  waiting for transfers between devices: 998 us -> 299 us
  matrix products: 38.6 us -> 74.4 us
  starting transfers between devices: 0.08 us -> 12.2 us
  local copies, waits for them, and re-layouts: 0.01 us -> 11 us
    all_gather x3 -> x5, waiting for transfers between devices: 995 us -> 84 us  [the longest x1 64 us: on_device(): lax.all_gather(tokens, 'row', axis=0, tiled=True)]
    ppermute x0 -> x6, waiting for transfers between devices: none -> 214 us  [rotated(): lax.ppermute(value, 'row', [(i, (i + shift) % rows) for i in range(rows)])]
    dot_general x2 -> x8, matrix products: 38.6 us -> 74.4 us  [the longest x4 42 us: on_device(): up += jnp.dot(features, both[1], preferred_element_type=jnp.float32)]
    ppermute x0 -> x6, starting transfers between devices: none -> 12 us  [rotated(): lax.ppermute(value, 'row', [(i, (i + shift) % rows) for i in range(rows)])]
  transfers between devices with their start and end apart: 3 -> 11, of which waited for: 3 -> 8; matrix products, arithmetic and copies ran while one was open for 2% -> 13% of each run, Pallas kernels for 0% -> 0%
where the time goes in v1:
time: 413 us; the launch traced here: 412 us
  waiting for transfers between devices  299 us (72%)
  matrix products  74.4 us (18%)
  between operations  13.4 us (3%)
  starting transfers between devices  12.2 us (3%)
  local copies, waits for them, and re-layouts  11 us (3%)
    ppermute x6, waiting for transfers between devices, rotated(): lax.ppermute(value, 'row', [(i, (i + shift) % rows) for i in range(rows)])  214 us
    all_gather x1, waiting for transfers between devices, on_device(): lax.all_gather(tokens, 'row', axis=0, tiled=True)  64 us
    dot_general x4, matrix products, on_device(): up += jnp.dot(features, both[1], preferred_element_type=jnp.float32)  42 us
    dot_general x4, matrix products, on_device(): gate += jnp.dot(features, both[0], preferred_element_type=jnp.float32)  32.5 us
    all_gather x3, waiting for transfers between devices, on_device(): both = lax.all_gather(rotated(sent, shift), 'parts', axis=1, tiled=True)  19.9 us
    ppermute x6, starting transfers between devices, rotated(): lax.ppermute(value, 'row', [(i, (i + shift) % rows) for i in range(rows)])  12 us
  transfers between devices with their start and end apart: 11, of which 8 were waited for; matrix products, arithmetic and copies ran while one was open for 13% of the time, Pallas kernels for 0%

profile of v1, /device:TPU:12, one launch (start us, length us, event | category | flops | bytes accessed | tf_op | source)
XLA Modules:
  0.0 411.5 jit_solution(17680068582653151352)
XLA Ops:
  6.5 0.0 all-gather.6.cloned.1.call-start
  6.5 0.7 all-gather.6.cloned.1.call-update
  7.3 0.0 all-gather.8.cloned.1.call-start
  7.3 64.0 %all-gather.6.cloned.1.call-done = bf16[1536,1024]{1,0:T(8,128)(2,1)} async-done(((bf16[384,1024]{1,0:T(8,128)(2,1)}), bf16[1536,1024]{1,0:T(8,128)(2,1)}) %all-gather.6.cloned.1.call-update) | async-done | bytes 3145744 | tf_op jit(solution)/shard_map/all_gather | solution.py:27
  71.3 0.0 all-gather.8.cloned.1.call-update
  71.3 0.0 all-gather.10.cloned.1.call-start
  71.4 4.0 dynamic-slice_bitcast_fusion
  75.4 0.2 pad_maximum_fusion
  75.6 2.5 collective-permute-start
  78.0 40.5 %collective-permute-done = bf16[2,512,896]{2,1,0:T(8,128)(2,1)} collective-permute-done((bf16[2,512,896]{2,1,0:T(8,128)(2,1)S(1)}, bf16[2,512,896]{2,1,0:T(8,128)(2,1)}, u32[]{:S(2)}, u32[]{:S(2)}) %collective-permute-start) | collective-permute-done | bytes 1835040 | tf_op jit(solution)/shard_map/ppermute | solution.py:30
  118.5 0.0 all-gather.10.cloned.1.call-update
  118.5 0.0 all-gather.12.cloned.1.call-start
  118.6 1.4 pad_maximum_fusion.1
  120.0 1.6 collective-permute-start.1
  121.5 77.9 %collective-permute-done.1 = bf16[2,512,896]{2,1,0:T(8,128)(2,1)} collective-permute-done((bf16[2,512,896]{2,1,0:T(8,128)(2,1)S(1)}, bf16[2,512,896]{2,1,0:T(8,128)(2,1)}, u32[]{:S(2)}, u32[]{:S(2)}) %collective-permute-start.1) | collective-permute-done | bytes 1835040 | tf_op jit(solution)/shard_map/ppermute | solution.py:30
  199.5 0.0 all-gather.12.cloned.1.call-update
  199.5 0.0 all-gather.14.cloned.1.call-start
  199.6 0.2 pad_maximum_fusion.2
  199.8 3.5 collective-permute-start.2
  203.3 39.5 %collective-permute-done.2 = bf16[2,512,896]{2,1,0:T(8,128)(2,1)S(1)} collective-permute-done((bf16[2,512,896]{2,1,0:T(8,128)(2,1)S(1)}, bf16[2,512,896]{2,1,0:T(8,128)(2,1)S(1)}, u32[]{:S(2)}, u32[]{:S(2)}) %collective-permute-start.2) | collective-permute-done | bytes 1835040 | tf_op jit(solution)/shard_map/ppermute | solution.py:30
  242.7 0.0 copy-start.1
  242.7 1.2 copy-done.1
  244.0 0.0 all-gather.14.cloned.1.call-update
  244.1 0.0 all-gather.8.cloned.1.call-done
  244.2 8.2 %fusion.14 = f32[1536,896]{1,0:T(8,128)} fusion(bf16[1536,4096]{1,0:T(8,128)(2,1)} %all-gather.8.cloned.1.call-done, s32[]{:T(128)S(6)} %select_n.108, bf16[1024,3584]{1,0:T(8,128)(2,1)} %param.5, s32[]{:T(128)S(6)} %select_n.109), kind=kOutput, calls=%fused_computation.13 | convolution fusion | flops 2818572288 | bytes 10485768 | tf_op jit(solution)/shard_map/dot_general | solution.py:48
  252.4 8.3 %fusion.16 = f32[1536,896]{1,0:T(8,128)} fusion(bf16[1536,4096]{1,0:T(8,128)(2,1)} %all-gather.8.cloned.1.call-done, s32[]{:T(128)S(6)} %select_n.108, bf16[1024,3584]{1,0:T(8,128)(2,1)} %param.4, s32[]{:T(128)S(6)} %select_n.109), kind=kOutput, calls=%fused_computation.15 | convolution fusion | flops 2818572288 | bytes 10485768 | tf_op jit(solution)/shard_map/dot_general | solution.py:47
  260.7 0.0 all-gather.10.cloned.1.call-done
  260.7 0.0 copy-start.2
  260.7 8.4 %fusion.10 = f32[1536,896]{1,0:T(8,128)} fusion(bf16[1536,4096]{1,0:T(8,128)(2,1)} %all-gather.8.cloned.1.call-done, s32[]{:T(128)S(6)} %select_n.111, bf16[2,1024,896]{2,1,0:T(8,128)(2,1)} %all-gather.10.cloned.1.call-done), kind=kOutput, calls=%fused_computation.9 | convolution fusion | flops 2818572288 | bytes 10485764 | tf_op jit(solution)/shard_map/dot_general | solution.py:48
  269.2 0.0 copy-done.2
  269.2 7.5 %fusion.12 = f32[1536,896]{1,0:T(8,128)} fusion(bf16[1536,4096]{1,0:T(8,128)(2,1)} %all-gather.8.cloned.1.call-done, s32[]{:T(128)S(6)} %select_n.111, bf16[2,1024,896]{2,1,0:T(8,128)(2,1)S(1)} %copy-done.2), kind=kOutput, calls=%fused_computation.11 | convolution fusion | flops 2818572288 | bytes 10485764 | tf_op jit(solution)/shard_map/dot_general | solution.py:47
  276.6 0.0 all-gather.12.cloned.1.call-done
  276.6 0.0 copy-start.3
  276.6 8.4 %fusion.8 = f32[1536,896]{1,0:T(8,128)} fusion(bf16[1536,4096]{1,0:T(8,128)(2,1)} %all-gather.8.cloned.1.call-done, s32[]{:T(128)S(6)} %select_n.116, bf16[2,1024,896]{2,1,0:T(8,128)(2,1)} %all-gather.12.cloned.1.call-done), kind=kOutput, calls=%fused_computation.7 | convolution fusion | flops 2818572288 | bytes 10485764 | tf_op jit(solution)/shard_map/dot_general | solution.py:47
  285.0 0.0 copy-done.3
  285.0 7.0 %fusion.6 = f32[1536,896]{1,0:T(8,128)} fusion(bf16[1536,4096]{1,0:T(8,128)(2,1)} %all-gather.8.cloned.1.call-done, s32[]{:T(128)S(6)} %select_n.116, bf16[2,1024,896]{2,1,0:T(8,128)(2,1)S(1)} %copy-done.3), kind=kOutput, calls=%fused_computation.5 | convolution fusion | flops 2818572288 | bytes 10485764 | tf_op jit(solution)/shard_map/dot_general | solution.py:48
  292.0 19.9 %all-gather.14.cloned.1.call-done = bf16[2,1024,896]{2,1,0:T(8,128)(2,1)} async-done(((bf16[2,512,896]{2,1,0:T(8,128)(2,1)}), bf16[2,1024,896]{2,1,0:T(8,128)(2,1)}) %all-gather.14.cloned.1.call-update) | async-done | bytes 3670032 | tf_op jit(solution)/shard_map/all_gather | solution.py:45
  312.0 8.3 %fusion.2 = f32[1536,896]{1,0:T(8,128)} fusion(bf16[1536,4096]{1,0:T(8,128)(2,1)} %all-gather.8.cloned.1.call-done, s32[]{:T(128)S(6)} %select_n.120, bf16[2,1024,896]{2,1,0:T(8,128)(2,1)} %all-gather.14.cloned.1.call-done), kind=kOutput, calls=%fused_computation.3 | convolution fusion | flops 2818572288 | bytes 10485764 | tf_op jit(solution)/shard_map/dot_general | solution.py:47
  320.2 18.3 %multiply_convert_fusion = bf16[1536,896]{1,0:T(8,128)(2,1)S(1)} fusion(f32[1536,896]{1,0:T(8,128)} %fusion.6, f32[1536,896]{1,0:T(8,128)} %fusion.14, f32[1536,896]{1,0:T(8,128)} %fusion.10, f32[1536,896]{1,0:T(8,128)} %fusion.2, f32[1536,896]{1,0:T(8,128)} %fusion.8, f32[1536,896]{1,0:T(8,128)} %fusion.16, f32[1536,896]{1,0:T(8,128)} %fusion.12, ...), kind=kOutput, calls=%fused_computation | convolution fusion | flops 2835087360 | bytes 46268420 | tf_op jit(solution)/shard_map/dot_general | solution.py:48
  338.6 0.2 broadcast_in_dim.3
  338.7 1.3 constant_dynamic-slice_fusion
  340.1 0.0 copy-start
  340.1 1.5 copy-done
  341.6 1.5 collective-permute-start.3
  343.1 1.1 collective-permute-start.4
  344.3 1.8 collective-permute-start.5
  346.0 42.8 %collective-permute-done.3 = bf16[384,896]{1,0:T(8,128)(2,1)S(1)} collective-permute-done((bf16[384,896]{1,0:T(8,128)(2,1)}, bf16[384,896]{1,0:T(8,128)(2,1)S(1)}, u32[]{:S(2)}, u32[]{:S(2)}) %collective-permute-start.3) | collective-permute-done | bytes 688160 | tf_op jit(solution)/shard_map/ppermute | solution.py:30
  388.8 0.9 constant_dynamic-update-slice_fusion.2
  389.7 12.7 %collective-permute-done.4 = bf16[384,896]{1,0:T(8,128)(2,1)S(1)} collective-permute-done((bf16[384,896]{1,0:T(8,128)(2,1)}, bf16[384,896]{1,0:T(8,128)(2,1)S(1)}, u32[]{:S(2)}, u32[]{:S(2)}) %collective-permute-start.4) | collective-permute-done | bytes 688160 | tf_op jit(solution)/shard_map/ppermute | solution.py:30
  402.4 0.9 constant_dynamic-update-slice_fusion.1
  403.3 0.8 collective-permute-done.5
  404.1 0.9 constant_dynamic-update-slice_fusion
Async XLA Ops:
  6.5 64.7 %all-gather.6.cloned.1.call-start = ((), (), s32[]{:S(2)}) async-start(), calls=%async_computation | async-start | bytes 3932160 | tf_op jit(solution)/shard_map/all_gather | solution.py:27
  7.3 236.9 %all-gather.8.cloned.1.call-start = ((), (), s32[]{:S(2)}) async-start(), calls=%async_computation.1 | async-start | bytes 15728640 | tf_op jit(solution)/shard_map/all_gather | solution.py:27
  71.3 189.4 %all-gather.10.cloned.1.call-start = ((), (), s32[]{:S(2)}) async-start(), calls=%async_computation.2 | async-start | bytes 5505024 | tf_op jit(solution)/shard_map/all_gather | solution.py:45
  75.6 43.0 %collective-permute-start = (bf16[2,512,896]{2,1,0:T(8,128)(2,1)S(1)}, bf16[2,512,896]{2,1,0:T(8,128)(2,1)}, u32[]{:S(2)}, u32[]{:S(2)}) collective-permute-start(bf16[2,512,896]{2,1,0:T(8,128)(2,1)S(1)} %pad_maximum_fusion), channel_id=1, source_target_pairs={{0,4},{4,8},{8,12},{12,0},{1,5},{5,9},{9,13},{13,1},{2,6},{6,10},{... | collective-permute-start | bytes 5505032 | tf_op jit(solution)/shard_map/ppermute | solution.py:30
  118.5 158.1 %all-gather.12.cloned.1.call-start = ((), (), s32[]{:S(2)}) async-start(), calls=%async_computation.3 | async-start | bytes 5505024 | tf_op jit(solution)/shard_map/all_gather | solution.py:45
  120.0 79.5 %collective-permute-start.1 = (bf16[2,512,896]{2,1,0:T(8,128)(2,1)S(1)}, bf16[2,512,896]{2,1,0:T(8,128)(2,1)}, u32[]{:S(2)}, u32[]{:S(2)}) collective-permute-start(bf16[2,512,896]{2,1,0:T(8,128)(2,1)S(1)} %pad_maximum_fusion.1), channel_id=1, source_target_pairs={{0,8},{4,12},{8,0},{12,4},{1,9},{5,13},{9,1},{13,5},{2,10},{6,14},... | collective-permute-start | bytes 5505032 | tf_op jit(solution)/shard_map/ppermute | solution.py:30
  199.5 112.5 %all-gather.14.cloned.1.call-start = ((), (), s32[]{:S(2)}) async-start(), calls=%async_computation.4 | async-start | bytes 5505024 | tf_op jit(solution)/shard_map/all_gather | solution.py:45
  199.8 43.0 %collective-permute-start.2 = (bf16[2,512,896]{2,1,0:T(8,128)(2,1)S(1)}, bf16[2,512,896]{2,1,0:T(8,128)(2,1)S(1)}, u32[]{:S(2)}, u32[]{:S(2)}) collective-permute-start(bf16[2,512,896]{2,1,0:T(8,128)(2,1)S(1)} %pad_maximum_fusion.2), channel_id=1, source_target_pairs={{0,12},{4,0},{8,4},{12,8},{1,13},{5,1},{9,5},{13,9},{2,14},{6,2},{... | collective-permute-start | bytes 5505032 | tf_op jit(solution)/shard_map/ppermute | solution.py:30
  242.7 1.2 copy-start.1
  260.7 8.4 %copy-start.2 = (bf16[2,1024,896]{2,1,0:T(8,128)(2,1)S(1)}, bf16[2,1024,896]{2,1,0:T(8,128)(2,1)}, u32[]{:S(2)}) copy-start(bf16[2,1024,896]{2,1,0:T(8,128)(2,1)} %all-gather.10.cloned.1.call-done) | copy-start | bytes 11010052
  276.6 8.4 %copy-start.3 = (bf16[2,1024,896]{2,1,0:T(8,128)(2,1)S(1)}, bf16[2,1024,896]{2,1,0:T(8,128)(2,1)}, u32[]{:S(2)}) copy-start(bf16[2,1024,896]{2,1,0:T(8,128)(2,1)} %all-gather.12.cloned.1.call-done) | copy-start | bytes 11010052
  340.1 1.5 copy-start
  341.6 47.2 %collective-permute-start.3 = (bf16[384,896]{1,0:T(8,128)(2,1)}, bf16[384,896]{1,0:T(8,128)(2,1)S(1)}, u32[]{:S(2)}, u32[]{:S(2)}) collective-permute-start(bf16[384,896]{1,0:T(8,128)(2,1)} %get-tuple-element.13), channel_id=1, source_target_pairs={{0,4},{4,8},{8,12},{12,0},{1,5},{5,9},{9,13},{13,1},{2,6},{6,10},{... | collective-permute-start | bytes 2064392 | tf_op jit(solution)/shard_map/ppermute | solution.py:30
  343.1 59.2 %collective-permute-start.4 = (bf16[384,896]{1,0:T(8,128)(2,1)}, bf16[384,896]{1,0:T(8,128)(2,1)S(1)}, u32[]{:S(2)}, u32[]{:S(2)}) collective-permute-start(bf16[384,896]{1,0:T(8,128)(2,1)} %get-tuple-element.12), channel_id=1, source_target_pairs={{0,8},{4,12},{8,0},{12,4},{1,9},{5,13},{9,1},{13,5},{2,10},{6,14},... | collective-permute-start | bytes 2064392 | tf_op jit(solution)/shard_map/ppermute | solution.py:30
  344.3 59.8 %collective-permute-start.5 = (bf16[384,896]{1,0:T(8,128)(2,1)S(1)}, bf16[384,896]{1,0:T(8,128)(2,1)S(1)}, u32[]{:S(2)}, u32[]{:S(2)}) collective-permute-start(bf16[384,896]{1,0:T(8,128)(2,1)S(1)} %get-tuple-element.11), channel_id=1, source_target_pairs={{0,12},{4,0},{8,4},{12,8},{1,13},{5,1},{9,5},{13,9},{2,14},{6,2},{... | collective-permute-start | bytes 2064392 | tf_op jit(solution)/shard_map/ppermute | solution.py:30
Sparse Core Ops, SparseCore 0:
  8.9 62.3 all-gather.5
  72.8 83.0 all-gather.7
  157.5 49.9 all-gather.9
  208.8 50.8 all-gather.11
  261.1 50.8 all-gather.13

commit v2 on v0

v2 whole, which is shorter than its diff:
```python
import jax
import jax.numpy as jnp
from jax import lax
from jax.sharding import PartitionSpec as P

PIECES = 4


def cut(width, pieces):
    unit = 128 if width % 128 == 0 else width
    units = width // unit
    pieces = min(pieces, units)
    edges = [unit * (-(-units * i // pieces)) for i in range(pieces + 1)]
    return list(zip(edges[:-1], edges[1:]))


def on_device(tokens, gate_weight, up_weight):
    rows = lax.axis_size("row")
    parts = lax.axis_size("parts")
    y = lax.axis_index("parts")
    mine, ff = tokens.shape[0], gate_weight.shape[1]
    depth = gate_weight.shape[0]
    share = depth // parts
    width = ff // rows

    whole = lax.all_gather(lax.all_gather(tokens, "row", axis=0, tiled=True), "col", axis=1, tiled=True)
    everyone = whole.shape[0]
    by_share = whole.reshape(everyone, rows, parts, share)
    features = [
        lax.dynamic_index_in_dim(by_share, (y + turn) % parts, 2, keepdims=False).reshape(everyone, rows * share)
        for turn in range(parts)
    ]
    halves = [
        lax.dynamic_slice(w, (y * share, 0), (share, ff)).reshape(share, rows, width)
        for w in (gate_weight, up_weight)
    ]

    hidden = []
    for low, high in cut(width, PIECES):
        wide = high - low
        sent = jnp.stack([h[:, :, low:high].transpose(1, 0, 2) for h in halves])
        held = lax.all_to_all(sent, "row", 1, 1, tiled=True)
        gate = up = 0.0
        for turn in range(parts):
            block = held if turn == 0 else lax.ppermute(
                held, "parts", [(i, (i - turn) % parts) for i in range(parts)]
            )
            block = block.reshape(2, rows * share, wide)
            gate += jnp.dot(features[turn], block[0], preferred_element_type=jnp.float32)
            up += jnp.dot(features[turn], block[1], preferred_element_type=jnp.float32)
        done = (jax.nn.silu(gate) * up).astype(jnp.bfloat16)
        back = lax.all_to_all(done.reshape(rows, mine, wide), "row", 0, 0, tiled=True)
        hidden.append(back)
    hidden = jnp.concatenate(hidden, axis=2)
    return hidden.transpose(1, 0, 2).reshape(mine, ff)


def solution(mesh):
    placed = (P(("parts", "row"), "col"), P("row", "col"), P("row", "col"))
    return jax.shard_map(
        on_device, mesh=mesh, in_specs=placed, out_specs=P(("parts", "row"), "col"), check_vma=False
    )
```

time: 1050 us -> 530 us (0.50)
  waiting for transfers between devices: 998 us -> 301 us
  local copies, waits for them, and re-layouts: 0.01 us -> 77.6 us
  starting transfers between devices: 0.08 us -> 49 us
  blocking collectives: 0 us -> 23.5 us
  matrix products: 38.6 us -> 53.6 us
    all_gather x3 -> x2, waiting for transfers between devices: 995 us -> 62.9 us  [the longest x1 62.9 us: on_device(): lax.all_gather(tokens, 'row', axis=0, tiled=True)]
    all_to_all x0 -> x7, waiting for transfers between devices: none -> 143 us  [the longest x4 133 us: on_device(): held = lax.all_to_all(sent, 'row', 1, 1, tiled=True)]
    ppermute x0 -> x4, waiting for transfers between devices: none -> 95.4 us  [on_device(): lax.ppermute(held, 'parts', [(i, (i - turn) % parts) for i in range(parts)])]
    all_to_all x0 -> x7, starting transfers between devices: none -> 45.7 us  [the longest x4 28.5 us: on_device(): held = lax.all_to_all(sent, 'row', 1, 1, tiled=True)]
    all_to_all x0 -> x1, blocking collectives: none -> 23.5 us  [on_device(): lax.all_to_all(done.reshape(rows, mine, wide), 'row', 0, 0, tiled=True)]
    slice x0 -> x8, local copies, waits for them, and re-layouts: none -> 18.1 us  [on_device(): block[0]]
    unnamed x2 -> x55, local copies, waits for them, and re-layouts: 0.01 us -> 17.5 us
    dynamic_slice x0 -> x2, local copies, waits for them, and re-layouts: none -> 16.6 us  [the longest x1 10 us: on_device(): lax.dynamic_index_in_dim(by_share, (y + turn) % parts, 2, keepdims=False)]
  transfers between devices with their start and end apart: 3 -> 13, of which waited for: 3 -> 10; matrix products, arithmetic and copies ran while one was open for 2% -> 20% of each run, Pallas kernels for 0% -> 0%
where the time goes in v2:
time: 530 us; the launch traced here: 523 us
  waiting for transfers between devices  301 us (57%)
  local copies, waits for them, and re-layouts  77.6 us (15%)
  matrix products  53.6 us (10%)
  starting transfers between devices  49 us (9%)
  blocking collectives  23.5 us (4%)
  between operations  14.2 us (3%)
    all_to_all x4, waiting for transfers between devices, on_device(): held = lax.all_to_all(sent, 'row', 1, 1, tiled=True)  133 us
    ppermute x4, waiting for transfers between devices, on_device(): lax.ppermute(held, 'parts', [(i, (i - turn) % parts) for i in range(parts)])  95.4 us
    all_gather x1, waiting for transfers between devices, on_device(): lax.all_gather(tokens, 'row', axis=0, tiled=True)  62.9 us
    dot_general x8, matrix products, on_device(): up += jnp.dot(features[turn], block[1], preferred_element_type=jnp.float32)  36 us
    all_to_all x4, starting transfers between devices, on_device(): held = lax.all_to_all(sent, 'row', 1, 1, tiled=True)  28.5 us
    all_to_all x1, blocking collectives, on_device(): lax.all_to_all(done.reshape(rows, mine, wide), 'row', 0, 0, tiled=True)  23.5 us
    slice x8, local copies, waits for them, and re-layouts, on_device(): block[0]  18.1 us
    dot_general x8, matrix products, on_device(): jnp.dot(features[turn], block[0], preferred_element_type=jnp.float32)  17.6 us
  transfers between devices with their start and end apart: 13, of which 10 were waited for; matrix products, arithmetic and copies ran while one was open for 20% of the time, Pallas kernels for 0%

profile of v2, /device:TPU:12, one launch (start us, length us, event | category | flops | bytes accessed | tf_op | source)
XLA Modules:
  0.0 522.8 jit_solution(14211771374893272284)
XLA Ops:
  6.5 2.3 copy.26
  8.9 62.9 %all-gather.3.cloned.1.call-done = bf16[1536,1024]{0,1:T(8,128)(2,1)} async-done(((bf16[384,1024]{0,1:T(8,128)(2,1)}), bf16[1536,1024]{0,1:T(8,128)(2,1)}) %all-gather.3.cloned.1.call-update) | async-done | bytes 3145744 | tf_op jit(solution)/shard_map/all_gather | solution.py:26
  71.9 6.6 %constant_dynamic-slice_fusion.1 = (bf16[512,3584]{1,0:T(8,128)(2,1)}, bf16[512,3584]{1,0:T(8,128)(2,1)}) fusion(bf16[1024,3584]{1,0:T(8,128)(2,1)} %param.5, s32[]{:T(128)S(6)} %select_n.24, bf16[1024,3584]{1,0:T(8,128)(2,1)} %param.4), kind=kLoop, calls=%fused_computation.30 | loop fusion | bytes 14680068 | tf_op jit(solution)/shard_map/dynamic_slice | solution.py:34
  78.4 6.1 %copy.47 = bf16[512,3584]{0,1:T(8,128)(2,1)} copy(bf16[512,3584]{1,0:T(8,128)(2,1)} %get-tuple-element.29) | data formatting | bytes 7340032
  84.5 6.1 %copy.46 = bf16[512,3584]{0,1:T(8,128)(2,1)} copy(bf16[512,3584]{1,0:T(8,128)(2,1)} %get-tuple-element.30) | data formatting | bytes 7340032
  90.6 1.1 slice_bitcast_fusion.6
  91.7 1.1 slice_bitcast_fusion.7
  92.9 1.1 copy.41
  94.0 6.0 %all-to-all-start.6 = ((bf16[2,4,512,128]{2,3,0,1:T(8,128)(2,1)}), bf16[2,4,512,128]{2,3,0,1:T(8,128)(2,1)S(1)}, u32[]{:S(2)}, u32[]{:S(2)}) async-start(bf16[2,4,512,128]{2,3,0,1:T(8,128)(2,1)} %copy.41), calls=%async_computation.6 | async-start | bytes 2097152 | tf_op jit(solution)/shard_map/all_to_all | solution.py:42
  100.0 3.3 slice_bitcast_fusion.4
  103.3 1.5 slice_bitcast_fusion.5
  105.0 1.5 copy.37
  106.6 16.1 %all-to-all-done.6 = bf16[2,4,512,128]{2,3,0,1:T(8,128)(2,1)S(1)} async-done(((bf16[2,4,512,128]{2,3,0,1:T(8,128)(2,1)}), bf16[2,4,512,128]{2,3,0,1:T(8,128)(2,1)S(1)}, u32[]{:S(2)}, u32[]{:S(2)}) %all-to-all-start.6) | async-done | bytes 1048608 | tf_op jit(solution)/shard_map/all_to_all | solution.py:42
  122.6 1.0 copy-done.4
  123.7 6.9 %all-to-all-start.4 = ((bf16[2,4,512,256]{2,3,0,1:T(8,128)(2,1)}), bf16[2,4,512,256]{2,3,0,1:T(8,128)(2,1)S(1)}, u32[]{:S(2)}, u32[]{:S(2)}) async-start(bf16[2,4,512,256]{2,3,0,1:T(8,128)(2,1)} %copy.37), calls=%async_computation.4 | async-start | bytes 4194304 | tf_op jit(solution)/shard_map/all_to_all | solution.py:42
  130.5 1.7 pad_maximum_fusion.1
  132.2 1.6 copy.33
  133.8 41.1 %all-to-all-done.4 = bf16[2,4,512,256]{2,3,0,1:T(8,128)(2,1)S(1)} async-done(((bf16[2,4,512,256]{2,3,0,1:T(8,128)(2,1)}), bf16[2,4,512,256]{2,3,0,1:T(8,128)(2,1)S(1)}, u32[]{:S(2)}, u32[]{:S(2)}) %all-to-all-start.4) | async-done | bytes 2097184 | tf_op jit(solution)/shard_map/all_to_all | solution.py:42
  175.0 7.7 %all-to-all-start.2 = ((bf16[2,4,512,256]{2,3,0,1:T(8,128)(2,1)}), bf16[2,4,512,256]{2,3,0,1:T(8,128)(2,1)}, u32[]{:S(2)}, u32[]{:S(2)}) async-start(bf16[2,4,512,256]{2,3,0,1:T(8,128)(2,1)} %copy.33), calls=%async_computation.2 | async-start | bytes 4194304 | tf_op jit(solution)/shard_map/all_to_all | solution.py:42
  182.6 1.4 pad_maximum_fusion
  184.0 1.6 copy.29
  185.6 41.4 %all-to-all-done.2 = bf16[2,4,512,256]{2,3,0,1:T(8,128)(2,1)} async-done(((bf16[2,4,512,256]{2,3,0,1:T(8,128)(2,1)}), bf16[2,4,512,256]{2,3,0,1:T(8,128)(2,1)}, u32[]{:S(2)}, u32[]{:S(2)}) %all-to-all-start.2) | async-done | bytes 2097184 | tf_op jit(solution)/shard_map/all_to_all | solution.py:42
  227.0 8.0 %all-to-all-start = ((bf16[2,4,512,256]{2,3,0,1:T(8,128)(2,1)}), bf16[2,4,512,256]{2,3,0,1:T(8,128)(2,1)}, u32[]{:S(2)}, u32[]{:S(2)}) async-start(bf16[2,4,512,256]{2,3,0,1:T(8,128)(2,1)} %copy.29), calls=%async_computation | async-start | bytes 4194304 | tf_op jit(solution)/shard_map/all_to_all | solution.py:42
  235.0 1.6 copy.42
  237.3 2.3 copy.38
  239.6 1.5 collective-permute-start.2
  241.1 2.8 copy.34
  244.5 34.9 %all-to-all-done = bf16[2,4,512,256]{2,3,0,1:T(8,128)(2,1)} async-done(((bf16[2,4,512,256]{2,3,0,1:T(8,128)(2,1)}), bf16[2,4,512,256]{2,3,0,1:T(8,128)(2,1)}, u32[]{:S(2)}, u32[]{:S(2)}) %all-to-all-start) | async-done | bytes 2097184 | tf_op jit(solution)/shard_map/all_to_all | solution.py:42
  279.4 4.1 copy.30
  284.1 1.1 fusion.15
  285.1 2.1 fusion.14
  287.2 3.0 fusion.13
  290.2 1.5 fusion.11
  292.5 1.5 fusion.9
  294.0 13.8 %collective-permute-done.2 = bf16[2,4,512,256]{3,2,1,0:T(8,128)(2,1)} collective-permute-done((bf16[2,4,512,256]{3,2,1,0:T(8,128)(2,1)}, bf16[2,4,512,256]{3,2,1,0:T(8,128)(2,1)}, u32[]{:S(2)}, u32[]{:S(2)}) %collective-permute-start.2) | collective-permute-done | bytes 2097184 | tf_op jit(solution)/shard_map/ppermute | solution.py:45
  307.9 3.0 fusion.12
  310.9 41.9 %collective-permute-done.1 = bf16[2,4,512,256]{3,2,1,0:T(8,128)(2,1)} collective-permute-done((bf16[2,4,512,256]{3,2,1,0:T(8,128)(2,1)S(1)}, bf16[2,4,512,256]{3,2,1,0:T(8,128)(2,1)}, u32[]{:S(2)}, u32[]{:S(2)}) %collective-permute-start.1) | collective-permute-done | bytes 2097184 | tf_op jit(solution)/shard_map/ppermute | solution.py:45
  352.8 3.0 fusion.10
  355.8 39.7 %collective-permute-done = bf16[2,4,512,256]{3,2,1,0:T(8,128)(2,1)} collective-permute-done((bf16[2,4,512,256]{3,2,1,0:T(8,128)(2,1)}, bf16[2,4,512,256]{3,2,1,0:T(8,128)(2,1)}, u32[]{:S(2)}, u32[]{:S(2)}) %collective-permute-start) | collective-permute-done | bytes 2097184 | tf_op jit(solution)/shard_map/ppermute | solution.py:45
  395.5 3.1 fusion.8
  398.5 10.0 %constant_dynamic-slice_fusion = (bf16[1536,4,1,512]{0,3,2,1:T(8,128)(2,1)}, bf16[1536,4,1,512]{0,3,2,1:T(8,128)(2,1)}) fusion(bf16[1536,4,2,512]{0,3,2,1:T(8,128)(2,1)} %bitcast.117, s32[]{:T(128)S(6)} %select_n.26, s32[]{:T(128)S(6)} %select_n.23), kind=kLoop, calls=%fused_computation.29 | loop fusion | bytes 25165832 | tf_op jit(solution)/shard_map/jit(dynamic_index_in_dim)/dynamic_slice | solution.py:30
  408.6 4.8 fusion.23
  413.4 1.8 fusion.22
  416.1 1.8 convolution_add_fusion.7
  418.0 2.6 fusion.7
  420.6 5.4 %all-to-all-start.7 = ((bf16[4,384,128]{2,1,0:T(8,128)(2,1)}), bf16[4,384,128]{2,1,0:T(8,128)(2,1)S(1)}, u32[]{:S(2)}, u32[]{:S(2)}) async-start(bf16[4,384,128]{2,1,0:T(8,128)(2,1)} %bitcast.136), calls=%async_computation.7 | async-start | bytes 786432 | tf_op jit(solution)/shard_map/all_to_all | solution.py:52
  426.1 4.8 fusion.21
  430.9 1.9 fusion.20
  432.9 1.9 fusion.18
  434.8 1.9 fusion.16
  436.8 1.9 convolution_add_fusion.1
  438.7 3.1 convolution_add_fusion.3
  441.8 3.3 fusion.5
  445.2 3.2 convolution_add_fusion.5
  448.3 5.1 all-to-all-start.5
  453.4 4.8 fusion.19
  458.3 5.9 %fusion.4 = bf16[1536,256]{1,0:T(8,128)(2,1)} fusion(f32[1536,256]{1,0:T(8,128)S(1)} %fusion.19, bf16[1536,2048]{0,1:T(8,128)(2,1)} %bitcast.103, bf16[2048,256]{1,0:T(8,128)(2,1)S(1)} %bitcast.124, f32[1536,256]{1,0:T(8,128)S(1)} %copy-done.21), kind=kOutput, calls=%fused_computation.11 | convolution fusion | flops 1613365248 | bytes 11272192 | tf_op jit(solution)/shard_map/dot_general | solution.py:50
  464.2 3.5 all-to-all-done.5
  467.7 6.7 %all-to-all-start.3 = ((bf16[4,384,256]{2,1,0:T(8,128)(2,1)}), bf16[4,384,256]{2,1,0:T(8,128)(2,1)S(1)}, u32[]{:S(2)}, u32[]{:S(2)}) async-start(bf16[4,384,256]{2,1,0:T(8,128)(2,1)} %bitcast.133), calls=%async_computation.3 | async-start | bytes 1572864 | tf_op jit(solution)/shard_map/all_to_all | solution.py:52
  474.5 4.8 fusion.17
  479.3 4.9 fusion.3
  484.2 5.7 %all-to-all-done.3 = bf16[4,384,256]{2,1,0:T(8,128)(2,1)S(1)} async-done(((bf16[4,384,256]{2,1,0:T(8,128)(2,1)}), bf16[4,384,256]{2,1,0:T(8,128)(2,1)S(1)}, u32[]{:S(2)}, u32[]{:S(2)}) %all-to-all-start.3) | async-done | bytes 786464 | tf_op jit(solution)/shard_map/all_to_all | solution.py:52
  489.9 23.5 %all_to_all.40 = bf16[4,384,256]{2,1,0:T(8,128)(2,1)S(1)} all-to-all(bf16[4,384,256]{2,1,0:T(8,128)(2,1)S(1)} %bitcast.134), channel_id=1, replica_groups=mesh['parts'=2,'row'=4,'col'=4] {'row'}, dimensions={0} | all-to-all | bytes 1572864 | tf_op jit(solution)/shard_map/all_to_all | solution.py:52
  513.7 1.8 copy.48
  (66 shorter events, 4.4 us)
Async XLA Ops:
  6.5 65.3 %all-gather.3.cloned.1.call-start = ((), (), s32[]{:S(2)}) async-start(), calls=%async_computation.8 | async-start | bytes 3932160 | tf_op jit(solution)/shard_map/all_gather | solution.py:26
  8.8 389.7 %all-gather.5.cloned.1.call-start = ((), (), s32[]{:S(2)}) async-start(), calls=%async_computation.9 | async-start | bytes 15728640 | tf_op jit(solution)/shard_map/all_gather | solution.py:26
  94.0 28.6 %all-to-all-start.6 = ((bf16[2,4,512,128]{2,3,0,1:T(8,128)(2,1)}), bf16[2,4,512,128]{2,3,0,1:T(8,128)(2,1)S(1)}, u32[]{:S(2)}, u32[]{:S(2)}) async-start(bf16[2,4,512,128]{2,3,0,1:T(8,128)(2,1)} %copy.41), calls=%async_computation.6 | async-start | bytes 2097152 | tf_op jit(solution)/shard_map/all_to_all | solution.py:42
  100.0 3.3 copy-start.2
  122.6 1.0 copy-start.4
  123.7 51.3 %all-to-all-start.4 = ((bf16[2,4,512,256]{2,3,0,1:T(8,128)(2,1)}), bf16[2,4,512,256]{2,3,0,1:T(8,128)(2,1)S(1)}, u32[]{:S(2)}, u32[]{:S(2)}) async-start(bf16[2,4,512,256]{2,3,0,1:T(8,128)(2,1)} %copy.37), calls=%async_computation.4 | async-start | bytes 4194304 | tf_op jit(solution)/shard_map/all_to_all | solution.py:42
  175.0 52.1 %all-to-all-start.2 = ((bf16[2,4,512,256]{2,3,0,1:T(8,128)(2,1)}), bf16[2,4,512,256]{2,3,0,1:T(8,128)(2,1)}, u32[]{:S(2)}, u32[]{:S(2)}) async-start(bf16[2,4,512,256]{2,3,0,1:T(8,128)(2,1)} %copy.33), calls=%async_computation.2 | async-start | bytes 4194304 | tf_op jit(solution)/shard_map/all_to_all | solution.py:42
  227.0 52.4 %all-to-all-start = ((bf16[2,4,512,256]{2,3,0,1:T(8,128)(2,1)}), bf16[2,4,512,256]{2,3,0,1:T(8,128)(2,1)}, u32[]{:S(2)}, u32[]{:S(2)}) async-start(bf16[2,4,512,256]{2,3,0,1:T(8,128)(2,1)} %copy.29), calls=%async_computation | async-start | bytes 4194304 | tf_op jit(solution)/shard_map/all_to_all | solution.py:42
  236.6 48.5 %collective-permute-start.3 = (bf16[2,4,512,128]{3,2,1,0:T(8,128)(2,1)S(1)}, bf16[2,4,512,128]{3,2,1,0:T(8,128)(2,1)}, u32[]{:S(2)}, u32[]{:S(2)}) collective-permute-start(bf16[2,4,512,128]{3,2,1,0:T(8,128)(2,1)S(1)} %copy.42), channel_id=1, source_target_pairs={{0,16},{16,0},{1,17},{17,1},{2,18},{18,2},{3,19},{19,3},{4,20},{20... | collective-permute-start | bytes 3145736 | tf_op jit(solution)/shard_map/ppermute | solution.py:45
  239.6 68.3 %collective-permute-start.2 = (bf16[2,4,512,256]{3,2,1,0:T(8,128)(2,1)}, bf16[2,4,512,256]{3,2,1,0:T(8,128)(2,1)}, u32[]{:S(2)}, u32[]{:S(2)}) collective-permute-start(bf16[2,4,512,256]{3,2,1,0:T(8,128)(2,1)} %copy.38), channel_id=1, source_target_pairs={{0,16},{16,0},{1,17},{17,1},{2,18},{18,2},{3,19},{19,3},{4,20},{20... | collective-permute-start | bytes 6291464 | tf_op jit(solution)/shard_map/ppermute | solution.py:45
  243.9 108.9 %collective-permute-start.1 = (bf16[2,4,512,256]{3,2,1,0:T(8,128)(2,1)S(1)}, bf16[2,4,512,256]{3,2,1,0:T(8,128)(2,1)}, u32[]{:S(2)}, u32[]{:S(2)}) collective-permute-start(bf16[2,4,512,256]{3,2,1,0:T(8,128)(2,1)S(1)} %copy.34), channel_id=1, source_target_pairs={{0,16},{16,0},{1,17},{17,1},{2,18},{18,2},{3,19},{19,3},{4,20},{20... | collective-permute-start | bytes 6291464 | tf_op jit(solution)/shard_map/ppermute | solution.py:45
  283.5 112.0 %collective-permute-start = (bf16[2,4,512,256]{3,2,1,0:T(8,128)(2,1)}, bf16[2,4,512,256]{3,2,1,0:T(8,128)(2,1)}, u32[]{:S(2)}, u32[]{:S(2)}) collective-permute-start(bf16[2,4,512,256]{3,2,1,0:T(8,128)(2,1)} %copy.30), channel_id=1, source_target_pairs={{0,16},{16,0},{1,17},{17,1},{2,18},{18,2},{3,19},{19,3},{4,20},{20... | collective-permute-start | bytes 6291464 | tf_op jit(solution)/shard_map/ppermute | solution.py:45
  290.2 2.3 copy-start.3
  398.5 10.0 %copy-start.6 = (bf16[1,4,512,128]{3,2,1,0:T(8,128)(2,1)S(1)}, bf16[1,4,512,128]{3,2,1,0:T(8,128)(2,1)}, u32[]{:S(2)}) copy-start(bf16[1,4,512,128]{3,2,1,0:T(8,128)(2,1)} %get-tuple-element.28) | copy-start | bytes 1572868
  408.6 4.8 copy-start
  408.6 4.8 copy-start.5
  413.4 2.8 copy-start.1
  416.1 1.8 copy-start.19
  418.0 8.0 %copy-start.15 = (bf16[1,4,512,256]{3,2,1,0:T(8,128)(2,1)S(1)}, bf16[1,4,512,256]{3,2,1,0:T(8,128)(2,1)}, u32[]{:S(2)}) copy-start(bf16[1,4,512,256]{3,2,1,0:T(8,128)(2,1)} %get-tuple-element.24) | copy-start | bytes 3145732
  420.6 10.3 %slice-start = ((s8[6291456]{0:T(1024)(128)(4,1)}), s8[2097152]{0:T(1024)(128)(4,1)S(1)}, s32[]{:S(2)}) async-start(s8[6291456]{0:T(1024)(128)(4,1)} %bitcast.98), calls=%async_computation.10 | async-start | bytes 4194304
  420.6 27.7 %all-to-all-start.7 = ((bf16[4,384,128]{2,1,0:T(8,128)(2,1)}), bf16[4,384,128]{2,1,0:T(8,128)(2,1)S(1)}, u32[]{:S(2)}, u32[]{:S(2)}) async-start(bf16[4,384,128]{2,1,0:T(8,128)(2,1)} %bitcast.136), calls=%async_computation.7 | async-start | bytes 786432 | tf_op jit(solution)/shard_map/all_to_all | solution.py:52
  426.0 4.9 slice-start.1
  426.0 4.9 copy-start.12
  430.9 1.9 copy-start.11
  432.9 1.9 copy-start.13
  432.9 3.9 slice-start.2
  434.8 1.9 slice-start.3
  434.8 2.0 copy-start.16
  436.8 2.0 copy-start.17
  438.7 3.1 copy-start.14
  441.8 3.3 copy-start.18
  445.2 8.3 %copy-start.8 = (bf16[1,4,512,256]{3,2,1,0:T(8,128)(2,1)S(1)}, bf16[1,4,512,256]{3,2,1,0:T(8,128)(2,1)}, u32[]{:S(2)}) copy-start(bf16[1,4,512,256]{3,2,1,0:T(8,128)(2,1)} %get-tuple-element.20) | copy-start | bytes 3145732
  448.3 19.4 %all-to-all-start.5 = ((bf16[4,384,256]{2,1,0:T(8,128)(2,1)}), bf16[4,384,256]{2,1,0:T(8,128)(2,1)S(1)}, u32[]{:S(2)}, u32[]{:S(2)}) async-start(bf16[4,384,256]{2,1,0:T(8,128)(2,1)} %bitcast.31), calls=%async_computation.5 | async-start | bytes 1572864 | tf_op jit(solution)/shard_map/all_to_all | solution.py:52
  453.4 4.8 copy-start.10
  453.4 4.8 copy-start.21
  458.3 16.2 %copy-start.7 = (bf16[1,4,512,256]{3,2,1,0:T(8,128)(2,1)S(1)}, bf16[1,4,512,256]{3,2,1,0:T(8,128)(2,1)}, u32[]{:S(2)}) copy-start(bf16[1,4,512,256]{3,2,1,0:T(8,128)(2,1)} %get-tuple-element.16) | copy-start | bytes 3145732
  467.7 22.2 %all-to-all-start.3 = ((bf16[4,384,256]{2,1,0:T(8,128)(2,1)}), bf16[4,384,256]{2,1,0:T(8,128)(2,1)S(1)}, u32[]{:S(2)}, u32[]{:S(2)}) async-start(bf16[4,384,256]{2,1,0:T(8,128)(2,1)} %bitcast.133), calls=%async_computation.3 | async-start | bytes 1572864 | tf_op jit(solution)/shard_map/all_to_all | solution.py:52
  474.5 4.8 copy-start.9
  474.5 4.8 copy-start.20
Sparse Core Ops, SparseCore 0:
  9.0 62.8 all-gather.2
  73.4 82.2 all-gather.4

commit v3 on v0

v3 whole, which is shorter than its diff:
```python
import jax
import jax.numpy as jnp
from jax import lax
from jax.experimental import pallas as pl
from jax.experimental.pallas import tpu as pltpu
from jax.sharding import PartitionSpec as P

PIECES = (4, 3)
LANES = 128
ANY = pl.BlockSpec(memory_space=pl.ANY)


def around(size, shift):
    return [(i, (i + shift) % size) for i in range(size)]


def run_all(copies):
    for copy in copies:
        copy.start()
    for copy in copies:
        copy.wait()


def pack(gate_weight, up_weight, shift, low, wide, after):
    depth, ff = gate_weight.shape
    rows, parts = lax.axis_size("row"), lax.axis_size("parts")
    share, width, tiles = depth // parts, ff // rows, wide // LANES

    def body(*refs):
        weights, sent, sems = refs[:2], refs[-2], refs[-1]
        to = lax.rem(lax.axis_index("row") + shift, rows)
        first = pl.multiple_of(lax.axis_index("parts") * share, share)
        copies = []
        for j in range(tiles):
            start = pl.multiple_of(to * width + low + j * LANES, LANES)
            for g, weight in enumerate(weights):
                copies.append(pltpu.make_async_copy(
                    weight.at[pl.ds(first, share), pl.ds(start, LANES)],
                    sent.at[:, pl.ds((2 * j + g) * LANES, LANES)],
                    sems.at[2 * j + g],
                ))
        run_all(copies)

    size = share * 2 * wide * 2
    return pl.pallas_call(
        body,
        out_shape=jax.ShapeDtypeStruct((share, 2 * wide), gate_weight.dtype),
        in_specs=[ANY] * (2 + len(after)),
        out_specs=ANY,
        scratch_shapes=[pltpu.SemaphoreType.DMA((2 * tiles,))],
        cost_estimate=pl.CostEstimate(flops=0, bytes_accessed=2 * size, transcendentals=0),
        name="pack",
    )(gate_weight, up_weight, *after)


def hold(value, after):
    def body(*refs):
        pass

    return pl.pallas_call(
        body,
        out_shape=jax.ShapeDtypeStruct(value.shape, value.dtype),
        in_specs=[ANY] * (1 + len(after)),
        out_specs=ANY,
        input_output_aliases={0: 0},
        name="hold",
    )(value, *after)


def product(tokens, gate_weight, up_weight, held, low, wide, mine, after):
    depth, ff = gate_weight.shape
    rows, parts = lax.axis_size("row"), lax.axis_size("parts")
    share, width, tiles = depth // parts, ff // rows, wide // LANES
    features = rows * depth
    order = list(range(1, rows)) + [0]
    pieces = [(shift, turn) for shift in range(1, rows) for turn in range(parts)]

    def body(tokens_ref, gate_ref, up_ref, *refs):
        held_refs = refs[:len(pieces)]
        outs = refs[len(pieces) + len(after):][:rows]
        stack, block, sems, block_sems = refs[-4:]
        z, y = lax.axis_index("row"), lax.axis_index("parts")

        def fetch(step):
            to = lax.rem(z + order[step], rows)
            return pltpu.make_async_copy(
                tokens_ref.at[pl.ds(pl.multiple_of(to * mine, mine), mine), :],
                block.at[step % 2],
                block_sems.at[step % 2],
            )

        copies = []
        for ref, (shift, turn) in zip(held_refs, pieces):
            came = lax.rem(z + rows - shift, rows)
            half = lax.rem(y + turn, parts)
            start = pl.multiple_of(came * depth + half * share, share)
            copies.append(pltpu.make_async_copy(ref, stack.at[pl.ds(start, share), :], sems.at[len(copies)]))
        own = pl.multiple_of(z * depth, depth)
        for j in range(tiles):
            start = pl.multiple_of(z * width + low + j * LANES, LANES)
            for g, weight in enumerate((gate_ref, up_ref)):
                copies.append(pltpu.make_async_copy(
                    weight.at[:, pl.ds(start, LANES)],
                    stack.at[pl.ds(own, depth), pl.ds((2 * j + g) * LANES, LANES)],
                    sems.at[len(copies)],
                ))
        fetch(0).start()
        run_all(copies)
        for step, shift in enumerate(order):
            fetch(step).wait()
            if step + 1 < rows:
                fetch(step + 1).start()

            def tile(j, carry, step=step, shift=shift):
                both = jnp.dot(
                    block[step % 2],
                    stack[:, pl.ds(pl.multiple_of(j * 2 * LANES, 2 * LANES), 2 * LANES)],
                    preferred_element_type=jnp.float32,
                )
                gate, up = both[:, :LANES], both[:, LANES:]
                outs[shift][:, pl.ds(pl.multiple_of(j * LANES, LANES), LANES)] = (
                    jax.nn.silu(gate) * up
                ).astype(jnp.bfloat16)
                return carry

            lax.fori_loop(0, tiles, tile, 0)

    moved = 2 * (rows * mine * features + features * 2 * wide + rows * mine * wide)
    return pl.pallas_call(
        body,
        out_shape=[jax.ShapeDtypeStruct((mine, wide), jnp.bfloat16)] * rows,
        in_specs=[ANY] * (3 + len(pieces) + len(after)),
        out_specs=[pl.BlockSpec(memory_space=pltpu.VMEM)] * rows,
        scratch_shapes=[
            pltpu.VMEM((features, 2 * wide), gate_weight.dtype),
            pltpu.VMEM((2, mine, features), tokens.dtype),
            pltpu.SemaphoreType.DMA((len(pieces) + 2 * tiles,)),
            pltpu.SemaphoreType.DMA((2,)),
        ],
        compiler_params=pltpu.CompilerParams(vmem_limit_bytes=32 * 2**20),
        cost_estimate=pl.CostEstimate(
            flops=4 * rows * mine * features * wide, bytes_accessed=moved, transcendentals=rows * mine * wide
        ),
        name="product",
    )(tokens, gate_weight, up_weight, *held, *after)


def place(blocks, mine, ff):
    rows = lax.axis_size("row")
    width = ff // rows

    def body(*refs):
        out, sems = refs[-2], refs[-1]
        z = lax.axis_index("row")
        copies = []
        for ref, (shift, low, value) in zip(refs, blocks):
            came = lax.rem(z + rows - shift, rows)
            start = pl.multiple_of(came * width + low, LANES)
            copies.append(pltpu.make_async_copy(
                ref, out.at[:, pl.ds(start, value.shape[1])], sems.at[len(copies)]
            ))
        run_all(copies)

    return pl.pallas_call(
        body,
        out_shape=jax.ShapeDtypeStruct((mine, ff), jnp.bfloat16),
        in_specs=[ANY] * len(blocks),
        out_specs=ANY,
        scratch_shapes=[pltpu.SemaphoreType.DMA((len(blocks),))],
        cost_estimate=pl.CostEstimate(flops=0, bytes_accessed=4 * mine * ff, transcendentals=0),
        name="place",
    )(*[value for _, _, value in blocks])


def in_tiles(tokens, gate_weight, up_weight):
    rows, parts = lax.axis_size("row"), lax.axis_size("parts")
    mine, ff = tokens.shape[0], gate_weight.shape[1]
    width = ff // rows
    units = width // LANES

    block_rows = lax.all_gather(tokens, "row", axis=0, tiled=True)

    edges, total = [0], sum(PIECES)
    for piece in range(len(PIECES)):
        edge = units * sum(PIECES[:piece + 1]) // total * LANES
        if edge > edges[-1]:
            edges.append(edge)
    spans = list(zip(edges[:-1], edges[1:]))

    sent, arrived, swapped, held = [], [], [], []
    for low, high in spans:
        pieces = []
        for shift in range(1, rows):
            sent.append(pack(gate_weight, up_weight, shift, low, high - low, arrived[-2:-1] + swapped[-3:-2]))
            came = lax.ppermute(sent[-1], "row", around(rows, shift))
            arrived.append(came)
            pieces.append(came)
            for turn in range(1, parts):
                swapped.append(lax.ppermute(came, "parts", around(parts, -turn)))
                pieces.append(swapped[-1])
        held.append(pieces)

    whole = lax.all_gather(hold(block_rows, sent[2:3]), "col", axis=1, tiled=True)
    blocks, after = [], sent[-1:]
    for pieces, (low, high) in zip(held, spans):
        outs = product(whole, gate_weight, up_weight, pieces, low, high - low, mine, after)
        after = outs[:1]
        for shift in range(rows):
            value = lax.ppermute(outs[shift], "row", around(rows, shift)) if shift else outs[shift]
            blocks.append((shift, low, value))
    return place(blocks, mine, ff)


def at_once(tokens, gate_weight, up_weight):
    rows, parts = lax.axis_size("row"), lax.axis_size("parts")
    y = lax.axis_index("parts")
    mine, ff = tokens.shape[0], gate_weight.shape[1]
    depth = gate_weight.shape[0]
    share, width = depth // parts, ff // rows

    whole = lax.all_gather(lax.all_gather(tokens, "row", axis=0, tiled=True), "col", axis=1, tiled=True)
    everyone = whole.shape[0]
    by_share = whole.reshape(everyone, rows, parts, share)
    sent = jnp.stack([
        lax.dynamic_slice(w, (y * share, 0), (share, ff)).reshape(share, rows, width).transpose(1, 0, 2)
        for w in (gate_weight, up_weight)
    ])
    held = lax.all_to_all(sent, "row", 1, 1, tiled=True)
    gate = up = 0.0
    for turn in range(parts):
        features = lax.dynamic_index_in_dim(by_share, (y + turn) % parts, 2, keepdims=False)
        features = features.reshape(everyone, rows * share)
        block = lax.ppermute(held, "parts", around(parts, -turn)) if turn else held
        block = block.reshape(2, rows * share, width)
        gate += jnp.dot(features, block[0], preferred_element_type=jnp.float32)
        up += jnp.dot(features, block[1], preferred_element_type=jnp.float32)
    done = (jax.nn.silu(gate) * up).astype(jnp.bfloat16)
    back = lax.all_to_all(done.reshape(rows, mine, width), "row", 0, 0, tiled=True)
    return back.transpose(1, 0, 2).reshape(mine, ff)


def on_device(tokens, gate_weight, up_weight):
    rows, parts = lax.axis_size("row"), lax.axis_size("parts")
    aligned = (
        gate_weight.shape[1] % (rows * LANES) == 0
        and gate_weight.shape[0] % (parts * 16) == 0
        and tokens.shape[0] % 16 == 0
    )
    return (in_tiles if aligned else at_once)(tokens, gate_weight, up_weight)


def solution(mesh):
    placed = (P(("parts", "row"), "col"), P("row", "col"), P("row", "col"))
    return jax.shard_map(
        on_device, mesh=mesh, in_specs=placed, out_specs=P(("parts", "row"), "col"), check_vma=False
    )
```

time: 1050 us -> 546 us (0.52)
  waiting for transfers between devices: 998 us -> 202 us
  Pallas kernels: 0 us -> 294 us
  matrix products: 38.6 us -> 0 us
  starting transfers between devices: 0.08 us -> 25.4 us
  local copies, waits for them, and re-layouts: 0.01 us -> 11 us
    all_gather x3 -> x2, waiting for transfers between devices: 995 us -> 0.02 us  [the longest x1 0.02 us: in_tiles(): block_rows = lax.all_gather(tokens, 'row', axis=0, tiled=True)]
    pallas_call x0 -> x10, Pallas kernels: none -> 294 us  [the longest x6 174 us: pack(): pl.pallas_call(body, out_shape=jax.ShapeDtypeStruct((share, 2 * wide), ga...]
    ppermute x0 -> x18, waiting for transfers between devices: none -> 201 us  [the longest x6 140 us: in_tiles(): came = lax.ppermute(sent[-1], 'row', around(rows, shift))]
    dot_general x2 -> x0, matrix products: 38.6 us -> none  [part_product(): return jnp.dot(whole, piece, preferred_element_type=jnp.float32)]
    ppermute x0 -> x18, starting transfers between devices: none -> 25.3 us  [the longest x6 11 us: in_tiles(): came = lax.ppermute(sent[-1], 'row', around(rows, shift))]
    unnamed x2 -> x34, local copies, waits for them, and re-layouts: 0.01 us -> 11 us
  transfers between devices with their start and end apart: 3 -> 20, of which waited for: 3 -> 8; matrix products, arithmetic and copies ran while one was open for 2% -> 0% of each run, Pallas kernels for 0% -> 36%
where the time goes in v3:
time: 546 us; the launch traced here: 545 us
  Pallas kernels  294 us (54%)
  waiting for transfers between devices  202 us (37%)
  starting transfers between devices  25.4 us (5%)
  between operations  13.7 us (3%)
  local copies, waits for them, and re-layouts  11 us (2%)
    pallas_call x6, Pallas kernels, pack(): pl.pallas_call(body, out_shape=jax.ShapeDtypeStruct((share, 2 * wide), ga...  174 us
    ppermute x6, waiting for transfers between devices, in_tiles(): came = lax.ppermute(sent[-1], 'row', around(rows, shift))  140 us
    pallas_call x1, Pallas kernels, place(): pl.pallas_call(body, out_shape=jax.ShapeDtypeStruct((mine, ff), jnp.bfloa...  84.6 us
    ppermute x6, waiting for transfers between devices, in_tiles(): lax.ppermute(outs[shift], 'row', around(rows, shift))  51.3 us
    pallas_call x2, Pallas kernels, product(): pl.pallas_call(body, out_shape=[jax.ShapeDtypeStruct((mine, wide), jnp.bf...  35.2 us
    unnamed x34, local copies, waits for them, and re-layouts  11 us
    ppermute x6, starting transfers between devices, in_tiles(): came = lax.ppermute(sent[-1], 'row', around(rows, shift))  11 us
  transfers between devices with their start and end apart: 20, of which 8 were waited for; matrix products, arithmetic and copies ran while one was open for 0% of the time, Pallas kernels for 36%

profile of v3, /device:TPU:12, one launch (start us, length us, event | category | flops | bytes accessed | tf_op | source)
XLA Modules:
  0.0 545.2 jit_solution(7017135919670027116)
XLA Ops:
  6.5 0.0 all-gather.3.cloned.1.call-start
  6.5 0.7 all-gather.3.cloned.1.call-update
  7.3 0.0 all-gather.5.cloned.1.call-start
  7.3 33.0 %pack.6 = bf16[512,1024]{1,0:T(8,128)(2,1)} custom-call(bf16[1024,3584]{1,0:T(8,128)(2,1)} %gate_ref.3, bf16[1024,3584]{1,0:T(8,128)(2,1)} %up_ref.3), custom_call_target="tpu_custom_call" | custom-call | bytes 2097152 | tf_op jit(solution)/shard_map/pack/pallas_call | solution.py:45
  40.3 1.6 collective-permute-start
  41.9 50.3 %collective-permute-done.refs_2_.refs_0_ = bf16[512,1024]{1,0:T(8,128)(2,1)S(1)} collective-permute-done((bf16[512,1024]{1,0:T(8,128)(2,1)}, bf16[512,1024]{1,0:T(8,128)(2,1)S(1)}, u32[]{:S(2)}, u32[]{:S(2)}) %collective-permute-start) | collective-permute-done | bytes 1048608 | tf_op jit(solution)/shard_map/ppermute | solution.py:195
  92.2 1.0 copy-done.2
  93.1 32.9 %pack.7.refs_1_ = bf16[512,1024]{1,0:T(8,128)(2,1)} custom-call(bf16[1024,3584]{1,0:T(8,128)(2,1)} %gate_ref.3, bf16[1024,3584]{1,0:T(8,128)(2,1)} %up_ref.3, bf16[512,1024]{1,0:T(8,128)(2,1)} %copy-done.2), custom_call_target="tpu_custom_call" | custom-call | bytes 2097152 | tf_op jit(solution)/shard_map/pack/pallas_call | solution.py:45
  126.1 0.0 all-gather.3.cloned.1.call-done.refs_0_
  126.1 0.0 all-gather.5.cloned.1.call-update
  126.1 0.0 copy-start.3
  126.1 33.0 %pack.8 = bf16[512,1024]{1,0:T(8,128)(2,1)} custom-call(bf16[1024,3584]{1,0:T(8,128)(2,1)} %gate_ref.3, bf16[1024,3584]{1,0:T(8,128)(2,1)} %up_ref.3), custom_call_target="tpu_custom_call" | custom-call | bytes 2097152 | tf_op jit(solution)/shard_map/pack/pallas_call | solution.py:45
  159.1 3.2 collective-permute-start.2
  162.3 0.7 collective-permute-start.4
  163.0 0.0 copy-done.3
  163.0 0.3 collective-permute-start.1
  163.3 66.7 %collective-permute-done.2.refs_2_ = bf16[512,1024]{1,0:T(8,128)(2,1)S(1)} collective-permute-done((bf16[512,1024]{1,0:T(8,128)(2,1)}, bf16[512,1024]{1,0:T(8,128)(2,1)S(1)}, u32[]{:S(2)}, u32[]{:S(2)}) %collective-permute-start.2) | collective-permute-done | bytes 1048608 | tf_op jit(solution)/shard_map/ppermute | solution.py:195
  230.1 0.4 collective-permute-start.3
  230.5 0.0 collective-permute-done.4.refs_4_.refs_2_
  230.5 1.6 collective-permute-start.5
  232.1 0.0 collective-permute-done.1.refs_3_.refs_1_
  232.1 1.0 copy-done.6
  233.1 25.0 %pack.9 = bf16[512,768]{1,0:T(8,128)(2,1)} custom-call(bf16[1024,3584]{1,0:T(8,128)(2,1)} %gate_ref.3, bf16[1024,3584]{1,0:T(8,128)(2,1)} %up_ref.3, bf16[512,1024]{1,0:T(8,128)(2,1)} %copy-done.4, bf16[512,1024]{1,0:T(8,128)(2,1)} %copy-done.6), custom_call_target="tpu_custom_call" | custom-call | bytes 1572864 | tf_op jit(solution)/shard_map/pack/pallas_call | solution.py:45
  258.1 0.1 collective-permute-start.6
  258.1 0.0 collective-permute-done.3.refs_3_
  258.1 25.0 %pack.11 = bf16[512,768]{1,0:T(8,128)(2,1)} custom-call(bf16[1024,3584]{1,0:T(8,128)(2,1)} %gate_ref.3, bf16[1024,3584]{1,0:T(8,128)(2,1)} %up_ref.3, bf16[512,1024]{1,0:T(8,128)(2,1)} %collective-permute-done.4.refs_4_.refs_2_, bf16[512,1024]{1,0:T(8,128)(2,1)} %collective-permute-done.3.refs_3_), custom_call_target="tpu_custom_call" | custom-call | bytes 1572864 | tf_op jit(solution)/shard_map/pack/pallas_call | solution.py:45
  283.1 0.0 copy-start.7
  283.2 3.3 collective-permute-start.11
  286.5 0.0 collective-permute-done.6.refs_2_.refs_0_
  286.5 0.0 collective-permute-done.5.refs_3_.refs_5_
  286.5 25.0 %pack.10.refs_6_ = bf16[512,768]{1,0:T(8,128)(2,1)} custom-call(bf16[1024,3584]{1,0:T(8,128)(2,1)} %gate_ref.3, bf16[1024,3584]{1,0:T(8,128)(2,1)} %up_ref.3, bf16[512,768]{1,0:T(8,128)(2,1)} %collective-permute-done.6.refs_2_.refs_0_, bf16[512,1024]{1,0:T(8,128)(2,1)} %collective-permute-done.5.refs_3_.refs_5_), custom_call_target="tpu_custom_call" | custom-call | bytes 1572864 | tf_op jit(solution)/shard_map/pack/pallas_call | solution.py:45
  311.5 2.0 collective-permute-start.13
  313.5 0.4 collective-permute-start.10
  313.9 22.9 %collective-permute-done.11.refs_2_ = bf16[512,768]{1,0:T(8,128)(2,1)} collective-permute-done((bf16[512,768]{1,0:T(8,128)(2,1)}, bf16[512,768]{1,0:T(8,128)(2,1)}, u32[]{:S(2)}, u32[]{:S(2)}) %collective-permute-start.11) | collective-permute-done | bytes 786464 | tf_op jit(solution)/shard_map/ppermute | solution.py:195
  336.8 0.5 collective-permute-start.12
  337.3 0.2 collective-permute-done.13.refs_4_
  337.6 1.2 collective-permute-start.14
  338.8 3.1 copy-done
  341.9 1.1 copy-done.8
  343.1 19.8 %product.2 = (bf16[384,512]{1,0:T(8,128)(2,1)S(1)}, bf16[384,512]{1,0:T(8,128)(2,1)S(1)}, bf16[384,512]{1,0:T(8,128)(2,1)S(1)}, bf16[384,512]{1,0:T(8,128)(2,1)S(1)}) custom-call(bf16[1536,4096]{1,0:T(8,128)(2,1)} %all-gather.5.cloned.1.call-done.tokens_ref, bf16[1024,3584]{1,0:T(8,128)(2,1)S(1)} %copy-done, bf16[1024,3584]{1,0:T(8,128)(2,1)} %up_ref.3, ...), custom_call_target="tpu_custom_call" | custom-call | flops 12884901888 | bytes 22544384 | tf_op jit(solution)/shard_map/product/pallas_call | solution.py:129
  362.8 0.0 copy-start.9
  362.9 0.0 collective-permute-done.10.refs_1_
  362.9 0.0 collective-permute-done.12.refs_3_
  362.9 9.3 %collective-permute-done.14.refs_5_ = bf16[512,768]{1,0:T(8,128)(2,1)} collective-permute-done((bf16[512,768]{1,0:T(8,128)(2,1)}, bf16[512,768]{1,0:T(8,128)(2,1)}, u32[]{:S(2)}, u32[]{:S(2)}) %collective-permute-start.14) | collective-permute-done | bytes 786464 | tf_op jit(solution)/shard_map/ppermute | solution.py:199
  372.2 3.1 copy-done.1
  375.3 15.4 %product.3 = (bf16[384,384]{1,0:T(8,128)(2,1)S(1)}, bf16[384,384]{1,0:T(8,128)(2,1)S(1)}, bf16[384,384]{1,0:T(8,128)(2,1)S(1)}, bf16[384,384]{1,0:T(8,128)(2,1)S(1)}) custom-call(bf16[1536,4096]{1,0:T(8,128)(2,1)} %all-gather.5.cloned.1.call-done.tokens_ref, bf16[1024,3584]{1,0:T(8,128)(2,1)S(1)} %copy-done, bf16[1024,3584]{1,0:T(8,128)(2,1)S(1)} %copy-done.1, ...), custom_call_target="tpu_custom_call" | custom-call | flops 9663676416 | bytes 20054016 | tf_op jit(solution)/shard_map/product/pallas_call | solution.py:129
  390.8 0.7 copy-done.10
  391.5 0.0 collective-permute-start.15
  391.5 3.9 collective-permute-start.7
  395.4 0.4 collective-permute-start.8
  395.9 1.1 collective-permute-start.9
  396.9 1.4 collective-permute-start.16
  398.3 3.1 collective-permute-done.15.refs_5_
  401.4 3.0 collective-permute-start.17
  404.4 44.3 %collective-permute-done.16.refs_6_ = bf16[384,384]{1,0:T(8,128)(2,1)S(1)} collective-permute-done((bf16[384,384]{1,0:T(8,128)(2,1)S(1)}, bf16[384,384]{1,0:T(8,128)(2,1)S(1)}, u32[]{:S(2)}, u32[]{:S(2)}) %collective-permute-start.16) | collective-permute-done | bytes 294944 | tf_op jit(solution)/shard_map/ppermute | solution.py:209
  448.7 3.9 collective-permute-done.17.refs_7_
  452.7 0.0 collective-permute-done.7.refs_1_
  452.7 0.0 collective-permute-done.8.refs_2_
  452.7 0.0 collective-permute-done.9.refs_3_
  452.7 0.7 copy-done.16
  453.4 0.1 copy-done.11
  453.5 0.2 copy-done.12
  453.7 0.1 copy-done.13
  453.8 84.6 %place.1 = bf16[384,3584]{1,0:T(8,128)(2,1)} custom-call(bf16[384,512]{1,0:T(8,128)(2,1)} %copy-done.9, bf16[384,512]{1,0:T(8,128)(2,1)} %copy-done.11, bf16[384,512]{1,0:T(8,128)(2,1)} %copy-done.12, bf16[384,512]{1,0:T(8,128)(2,1)} %copy-done.13, bf16[384,384]{1,0:T(8,128)(2,1)} %copy-done.10, bf16[384,384]{1,0:T(8,128)(2,1)} %copy-done.14, ...), custom_call_target="tpu_custom_call" | custom-call | bytes 5505024 | tf_op jit(solution)/shard_map/place/pallas_call | solution.py:164
  (22 shorter events, 0.0 us)
Async XLA Ops:
  6.5 119.6 %all-gather.3.cloned.1.call-start = ((), (), s32[]{:S(2)}) async-start(), calls=%async_computation | async-start | bytes 3932160 | tf_op jit(solution)/shard_map/all_gather | solution.py:181
  7.3 331.6 %all-gather.5.cloned.1.call-start = ((), (), s32[]{:S(2)}) async-start(), calls=%async_computation.1 | async-start | bytes 15728640 | tf_op jit(solution)/shard_map/all_gather | solution.py:203
  40.3 51.9 %collective-permute-start = (bf16[512,1024]{1,0:T(8,128)(2,1)}, bf16[512,1024]{1,0:T(8,128)(2,1)S(1)}, u32[]{:S(2)}, u32[]{:S(2)}) collective-permute-start(bf16[512,1024]{1,0:T(8,128)(2,1)} %pack.6), channel_id=1, source_target_pairs={{0,4},{4,8},{8,12},{12,0},{1,5},{5,9},{9,13},{13,1},{2,6},{6,10},{... | collective-permute-start | bytes 3145736 | tf_op jit(solution)/shard_map/ppermute | solution.py:195
  92.2 1.0 copy-start.2
  126.1 36.9 %copy-start.3 = (bf16[512,1024]{1,0:T(8,128)(2,1)S(1)}, bf16[512,1024]{1,0:T(8,128)(2,1)}, u32[]{:S(2)}) copy-start(bf16[512,1024]{1,0:T(8,128)(2,1)} %copy-done.2) | copy-start | bytes 3145732
  159.1 71.0 %collective-permute-start.2 = (bf16[512,1024]{1,0:T(8,128)(2,1)}, bf16[512,1024]{1,0:T(8,128)(2,1)S(1)}, u32[]{:S(2)}, u32[]{:S(2)}) collective-permute-start(bf16[512,1024]{1,0:T(8,128)(2,1)} %pack.8), channel_id=1, source_target_pairs={{0,8},{4,12},{8,0},{12,4},{1,9},{5,13},{9,1},{13,5},{2,10},{6,14},... | collective-permute-start | bytes 3145736 | tf_op jit(solution)/shard_map/ppermute | solution.py:195
  162.3 68.2 %collective-permute-start.4 = (bf16[512,1024]{1,0:T(8,128)(2,1)}, bf16[512,1024]{1,0:T(8,128)(2,1)}, u32[]{:S(2)}, u32[]{:S(2)}) collective-permute-start(bf16[512,1024]{1,0:T(8,128)(2,1)} %pack.7.refs_1_), channel_id=1, source_target_pairs={{0,12},{4,0},{8,4},{12,8},{1,13},{5,1},{9,5},{13,9},{2,14},{6,2},{... | collective-permute-start | bytes 3145736 | tf_op jit(solution)/shard_map/ppermute | solution.py:195
  163.0 69.1 %collective-permute-start.1 = (bf16[512,1024]{1,0:T(8,128)(2,1)S(1)}, bf16[512,1024]{1,0:T(8,128)(2,1)S(1)}, u32[]{:S(2)}, u32[]{:S(2)}) collective-permute-start(bf16[512,1024]{1,0:T(8,128)(2,1)S(1)} %copy-done.3), channel_id=1, source_target_pairs={{0,16},{16,0},{1,17},{17,1},{2,18},{18,2},{3,19},{19,3},{4,20},{20... | collective-permute-start | bytes 3145736 | tf_op jit(solution)/shard_map/ppermute | solution.py:199
  230.1 2.0 copy-start.4
  230.1 28.1 %collective-permute-start.3 = (bf16[512,1024]{1,0:T(8,128)(2,1)S(1)}, bf16[512,1024]{1,0:T(8,128)(2,1)}, u32[]{:S(2)}, u32[]{:S(2)}) collective-permute-start(bf16[512,1024]{1,0:T(8,128)(2,1)S(1)} %collective-permute-done.2.refs_2_), channel_id=1, source_target_pairs={{0,16},{16,0},{1,17},{17,1},{2,18},{18,2},{3,19},{19,3},{4,20},{20... | collective-permute-start | bytes 3145736 | tf_op jit(solution)/shard_map/ppermute | solution.py:199
  230.5 56.0 %collective-permute-start.5 = (bf16[512,1024]{1,0:T(8,128)(2,1)}, bf16[512,1024]{1,0:T(8,128)(2,1)}, u32[]{:S(2)}, u32[]{:S(2)}) collective-permute-start(bf16[512,1024]{1,0:T(8,128)(2,1)} %collective-permute-done.4.refs_4_.refs_2_), channel_id=1, source_target_pairs={{0,16},{16,0},{1,17},{17,1},{2,18},{18,2},{3,19},{19,3},{4,20},{20... | collective-permute-start | bytes 3145736 | tf_op jit(solution)/shard_map/ppermute | solution.py:199
  232.1 1.0 copy-start.6
  258.1 28.4 %collective-permute-start.6 = (bf16[512,768]{1,0:T(8,128)(2,1)}, bf16[512,768]{1,0:T(8,128)(2,1)}, u32[]{:S(2)}, u32[]{:S(2)}) collective-permute-start(bf16[512,768]{1,0:T(8,128)(2,1)} %pack.9), channel_id=1, source_target_pairs={{0,4},{4,8},{8,12},{12,0},{1,5},{5,9},{9,13},{13,1},{2,6},{6,10},{... | collective-permute-start | bytes 2359304 | tf_op jit(solution)/shard_map/ppermute | solution.py:195
  283.1 55.7 %copy-start.5 = (bf16[512,1024]{1,0:T(8,128)(2,1)S(1)}, bf16[512,1024]{1,0:T(8,128)(2,1)}, u32[]{:S(2)}) copy-start(bf16[512,1024]{1,0:T(8,128)(2,1)} %copy-done.4) | copy-start | bytes 3145732
  283.1 55.7 %copy-start.7 = (bf16[512,1024]{1,0:T(8,128)(2,1)S(1)}, bf16[512,1024]{1,0:T(8,128)(2,1)}, u32[]{:S(2)}) copy-start(bf16[512,1024]{1,0:T(8,128)(2,1)} %copy-done.6) | copy-start | bytes 3145732
  283.2 53.6 %collective-permute-start.11 = (bf16[512,768]{1,0:T(8,128)(2,1)}, bf16[512,768]{1,0:T(8,128)(2,1)}, u32[]{:S(2)}, u32[]{:S(2)}) collective-permute-start(bf16[512,768]{1,0:T(8,128)(2,1)} %pack.11), channel_id=1, source_target_pairs={{0,8},{4,12},{8,0},{12,4},{1,9},{5,13},{9,1},{13,5},{2,10},{6,14},... | collective-permute-start | bytes 2359304 | tf_op jit(solution)/shard_map/ppermute | solution.py:195
  311.5 26.1 %collective-permute-start.13 = (bf16[512,768]{1,0:T(8,128)(2,1)}, bf16[512,768]{1,0:T(8,128)(2,1)}, u32[]{:S(2)}, u32[]{:S(2)}) collective-permute-start(bf16[512,768]{1,0:T(8,128)(2,1)} %pack.10.refs_6_), channel_id=1, source_target_pairs={{0,12},{4,0},{8,4},{12,8},{1,13},{5,1},{9,5},{13,9},{2,14},{6,2},{... | collective-permute-start | bytes 2359304 | tf_op jit(solution)/shard_map/ppermute | solution.py:195
  313.5 49.3 %collective-permute-start.10 = (bf16[512,768]{1,0:T(8,128)(2,1)}, bf16[512,768]{1,0:T(8,128)(2,1)}, u32[]{:S(2)}, u32[]{:S(2)}) collective-permute-start(bf16[512,768]{1,0:T(8,128)(2,1)} %collective-permute-done.6.refs_2_.refs_0_), channel_id=1, source_target_pairs={{0,16},{16,0},{1,17},{17,1},{2,18},{18,2},{3,19},{19,3},{4,20},{20... | collective-permute-start | bytes 2359304 | tf_op jit(solution)/shard_map/ppermute | solution.py:199
  336.8 26.1 %collective-permute-start.12 = (bf16[512,768]{1,0:T(8,128)(2,1)}, bf16[512,768]{1,0:T(8,128)(2,1)}, u32[]{:S(2)}, u32[]{:S(2)}) collective-permute-start(bf16[512,768]{1,0:T(8,128)(2,1)} %collective-permute-done.11.refs_2_), channel_id=1, source_target_pairs={{0,16},{16,0},{1,17},{17,1},{2,18},{18,2},{3,19},{19,3},{4,20},{20... | collective-permute-start | bytes 2359304 | tf_op jit(solution)/shard_map/ppermute | solution.py:199
  337.6 34.6 %collective-permute-start.14 = (bf16[512,768]{1,0:T(8,128)(2,1)}, bf16[512,768]{1,0:T(8,128)(2,1)}, u32[]{:S(2)}, u32[]{:S(2)}) collective-permute-start(bf16[512,768]{1,0:T(8,128)(2,1)} %collective-permute-done.13.refs_4_), channel_id=1, source_target_pairs={{0,16},{16,0},{1,17},{17,1},{2,18},{18,2},{3,19},{19,3},{4,20},{20... | collective-permute-start | bytes 2359304 | tf_op jit(solution)/shard_map/ppermute | solution.py:199
  338.8 3.1 copy-start
  341.9 1.1 copy-start.8
  362.8 27.9 %copy-start.9 = (bf16[384,512]{1,0:T(8,128)(2,1)}, bf16[384,512]{1,0:T(8,128)(2,1)S(1)}, u32[]{:S(2)}) copy-start(bf16[384,512]{1,0:T(8,128)(2,1)S(1)} %get-tuple-element.13.refs_6_.refs_0_) | copy-start | bytes 1179652
  372.2 3.1 copy-start.1
  390.8 0.7 copy-start.10
  391.5 9.9 %collective-permute-start.15 = (bf16[384,384]{1,0:T(8,128)(2,1)S(1)}, bf16[384,384]{1,0:T(8,128)(2,1)S(1)}, u32[]{:S(2)}, u32[]{:S(2)}) collective-permute-start(bf16[384,384]{1,0:T(8,128)(2,1)S(1)} %get-tuple-element.18), channel_id=1, source_target_pairs={{0,4},{4,8},{8,12},{12,0},{1,5},{5,9},{9,13},{13,1},{2,6},{6,10},{... | collective-permute-start | bytes 884744 | tf_op jit(solution)/shard_map/ppermute | solution.py:209
  391.5 61.2 %collective-permute-start.7 = (bf16[384,512]{1,0:T(8,128)(2,1)S(1)}, bf16[384,512]{1,0:T(8,128)(2,1)S(1)}, u32[]{:S(2)}, u32[]{:S(2)}) collective-permute-start(bf16[384,512]{1,0:T(8,128)(2,1)S(1)} %get-tuple-element.14), channel_id=1, source_target_pairs={{0,4},{4,8},{8,12},{12,0},{1,5},{5,9},{9,13},{13,1},{2,6},{6,10},{... | collective-permute-start | bytes 1179656 | tf_op jit(solution)/shard_map/ppermute | solution.py:209
  395.4 57.3 %collective-permute-start.8 = (bf16[384,512]{1,0:T(8,128)(2,1)S(1)}, bf16[384,512]{1,0:T(8,128)(2,1)S(1)}, u32[]{:S(2)}, u32[]{:S(2)}) collective-permute-start(bf16[384,512]{1,0:T(8,128)(2,1)S(1)} %get-tuple-element.15), channel_id=1, source_target_pairs={{0,8},{4,12},{8,0},{12,4},{1,9},{5,13},{9,1},{13,5},{2,10},{6,14},... | collective-permute-start | bytes 1179656 | tf_op jit(solution)/shard_map/ppermute | solution.py:209
  395.9 56.8 %collective-permute-start.9 = (bf16[384,512]{1,0:T(8,128)(2,1)S(1)}, bf16[384,512]{1,0:T(8,128)(2,1)S(1)}, u32[]{:S(2)}, u32[]{:S(2)}) collective-permute-start(bf16[384,512]{1,0:T(8,128)(2,1)S(1)} %get-tuple-element.16), channel_id=1, source_target_pairs={{0,12},{4,0},{8,4},{12,8},{1,13},{5,1},{9,5},{13,9},{2,14},{6,2},{... | collective-permute-start | bytes 1179656 | tf_op jit(solution)/shard_map/ppermute | solution.py:209
  396.9 51.8 %collective-permute-start.16 = (bf16[384,384]{1,0:T(8,128)(2,1)S(1)}, bf16[384,384]{1,0:T(8,128)(2,1)S(1)}, u32[]{:S(2)}, u32[]{:S(2)}) collective-permute-start(bf16[384,384]{1,0:T(8,128)(2,1)S(1)} %get-tuple-element.19), channel_id=1, source_target_pairs={{0,8},{4,12},{8,0},{12,4},{1,9},{5,13},{9,1},{13,5},{2,10},{6,14},... | collective-permute-start | bytes 884744 | tf_op jit(solution)/shard_map/ppermute | solution.py:209
  401.4 51.3 %copy-start.14 = (bf16[384,384]{1,0:T(8,128)(2,1)}, bf16[384,384]{1,0:T(8,128)(2,1)S(1)}, u32[]{:S(2)}) copy-start(bf16[384,384]{1,0:T(8,128)(2,1)S(1)} %collective-permute-done.15.refs_5_) | copy-start | bytes 884740
  401.4 51.2 %collective-permute-start.17 = (bf16[384,384]{1,0:T(8,128)(2,1)S(1)}, bf16[384,384]{1,0:T(8,128)(2,1)S(1)}, u32[]{:S(2)}, u32[]{:S(2)}) collective-permute-start(bf16[384,384]{1,0:T(8,128)(2,1)S(1)} %get-tuple-element.20), channel_id=1, source_target_pairs={{0,12},{4,0},{8,4},{12,8},{1,13},{5,1},{9,5},{13,9},{2,14},{6,2},{... | collective-permute-start | bytes 884744 | tf_op jit(solution)/shard_map/ppermute | solution.py:209
  448.7 4.0 copy-start.15
  452.7 0.7 copy-start.16
  452.7 0.9 copy-start.11
  452.7 1.0 copy-start.12
  452.7 1.1 copy-start.13
Sparse Core Ops, SparseCore 0:
  8.9 84.5 all-gather.2
  126.3 83.6 all-gather.4

commit v4 on v3

--- a/solution.py
+++ b/solution.py
@@ -5,7 +5,8 @@
 from jax.experimental.pallas import tpu as pltpu
 from jax.sharding import PartitionSpec as P
 
-PIECES = (4, 3)
+PIECES = (3, 2, 2)
+GRANT = 60 * 2**20
 LANES = 128
 ANY = pl.BlockSpec(memory_space=pl.ANY)
 
@@ -46,8 +47,9 @@
         body,
         out_shape=jax.ShapeDtypeStruct((share, 2 * wide), gate_weight.dtype),
         in_specs=[ANY] * (2 + len(after)),
-        out_specs=ANY,
+        out_specs=pl.BlockSpec(memory_space=pltpu.VMEM),
         scratch_shapes=[pltpu.SemaphoreType.DMA((2 * tiles,))],
+        compiler_params=pltpu.CompilerParams(vmem_limit_bytes=GRANT),
         cost_estimate=pl.CostEstimate(flops=0, bytes_accessed=2 * size, transcendentals=0),
         name="pack",
     )(gate_weight, up_weight, *after)
@@ -137,7 +139,7 @@
             pltpu.SemaphoreType.DMA((len(pieces) + 2 * tiles,)),
             pltpu.SemaphoreType.DMA((2,)),
         ],
-        compiler_params=pltpu.CompilerParams(vmem_limit_bytes=32 * 2**20),
+        compiler_params=pltpu.CompilerParams(vmem_limit_bytes=GRANT),
         cost_estimate=pl.CostEstimate(
             flops=4 * rows * mine * features * wide, bytes_accessed=moved, transcendentals=rows * mine * wide
         ),
@@ -165,8 +167,9 @@
         body,
         out_shape=jax.ShapeDtypeStruct((mine, ff), jnp.bfloat16),
         in_specs=[ANY] * len(blocks),
-        out_specs=ANY,
+        out_specs=pl.BlockSpec(memory_space=pltpu.VMEM),
         scratch_shapes=[pltpu.SemaphoreType.DMA((len(blocks),))],
+        compiler_params=pltpu.CompilerParams(vmem_limit_bytes=GRANT),
         cost_estimate=pl.CostEstimate(flops=0, bytes_accessed=4 * mine * ff, transcendentals=0),
         name="place",
     )(*[value for _, _, value in blocks])
@@ -191,7 +194,7 @@
     for low, high in spans:
         pieces = []
         for shift in range(1, rows):
-            sent.append(pack(gate_weight, up_weight, shift, low, high - low, arrived[-2:-1] + swapped[-3:-2]))
+            sent.append(pack(gate_weight, up_weight, shift, low, high - low, sent[-1:] + arrived[-2:-1] + swapped[-3:-2]))
             came = lax.ppermute(sent[-1], "row", around(rows, shift))
             arrived.append(came)
             pieces.append(came)
@@ -200,14 +203,14 @@
                 pieces.append(swapped[-1])
         held.append(pieces)
 
-    whole = lax.all_gather(hold(block_rows, sent[2:3]), "col", axis=1, tiled=True)
-    blocks, after = [], sent[-1:]
+    whole = lax.all_gather(hold(block_rows, arrived[1:2]), "col", axis=1, tiled=True)
+    blocks, done, returned = [], [], [[]]
     for pieces, (low, high) in zip(held, spans):
-        outs = product(whole, gate_weight, up_weight, pieces, low, high - low, mine, after)
-        after = outs[:1]
-        for shift in range(rows):
-            value = lax.ppermute(outs[shift], "row", around(rows, shift)) if shift else outs[shift]
-            blocks.append((shift, low, value))
+        outs = product(whole, gate_weight, up_weight, pieces, low, high - low, mine, done[-1:] + returned[-2:][0])
+        done.append(outs[0])
+        back = [lax.ppermute(outs[shift], "row", around(rows, shift)) for shift in range(1, rows)]
+        returned.append(back)
+        blocks += [(shift, low, value) for shift, value in enumerate([outs[0]] + back)]
     return place(blocks, mine, ff)
 
 

time: 546 us -> 345 us (0.63)
  Pallas kernels: 294 us -> 61.9 us
  waiting for transfers between devices: 202 us -> 232 us
    pallas_call x6 -> x9, Pallas kernels: 174 us -> 18.2 us  [pack(): pl.pallas_call(body, out_shape=jax.ShapeDtypeStruct((share, 2 * wide), ga...]
    pallas_call x1, Pallas kernels: 84.6 us -> 3.33 us  [place(): pl.pallas_call(body, out_shape=jax.ShapeDtypeStruct((mine, ff), jnp.bfloa...]
    ppermute x6 -> x9, waiting for transfers between devices: 9.36 us -> 45.2 us  [in_tiles(): swapped.append(lax.ppermute(came, 'parts', around(parts, -turn)))]
    ppermute x6 -> x9, waiting for transfers between devices: 51.3 us -> 31.4 us  [in_tiles(): lax.ppermute(outs[shift], 'row', around(rows, shift))]
    all_gather x1, waiting for transfers between devices: 0.02 us -> 8.45 us  [in_tiles(): block_rows = lax.all_gather(tokens, 'row', axis=0, tiled=True)]
    ppermute x6 -> x9, waiting for transfers between devices: 140 us -> 146 us  [in_tiles(): came = lax.ppermute(sent[-1], 'row', around(rows, shift))]
    pallas_call x2 -> x3, Pallas kernels: 35.2 us -> 40.5 us  [product(): pl.pallas_call(body, out_shape=[jax.ShapeDtypeStruct((mine, wide), jnp.bf...]
    unnamed x34 -> x54, local copies, waits for them, and re-layouts: 11 us -> 5.91 us
  transfers between devices with their start and end apart: 20 -> 29, of which waited for: 8 -> 17; matrix products, arithmetic and copies ran while one was open for 0% -> 0% of each run, Pallas kernels for 36% -> 17%
where the time goes in v4:
time: 345 us; the launch traced here: 344 us
  waiting for transfers between devices  232 us (67%)
  Pallas kernels  61.9 us (18%)
  starting transfers between devices  30.3 us (9%)
  between operations  13.7 us (4%)
  local copies, waits for them, and re-layouts  5.91 us (2%)
    ppermute x9, waiting for transfers between devices, in_tiles(): came = lax.ppermute(sent[-1], 'row', around(rows, shift))  146 us
    ppermute x9, waiting for transfers between devices, in_tiles(): swapped.append(lax.ppermute(came, 'parts', around(parts, -turn)))  45.2 us
    pallas_call x3, Pallas kernels, product(): pl.pallas_call(body, out_shape=[jax.ShapeDtypeStruct((mine, wide), jnp.bf...  40.5 us
    ppermute x9, waiting for transfers between devices, in_tiles(): lax.ppermute(outs[shift], 'row', around(rows, shift))  31.4 us
    pallas_call x9, Pallas kernels, pack(): pl.pallas_call(body, out_shape=jax.ShapeDtypeStruct((share, 2 * wide), ga...  18.2 us
    ppermute x9, starting transfers between devices, in_tiles(): came = lax.ppermute(sent[-1], 'row', around(rows, shift))  11.7 us
    ppermute x9, starting transfers between devices, in_tiles(): lax.ppermute(outs[shift], 'row', around(rows, shift))  11.4 us
    all_gather x1, waiting for transfers between devices, in_tiles(): block_rows = lax.all_gather(tokens, 'row', axis=0, tiled=True)  8.45 us
  transfers between devices with their start and end apart: 29, of which 17 were waited for; matrix products, arithmetic and copies ran while one was open for 0% of the time, Pallas kernels for 17%

profile of v4, /device:TPU:12, one launch (start us, length us, event | category | flops | bytes accessed | tf_op | source)
XLA Modules:
  0.0 344.0 jit_solution(14874284172793429128)
XLA Ops:
  6.5 0.7 all-gather.3.cloned.1.call-update
  7.3 2.2 pack.9.refs_2_
  9.5 2.2 pack.10.refs_2_
  11.7 2.7 collective-permute-start
  14.3 76.0 %collective-permute-done.refs_1_.refs_2_.refs_3_ = bf16[512,768]{1,0:T(8,128)(2,1)S(1)} collective-permute-done((bf16[512,768]{1,0:T(8,128)(2,1)}, bf16[512,768]{1,0:T(8,128)(2,1)S(1)}, u32[]{:S(2)}, u32[]{:S(2)}) %collective-permute-start) | collective-permute-done | bytes 786464 | tf_op jit(solution)/shard_map/ppermute | solution.py:198
  90.4 8.4 %all-gather.3.cloned.1.call-done.refs_0_ = bf16[1536,1024]{1,0:T(8,128)(2,1)} async-done(((bf16[384,1024]{1,0:T(8,128)(2,1)}), bf16[1536,1024]{1,0:T(8,128)(2,1)}) %all-gather.3.cloned.1.call-update) | async-done | bytes 3145744 | tf_op jit(solution)/shard_map/all_gather | solution.py:184
  98.9 0.1 collective-permute-start.1
  98.9 19.5 %collective-permute-done.1.refs_3_.refs_0_ = bf16[512,768]{1,0:T(8,128)(2,1)S(1)} collective-permute-done((bf16[512,768]{1,0:T(8,128)(2,1)S(1)}, bf16[512,768]{1,0:T(8,128)(2,1)S(1)}, u32[]{:S(2)}, u32[]{:S(2)}) %collective-permute-start.1) | collective-permute-done | bytes 786464 | tf_op jit(solution)/shard_map/ppermute | solution.py:198
  118.4 0.9 copy-done.13
  119.3 2.2 pack.11.refs_2_
  121.5 3.4 collective-permute-start.4
  124.9 0.5 collective-permute-start.2
  125.3 1.6 collective-permute-start.3
  126.9 14.5 %collective-permute-done.4.refs_4_.refs_3_ = bf16[512,768]{1,0:T(8,128)(2,1)S(1)} collective-permute-done((bf16[512,768]{1,0:T(8,128)(2,1)}, bf16[512,768]{1,0:T(8,128)(2,1)S(1)}, u32[]{:S(2)}, u32[]{:S(2)}) %collective-permute-start.4) | collective-permute-done | bytes 786464 | tf_op jit(solution)/shard_map/ppermute | solution.py:198
  141.4 0.5 collective-permute-start.5
  141.8 3.7 %collective-permute-done.2.refs_1_.refs_4_ = bf16[512,768]{1,0:T(8,128)(2,1)S(1)} collective-permute-done((bf16[512,768]{1,0:T(8,128)(2,1)}, bf16[512,768]{1,0:T(8,128)(2,1)S(1)}, u32[]{:S(2)}, u32[]{:S(2)}) %collective-permute-start.2) | collective-permute-done | bytes 786464 | tf_op jit(solution)/shard_map/ppermute | solution.py:202
  145.6 0.9 copy-done.15
  146.5 1.9 pack.12.refs_2_
  148.5 14.0 %collective-permute-done.3.refs_3_.refs_4_ = bf16[512,768]{1,0:T(8,128)(2,1)} collective-permute-done((bf16[512,768]{1,0:T(8,128)(2,1)S(1)}, bf16[512,768]{1,0:T(8,128)(2,1)}, u32[]{:S(2)}, u32[]{:S(2)}) %collective-permute-start.3) | collective-permute-done | bytes 786464 | tf_op jit(solution)/shard_map/ppermute | solution.py:202
  162.5 1.9 pack.13.refs_2_
  164.5 0.4 collective-permute-start.11
  164.9 0.5 collective-permute-start.10
  165.4 14.0 %collective-permute-done.5.refs_5_.refs_4_ = bf16[512,768]{1,0:T(8,128)(2,1)} collective-permute-done((bf16[512,768]{1,0:T(8,128)(2,1)S(1)}, bf16[512,768]{1,0:T(8,128)(2,1)}, u32[]{:S(2)}, u32[]{:S(2)}) %collective-permute-start.5) | collective-permute-done | bytes 786464 | tf_op jit(solution)/shard_map/ppermute | solution.py:202
  179.4 1.9 pack.14.refs_2_
  181.3 1.7 collective-permute-start.13
  183.1 12.6 %collective-permute-done.11.refs_2_.refs_3_ = bf16[512,512]{1,0:T(8,128)(2,1)S(1)} collective-permute-done((bf16[512,512]{1,0:T(8,128)(2,1)}, bf16[512,512]{1,0:T(8,128)(2,1)S(1)}, u32[]{:S(2)}, u32[]{:S(2)}) %collective-permute-start.11) | collective-permute-done | bytes 524320 | tf_op jit(solution)/shard_map/ppermute | solution.py:198
  195.7 0.5 collective-permute-start.12
  196.2 0.3 copy-done.5
  196.5 0.8 copy-done.6
  197.3 1.9 pack.15.refs_2_
  199.2 0.1 collective-permute-start.18
  199.3 1.3 collective-permute-start.14
  200.6 9.9 %collective-permute-done.12.refs_3_.refs_4_ = bf16[512,512]{1,0:T(8,128)(2,1)S(1)} collective-permute-done((bf16[512,512]{1,0:T(8,128)(2,1)S(1)}, bf16[512,512]{1,0:T(8,128)(2,1)S(1)}, u32[]{:S(2)}, u32[]{:S(2)}) %collective-permute-start.12) | collective-permute-done | bytes 524320 | tf_op jit(solution)/shard_map/ppermute | solution.py:202
  210.6 0.8 copy-done.8
  211.4 1.9 pack.16.refs_2_
  213.3 3.3 collective-permute-start.20
  216.7 3.5 %collective-permute-done.14.refs_5_.refs_4_ = bf16[512,512]{1,0:T(8,128)(2,1)S(1)} collective-permute-done((bf16[512,512]{1,0:T(8,128)(2,1)S(1)}, bf16[512,512]{1,0:T(8,128)(2,1)S(1)}, u32[]{:S(2)}, u32[]{:S(2)}) %collective-permute-start.14) | collective-permute-done | bytes 524320 | tf_op jit(solution)/shard_map/ppermute | solution.py:202
  220.2 0.8 copy-done.9
  221.0 2.0 pack.17
  223.0 0.5 collective-permute-start.19
  223.6 22.0 %collective-permute-done.20.refs_2_ = bf16[512,512]{1,0:T(8,128)(2,1)S(1)} collective-permute-done((bf16[512,512]{1,0:T(8,128)(2,1)}, bf16[512,512]{1,0:T(8,128)(2,1)S(1)}, u32[]{:S(2)}, u32[]{:S(2)}) %collective-permute-start.20) | collective-permute-done | bytes 524320 | tf_op jit(solution)/shard_map/ppermute | solution.py:198
  245.5 0.8 collective-permute-start.21
  246.3 1.7 collective-permute-done.22.refs_4_
  248.0 1.0 collective-permute-start.23
  249.0 16.6 %product.3 = (bf16[384,384]{1,0:T(8,128)(2,1)}, bf16[384,384]{1,0:T(8,128)(2,1)}, bf16[384,384]{1,0:T(8,128)(2,1)}, bf16[384,384]{1,0:T(8,128)(2,1)}) custom-call(bf16[1536,4096]{1,0:T(8,128)(2,1)} %all-gather.5.cloned.1.call-done.tokens_ref, bf16[1024,3584]{1,0:T(8,128)(2,1)} %gate_ref.5, bf16[1024,3584]{1,0:T(8,128)(2,1)} %up_ref.5, ...), custom_call_target="tpu_custom_call" | custom-call | flops 9663676416 | bytes 20054016 | tf_op jit(solution)/shard_map/product/pallas_call | solution.py:131
  265.6 0.1 collective-permute-start.6
  265.7 1.9 collective-permute-start.7
  267.6 1.9 collective-permute-start.8
  269.6 11.9 %product.4 = (bf16[384,256]{1,0:T(8,128)(2,1)}, bf16[384,256]{1,0:T(8,128)(2,1)}, bf16[384,256]{1,0:T(8,128)(2,1)}, bf16[384,256]{1,0:T(8,128)(2,1)}) custom-call(bf16[1536,4096]{1,0:T(8,128)(2,1)} %all-gather.5.cloned.1.call-done.tokens_ref, bf16[1024,3584]{1,0:T(8,128)(2,1)} %gate_ref.5, bf16[1024,3584]{1,0:T(8,128)(2,1)} %up_ref.5, ...), custom_call_target="tpu_custom_call" | custom-call | flops 6442450944 | bytes 17563648 | tf_op jit(solution)/shard_map/product/pallas_call | solution.py:131
  281.5 0.1 collective-permute-start.15
  281.6 2.8 collective-permute-start.16
  284.5 0.2 collective-permute-start.17
  284.6 16.2 %collective-permute-done.7.refs_8_.refs_2_ = bf16[384,384]{1,0:T(8,128)(2,1)S(1)} collective-permute-done((bf16[384,384]{1,0:T(8,128)(2,1)}, bf16[384,384]{1,0:T(8,128)(2,1)S(1)}, u32[]{:S(2)}, u32[]{:S(2)}) %collective-permute-start.7) | collective-permute-done | bytes 294944 | tf_op jit(solution)/shard_map/ppermute | solution.py:211
  300.8 1.1 collective-permute-done.8.refs_9_.refs_3_
  301.9 0.7 copy-done.12
  302.6 12.0 %product.5 = (bf16[384,256]{1,0:T(8,128)(2,1)}, bf16[384,256]{1,0:T(8,128)(2,1)}, bf16[384,256]{1,0:T(8,128)(2,1)}, bf16[384,256]{1,0:T(8,128)(2,1)}) custom-call(bf16[1536,4096]{1,0:T(8,128)(2,1)} %all-gather.5.cloned.1.call-done.tokens_ref, bf16[1024,3584]{1,0:T(8,128)(2,1)} %gate_ref.5, bf16[1024,3584]{1,0:T(8,128)(2,1)} %up_ref.5, ...), custom_call_target="tpu_custom_call" | custom-call | flops 6442450944 | bytes 17563648 | tf_op jit(solution)/shard_map/product/pallas_call | solution.py:131
  314.7 0.1 collective-permute-start.24
  314.7 2.3 collective-permute-start.25
  317.0 1.9 collective-permute-start.26
  319.0 3.7 %collective-permute-done.24.refs_9_ = bf16[384,256]{1,0:T(8,128)(2,1)S(1)} collective-permute-done((bf16[384,256]{1,0:T(8,128)(2,1)}, bf16[384,256]{1,0:T(8,128)(2,1)S(1)}, u32[]{:S(2)}, u32[]{:S(2)}) %collective-permute-start.24) | collective-permute-done | bytes 196640 | tf_op jit(solution)/shard_map/ppermute | solution.py:211
  322.7 9.5 %collective-permute-done.25.refs_10_ = bf16[384,256]{1,0:T(8,128)(2,1)S(1)} collective-permute-done((bf16[384,256]{1,0:T(8,128)(2,1)}, bf16[384,256]{1,0:T(8,128)(2,1)S(1)}, u32[]{:S(2)}, u32[]{:S(2)}) %collective-permute-start.25) | collective-permute-done | bytes 196640 | tf_op jit(solution)/shard_map/ppermute | solution.py:211
  332.2 1.0 collective-permute-done.26.refs_11_
  333.2 0.6 copy-done.26
  333.8 3.3 place.1
  (64 shorter events, 0.3 us)
Async XLA Ops:
  6.5 92.3 %all-gather.3.cloned.1.call-start = ((), (), s32[]{:S(2)}) async-start(), calls=%async_computation | async-start | bytes 3932160 | tf_op jit(solution)/shard_map/all_gather | solution.py:184
  7.3 241.7 %all-gather.5.cloned.1.call-start = ((), (), s32[]{:S(2)}) async-start(), calls=%async_computation.1 | async-start | bytes 15728640 | tf_op jit(solution)/shard_map/all_gather | solution.py:206
  11.7 87.2 %copy-start.2 = (bf16[512,768]{1,0:T(8,128)(2,1)S(1)}, bf16[512,768]{1,0:T(8,128)(2,1)}, u32[]{:S(2)}) copy-start(bf16[512,768]{1,0:T(8,128)(2,1)} %pack.9.refs_2_) | copy-start | bytes 2359300
  11.7 78.7 %collective-permute-start = (bf16[512,768]{1,0:T(8,128)(2,1)}, bf16[512,768]{1,0:T(8,128)(2,1)S(1)}, u32[]{:S(2)}, u32[]{:S(2)}) collective-permute-start(bf16[512,768]{1,0:T(8,128)(2,1)} %pack.10.refs_2_), channel_id=1, source_target_pairs={{0,8},{4,12},{8,0},{12,4},{1,9},{5,13},{9,1},{13,5},{2,10},{6,14},... | collective-permute-start | bytes 2359304 | tf_op jit(solution)/shard_map/ppermute | solution.py:198
  90.4 8.5 %copy-start = (bf16[512,768]{1,0:T(8,128)(2,1)}, bf16[512,768]{1,0:T(8,128)(2,1)S(1)}, u32[]{:S(2)}) copy-start(bf16[512,768]{1,0:T(8,128)(2,1)S(1)} %collective-permute-done.refs_1_.refs_2_.refs_3_) | copy-start | bytes 2359300
  98.8 26.5 %copy-start.1 = (bf16[512,768]{1,0:T(8,128)(2,1)S(1)}, bf16[512,768]{1,0:T(8,128)(2,1)}, u32[]{:S(2)}) copy-start(bf16[512,768]{1,0:T(8,128)(2,1)} %copy-done) | copy-start | bytes 2359300
  98.9 19.6 %collective-permute-start.1 = (bf16[512,768]{1,0:T(8,128)(2,1)S(1)}, bf16[512,768]{1,0:T(8,128)(2,1)S(1)}, u32[]{:S(2)}, u32[]{:S(2)}) collective-permute-start(bf16[512,768]{1,0:T(8,128)(2,1)S(1)} %copy-done.2), channel_id=1, source_target_pairs={{0,4},{4,8},{8,12},{12,0},{1,5},{5,9},{9,13},{13,1},{2,6},{6,10},{... | collective-permute-start | bytes 2359304 | tf_op jit(solution)/shard_map/ppermute | solution.py:198
  118.4 0.9 copy-start.13
  121.5 19.9 %collective-permute-start.4 = (bf16[512,768]{1,0:T(8,128)(2,1)}, bf16[512,768]{1,0:T(8,128)(2,1)S(1)}, u32[]{:S(2)}, u32[]{:S(2)}) collective-permute-start(bf16[512,768]{1,0:T(8,128)(2,1)} %pack.11.refs_2_), channel_id=1, source_target_pairs={{0,12},{4,0},{8,4},{12,8},{1,13},{5,1},{9,5},{13,9},{2,14},{6,2},{... | collective-permute-start | bytes 2359304 | tf_op jit(solution)/shard_map/ppermute | solution.py:198
  124.9 20.7 %collective-permute-start.2 = (bf16[512,768]{1,0:T(8,128)(2,1)}, bf16[512,768]{1,0:T(8,128)(2,1)S(1)}, u32[]{:S(2)}, u32[]{:S(2)}) collective-permute-start(bf16[512,768]{1,0:T(8,128)(2,1)} %copy-done.13), channel_id=1, source_target_pairs={{0,16},{16,0},{1,17},{17,1},{2,18},{18,2},{3,19},{19,3},{4,20},{20... | collective-permute-start | bytes 2359304 | tf_op jit(solution)/shard_map/ppermute | solution.py:202
  125.3 37.2 %collective-permute-start.3 = (bf16[512,768]{1,0:T(8,128)(2,1)S(1)}, bf16[512,768]{1,0:T(8,128)(2,1)}, u32[]{:S(2)}, u32[]{:S(2)}) collective-permute-start(bf16[512,768]{1,0:T(8,128)(2,1)S(1)} %copy-done.1), channel_id=1, source_target_pairs={{0,16},{16,0},{1,17},{17,1},{2,18},{18,2},{3,19},{19,3},{4,20},{20... | collective-permute-start | bytes 2359304 | tf_op jit(solution)/shard_map/ppermute | solution.py:202
  141.4 7.0 %copy-start.14 = (bf16[512,768]{1,0:T(8,128)(2,1)}, bf16[512,768]{1,0:T(8,128)(2,1)S(1)}, u32[]{:S(2)}) copy-start(bf16[512,768]{1,0:T(8,128)(2,1)S(1)} %collective-permute-done.4.refs_4_.refs_3_) | copy-start | bytes 2359300
  141.4 38.0 %collective-permute-start.5 = (bf16[512,768]{1,0:T(8,128)(2,1)S(1)}, bf16[512,768]{1,0:T(8,128)(2,1)}, u32[]{:S(2)}, u32[]{:S(2)}) collective-permute-start(bf16[512,768]{1,0:T(8,128)(2,1)S(1)} %collective-permute-done.4.refs_4_.refs_3_), channel_id=1, source_target_pairs={{0,16},{16,0},{1,17},{17,1},{2,18},{18,2},{3,19},{19,3},{4,20},{20... | collective-permute-start | bytes 2359304 | tf_op jit(solution)/shard_map/ppermute | solution.py:202
  145.6 0.9 copy-start.15
  148.4 16.4 %collective-permute-start.9 = (bf16[512,512]{1,0:T(8,128)(2,1)}, bf16[512,512]{1,0:T(8,128)(2,1)S(1)}, u32[]{:S(2)}, u32[]{:S(2)}) collective-permute-start(bf16[512,512]{1,0:T(8,128)(2,1)} %pack.12.refs_2_), channel_id=1, source_target_pairs={{0,4},{4,8},{8,12},{12,0},{1,5},{5,9},{9,13},{13,1},{2,6},{6,10},{... | collective-permute-start | bytes 1572872 | tf_op jit(solution)/shard_map/ppermute | solution.py:198
  164.5 31.2 %collective-permute-start.11 = (bf16[512,512]{1,0:T(8,128)(2,1)}, bf16[512,512]{1,0:T(8,128)(2,1)S(1)}, u32[]{:S(2)}, u32[]{:S(2)}) collective-permute-start(bf16[512,512]{1,0:T(8,128)(2,1)} %pack.13.refs_2_), channel_id=1, source_target_pairs={{0,8},{4,12},{8,0},{12,4},{1,9},{5,13},{9,1},{13,5},{2,10},{6,14},... | collective-permute-start | bytes 1572872 | tf_op jit(solution)/shard_map/ppermute | solution.py:198
  164.9 14.5 %copy-start.4 = (bf16[512,512]{1,0:T(8,128)(2,1)}, bf16[512,512]{1,0:T(8,128)(2,1)S(1)}, u32[]{:S(2)}) copy-start(bf16[512,512]{1,0:T(8,128)(2,1)S(1)} %collective-permute-done.9.refs_3_.refs_0_) | copy-start | bytes 1572868
  164.9 31.3 %collective-permute-start.10 = (bf16[512,512]{1,0:T(8,128)(2,1)S(1)}, bf16[512,512]{1,0:T(8,128)(2,1)S(1)}, u32[]{:S(2)}, u32[]{:S(2)}) collective-permute-start(bf16[512,512]{1,0:T(8,128)(2,1)S(1)} %collective-permute-done.9.refs_3_.refs_0_), channel_id=1, source_target_pairs={{0,16},{16,0},{1,17},{17,1},{2,18},{18,2},{3,19},{19,3},{4,20},{20... | collective-permute-start | bytes 1572872 | tf_op jit(solution)/shard_map/ppermute | solution.py:202
  181.3 18.0 %collective-permute-start.13 = (bf16[512,512]{1,0:T(8,128)(2,1)}, bf16[512,512]{1,0:T(8,128)(2,1)S(1)}, u32[]{:S(2)}, u32[]{:S(2)}) collective-permute-start(bf16[512,512]{1,0:T(8,128)(2,1)} %pack.14.refs_2_), channel_id=1, source_target_pairs={{0,12},{4,0},{8,4},{12,8},{1,13},{5,1},{9,5},{13,9},{2,14},{6,2},{... | collective-permute-start | bytes 1572872 | tf_op jit(solution)/shard_map/ppermute | solution.py:198
  195.7 0.8 copy-start.5
  195.7 14.9 %collective-permute-start.12 = (bf16[512,512]{1,0:T(8,128)(2,1)S(1)}, bf16[512,512]{1,0:T(8,128)(2,1)S(1)}, u32[]{:S(2)}, u32[]{:S(2)}) collective-permute-start(bf16[512,512]{1,0:T(8,128)(2,1)S(1)} %collective-permute-done.11.refs_2_.refs_3_), channel_id=1, source_target_pairs={{0,16},{16,0},{1,17},{17,1},{2,18},{18,2},{3,19},{19,3},{4,20},{20... | collective-permute-start | bytes 1572872 | tf_op jit(solution)/shard_map/ppermute | solution.py:202
  196.5 0.8 copy-start.6
  199.2 17.4 %collective-permute-start.18 = (bf16[512,512]{1,0:T(8,128)(2,1)}, bf16[512,512]{1,0:T(8,128)(2,1)S(1)}, u32[]{:S(2)}, u32[]{:S(2)}) collective-permute-start(bf16[512,512]{1,0:T(8,128)(2,1)} %pack.15.refs_2_), channel_id=1, source_target_pairs={{0,4},{4,8},{8,12},{12,0},{1,5},{5,9},{9,13},{13,1},{2,6},{6,10},{... | collective-permute-start | bytes 1572872 | tf_op jit(solution)/shard_map/ppermute | solution.py:198
  199.3 11.2 %copy-start.7 = (bf16[512,512]{1,0:T(8,128)(2,1)}, bf16[512,512]{1,0:T(8,128)(2,1)S(1)}, u32[]{:S(2)}) copy-start(bf16[512,512]{1,0:T(8,128)(2,1)S(1)} %collective-permute-done.13.refs_4_.refs_3_) | copy-start | bytes 1572868
  199.3 20.8 %collective-permute-start.14 = (bf16[512,512]{1,0:T(8,128)(2,1)S(1)}, bf16[512,512]{1,0:T(8,128)(2,1)S(1)}, u32[]{:S(2)}, u32[]{:S(2)}) collective-permute-start(bf16[512,512]{1,0:T(8,128)(2,1)S(1)} %collective-permute-done.13.refs_4_.refs_3_), channel_id=1, source_target_pairs={{0,16},{16,0},{1,17},{17,1},{2,18},{18,2},{3,19},{19,3},{4,20},{20... | collective-permute-start | bytes 1572872 | tf_op jit(solution)/shard_map/ppermute | solution.py:202
  210.6 0.8 copy-start.8
  213.3 32.2 %collective-permute-start.20 = (bf16[512,512]{1,0:T(8,128)(2,1)}, bf16[512,512]{1,0:T(8,128)(2,1)S(1)}, u32[]{:S(2)}, u32[]{:S(2)}) collective-permute-start(bf16[512,512]{1,0:T(8,128)(2,1)} %pack.16.refs_2_), channel_id=1, source_target_pairs={{0,8},{4,12},{8,0},{12,4},{1,9},{5,13},{9,1},{13,5},{2,10},{6,14},... | collective-permute-start | bytes 1572872 | tf_op jit(solution)/shard_map/ppermute | solution.py:198
  216.7 3.5 %copy-start.3 = (bf16[512,512]{1,0:T(8,128)(2,1)}, bf16[512,512]{1,0:T(8,128)(2,1)S(1)}, u32[]{:S(2)}) copy-start(bf16[512,512]{1,0:T(8,128)(2,1)S(1)} %collective-permute-done.18.refs_3_.refs_0_) | copy-start | bytes 1572868
  220.2 0.8 copy-start.9
  223.0 25.1 %collective-permute-start.22 = (bf16[512,512]{1,0:T(8,128)(2,1)}, bf16[512,512]{1,0:T(8,128)(2,1)S(1)}, u32[]{:S(2)}, u32[]{:S(2)}) collective-permute-start(bf16[512,512]{1,0:T(8,128)(2,1)} %pack.17), channel_id=1, source_target_pairs={{0,12},{4,0},{8,4},{12,8},{1,13},{5,1},{9,5},{13,9},{2,14},{6,2},{... | collective-permute-start | bytes 1572872 | tf_op jit(solution)/shard_map/ppermute | solution.py:198
  223.0 44.6 %collective-permute-start.19 = (bf16[512,512]{1,0:T(8,128)(2,1)}, bf16[512,512]{1,0:T(8,128)(2,1)S(1)}, u32[]{:S(2)}, u32[]{:S(2)}) collective-permute-start(bf16[512,512]{1,0:T(8,128)(2,1)} %copy-done.3), channel_id=1, source_target_pairs={{0,16},{16,0},{1,17},{17,1},{2,18},{18,2},{3,19},{19,3},{4,20},{20... | collective-permute-start | bytes 1572872 | tf_op jit(solution)/shard_map/ppermute | solution.py:202
  245.5 20.0 %copy-start.16 = (bf16[512,512]{1,0:T(8,128)(2,1)}, bf16[512,512]{1,0:T(8,128)(2,1)S(1)}, u32[]{:S(2)}) copy-start(bf16[512,512]{1,0:T(8,128)(2,1)S(1)} %collective-permute-done.20.refs_2_) | copy-start | bytes 1572868
  245.5 35.9 %collective-permute-start.21 = (bf16[512,512]{1,0:T(8,128)(2,1)S(1)}, bf16[512,512]{1,0:T(8,128)(2,1)S(1)}, u32[]{:S(2)}, u32[]{:S(2)}) collective-permute-start(bf16[512,512]{1,0:T(8,128)(2,1)S(1)} %collective-permute-done.20.refs_2_), channel_id=1, source_target_pairs={{0,16},{16,0},{1,17},{17,1},{2,18},{18,2},{3,19},{19,3},{4,20},{20... | collective-permute-start | bytes 1572872 | tf_op jit(solution)/shard_map/ppermute | solution.py:202
  248.0 17.6 %copy-start.17 = (bf16[512,512]{1,0:T(8,128)(2,1)}, bf16[512,512]{1,0:T(8,128)(2,1)S(1)}, u32[]{:S(2)}) copy-start(bf16[512,512]{1,0:T(8,128)(2,1)S(1)} %collective-permute-done.22.refs_4_) | copy-start | bytes 1572868
  248.0 33.6 %collective-permute-start.23 = (bf16[512,512]{1,0:T(8,128)(2,1)S(1)}, bf16[512,512]{1,0:T(8,128)(2,1)S(1)}, u32[]{:S(2)}, u32[]{:S(2)}) collective-permute-start(bf16[512,512]{1,0:T(8,128)(2,1)S(1)} %collective-permute-done.22.refs_4_), channel_id=1, source_target_pairs={{0,16},{16,0},{1,17},{17,1},{2,18},{18,2},{3,19},{19,3},{4,20},{20... | collective-permute-start | bytes 1572872 | tf_op jit(solution)/shard_map/ppermute | solution.py:202
  265.6 18.9 %collective-permute-start.6 = (bf16[384,384]{1,0:T(8,128)(2,1)}, bf16[384,384]{1,0:T(8,128)(2,1)S(1)}, u32[]{:S(2)}, u32[]{:S(2)}) collective-permute-start(bf16[384,384]{1,0:T(8,128)(2,1)} %get-tuple-element.18), channel_id=1, source_target_pairs={{0,4},{4,8},{8,12},{12,0},{1,5},{5,9},{9,13},{13,1},{2,6},{6,10},{... | collective-permute-start | bytes 884744 | tf_op jit(solution)/shard_map/ppermute | solution.py:211
  265.7 35.1 %collective-permute-start.7 = (bf16[384,384]{1,0:T(8,128)(2,1)}, bf16[384,384]{1,0:T(8,128)(2,1)S(1)}, u32[]{:S(2)}, u32[]{:S(2)}) collective-permute-start(bf16[384,384]{1,0:T(8,128)(2,1)} %get-tuple-element.19), channel_id=1, source_target_pairs={{0,8},{4,12},{8,0},{12,4},{1,9},{5,13},{9,1},{13,5},{2,10},{6,14},... | collective-permute-start | bytes 884744 | tf_op jit(solution)/shard_map/ppermute | solution.py:211
  267.6 13.8 %copy-start.18 = (bf16[512,512]{1,0:T(8,128)(2,1)}, bf16[512,512]{1,0:T(8,128)(2,1)S(1)}, u32[]{:S(2)}) copy-start(bf16[512,512]{1,0:T(8,128)(2,1)S(1)} %collective-permute-done.19.refs_1_) | copy-start | bytes 1572868
  267.6 34.3 %collective-permute-start.8 = (bf16[384,384]{1,0:T(8,128)(2,1)}, bf16[384,384]{1,0:T(8,128)(2,1)S(1)}, u32[]{:S(2)}, u32[]{:S(2)}) collective-permute-start(bf16[384,384]{1,0:T(8,128)(2,1)} %get-tuple-element.20), channel_id=1, source_target_pairs={{0,12},{4,0},{8,4},{12,8},{1,13},{5,1},{9,5},{13,9},{2,14},{6,2},{... | collective-permute-start | bytes 884744 | tf_op jit(solution)/shard_map/ppermute | solution.py:211
  281.5 20.5 %copy-start.19 = (bf16[512,512]{1,0:T(8,128)(2,1)}, bf16[512,512]{1,0:T(8,128)(2,1)S(1)}, u32[]{:S(2)}) copy-start(bf16[512,512]{1,0:T(8,128)(2,1)S(1)} %collective-permute-done.21.refs_3_) | copy-start | bytes 1572868
  281.5 35.6 %collective-permute-start.15 = (bf16[384,256]{1,0:T(8,128)(2,1)}, bf16[384,256]{1,0:T(8,128)(2,1)S(1)}, u32[]{:S(2)}, u32[]{:S(2)}) collective-permute-start(bf16[384,256]{1,0:T(8,128)(2,1)} %get-tuple-element.22), channel_id=1, source_target_pairs={{0,4},{4,8},{8,12},{12,0},{1,5},{5,9},{9,13},{13,1},{2,6},{6,10},{... | collective-permute-start | bytes 589832 | tf_op jit(solution)/shard_map/ppermute | solution.py:211
  281.6 20.3 %copy-start.20 = (bf16[512,512]{1,0:T(8,128)(2,1)}, bf16[512,512]{1,0:T(8,128)(2,1)S(1)}, u32[]{:S(2)}) copy-start(bf16[512,512]{1,0:T(8,128)(2,1)S(1)} %collective-permute-done.23.refs_5_) | copy-start | bytes 1572868
  281.6 37.4 %collective-permute-start.16 = (bf16[384,256]{1,0:T(8,128)(2,1)}, bf16[384,256]{1,0:T(8,128)(2,1)S(1)}, u32[]{:S(2)}, u32[]{:S(2)}) collective-permute-start(bf16[384,256]{1,0:T(8,128)(2,1)} %get-tuple-element.23), channel_id=1, source_target_pairs={{0,8},{4,12},{8,0},{12,4},{1,9},{5,13},{9,1},{13,5},{2,10},{6,14},... | collective-permute-start | bytes 589832 | tf_op jit(solution)/shard_map/ppermute | solution.py:211
  284.5 17.5 %copy-start.10 = (bf16[384,384]{1,0:T(8,128)(2,1)}, bf16[384,384]{1,0:T(8,128)(2,1)S(1)}, u32[]{:S(2)}) copy-start(bf16[384,384]{1,0:T(8,128)(2,1)S(1)} %collective-permute-done.6.refs_7_.refs_1_) | copy-start | bytes 884740
  284.5 34.5 %collective-permute-start.17 = (bf16[384,256]{1,0:T(8,128)(2,1)}, bf16[384,256]{1,0:T(8,128)(2,1)S(1)}, u32[]{:S(2)}, u32[]{:S(2)}) collective-permute-start(bf16[384,256]{1,0:T(8,128)(2,1)} %get-tuple-element.24), channel_id=1, source_target_pairs={{0,12},{4,0},{8,4},{12,8},{1,13},{5,1},{9,5},{13,9},{2,14},{6,2},{... | collective-permute-start | bytes 589832 | tf_op jit(solution)/shard_map/ppermute | solution.py:211
  300.8 1.1 copy-start.11
  301.9 0.7 copy-start.12
  314.7 8.0 %collective-permute-start.24 = (bf16[384,256]{1,0:T(8,128)(2,1)}, bf16[384,256]{1,0:T(8,128)(2,1)S(1)}, u32[]{:S(2)}, u32[]{:S(2)}) collective-permute-start(bf16[384,256]{1,0:T(8,128)(2,1)} %get-tuple-element.26), channel_id=1, source_target_pairs={{0,4},{4,8},{8,12},{12,0},{1,5},{5,9},{9,13},{13,1},{2,6},{6,10},{... | collective-permute-start | bytes 589832 | tf_op jit(solution)/shard_map/ppermute | solution.py:211
  314.7 17.5 %collective-permute-start.25 = (bf16[384,256]{1,0:T(8,128)(2,1)}, bf16[384,256]{1,0:T(8,128)(2,1)S(1)}, u32[]{:S(2)}, u32[]{:S(2)}) collective-permute-start(bf16[384,256]{1,0:T(8,128)(2,1)} %get-tuple-element.27), channel_id=1, source_target_pairs={{0,8},{4,12},{8,0},{12,4},{1,9},{5,13},{9,1},{13,5},{2,10},{6,14},... | collective-permute-start | bytes 589832 | tf_op jit(solution)/shard_map/ppermute | solution.py:211
  317.0 16.1 %copy-start.21 = (bf16[384,256]{1,0:T(8,128)(2,1)}, bf16[384,256]{1,0:T(8,128)(2,1)S(1)}, u32[]{:S(2)}) copy-start(bf16[384,256]{1,0:T(8,128)(2,1)S(1)} %collective-permute-done.15.refs_5_) | copy-start | bytes 589828
  317.0 16.1 %collective-permute-start.26 = (bf16[384,256]{1,0:T(8,128)(2,1)}, bf16[384,256]{1,0:T(8,128)(2,1)S(1)}, u32[]{:S(2)}, u32[]{:S(2)}) collective-permute-start(bf16[384,256]{1,0:T(8,128)(2,1)} %get-tuple-element.28), channel_id=1, source_target_pairs={{0,12},{4,0},{8,4},{12,8},{1,13},{5,1},{9,5},{13,9},{2,14},{6,2},{... | collective-permute-start | bytes 589832 | tf_op jit(solution)/shard_map/ppermute | solution.py:211
  319.0 14.2 %copy-start.22 = (bf16[384,256]{1,0:T(8,128)(2,1)}, bf16[384,256]{1,0:T(8,128)(2,1)S(1)}, u32[]{:S(2)}) copy-start(bf16[384,256]{1,0:T(8,128)(2,1)S(1)} %collective-permute-done.16.refs_6_) | copy-start | bytes 589828
  319.0 14.2 %copy-start.23 = (bf16[384,256]{1,0:T(8,128)(2,1)}, bf16[384,256]{1,0:T(8,128)(2,1)S(1)}, u32[]{:S(2)}) copy-start(bf16[384,256]{1,0:T(8,128)(2,1)S(1)} %collective-permute-done.17.refs_7_) | copy-start | bytes 589828
  322.7 10.5 %copy-start.24 = (bf16[384,256]{1,0:T(8,128)(2,1)}, bf16[384,256]{1,0:T(8,128)(2,1)S(1)}, u32[]{:S(2)}) copy-start(bf16[384,256]{1,0:T(8,128)(2,1)S(1)} %collective-permute-done.24.refs_9_) | copy-start | bytes 589828
  332.2 1.0 copy-start.25
  333.2 0.7 copy-start.26
Sparse Core Ops, SparseCore 0:
  8.9 89.8 all-gather.2
  100.4 84.2 all-gather.4

commit v5 on v4

--- a/solution.py
+++ b/solution.py
@@ -190,27 +190,39 @@
             edges.append(edge)
     spans = list(zip(edges[:-1], edges[1:]))
 
-    sent, arrived, swapped, held = [], [], [], []
-    for low, high in spans:
-        pieces = []
+    def weights_of(n):
+        low, high = spans[n]
         for shift in range(1, rows):
-            sent.append(pack(gate_weight, up_weight, shift, low, high - low, sent[-1:] + arrived[-2:-1] + swapped[-3:-2]))
-            came = lax.ppermute(sent[-1], "row", around(rows, shift))
-            arrived.append(came)
-            pieces.append(came)
+            after = sent[-1:] + arrived[-2:-1] + swapped[-3:-2]
+            sent.append(pack(gate_weight, up_weight, shift, low, high - low, after))
+            arrived.append(lax.ppermute(sent[-1], "row", around(rows, shift)))
+            came = arrived[-1]
+            if done and shift == rows - 1:
+                came = hold(came, done)
+            held[n].append(came)
             for turn in range(1, parts):
                 swapped.append(lax.ppermute(came, "parts", around(parts, -turn)))
-                pieces.append(swapped[-1])
-        held.append(pieces)
-
-    whole = lax.all_gather(hold(block_rows, arrived[1:2]), "col", axis=1, tiled=True)
-    blocks, done, returned = [], [], [[]]
-    for pieces, (low, high) in zip(held, spans):
-        outs = product(whole, gate_weight, up_weight, pieces, low, high - low, mine, done[-1:] + returned[-2:][0])
+                held[n].append(swapped[-1])
+
+    def hidden_of(n, after):
+        low, high = spans[n]
+        outs = product(whole, gate_weight, up_weight, held[n], low, high - low, mine, after)
+        back = [lax.ppermute(outs[shift], "row", around(rows, shift)) for shift in range(1, rows)]
+        blocks.extend((shift, low, value) for shift, value in enumerate([outs[0]] + back))
         done.append(outs[0])
-        back = [lax.ppermute(outs[shift], "row", around(rows, shift)) for shift in range(1, rows)]
         returned.append(back)
-        blocks += [(shift, low, value) for shift, value in enumerate([outs[0]] + back)]
+
+    last = len(spans) - 1
+    sent, arrived, swapped, done, returned, blocks = [], [], [], [], [], []
+    held = [[] for _ in spans]
+    for n in range(last):
+        weights_of(n)
+    whole = lax.all_gather(hold(block_rows, arrived[1:3] + sent[3:4]), "col", axis=1, tiled=True)
+    if last:
+        hidden_of(0, [])
+    weights_of(last)
+    for n in range(min(last, 1), last + 1):
+        hidden_of(n, done[-1:] + (returned[n - 2] if n > 1 else []))
     return place(blocks, mine, ff)
 
 

time: 345 us -> 338 us (0.980)
  waiting for transfers between devices: 232 us -> 220 us
    all_gather x1, waiting for transfers between devices: 8.45 us -> 0.02 us  [in_tiles(): block_rows = lax.all_gather(tokens, 'row', axis=0, tiled=True)]
    ppermute x27, waiting for transfers between devices: 223 us -> 219 us  [the longest x9 144 us: weights_of(): arrived.append(lax.ppermute(sent[-1], 'row', around(rows, shift)))]
    unnamed x54 -> x56, local copies, waits for them, and re-layouts: 5.91 us -> 8.22 us
  transfers between devices with their start and end apart: 29 -> 29, of which waited for: 17 -> 13; matrix products, arithmetic and copies ran while one was open for 0% -> 0% of each run, Pallas kernels for 17% -> 17%
where the time goes in v5:
time: 338 us; the launch traced here: 337 us
  waiting for transfers between devices  220 us (65%)
  Pallas kernels  62 us (18%)
  starting transfers between devices  32.6 us (10%)
  between operations  13.8 us (4%)
  local copies, waits for them, and re-layouts  8.22 us (2%)
    ppermute x9, waiting for transfers between devices, weights_of(): arrived.append(lax.ppermute(sent[-1], 'row', around(rows, shift)))  144 us
    ppermute x9, waiting for transfers between devices, weights_of(): swapped.append(lax.ppermute(came, 'parts', around(parts, -turn)))  43.2 us
    pallas_call x3, Pallas kernels, product(): pl.pallas_call(body, out_shape=[jax.ShapeDtypeStruct((mine, wide), jnp.bf...  40.4 us
    ppermute x9, waiting for transfers between devices, hidden_of(): lax.ppermute(outs[shift], 'row', around(rows, shift))  32.5 us
    pallas_call x9, Pallas kernels, pack(): pl.pallas_call(body, out_shape=jax.ShapeDtypeStruct((share, 2 * wide), ga...  18.2 us
    ppermute x9, starting transfers between devices, weights_of(): swapped.append(lax.ppermute(came, 'parts', around(parts, -turn)))  11.9 us
    ppermute x9, starting transfers between devices, hidden_of(): lax.ppermute(outs[shift], 'row', around(rows, shift))  10.9 us
    ppermute x9, starting transfers between devices, weights_of(): arrived.append(lax.ppermute(sent[-1], 'row', around(rows, shift)))  9.84 us
  transfers between devices with their start and end apart: 29, of which 13 were waited for; matrix products, arithmetic and copies ran while one was open for 0% of the time, Pallas kernels for 17%

profile of v5, /device:TPU:12, one launch (start us, length us, event | category | flops | bytes accessed | tf_op | source)
XLA Modules:
  0.0 336.6 jit_solution(1551817122725211612)
XLA Ops:
  6.5 0.7 all-gather.3.cloned.1.call-update
  7.3 0.0 all-gather.5.cloned.1.call-start
  7.3 2.2 pack.9.refs_2_
  9.5 1.6 collective-permute-start.1
  11.1 2.2 pack.10.refs_2_
  13.3 1.3 collective-permute-start
  14.6 46.7 %collective-permute-done.1.refs_3_.refs_0_ = bf16[512,768]{1,0:T(8,128)(2,1)S(1)} collective-permute-done((bf16[512,768]{1,0:T(8,128)(2,1)}, bf16[512,768]{1,0:T(8,128)(2,1)S(1)}, u32[]{:S(2)}, u32[]{:S(2)}) %collective-permute-start.1) | collective-permute-done | bytes 786464 | tf_op jit(solution)/shard_map/ppermute | solution.py:198
  61.3 4.8 %collective-permute-start.3 = (bf16[512,768]{1,0:T(8,128)(2,1)S(1)}, bf16[512,768]{1,0:T(8,128)(2,1)S(1)}, u32[]{:S(2)}, u32[]{:S(2)}) collective-permute-start(bf16[512,768]{1,0:T(8,128)(2,1)S(1)} %collective-permute-done.1.refs_3_.refs_0_), channel_id=1, source_target_pairs={{0,16},{16,0},{1,17},{17,1},{2,18},{18,2},{3,19},{19,3},{4,20},{20... | collective-permute-start | bytes 2359304 | tf_op jit(solution)/shard_map/ppermute | solution.py:204
  66.1 2.2 pack.11.refs_2_
  68.3 0.1 collective-permute-start.2
  68.4 60.9 %collective-permute-done.refs_3_.refs_1_.refs_2_ = bf16[512,768]{1,0:T(8,128)(2,1)S(1)} collective-permute-done((bf16[512,768]{1,0:T(8,128)(2,1)}, bf16[512,768]{1,0:T(8,128)(2,1)S(1)}, u32[]{:S(2)}, u32[]{:S(2)}) %collective-permute-start) | collective-permute-done | bytes 786464 | tf_op jit(solution)/shard_map/ppermute | solution.py:198
  129.3 0.9 copy-done.1
  130.2 0.9 copy-done.16
  131.1 1.9 pack.12.refs_3_.refs_2_
  133.1 0.9 copy-done.3
  134.0 0.5 copy-done.2
  134.5 0.5 collective-permute-start.4
  135.0 1.5 collective-permute-start.5
  136.5 18.4 %collective-permute-done.4.refs_3_.refs_4_ = bf16[512,768]{1,0:T(8,128)(2,1)S(1)} collective-permute-done((bf16[512,768]{1,0:T(8,128)(2,1)S(1)}, bf16[512,768]{1,0:T(8,128)(2,1)S(1)}, u32[]{:S(2)}, u32[]{:S(2)}) %collective-permute-start.4) | collective-permute-done | bytes 786464 | tf_op jit(solution)/shard_map/ppermute | solution.py:204
  155.0 0.9 copy-done.17
  155.8 1.9 pack.13.refs_2_
  157.8 3.3 collective-permute-start.11
  161.1 0.5 collective-permute-start.10
  161.6 10.3 %collective-permute-done.5.refs_5_.refs_4_ = bf16[512,768]{1,0:T(8,128)(2,1)} collective-permute-done((bf16[512,768]{1,0:T(8,128)(2,1)}, bf16[512,768]{1,0:T(8,128)(2,1)}, u32[]{:S(2)}, u32[]{:S(2)}) %collective-permute-start.5) | collective-permute-done | bytes 786464 | tf_op jit(solution)/shard_map/ppermute | solution.py:204
  171.9 1.9 pack.14.refs_2_
  173.9 0.1 collective-permute-start.13
  173.9 14.5 %collective-permute-done.11.refs_2_.refs_3_ = bf16[512,512]{1,0:T(8,128)(2,1)S(1)} collective-permute-done((bf16[512,512]{1,0:T(8,128)(2,1)}, bf16[512,512]{1,0:T(8,128)(2,1)S(1)}, u32[]{:S(2)}, u32[]{:S(2)}) %collective-permute-start.11) | collective-permute-done | bytes 524320 | tf_op jit(solution)/shard_map/ppermute | solution.py:198
  188.4 0.6 collective-permute-start.12
  189.0 0.2 copy-done.6
  189.2 0.8 copy-done.7
  190.0 1.9 pack.15.refs_2_
  191.9 0.1 collective-permute-start.18
  192.0 1.3 collective-permute-start.14
  193.3 9.9 %collective-permute-done.12.refs_3_.refs_4_ = bf16[512,512]{1,0:T(8,128)(2,1)S(1)} collective-permute-done((bf16[512,512]{1,0:T(8,128)(2,1)S(1)}, bf16[512,512]{1,0:T(8,128)(2,1)S(1)}, u32[]{:S(2)}, u32[]{:S(2)}) %collective-permute-start.12) | collective-permute-done | bytes 524320 | tf_op jit(solution)/shard_map/ppermute | solution.py:204
  203.2 0.8 copy-done.9
  204.0 1.9 pack.16.refs_2_
  206.0 3.3 collective-permute-start.20
  209.3 0.6 collective-permute-start.19
  209.9 4.6 %collective-permute-done.14.refs_5_.refs_4_ = bf16[512,512]{1,0:T(8,128)(2,1)S(1)} collective-permute-done((bf16[512,512]{1,0:T(8,128)(2,1)S(1)}, bf16[512,512]{1,0:T(8,128)(2,1)S(1)}, u32[]{:S(2)}, u32[]{:S(2)}) %collective-permute-start.14) | collective-permute-done | bytes 524320 | tf_op jit(solution)/shard_map/ppermute | solution.py:204
  214.4 0.8 copy-done.10
  215.3 2.0 pack.17
  217.3 0.1 collective-permute-start.22
  217.3 21.5 %collective-permute-done.20.refs_2_ = bf16[512,512]{1,0:T(8,128)(2,1)S(1)} collective-permute-done((bf16[512,512]{1,0:T(8,128)(2,1)}, bf16[512,512]{1,0:T(8,128)(2,1)S(1)}, u32[]{:S(2)}, u32[]{:S(2)}) %collective-permute-start.20) | collective-permute-done | bytes 524320 | tf_op jit(solution)/shard_map/ppermute | solution.py:198
  238.8 1.0 collective-permute-start.21
  239.8 16.6 %product.3 = (bf16[384,384]{1,0:T(8,128)(2,1)}, bf16[384,384]{1,0:T(8,128)(2,1)}, bf16[384,384]{1,0:T(8,128)(2,1)}, bf16[384,384]{1,0:T(8,128)(2,1)}) custom-call(bf16[1536,4096]{1,0:T(8,128)(2,1)} %all-gather.5.cloned.1.call-done.tokens_ref, bf16[1024,3584]{1,0:T(8,128)(2,1)} %gate_ref.5, bf16[1024,3584]{1,0:T(8,128)(2,1)} %up_ref.5, ...), custom_call_target="tpu_custom_call" | custom-call | flops 9663676416 | bytes 20054016 | tf_op jit(solution)/shard_map/product/pallas_call | solution.py:131
  256.4 0.1 collective-permute-start.6
  256.5 3.3 collective-permute-start.7
  259.8 1.9 collective-permute-start.8
  261.8 1.1 collective-permute-start.23
  262.9 11.9 %product.4 = (bf16[384,256]{1,0:T(8,128)(2,1)}, bf16[384,256]{1,0:T(8,128)(2,1)}, bf16[384,256]{1,0:T(8,128)(2,1)}, bf16[384,256]{1,0:T(8,128)(2,1)}) custom-call(bf16[1536,4096]{1,0:T(8,128)(2,1)} %all-gather.5.cloned.1.call-done.tokens_ref, bf16[1024,3584]{1,0:T(8,128)(2,1)} %gate_ref.5, bf16[1024,3584]{1,0:T(8,128)(2,1)} %up_ref.5, ...), custom_call_target="tpu_custom_call" | custom-call | flops 6442450944 | bytes 17563648 | tf_op jit(solution)/shard_map/product/pallas_call | solution.py:131
  274.8 0.1 collective-permute-start.15
  275.0 3.1 collective-permute-start.16
  278.1 9.4 %collective-permute-done.7.refs_8_.refs_2_ = bf16[384,384]{1,0:T(8,128)(2,1)S(1)} collective-permute-done((bf16[384,384]{1,0:T(8,128)(2,1)}, bf16[384,384]{1,0:T(8,128)(2,1)S(1)}, u32[]{:S(2)}, u32[]{:S(2)}) %collective-permute-start.7) | collective-permute-done | bytes 294944 | tf_op jit(solution)/shard_map/ppermute | solution.py:210
  287.5 6.9 %collective-permute-done.8.refs_9_.refs_3_ = bf16[384,384]{1,0:T(8,128)(2,1)S(1)} collective-permute-done((bf16[384,384]{1,0:T(8,128)(2,1)}, bf16[384,384]{1,0:T(8,128)(2,1)S(1)}, u32[]{:S(2)}, u32[]{:S(2)}) %collective-permute-start.8) | collective-permute-done | bytes 294944 | tf_op jit(solution)/shard_map/ppermute | solution.py:210
  294.4 0.7 copy-done.14
  295.1 0.2 copy-done.21
  295.3 12.0 %product.5 = (bf16[384,256]{1,0:T(8,128)(2,1)}, bf16[384,256]{1,0:T(8,128)(2,1)}, bf16[384,256]{1,0:T(8,128)(2,1)}, bf16[384,256]{1,0:T(8,128)(2,1)}) custom-call(bf16[1536,4096]{1,0:T(8,128)(2,1)} %all-gather.5.cloned.1.call-done.tokens_ref, bf16[1024,3584]{1,0:T(8,128)(2,1)} %gate_ref.5, bf16[1024,3584]{1,0:T(8,128)(2,1)} %up_ref.5, ...), custom_call_target="tpu_custom_call" | custom-call | flops 6442450944 | bytes 17563648 | tf_op jit(solution)/shard_map/product/pallas_call | solution.py:131
  307.2 0.1 collective-permute-start.24
  307.3 2.2 collective-permute-start.25
  309.6 5.7 %collective-permute-done.24.refs_9_ = bf16[384,256]{1,0:T(8,128)(2,1)S(1)} collective-permute-done((bf16[384,256]{1,0:T(8,128)(2,1)}, bf16[384,256]{1,0:T(8,128)(2,1)S(1)}, u32[]{:S(2)}, u32[]{:S(2)}) %collective-permute-start.24) | collective-permute-done | bytes 196640 | tf_op jit(solution)/shard_map/ppermute | solution.py:210
  315.3 9.5 %collective-permute-done.25.refs_10_ = bf16[384,256]{1,0:T(8,128)(2,1)S(1)} collective-permute-done((bf16[384,256]{1,0:T(8,128)(2,1)}, bf16[384,256]{1,0:T(8,128)(2,1)S(1)}, u32[]{:S(2)}, u32[]{:S(2)}) %collective-permute-start.25) | collective-permute-done | bytes 196640 | tf_op jit(solution)/shard_map/ppermute | solution.py:210
  324.8 1.0 collective-permute-done.26.refs_11_
  325.8 0.6 copy-done.27
  326.4 3.3 place.1
  (67 shorter events, 0.2 us)
Async XLA Ops:
  6.5 126.6 %all-gather.3.cloned.1.call-start = ((), (), s32[]{:S(2)}) async-start(), calls=%async_computation | async-start | bytes 3932160 | tf_op jit(solution)/shard_map/all_gather | solution.py:184
  7.3 232.6 %all-gather.5.cloned.1.call-start = ((), (), s32[]{:S(2)}) async-start(), calls=%async_computation.1 | async-start | bytes 15728640 | tf_op jit(solution)/shard_map/all_gather | solution.py:220
  9.5 51.8 %collective-permute-start.1 = (bf16[512,768]{1,0:T(8,128)(2,1)}, bf16[512,768]{1,0:T(8,128)(2,1)S(1)}, u32[]{:S(2)}, u32[]{:S(2)}) collective-permute-start(bf16[512,768]{1,0:T(8,128)(2,1)} %pack.9.refs_2_), channel_id=1, source_target_pairs={{0,4},{4,8},{8,12},{12,0},{1,5},{5,9},{9,13},{13,1},{2,6},{6,10},{... | collective-permute-start | bytes 2359304 | tf_op jit(solution)/shard_map/ppermute | solution.py:198
  13.3 116.0 %collective-permute-start = (bf16[512,768]{1,0:T(8,128)(2,1)}, bf16[512,768]{1,0:T(8,128)(2,1)S(1)}, u32[]{:S(2)}, u32[]{:S(2)}) collective-permute-start(bf16[512,768]{1,0:T(8,128)(2,1)} %pack.10.refs_2_), channel_id=1, source_target_pairs={{0,8},{4,12},{8,0},{12,4},{1,9},{5,13},{9,1},{13,5},{2,10},{6,14},... | collective-permute-start | bytes 2359304 | tf_op jit(solution)/shard_map/ppermute | solution.py:198
  61.3 4.8 %copy-start.15 = (bf16[512,768]{1,0:T(8,128)(2,1)}, bf16[512,768]{1,0:T(8,128)(2,1)S(1)}, u32[]{:S(2)}) copy-start(bf16[512,768]{1,0:T(8,128)(2,1)S(1)} %collective-permute-done.1.refs_3_.refs_0_) | copy-start | bytes 2359300
  61.3 68.0 %collective-permute-start.3 = (bf16[512,768]{1,0:T(8,128)(2,1)S(1)}, bf16[512,768]{1,0:T(8,128)(2,1)S(1)}, u32[]{:S(2)}, u32[]{:S(2)}) collective-permute-start(bf16[512,768]{1,0:T(8,128)(2,1)S(1)} %collective-permute-done.1.refs_3_.refs_0_), channel_id=1, source_target_pairs={{0,16},{16,0},{1,17},{17,1},{2,18},{18,2},{3,19},{19,3},{4,20},{20... | collective-permute-start | bytes 2359304 | tf_op jit(solution)/shard_map/ppermute | solution.py:204
  68.3 64.7 %collective-permute-start.2 = (bf16[512,768]{1,0:T(8,128)(2,1)}, bf16[512,768]{1,0:T(8,128)(2,1)S(1)}, u32[]{:S(2)}, u32[]{:S(2)}) collective-permute-start(bf16[512,768]{1,0:T(8,128)(2,1)} %pack.11.refs_2_), channel_id=1, source_target_pairs={{0,12},{4,0},{8,4},{12,8},{1,13},{5,1},{9,5},{13,9},{2,14},{6,2},{... | collective-permute-start | bytes 2359304 | tf_op jit(solution)/shard_map/ppermute | solution.py:198
  129.3 0.9 copy-start.1
  130.2 0.9 copy-start.16
  133.1 1.4 copy-start.2
  133.1 3.4 %copy-start = (bf16[512,512]{1,0:T(8,128)(2,1)S(1)}, bf16[512,512]{1,0:T(8,128)(2,1)}, u32[]{:S(2)}) copy-start(bf16[512,512]{1,0:T(8,128)(2,1)} %pack.12.refs_3_.refs_2_) | copy-start | bytes 1572868
  133.1 0.9 copy-start.3
  134.5 20.5 %collective-permute-start.4 = (bf16[512,768]{1,0:T(8,128)(2,1)S(1)}, bf16[512,768]{1,0:T(8,128)(2,1)S(1)}, u32[]{:S(2)}, u32[]{:S(2)}) collective-permute-start(bf16[512,768]{1,0:T(8,128)(2,1)S(1)} %copy-done.2), channel_id=1, source_target_pairs={{0,16},{16,0},{1,17},{17,1},{2,18},{18,2},{3,19},{19,3},{4,20},{20... | collective-permute-start | bytes 2359304 | tf_op jit(solution)/shard_map/ppermute | solution.py:204
  135.0 36.9 %collective-permute-start.5 = (bf16[512,768]{1,0:T(8,128)(2,1)}, bf16[512,768]{1,0:T(8,128)(2,1)}, u32[]{:S(2)}, u32[]{:S(2)}) collective-permute-start(bf16[512,768]{1,0:T(8,128)(2,1)} %copy-done.3), channel_id=1, source_target_pairs={{0,16},{16,0},{1,17},{17,1},{2,18},{18,2},{3,19},{19,3},{4,20},{20... | collective-permute-start | bytes 2359304 | tf_op jit(solution)/shard_map/ppermute | solution.py:204
  136.5 24.6 %collective-permute-start.9 = (bf16[512,512]{1,0:T(8,128)(2,1)S(1)}, bf16[512,512]{1,0:T(8,128)(2,1)S(1)}, u32[]{:S(2)}, u32[]{:S(2)}) collective-permute-start(bf16[512,512]{1,0:T(8,128)(2,1)S(1)} %copy-done), channel_id=1, source_target_pairs={{0,4},{4,8},{8,12},{12,0},{1,5},{5,9},{9,13},{13,1},{2,6},{6,10},{... | collective-permute-start | bytes 1572872 | tf_op jit(solution)/shard_map/ppermute | solution.py:198
  155.0 0.9 copy-start.17
  157.8 30.6 %collective-permute-start.11 = (bf16[512,512]{1,0:T(8,128)(2,1)}, bf16[512,512]{1,0:T(8,128)(2,1)S(1)}, u32[]{:S(2)}, u32[]{:S(2)}) collective-permute-start(bf16[512,512]{1,0:T(8,128)(2,1)} %pack.13.refs_2_), channel_id=1, source_target_pairs={{0,8},{4,12},{8,0},{12,4},{1,9},{5,13},{9,1},{13,5},{2,10},{6,14},... | collective-permute-start | bytes 1572872 | tf_op jit(solution)/shard_map/ppermute | solution.py:198
  161.1 10.8 %copy-start.5 = (bf16[512,512]{1,0:T(8,128)(2,1)}, bf16[512,512]{1,0:T(8,128)(2,1)S(1)}, u32[]{:S(2)}) copy-start(bf16[512,512]{1,0:T(8,128)(2,1)S(1)} %collective-permute-done.9.refs_3_.refs_0_) | copy-start | bytes 1572868
  161.1 27.8 %collective-permute-start.10 = (bf16[512,512]{1,0:T(8,128)(2,1)S(1)}, bf16[512,512]{1,0:T(8,128)(2,1)S(1)}, u32[]{:S(2)}, u32[]{:S(2)}) collective-permute-start(bf16[512,512]{1,0:T(8,128)(2,1)S(1)} %collective-permute-done.9.refs_3_.refs_0_), channel_id=1, source_target_pairs={{0,16},{16,0},{1,17},{17,1},{2,18},{18,2},{3,19},{19,3},{4,20},{20... | collective-permute-start | bytes 1572872 | tf_op jit(solution)/shard_map/ppermute | solution.py:204
  173.9 18.1 %collective-permute-start.13 = (bf16[512,512]{1,0:T(8,128)(2,1)}, bf16[512,512]{1,0:T(8,128)(2,1)S(1)}, u32[]{:S(2)}, u32[]{:S(2)}) collective-permute-start(bf16[512,512]{1,0:T(8,128)(2,1)} %pack.14.refs_2_), channel_id=1, source_target_pairs={{0,12},{4,0},{8,4},{12,8},{1,13},{5,1},{9,5},{13,9},{2,14},{6,2},{... | collective-permute-start | bytes 1572872 | tf_op jit(solution)/shard_map/ppermute | solution.py:198
  188.4 0.8 copy-start.6
  188.4 14.8 %collective-permute-start.12 = (bf16[512,512]{1,0:T(8,128)(2,1)S(1)}, bf16[512,512]{1,0:T(8,128)(2,1)S(1)}, u32[]{:S(2)}, u32[]{:S(2)}) collective-permute-start(bf16[512,512]{1,0:T(8,128)(2,1)S(1)} %collective-permute-done.11.refs_2_.refs_3_), channel_id=1, source_target_pairs={{0,16},{16,0},{1,17},{17,1},{2,18},{18,2},{3,19},{19,3},{4,20},{20... | collective-permute-start | bytes 1572872 | tf_op jit(solution)/shard_map/ppermute | solution.py:204
  189.2 0.8 copy-start.7
  191.9 17.4 %collective-permute-start.18 = (bf16[512,512]{1,0:T(8,128)(2,1)}, bf16[512,512]{1,0:T(8,128)(2,1)S(1)}, u32[]{:S(2)}, u32[]{:S(2)}) collective-permute-start(bf16[512,512]{1,0:T(8,128)(2,1)} %pack.15.refs_2_), channel_id=1, source_target_pairs={{0,4},{4,8},{8,12},{12,0},{1,5},{5,9},{9,13},{13,1},{2,6},{6,10},{... | collective-permute-start | bytes 1572872 | tf_op jit(solution)/shard_map/ppermute | solution.py:198
  192.0 11.2 %copy-start.8 = (bf16[512,512]{1,0:T(8,128)(2,1)}, bf16[512,512]{1,0:T(8,128)(2,1)S(1)}, u32[]{:S(2)}) copy-start(bf16[512,512]{1,0:T(8,128)(2,1)S(1)} %collective-permute-done.13.refs_4_.refs_3_) | copy-start | bytes 1572868
  192.0 22.4 %collective-permute-start.14 = (bf16[512,512]{1,0:T(8,128)(2,1)S(1)}, bf16[512,512]{1,0:T(8,128)(2,1)S(1)}, u32[]{:S(2)}, u32[]{:S(2)}) collective-permute-start(bf16[512,512]{1,0:T(8,128)(2,1)S(1)} %collective-permute-done.13.refs_4_.refs_3_), channel_id=1, source_target_pairs={{0,16},{16,0},{1,17},{17,1},{2,18},{18,2},{3,19},{19,3},{4,20},{20... | collective-permute-start | bytes 1572872 | tf_op jit(solution)/shard_map/ppermute | solution.py:204
  203.2 0.8 copy-start.9
  206.0 32.9 %collective-permute-start.20 = (bf16[512,512]{1,0:T(8,128)(2,1)}, bf16[512,512]{1,0:T(8,128)(2,1)S(1)}, u32[]{:S(2)}, u32[]{:S(2)}) collective-permute-start(bf16[512,512]{1,0:T(8,128)(2,1)} %pack.16.refs_2_), channel_id=1, source_target_pairs={{0,8},{4,12},{8,0},{12,4},{1,9},{5,13},{9,1},{13,5},{2,10},{6,14},... | collective-permute-start | bytes 1572872 | tf_op jit(solution)/shard_map/ppermute | solution.py:198
  209.3 5.1 %copy-start.4 = (bf16[512,512]{1,0:T(8,128)(2,1)}, bf16[512,512]{1,0:T(8,128)(2,1)S(1)}, u32[]{:S(2)}) copy-start(bf16[512,512]{1,0:T(8,128)(2,1)S(1)} %collective-permute-done.18.refs_3_.refs_0_) | copy-start | bytes 1572868
  209.3 52.5 %collective-permute-start.19 = (bf16[512,512]{1,0:T(8,128)(2,1)S(1)}, bf16[512,512]{1,0:T(8,128)(2,1)S(1)}, u32[]{:S(2)}, u32[]{:S(2)}) collective-permute-start(bf16[512,512]{1,0:T(8,128)(2,1)S(1)} %collective-permute-done.18.refs_3_.refs_0_), channel_id=1, source_target_pairs={{0,16},{16,0},{1,17},{17,1},{2,18},{18,2},{3,19},{19,3},{4,20},{20... | collective-permute-start | bytes 1572872 | tf_op jit(solution)/shard_map/ppermute | solution.py:204
  214.4 0.8 copy-start.10
  217.3 42.6 %collective-permute-start.22 = (bf16[512,512]{1,0:T(8,128)(2,1)}, bf16[512,512]{1,0:T(8,128)(2,1)S(1)}, u32[]{:S(2)}, u32[]{:S(2)}) collective-permute-start(bf16[512,512]{1,0:T(8,128)(2,1)} %pack.17), channel_id=1, source_target_pairs={{0,12},{4,0},{8,4},{12,8},{1,13},{5,1},{9,5},{13,9},{2,14},{6,2},{... | collective-permute-start | bytes 1572872 | tf_op jit(solution)/shard_map/ppermute | solution.py:198
  238.8 17.5 %copy-start.18 = (bf16[512,512]{1,0:T(8,128)(2,1)}, bf16[512,512]{1,0:T(8,128)(2,1)S(1)}, u32[]{:S(2)}) copy-start(bf16[512,512]{1,0:T(8,128)(2,1)S(1)} %collective-permute-done.20.refs_2_) | copy-start | bytes 1572868
  238.8 36.0 %collective-permute-start.21 = (bf16[512,512]{1,0:T(8,128)(2,1)S(1)}, bf16[512,512]{1,0:T(8,128)(2,1)S(1)}, u32[]{:S(2)}, u32[]{:S(2)}) collective-permute-start(bf16[512,512]{1,0:T(8,128)(2,1)S(1)} %collective-permute-done.20.refs_2_), channel_id=1, source_target_pairs={{0,16},{16,0},{1,17},{17,1},{2,18},{18,2},{3,19},{19,3},{4,20},{20... | collective-permute-start | bytes 1572872 | tf_op jit(solution)/shard_map/ppermute | solution.py:204
  256.4 18.6 %collective-permute-start.6 = (bf16[384,384]{1,0:T(8,128)(2,1)}, bf16[384,384]{1,0:T(8,128)(2,1)S(1)}, u32[]{:S(2)}, u32[]{:S(2)}) collective-permute-start(bf16[384,384]{1,0:T(8,128)(2,1)} %get-tuple-element.18), channel_id=1, source_target_pairs={{0,4},{4,8},{8,12},{12,0},{1,5},{5,9},{9,13},{13,1},{2,6},{6,10},{... | collective-permute-start | bytes 884744 | tf_op jit(solution)/shard_map/ppermute | solution.py:210
  256.5 31.0 %collective-permute-start.7 = (bf16[384,384]{1,0:T(8,128)(2,1)}, bf16[384,384]{1,0:T(8,128)(2,1)S(1)}, u32[]{:S(2)}, u32[]{:S(2)}) collective-permute-start(bf16[384,384]{1,0:T(8,128)(2,1)} %get-tuple-element.19), channel_id=1, source_target_pairs={{0,8},{4,12},{8,0},{12,4},{1,9},{5,13},{9,1},{13,5},{2,10},{6,14},... | collective-permute-start | bytes 884744 | tf_op jit(solution)/shard_map/ppermute | solution.py:210
  259.8 2.0 copy-start.11
  259.8 34.6 %collective-permute-start.8 = (bf16[384,384]{1,0:T(8,128)(2,1)}, bf16[384,384]{1,0:T(8,128)(2,1)S(1)}, u32[]{:S(2)}, u32[]{:S(2)}) collective-permute-start(bf16[384,384]{1,0:T(8,128)(2,1)} %get-tuple-element.20), channel_id=1, source_target_pairs={{0,12},{4,0},{8,4},{12,8},{1,13},{5,1},{9,5},{13,9},{2,14},{6,2},{... | collective-permute-start | bytes 884744 | tf_op jit(solution)/shard_map/ppermute | solution.py:210
  261.8 13.0 %copy-start.19 = (bf16[512,512]{1,0:T(8,128)(2,1)}, bf16[512,512]{1,0:T(8,128)(2,1)S(1)}, u32[]{:S(2)}) copy-start(bf16[512,512]{1,0:T(8,128)(2,1)S(1)} %collective-permute-done.19.refs_1_) | copy-start | bytes 1572868
  261.8 32.6 %collective-permute-start.23 = (bf16[512,512]{1,0:T(8,128)(2,1)}, bf16[512,512]{1,0:T(8,128)(2,1)S(1)}, u32[]{:S(2)}, u32[]{:S(2)}) collective-permute-start(bf16[512,512]{1,0:T(8,128)(2,1)} %hold.3.refs_4_), channel_id=1, source_target_pairs={{0,16},{16,0},{1,17},{17,1},{2,18},{18,2},{3,19},{19,3},{4,20},{20... | collective-permute-start | bytes 1572872 | tf_op jit(solution)/shard_map/ppermute | solution.py:204
  274.8 19.6 %copy-start.20 = (bf16[512,512]{1,0:T(8,128)(2,1)}, bf16[512,512]{1,0:T(8,128)(2,1)S(1)}, u32[]{:S(2)}) copy-start(bf16[512,512]{1,0:T(8,128)(2,1)S(1)} %collective-permute-done.21.refs_3_) | copy-start | bytes 1572868
  274.8 34.7 %collective-permute-start.15 = (bf16[384,256]{1,0:T(8,128)(2,1)}, bf16[384,256]{1,0:T(8,128)(2,1)S(1)}, u32[]{:S(2)}, u32[]{:S(2)}) collective-permute-start(bf16[384,256]{1,0:T(8,128)(2,1)} %get-tuple-element.22), channel_id=1, source_target_pairs={{0,4},{4,8},{8,12},{12,0},{1,5},{5,9},{9,13},{13,1},{2,6},{6,10},{... | collective-permute-start | bytes 589832 | tf_op jit(solution)/shard_map/ppermute | solution.py:210
  275.0 19.4 %copy-start.12 = (bf16[384,384]{1,0:T(8,128)(2,1)}, bf16[384,384]{1,0:T(8,128)(2,1)S(1)}, u32[]{:S(2)}) copy-start(bf16[384,384]{1,0:T(8,128)(2,1)S(1)} %collective-permute-done.6.refs_7_.refs_1_) | copy-start | bytes 884740
  275.0 34.6 %collective-permute-start.16 = (bf16[384,256]{1,0:T(8,128)(2,1)}, bf16[384,256]{1,0:T(8,128)(2,1)S(1)}, u32[]{:S(2)}, u32[]{:S(2)}) collective-permute-start(bf16[384,256]{1,0:T(8,128)(2,1)} %get-tuple-element.23), channel_id=1, source_target_pairs={{0,8},{4,12},{8,0},{12,4},{1,9},{5,13},{9,1},{13,5},{2,10},{6,14},... | collective-permute-start | bytes 589832 | tf_op jit(solution)/shard_map/ppermute | solution.py:210
  287.5 6.9 %copy-start.13 = (bf16[384,384]{1,0:T(8,128)(2,1)}, bf16[384,384]{1,0:T(8,128)(2,1)S(1)}, u32[]{:S(2)}) copy-start(bf16[384,384]{1,0:T(8,128)(2,1)S(1)} %collective-permute-done.7.refs_8_.refs_2_) | copy-start | bytes 884740
  287.5 22.1 %collective-permute-start.17 = (bf16[384,256]{1,0:T(8,128)(2,1)}, bf16[384,256]{1,0:T(8,128)(2,1)S(1)}, u32[]{:S(2)}, u32[]{:S(2)}) collective-permute-start(bf16[384,256]{1,0:T(8,128)(2,1)} %get-tuple-element.24), channel_id=1, source_target_pairs={{0,12},{4,0},{8,4},{12,8},{1,13},{5,1},{9,5},{13,9},{2,14},{6,2},{... | collective-permute-start | bytes 589832 | tf_op jit(solution)/shard_map/ppermute | solution.py:210
  294.4 0.7 copy-start.14
  294.4 0.9 copy-start.21
  307.2 8.0 %collective-permute-start.24 = (bf16[384,256]{1,0:T(8,128)(2,1)}, bf16[384,256]{1,0:T(8,128)(2,1)S(1)}, u32[]{:S(2)}, u32[]{:S(2)}) collective-permute-start(bf16[384,256]{1,0:T(8,128)(2,1)} %get-tuple-element.26), channel_id=1, source_target_pairs={{0,4},{4,8},{8,12},{12,0},{1,5},{5,9},{9,13},{13,1},{2,6},{6,10},{... | collective-permute-start | bytes 589832 | tf_op jit(solution)/shard_map/ppermute | solution.py:210
  307.3 17.5 %collective-permute-start.25 = (bf16[384,256]{1,0:T(8,128)(2,1)}, bf16[384,256]{1,0:T(8,128)(2,1)S(1)}, u32[]{:S(2)}, u32[]{:S(2)}) collective-permute-start(bf16[384,256]{1,0:T(8,128)(2,1)} %get-tuple-element.27), channel_id=1, source_target_pairs={{0,8},{4,12},{8,0},{12,4},{1,9},{5,13},{9,1},{13,5},{2,10},{6,14},... | collective-permute-start | bytes 589832 | tf_op jit(solution)/shard_map/ppermute | solution.py:210
  309.5 16.2 %copy-start.22 = (bf16[384,256]{1,0:T(8,128)(2,1)}, bf16[384,256]{1,0:T(8,128)(2,1)S(1)}, u32[]{:S(2)}) copy-start(bf16[384,256]{1,0:T(8,128)(2,1)S(1)} %collective-permute-done.15.refs_5_) | copy-start | bytes 589828
  309.5 16.2 %collective-permute-start.26 = (bf16[384,256]{1,0:T(8,128)(2,1)}, bf16[384,256]{1,0:T(8,128)(2,1)S(1)}, u32[]{:S(2)}, u32[]{:S(2)}) collective-permute-start(bf16[384,256]{1,0:T(8,128)(2,1)} %get-tuple-element.28), channel_id=1, source_target_pairs={{0,12},{4,0},{8,4},{12,8},{1,13},{5,1},{9,5},{13,9},{2,14},{6,2},{... | collective-permute-start | bytes 589832 | tf_op jit(solution)/shard_map/ppermute | solution.py:210
  309.5 16.2 %copy-start.23 = (bf16[384,256]{1,0:T(8,128)(2,1)}, bf16[384,256]{1,0:T(8,128)(2,1)S(1)}, u32[]{:S(2)}) copy-start(bf16[384,256]{1,0:T(8,128)(2,1)S(1)} %collective-permute-done.16.refs_6_) | copy-start | bytes 589828
  309.5 16.2 %copy-start.24 = (bf16[384,256]{1,0:T(8,128)(2,1)}, bf16[384,256]{1,0:T(8,128)(2,1)S(1)}, u32[]{:S(2)}) copy-start(bf16[384,256]{1,0:T(8,128)(2,1)S(1)} %collective-permute-done.17.refs_7_) | copy-start | bytes 589828
  315.3 10.5 %copy-start.25 = (bf16[384,256]{1,0:T(8,128)(2,1)}, bf16[384,256]{1,0:T(8,128)(2,1)S(1)}, u32[]{:S(2)}) copy-start(bf16[384,256]{1,0:T(8,128)(2,1)S(1)} %collective-permute-done.24.refs_9_) | copy-start | bytes 589828
  324.8 1.0 copy-start.26
  325.7 0.7 copy-start.27
Sparse Core Ops, SparseCore 0:
  8.9 119.6 all-gather.2
  134.1 83.8 all-gather.4

commit v6 on v5

--- a/solution.py
+++ b/solution.py
@@ -13,6 +13,10 @@
 
 def around(size, shift):
     return [(i, (i + shift) % size) for i in range(size)]
+
+
+def by_distance(size):
+    return sorted(range(1, size), key=lambda shift: -min(shift, size - shift))
 
 
 def run_all(copies):
@@ -74,8 +78,9 @@
     rows, parts = lax.axis_size("row"), lax.axis_size("parts")
     share, width, tiles = depth // parts, ff // rows, wide // LANES
     features = rows * depth
-    order = list(range(1, rows)) + [0]
-    pieces = [(shift, turn) for shift in range(1, rows) for turn in range(parts)]
+    columns, near = tokens.shape[1], tokens.shape[3]
+    order = by_distance(rows) + [0]
+    pieces = [(shift, turn) for shift in by_distance(rows) for turn in range(parts)]
 
     def body(tokens_ref, gate_ref, up_ref, *refs):
         held_refs = refs[:len(pieces)]
@@ -85,11 +90,12 @@
 
         def fetch(step):
             to = lax.rem(z + order[step], rows)
-            return pltpu.make_async_copy(
-                tokens_ref.at[pl.ds(pl.multiple_of(to * mine, mine), mine), :],
-                block.at[step % 2],
-                block_sems.at[step % 2],
-            )
+            return [
+                pltpu.make_async_copy(
+                    tokens_ref.at[to, j], block.at[step % 2, :, pl.ds(j * near, near)], block_sems.at[step % 2, j]
+                )
+                for j in range(columns)
+            ]
 
         copies = []
         for ref, (shift, turn) in zip(held_refs, pieces):
@@ -106,12 +112,15 @@
                     stack.at[pl.ds(own, depth), pl.ds((2 * j + g) * LANES, LANES)],
                     sems.at[len(copies)],
                 ))
-        fetch(0).start()
+        for copy in fetch(0):
+            copy.start()
         run_all(copies)
         for step, shift in enumerate(order):
-            fetch(step).wait()
+            for copy in fetch(step):
+                copy.wait()
             if step + 1 < rows:
-                fetch(step + 1).start()
+                for copy in fetch(step + 1):
+                    copy.start()
 
             def tile(j, carry, step=step, shift=shift):
                 both = jnp.dot(
@@ -137,7 +146,7 @@
             pltpu.VMEM((features, 2 * wide), gate_weight.dtype),
             pltpu.VMEM((2, mine, features), tokens.dtype),
             pltpu.SemaphoreType.DMA((len(pieces) + 2 * tiles,)),
-            pltpu.SemaphoreType.DMA((2,)),
+            pltpu.SemaphoreType.DMA((2, columns)),
         ],
         compiler_params=pltpu.CompilerParams(vmem_limit_bytes=GRANT),
         cost_estimate=pl.CostEstimate(
@@ -181,7 +190,7 @@
     width = ff // rows
     units = width // LANES
 
-    block_rows = lax.all_gather(tokens, "row", axis=0, tiled=True)
+    whole = lax.all_gather(tokens, ("row", "col")).reshape(rows, -1, *tokens.shape)
 
     edges, total = [0], sum(PIECES)
     for piece in range(len(PIECES)):
@@ -192,12 +201,12 @@
 
     def weights_of(n):
         low, high = spans[n]
-        for shift in range(1, rows):
+        for shift in by_distance(rows):
             after = sent[-1:] + arrived[-2:-1] + swapped[-3:-2]
             sent.append(pack(gate_weight, up_weight, shift, low, high - low, after))
             arrived.append(lax.ppermute(sent[-1], "row", around(rows, shift)))
             came = arrived[-1]
-            if done and shift == rows - 1:
+            if done and len(sent) > len(spans) * (rows - 1) - 2:
                 came = hold(came, done)
             held[n].append(came)
             for turn in range(1, parts):
@@ -217,7 +226,6 @@
     held = [[] for _ in spans]
     for n in range(last):
         weights_of(n)
-    whole = lax.all_gather(hold(block_rows, arrived[1:3] + sent[3:4]), "col", axis=1, tiled=True)
     if last:
         hidden_of(0, [])
     weights_of(last)

time: 338 us -> 342 us (1.012)
  starting transfers between devices: 32.6 us -> 81.2 us
  waiting for transfers between devices: 220 us -> 176 us
    ppermute x9, starting transfers between devices: 9.84 us -> 62.6 us  [weights_of(): arrived.append(lax.ppermute(sent[-1], 'row', around(rows, shift)))]
    ppermute x9, waiting for transfers between devices: 43.2 us -> 1.2 us  [weights_of(): swapped.append(lax.ppermute(came, 'parts', around(parts, -turn)))]
    ppermute x9, waiting for transfers between devices: 32.5 us -> 27.7 us  [hidden_of(): lax.ppermute(outs[shift], 'row', around(rows, shift))]
    ppermute x9, starting transfers between devices: 11.9 us -> 7.52 us  [weights_of(): swapped.append(lax.ppermute(came, 'parts', around(parts, -turn)))]
    unnamed x56 -> x52, local copies, waits for them, and re-layouts: 8.22 us -> 8.12 us
  transfers between devices with their start and end apart: 29 -> 28, of which waited for: 13 -> 9; matrix products, arithmetic and copies ran while one was open for 0% -> 0% of each run, Pallas kernels for 17% -> 17%
where the time goes in v6:
time: 342 us; the launch traced here: 341 us
  waiting for transfers between devices  176 us (51%)
  starting transfers between devices  81.2 us (24%)
  Pallas kernels  61.8 us (18%)
  between operations  13.8 us (4%)
  local copies, waits for them, and re-layouts  8.12 us (2%)
    ppermute x9, waiting for transfers between devices, weights_of(): arrived.append(lax.ppermute(sent[-1], 'row', around(rows, shift)))  146 us
    ppermute x9, starting transfers between devices, weights_of(): arrived.append(lax.ppermute(sent[-1], 'row', around(rows, shift)))  62.6 us
    pallas_call x3, Pallas kernels, product(): pl.pallas_call(body, out_shape=[jax.ShapeDtypeStruct((mine, wide), jnp.bf...  40.4 us
    ppermute x9, waiting for transfers between devices, hidden_of(): lax.ppermute(outs[shift], 'row', around(rows, shift))  27.7 us
    pallas_call x9, Pallas kernels, pack(): pl.pallas_call(body, out_shape=jax.ShapeDtypeStruct((share, 2 * wide), ga...  18.1 us
    ppermute x9, starting transfers between devices, hidden_of(): lax.ppermute(outs[shift], 'row', around(rows, shift))  11.1 us
    unnamed x52, local copies, waits for them, and re-layouts  8.12 us
    ppermute x9, starting transfers between devices, weights_of(): swapped.append(lax.ppermute(came, 'parts', around(parts, -turn)))  7.52 us
  transfers between devices with their start and end apart: 28, of which 9 were waited for; matrix products, arithmetic and copies ran while one was open for 0% of the time, Pallas kernels for 17%

profile of v6, /device:TPU:12, one launch (start us, length us, event | category | flops | bytes accessed | tf_op | source)
XLA Modules:
  0.0 340.9 jit_solution(15190421721399142472)
XLA Ops:
  6.5 0.7 all-gather.3.cloned.1.call-update
  7.3 2.2 pack.9.refs_2_
  9.4 2.7 collective-permute-start
  12.1 2.2 pack.10.refs_2_
  14.3 0.1 collective-permute-start.2
  14.3 53.9 %collective-permute-done.refs_3_.refs_0_ = bf16[512,768]{1,0:T(8,128)(2,1)S(1)} collective-permute-done((bf16[512,768]{1,0:T(8,128)(2,1)}, bf16[512,768]{1,0:T(8,128)(2,1)S(1)}, u32[]{:S(2)}, u32[]{:S(2)}) %collective-permute-start) | collective-permute-done | bytes 786464 | tf_op jit(solution)/shard_map/ppermute | solution.py:207
  68.2 0.9 copy-done.12
  69.1 2.2 pack.11.refs_2_
  71.2 21.5 %collective-permute-start.4 = (bf16[512,768]{1,0:T(8,128)(2,1)}, bf16[512,768]{1,0:T(8,128)(2,1)S(1)}, u32[]{:S(2)}, u32[]{:S(2)}) collective-permute-start(bf16[512,768]{1,0:T(8,128)(2,1)} %pack.11.refs_2_), channel_id=1, source_target_pairs={{0,12},{4,0},{8,4},{12,8},{1,13},{5,1},{9,5},{13,9},{2,14},{6,2},{... | collective-permute-start | bytes 2359304 | tf_op jit(solution)/shard_map/ppermute | solution.py:207
  92.8 0.5 collective-permute-start.1
  93.2 0.0 collective-permute-done.2.refs_2_.refs_3_
  93.2 1.6 collective-permute-start.3
  94.8 51.5 %collective-permute-done.4.refs_4_.refs_3_ = bf16[512,768]{1,0:T(8,128)(2,1)S(1)} collective-permute-done((bf16[512,768]{1,0:T(8,128)(2,1)}, bf16[512,768]{1,0:T(8,128)(2,1)S(1)}, u32[]{:S(2)}, u32[]{:S(2)}) %collective-permute-start.4) | collective-permute-done | bytes 786464 | tf_op jit(solution)/shard_map/ppermute | solution.py:207
  146.3 0.0 collective-permute-start.5
  146.3 0.0 collective-permute-done.1.refs_1_.refs_4_
  146.3 0.9 copy-done.15
  147.2 1.9 pack.12.refs_2_
  149.2 0.1 collective-permute-start.9
  149.2 0.0 collective-permute-done.3.refs_3_.refs_4_
  149.3 0.9 copy-done.16
  150.1 1.9 pack.13.refs_2_
  152.1 4.7 %collective-permute-start.11 = (bf16[512,512]{1,0:T(8,128)(2,1)}, bf16[512,512]{1,0:T(8,128)(2,1)S(1)}, u32[]{:S(2)}, u32[]{:S(2)}) collective-permute-start(bf16[512,512]{1,0:T(8,128)(2,1)} %pack.13.refs_2_), channel_id=1, source_target_pairs={{0,4},{4,8},{8,12},{12,0},{1,5},{5,9},{9,13},{13,1},{2,6},{6,10},{... | collective-permute-start | bytes 1572872 | tf_op jit(solution)/shard_map/ppermute | solution.py:207
  156.8 23.8 %collective-permute-done.9.refs_3_.refs_0_ = bf16[512,512]{1,0:T(8,128)(2,1)S(1)} collective-permute-done((bf16[512,512]{1,0:T(8,128)(2,1)}, bf16[512,512]{1,0:T(8,128)(2,1)S(1)}, u32[]{:S(2)}, u32[]{:S(2)}) %collective-permute-start.9) | collective-permute-done | bytes 524320 | tf_op jit(solution)/shard_map/ppermute | solution.py:207
  180.6 0.4 collective-permute-start.10
  181.0 0.5 copy-done.1
  181.4 1.9 pack.14.refs_2_
  183.4 12.7 %collective-permute-start.13 = (bf16[512,512]{1,0:T(8,128)(2,1)}, bf16[512,512]{1,0:T(8,128)(2,1)S(1)}, u32[]{:S(2)}, u32[]{:S(2)}) collective-permute-start(bf16[512,512]{1,0:T(8,128)(2,1)} %pack.14.refs_2_), channel_id=1, source_target_pairs={{0,12},{4,0},{8,4},{12,8},{1,13},{5,1},{9,5},{13,9},{2,14},{6,2},{... | collective-permute-start | bytes 1572872 | tf_op jit(solution)/shard_map/ppermute | solution.py:207
  196.1 1.2 collective-permute-start.12
  197.3 0.8 copy-done.3
  198.1 1.9 pack.15.refs_2_
  200.0 0.1 collective-permute-start.18
  200.1 7.5 %collective-permute-done.13.refs_4_.refs_3_ = bf16[512,512]{1,0:T(8,128)(2,1)S(1)} collective-permute-done((bf16[512,512]{1,0:T(8,128)(2,1)}, bf16[512,512]{1,0:T(8,128)(2,1)S(1)}, u32[]{:S(2)}, u32[]{:S(2)}) %collective-permute-start.13) | collective-permute-done | bytes 524320 | tf_op jit(solution)/shard_map/ppermute | solution.py:207
  207.7 0.9 collective-permute-start.14
  208.6 1.2 collective-permute-done.12.refs_3_.refs_4_
  209.8 0.8 copy-done.5
  210.6 1.9 pack.16.refs_2_
  212.5 7.8 %collective-permute-start.20 = (bf16[512,512]{1,0:T(8,128)(2,1)}, bf16[512,512]{1,0:T(8,128)(2,1)S(1)}, u32[]{:S(2)}, u32[]{:S(2)}) collective-permute-start(bf16[512,512]{1,0:T(8,128)(2,1)} %pack.16.refs_2_), channel_id=1, source_target_pairs={{0,4},{4,8},{8,12},{12,0},{1,5},{5,9},{9,13},{13,1},{2,6},{6,10},{... | collective-permute-start | bytes 1572872 | tf_op jit(solution)/shard_map/ppermute | solution.py:207
  220.3 9.7 %collective-permute-done.18.refs_3_.refs_0_ = bf16[512,512]{1,0:T(8,128)(2,1)S(1)} collective-permute-done((bf16[512,512]{1,0:T(8,128)(2,1)}, bf16[512,512]{1,0:T(8,128)(2,1)S(1)}, u32[]{:S(2)}, u32[]{:S(2)}) %collective-permute-start.18) | collective-permute-done | bytes 524320 | tf_op jit(solution)/shard_map/ppermute | solution.py:207
  230.0 0.9 collective-permute-start.19
  230.9 0.8 copy-done.6
  231.7 1.9 pack.17
  233.6 12.9 %collective-permute-start.22 = (bf16[512,512]{1,0:T(8,128)(2,1)}, bf16[512,512]{1,0:T(8,128)(2,1)S(1)}, u32[]{:S(2)}, u32[]{:S(2)}) collective-permute-start(bf16[512,512]{1,0:T(8,128)(2,1)} %pack.17), channel_id=1, source_target_pairs={{0,12},{4,0},{8,4},{12,8},{1,13},{5,1},{9,5},{13,9},{2,14},{6,2},{... | collective-permute-start | bytes 1572872 | tf_op jit(solution)/shard_map/ppermute | solution.py:207
  246.5 16.6 %product.3 = (bf16[384,384]{1,0:T(8,128)(2,1)}, bf16[384,384]{1,0:T(8,128)(2,1)}, bf16[384,384]{1,0:T(8,128)(2,1)}, bf16[384,384]{1,0:T(8,128)(2,1)}) custom-call(bf16[4,4,384,1024]{3,2,1,0:T(8,128)(2,1)} %bitcast.1, bf16[1024,3584]{1,0:T(8,128)(2,1)} %gate_ref.5, bf16[1024,3584]{1,0:T(8,128)(2,1)} %up_ref.5, bf16[512,768]{1,0:T(8,128)(2,1)} %copy-done.12, ...), custom_call_target="tpu_custom_call" | custom-call | flops 9663676416 | bytes 20054016 | tf_op jit(solution)/shard_map/product/pallas_call | solution.py:140
  263.1 0.1 collective-permute-start.6
  263.2 2.4 collective-permute-start.7
  265.6 0.8 copy-done.7
  266.4 1.1 collective-permute-start.21
  267.6 1.0 collective-permute-start.23
  268.5 11.9 %product.4 = (bf16[384,256]{1,0:T(8,128)(2,1)}, bf16[384,256]{1,0:T(8,128)(2,1)}, bf16[384,256]{1,0:T(8,128)(2,1)}, bf16[384,256]{1,0:T(8,128)(2,1)}) custom-call(bf16[4,4,384,1024]{3,2,1,0:T(8,128)(2,1)} %bitcast.2, bf16[1024,3584]{1,0:T(8,128)(2,1)} %gate_ref.5, bf16[1024,3584]{1,0:T(8,128)(2,1)} %up_ref.5, bf16[512,512]{1,0:T(8,128)(2,1)} %copy-done.1, ...), custom_call_target="tpu_custom_call" | custom-call | flops 6442450944 | bytes 17563648 | tf_op jit(solution)/shard_map/product/pallas_call | solution.py:140
  280.5 1.4 collective-permute-start.15
  281.8 14.4 %collective-permute-done.7.refs_8_.refs_2_ = bf16[384,384]{1,0:T(8,128)(2,1)S(1)} collective-permute-done((bf16[384,384]{1,0:T(8,128)(2,1)}, bf16[384,384]{1,0:T(8,128)(2,1)S(1)}, u32[]{:S(2)}, u32[]{:S(2)}) %collective-permute-start.7) | collective-permute-done | bytes 294944 | tf_op jit(solution)/shard_map/ppermute | solution.py:219
  296.3 3.3 collective-permute-start.16
  299.5 0.0 collective-permute-start.17
  299.6 0.6 copy-done.11
  300.3 0.2 copy-done.18
  300.4 0.2 copy-done.19
  300.6 11.9 %product.5 = (bf16[384,256]{1,0:T(8,128)(2,1)}, bf16[384,256]{1,0:T(8,128)(2,1)}, bf16[384,256]{1,0:T(8,128)(2,1)}, bf16[384,256]{1,0:T(8,128)(2,1)}) custom-call(bf16[4,4,384,1024]{3,2,1,0:T(8,128)(2,1)} %bitcast.3, bf16[1024,3584]{1,0:T(8,128)(2,1)} %gate_ref.5, bf16[1024,3584]{1,0:T(8,128)(2,1)} %up_ref.5, bf16[512,512]{1,0:T(8,128)(2,1)} %copy-done, ...), custom_call_target="tpu_custom_call" | custom-call | flops 6442450944 | bytes 17563648 | tf_op jit(solution)/shard_map/product/pallas_call | solution.py:140
  312.5 2.0 collective-permute-start.24
  314.5 2.0 collective-permute-start.25
  316.6 11.2 %collective-permute-done.24.refs_9_ = bf16[384,256]{1,0:T(8,128)(2,1)S(1)} collective-permute-done((bf16[384,256]{1,0:T(8,128)(2,1)}, bf16[384,256]{1,0:T(8,128)(2,1)S(1)}, u32[]{:S(2)}, u32[]{:S(2)}) %collective-permute-start.24) | collective-permute-done | bytes 196640 | tf_op jit(solution)/shard_map/ppermute | solution.py:219
  327.8 2.1 collective-permute-done.25.refs_10_
  329.9 0.6 copy-done.24
  330.6 0.1 copy-done.25
  330.7 3.3 place.1
  (60 shorter events, 0.1 us)
Async XLA Ops:
  6.5 240.0 %all-gather.3.cloned.1.call-start = ((), (), s32[]{:S(2)}) async-start(), calls=%async_computation | async-start | bytes 13369344 | tf_op jit(solution)/shard_map/all_gather | solution.py:193
  9.4 58.8 %collective-permute-start = (bf16[512,768]{1,0:T(8,128)(2,1)}, bf16[512,768]{1,0:T(8,128)(2,1)S(1)}, u32[]{:S(2)}, u32[]{:S(2)}) collective-permute-start(bf16[512,768]{1,0:T(8,128)(2,1)} %pack.9.refs_2_), channel_id=1, source_target_pairs={{0,8},{4,12},{8,0},{12,4},{1,9},{5,13},{9,1},{13,5},{2,10},{6,14},... | collective-permute-start | bytes 2359304 | tf_op jit(solution)/shard_map/ppermute | solution.py:207
  14.3 79.0 %collective-permute-start.2 = (bf16[512,768]{1,0:T(8,128)(2,1)}, bf16[512,768]{1,0:T(8,128)(2,1)S(1)}, u32[]{:S(2)}, u32[]{:S(2)}) collective-permute-start(bf16[512,768]{1,0:T(8,128)(2,1)} %pack.10.refs_2_), channel_id=1, source_target_pairs={{0,4},{4,8},{8,12},{12,0},{1,5},{5,9},{9,13},{13,1},{2,6},{6,10},{... | collective-permute-start | bytes 2359304 | tf_op jit(solution)/shard_map/ppermute | solution.py:207
  68.2 0.9 copy-start.12
  71.2 75.0 %collective-permute-start.4 = (bf16[512,768]{1,0:T(8,128)(2,1)}, bf16[512,768]{1,0:T(8,128)(2,1)S(1)}, u32[]{:S(2)}, u32[]{:S(2)}) collective-permute-start(bf16[512,768]{1,0:T(8,128)(2,1)} %pack.11.refs_2_), channel_id=1, source_target_pairs={{0,12},{4,0},{8,4},{12,8},{1,13},{5,1},{9,5},{13,9},{2,14},{6,2},{... | collective-permute-start | bytes 2359304 | tf_op jit(solution)/shard_map/ppermute | solution.py:207
  92.8 53.5 %collective-permute-start.1 = (bf16[512,768]{1,0:T(8,128)(2,1)}, bf16[512,768]{1,0:T(8,128)(2,1)S(1)}, u32[]{:S(2)}, u32[]{:S(2)}) collective-permute-start(bf16[512,768]{1,0:T(8,128)(2,1)} %copy-done.12), channel_id=1, source_target_pairs={{0,16},{16,0},{1,17},{17,1},{2,18},{18,2},{3,19},{19,3},{4,20},{20... | collective-permute-start | bytes 2359304 | tf_op jit(solution)/shard_map/ppermute | solution.py:213
  93.2 53.1 %copy-start.13 = (bf16[512,768]{1,0:T(8,128)(2,1)}, bf16[512,768]{1,0:T(8,128)(2,1)S(1)}, u32[]{:S(2)}) copy-start(bf16[512,768]{1,0:T(8,128)(2,1)S(1)} %collective-permute-done.2.refs_2_.refs_3_) | copy-start | bytes 2359300
  93.2 56.0 %collective-permute-start.3 = (bf16[512,768]{1,0:T(8,128)(2,1)S(1)}, bf16[512,768]{1,0:T(8,128)(2,1)S(1)}, u32[]{:S(2)}, u32[]{:S(2)}) collective-permute-start(bf16[512,768]{1,0:T(8,128)(2,1)S(1)} %collective-permute-done.2.refs_2_.refs_3_), channel_id=1, source_target_pairs={{0,16},{16,0},{1,17},{17,1},{2,18},{18,2},{3,19},{19,3},{4,20},{20... | collective-permute-start | bytes 2359304 | tf_op jit(solution)/shard_map/ppermute | solution.py:213
  146.3 2.9 copy-start.14
  146.3 34.7 %collective-permute-start.5 = (bf16[512,768]{1,0:T(8,128)(2,1)S(1)}, bf16[512,768]{1,0:T(8,128)(2,1)}, u32[]{:S(2)}, u32[]{:S(2)}) collective-permute-start(bf16[512,768]{1,0:T(8,128)(2,1)S(1)} %collective-permute-done.4.refs_4_.refs_3_), channel_id=1, source_target_pairs={{0,16},{16,0},{1,17},{17,1},{2,18},{18,2},{3,19},{19,3},{4,20},{20... | collective-permute-start | bytes 2359304 | tf_op jit(solution)/shard_map/ppermute | solution.py:213
  146.3 0.9 copy-start.15
  149.2 31.4 %collective-permute-start.9 = (bf16[512,512]{1,0:T(8,128)(2,1)}, bf16[512,512]{1,0:T(8,128)(2,1)S(1)}, u32[]{:S(2)}, u32[]{:S(2)}) collective-permute-start(bf16[512,512]{1,0:T(8,128)(2,1)} %pack.12.refs_2_), channel_id=1, source_target_pairs={{0,8},{4,12},{8,0},{12,4},{1,9},{5,13},{9,1},{13,5},{2,10},{6,14},... | collective-permute-start | bytes 1572872 | tf_op jit(solution)/shard_map/ppermute | solution.py:207
  149.2 0.9 copy-start.16
  152.1 44.0 %collective-permute-start.11 = (bf16[512,512]{1,0:T(8,128)(2,1)}, bf16[512,512]{1,0:T(8,128)(2,1)S(1)}, u32[]{:S(2)}, u32[]{:S(2)}) collective-permute-start(bf16[512,512]{1,0:T(8,128)(2,1)} %pack.13.refs_2_), channel_id=1, source_target_pairs={{0,4},{4,8},{8,12},{12,0},{1,5},{5,9},{9,13},{13,1},{2,6},{6,10},{... | collective-permute-start | bytes 1572872 | tf_op jit(solution)/shard_map/ppermute | solution.py:207
  180.6 0.8 copy-start.1
  180.6 16.7 %collective-permute-start.10 = (bf16[512,512]{1,0:T(8,128)(2,1)S(1)}, bf16[512,512]{1,0:T(8,128)(2,1)S(1)}, u32[]{:S(2)}, u32[]{:S(2)}) collective-permute-start(bf16[512,512]{1,0:T(8,128)(2,1)S(1)} %collective-permute-done.9.refs_3_.refs_0_), channel_id=1, source_target_pairs={{0,16},{16,0},{1,17},{17,1},{2,18},{18,2},{3,19},{19,3},{4,20},{20... | collective-permute-start | bytes 1572872 | tf_op jit(solution)/shard_map/ppermute | solution.py:213
  183.4 24.3 %collective-permute-start.13 = (bf16[512,512]{1,0:T(8,128)(2,1)}, bf16[512,512]{1,0:T(8,128)(2,1)S(1)}, u32[]{:S(2)}, u32[]{:S(2)}) collective-permute-start(bf16[512,512]{1,0:T(8,128)(2,1)} %pack.14.refs_2_), channel_id=1, source_target_pairs={{0,12},{4,0},{8,4},{12,8},{1,13},{5,1},{9,5},{13,9},{2,14},{6,2},{... | collective-permute-start | bytes 1572872 | tf_op jit(solution)/shard_map/ppermute | solution.py:207
  196.1 1.2 copy-start.2
  196.1 13.6 %collective-permute-start.12 = (bf16[512,512]{1,0:T(8,128)(2,1)S(1)}, bf16[512,512]{1,0:T(8,128)(2,1)S(1)}, u32[]{:S(2)}, u32[]{:S(2)}) collective-permute-start(bf16[512,512]{1,0:T(8,128)(2,1)S(1)} %collective-permute-done.11.refs_2_.refs_3_), channel_id=1, source_target_pairs={{0,16},{16,0},{1,17},{17,1},{2,18},{18,2},{3,19},{19,3},{4,20},{20... | collective-permute-start | bytes 1572872 | tf_op jit(solution)/shard_map/ppermute | solution.py:213
  197.3 0.8 copy-start.3
  200.0 29.9 %collective-permute-start.18 = (bf16[512,512]{1,0:T(8,128)(2,1)}, bf16[512,512]{1,0:T(8,128)(2,1)S(1)}, u32[]{:S(2)}, u32[]{:S(2)}) collective-permute-start(bf16[512,512]{1,0:T(8,128)(2,1)} %pack.15.refs_2_), channel_id=1, source_target_pairs={{0,8},{4,12},{8,0},{12,4},{1,9},{5,13},{9,1},{13,5},{2,10},{6,14},... | collective-permute-start | bytes 1572872 | tf_op jit(solution)/shard_map/ppermute | solution.py:207
  207.7 2.1 copy-start.4
  207.7 23.3 %collective-permute-start.14 = (bf16[512,512]{1,0:T(8,128)(2,1)S(1)}, bf16[512,512]{1,0:T(8,128)(2,1)S(1)}, u32[]{:S(2)}, u32[]{:S(2)}) collective-permute-start(bf16[512,512]{1,0:T(8,128)(2,1)S(1)} %collective-permute-done.13.refs_4_.refs_3_), channel_id=1, source_target_pairs={{0,16},{16,0},{1,17},{17,1},{2,18},{18,2},{3,19},{19,3},{4,20},{20... | collective-permute-start | bytes 1572872 | tf_op jit(solution)/shard_map/ppermute | solution.py:213
  209.8 0.8 copy-start.5
  212.5 53.1 %collective-permute-start.20 = (bf16[512,512]{1,0:T(8,128)(2,1)}, bf16[512,512]{1,0:T(8,128)(2,1)S(1)}, u32[]{:S(2)}, u32[]{:S(2)}) collective-permute-start(bf16[512,512]{1,0:T(8,128)(2,1)} %pack.16.refs_2_), channel_id=1, source_target_pairs={{0,4},{4,8},{8,12},{12,0},{1,5},{5,9},{9,13},{13,1},{2,6},{6,10},{... | collective-permute-start | bytes 1572872 | tf_op jit(solution)/shard_map/ppermute | solution.py:207
  230.0 0.9 copy-start
  230.0 37.6 %collective-permute-start.19 = (bf16[512,512]{1,0:T(8,128)(2,1)S(1)}, bf16[512,512]{1,0:T(8,128)(2,1)S(1)}, u32[]{:S(2)}, u32[]{:S(2)}) collective-permute-start(bf16[512,512]{1,0:T(8,128)(2,1)S(1)} %collective-permute-done.18.refs_3_.refs_0_), channel_id=1, source_target_pairs={{0,16},{16,0},{1,17},{17,1},{2,18},{18,2},{3,19},{19,3},{4,20},{20... | collective-permute-start | bytes 1572872 | tf_op jit(solution)/shard_map/ppermute | solution.py:213
  230.9 0.8 copy-start.6
  233.6 32.8 %collective-permute-start.22 = (bf16[512,512]{1,0:T(8,128)(2,1)}, bf16[512,512]{1,0:T(8,128)(2,1)S(1)}, u32[]{:S(2)}, u32[]{:S(2)}) collective-permute-start(bf16[512,512]{1,0:T(8,128)(2,1)} %pack.17), channel_id=1, source_target_pairs={{0,12},{4,0},{8,4},{12,8},{1,13},{5,1},{9,5},{13,9},{2,14},{6,2},{... | collective-permute-start | bytes 1572872 | tf_op jit(solution)/shard_map/ppermute | solution.py:207
  263.1 17.3 %collective-permute-start.6 = (bf16[384,384]{1,0:T(8,128)(2,1)}, bf16[384,384]{1,0:T(8,128)(2,1)S(1)}, u32[]{:S(2)}, u32[]{:S(2)}) collective-permute-start(bf16[384,384]{1,0:T(8,128)(2,1)} %get-tuple-element.18), channel_id=1, source_target_pairs={{0,4},{4,8},{8,12},{12,0},{1,5},{5,9},{9,13},{13,1},{2,6},{6,10},{... | collective-permute-start | bytes 884744 | tf_op jit(solution)/shard_map/ppermute | solution.py:219
  263.2 33.0 %collective-permute-start.7 = (bf16[384,384]{1,0:T(8,128)(2,1)}, bf16[384,384]{1,0:T(8,128)(2,1)S(1)}, u32[]{:S(2)}, u32[]{:S(2)}) collective-permute-start(bf16[384,384]{1,0:T(8,128)(2,1)} %get-tuple-element.19), channel_id=1, source_target_pairs={{0,8},{4,12},{8,0},{12,4},{1,9},{5,13},{9,1},{13,5},{2,10},{6,14},... | collective-permute-start | bytes 884744 | tf_op jit(solution)/shard_map/ppermute | solution.py:219
  265.6 0.8 copy-start.7
  265.6 33.9 %collective-permute-start.8 = (bf16[384,384]{1,0:T(8,128)(2,1)}, bf16[384,384]{1,0:T(8,128)(2,1)S(1)}, u32[]{:S(2)}, u32[]{:S(2)}) collective-permute-start(bf16[384,384]{1,0:T(8,128)(2,1)} %get-tuple-element.20), channel_id=1, source_target_pairs={{0,12},{4,0},{8,4},{12,8},{1,13},{5,1},{9,5},{13,9},{2,14},{6,2},{... | collective-permute-start | bytes 884744 | tf_op jit(solution)/shard_map/ppermute | solution.py:219
  266.4 1.1 copy-start.8
  266.4 33.1 %collective-permute-start.21 = (bf16[512,512]{1,0:T(8,128)(2,1)}, bf16[512,512]{1,0:T(8,128)(2,1)S(1)}, u32[]{:S(2)}, u32[]{:S(2)}) collective-permute-start(bf16[512,512]{1,0:T(8,128)(2,1)} %hold.2.refs_2_), channel_id=1, source_target_pairs={{0,16},{16,0},{1,17},{17,1},{2,18},{18,2},{3,19},{19,3},{4,20},{20... | collective-permute-start | bytes 1572872 | tf_op jit(solution)/shard_map/ppermute | solution.py:213
  267.6 12.9 %copy-start.17 = (bf16[512,512]{1,0:T(8,128)(2,1)}, bf16[512,512]{1,0:T(8,128)(2,1)S(1)}, u32[]{:S(2)}) copy-start(bf16[512,512]{1,0:T(8,128)(2,1)S(1)} %collective-permute-done.19.refs_1_) | copy-start | bytes 1572868
  267.6 32.0 %collective-permute-start.23 = (bf16[512,512]{1,0:T(8,128)(2,1)}, bf16[512,512]{1,0:T(8,128)(2,1)S(1)}, u32[]{:S(2)}, u32[]{:S(2)}) collective-permute-start(bf16[512,512]{1,0:T(8,128)(2,1)} %hold.3.refs_4_), channel_id=1, source_target_pairs={{0,16},{16,0},{1,17},{17,1},{2,18},{18,2},{3,19},{19,3},{4,20},{20... | collective-permute-start | bytes 1572872 | tf_op jit(solution)/shard_map/ppermute | solution.py:213
  280.5 19.1 %copy-start.9 = (bf16[384,384]{1,0:T(8,128)(2,1)}, bf16[384,384]{1,0:T(8,128)(2,1)S(1)}, u32[]{:S(2)}) copy-start(bf16[384,384]{1,0:T(8,128)(2,1)S(1)} %collective-permute-done.6.refs_7_.refs_1_) | copy-start | bytes 884740
  280.5 36.1 %collective-permute-start.15 = (bf16[384,256]{1,0:T(8,128)(2,1)}, bf16[384,256]{1,0:T(8,128)(2,1)S(1)}, u32[]{:S(2)}, u32[]{:S(2)}) collective-permute-start(bf16[384,256]{1,0:T(8,128)(2,1)} %get-tuple-element.22), channel_id=1, source_target_pairs={{0,4},{4,8},{8,12},{12,0},{1,5},{5,9},{9,13},{13,1},{2,6},{6,10},{... | collective-permute-start | bytes 589832 | tf_op jit(solution)/shard_map/ppermute | solution.py:219
  296.3 3.3 copy-start.10
  296.3 20.3 %collective-permute-start.16 = (bf16[384,256]{1,0:T(8,128)(2,1)}, bf16[384,256]{1,0:T(8,128)(2,1)S(1)}, u32[]{:S(2)}, u32[]{:S(2)}) collective-permute-start(bf16[384,256]{1,0:T(8,128)(2,1)} %get-tuple-element.23), channel_id=1, source_target_pairs={{0,8},{4,12},{8,0},{12,4},{1,9},{5,13},{9,1},{13,5},{2,10},{6,14},... | collective-permute-start | bytes 589832 | tf_op jit(solution)/shard_map/ppermute | solution.py:219
  299.5 0.7 copy-start.11
  299.5 17.1 %collective-permute-start.17 = (bf16[384,256]{1,0:T(8,128)(2,1)}, bf16[384,256]{1,0:T(8,128)(2,1)S(1)}, u32[]{:S(2)}, u32[]{:S(2)}) collective-permute-start(bf16[384,256]{1,0:T(8,128)(2,1)} %get-tuple-element.24), channel_id=1, source_target_pairs={{0,12},{4,0},{8,4},{12,8},{1,13},{5,1},{9,5},{13,9},{2,14},{6,2},{... | collective-permute-start | bytes 589832 | tf_op jit(solution)/shard_map/ppermute | solution.py:219
  299.6 0.9 copy-start.18
  299.6 1.0 copy-start.19
  312.5 15.3 %collective-permute-start.24 = (bf16[384,256]{1,0:T(8,128)(2,1)}, bf16[384,256]{1,0:T(8,128)(2,1)S(1)}, u32[]{:S(2)}, u32[]{:S(2)}) collective-permute-start(bf16[384,256]{1,0:T(8,128)(2,1)} %get-tuple-element.26), channel_id=1, source_target_pairs={{0,4},{4,8},{8,12},{12,0},{1,5},{5,9},{9,13},{13,1},{2,6},{6,10},{... | collective-permute-start | bytes 589832 | tf_op jit(solution)/shard_map/ppermute | solution.py:219
  314.5 15.4 %collective-permute-start.25 = (bf16[384,256]{1,0:T(8,128)(2,1)}, bf16[384,256]{1,0:T(8,128)(2,1)S(1)}, u32[]{:S(2)}, u32[]{:S(2)}) collective-permute-start(bf16[384,256]{1,0:T(8,128)(2,1)} %get-tuple-element.27), channel_id=1, source_target_pairs={{0,8},{4,12},{8,0},{12,4},{1,9},{5,13},{9,1},{13,5},{2,10},{6,14},... | collective-permute-start | bytes 589832 | tf_op jit(solution)/shard_map/ppermute | solution.py:219
  316.6 13.4 %copy-start.20 = (bf16[384,256]{1,0:T(8,128)(2,1)}, bf16[384,256]{1,0:T(8,128)(2,1)S(1)}, u32[]{:S(2)}) copy-start(bf16[384,256]{1,0:T(8,128)(2,1)S(1)} %collective-permute-done.15.refs_5_) | copy-start | bytes 589828
  316.6 13.4 %collective-permute-start.26 = (bf16[384,256]{1,0:T(8,128)(2,1)}, bf16[384,256]{1,0:T(8,128)(2,1)S(1)}, u32[]{:S(2)}, u32[]{:S(2)}) collective-permute-start(bf16[384,256]{1,0:T(8,128)(2,1)} %get-tuple-element.28), channel_id=1, source_target_pairs={{0,12},{4,0},{8,4},{12,8},{1,13},{5,1},{9,5},{13,9},{2,14},{6,2},{... | collective-permute-start | bytes 589832 | tf_op jit(solution)/shard_map/ppermute | solution.py:219
  316.6 13.3 %copy-start.21 = (bf16[384,256]{1,0:T(8,128)(2,1)}, bf16[384,256]{1,0:T(8,128)(2,1)S(1)}, u32[]{:S(2)}) copy-start(bf16[384,256]{1,0:T(8,128)(2,1)S(1)} %collective-permute-done.16.refs_6_) | copy-start | bytes 589828
  316.6 13.3 %copy-start.22 = (bf16[384,256]{1,0:T(8,128)(2,1)}, bf16[384,256]{1,0:T(8,128)(2,1)S(1)}, u32[]{:S(2)}) copy-start(bf16[384,256]{1,0:T(8,128)(2,1)S(1)} %collective-permute-done.17.refs_7_) | copy-start | bytes 589828
  327.8 2.1 copy-start.23
  329.9 0.7 copy-start.24
  329.9 0.8 copy-start.25
Sparse Core Ops, SparseCore 0:
  9.6 164.5 all-gather.2

commit v7 on v5

--- a/solution.py
+++ b/solution.py
@@ -13,6 +13,10 @@
 
 def around(size, shift):
     return [(i, (i + shift) % size) for i in range(size)]
+
+
+def by_distance(size):
+    return sorted(range(1, size), key=lambda shift: -min(shift, size - shift))
 
 
 def run_all(copies):
@@ -74,8 +78,8 @@
     rows, parts = lax.axis_size("row"), lax.axis_size("parts")
     share, width, tiles = depth // parts, ff // rows, wide // LANES
     features = rows * depth
-    order = list(range(1, rows)) + [0]
-    pieces = [(shift, turn) for shift in range(1, rows) for turn in range(parts)]
+    order = by_distance(rows) + [0]
+    pieces = [(shift, turn) for shift in by_distance(rows) for turn in range(parts)]
 
     def body(tokens_ref, gate_ref, up_ref, *refs):
         held_refs = refs[:len(pieces)]
@@ -192,12 +196,12 @@
 
     def weights_of(n):
         low, high = spans[n]
-        for shift in range(1, rows):
+        for shift in by_distance(rows):
             after = sent[-1:] + arrived[-2:-1] + swapped[-3:-2]
             sent.append(pack(gate_weight, up_weight, shift, low, high - low, after))
             arrived.append(lax.ppermute(sent[-1], "row", around(rows, shift)))
             came = arrived[-1]
-            if done and shift == rows - 1:
+            if done and len(sent) > len(spans) * (rows - 1) - 2:
                 came = hold(came, done)
             held[n].append(came)
             for turn in range(1, parts):

time: 338 us -> 324 us (0.959)
  waiting for transfers between devices: 220 us -> 164 us
  starting transfers between devices: 32.6 us -> 73.9 us
    ppermute x9, waiting for transfers between devices: 144 us -> 96.5 us  [weights_of(): arrived.append(lax.ppermute(sent[-1], 'row', around(rows, shift)))]
    ppermute x9, starting transfers between devices: 9.84 us -> 54.4 us  [weights_of(): arrived.append(lax.ppermute(sent[-1], 'row', around(rows, shift)))]
    ppermute x9, waiting for transfers between devices: 32.5 us -> 27.7 us  [hidden_of(): lax.ppermute(outs[shift], 'row', around(rows, shift))]
    ppermute x9, waiting for transfers between devices: 43.2 us -> 38.8 us  [weights_of(): swapped.append(lax.ppermute(came, 'parts', around(parts, -turn)))]
    ppermute x9, starting transfers between devices: 11.9 us -> 8.28 us  [weights_of(): swapped.append(lax.ppermute(came, 'parts', around(parts, -turn)))]
  transfers between devices with their start and end apart: 29 -> 29, of which waited for: 13 -> 11; matrix products, arithmetic and copies ran while one was open for 0% -> 0% of each run, Pallas kernels for 17% -> 18%
where the time goes in v7:
time: 324 us; the launch traced here: 323 us
  waiting for transfers between devices  164 us (51%)
  starting transfers between devices  73.9 us (23%)
  Pallas kernels  62 us (19%)
  between operations  13.8 us (4%)
  local copies, waits for them, and re-layouts  9.33 us (3%)
    ppermute x9, waiting for transfers between devices, weights_of(): arrived.append(lax.ppermute(sent[-1], 'row', around(rows, shift)))  96.5 us
    ppermute x9, starting transfers between devices, weights_of(): arrived.append(lax.ppermute(sent[-1], 'row', around(rows, shift)))  54.4 us
    pallas_call x3, Pallas kernels, product(): pl.pallas_call(body, out_shape=[jax.ShapeDtypeStruct((mine, wide), jnp.bf...  40.5 us
    ppermute x9, waiting for transfers between devices, weights_of(): swapped.append(lax.ppermute(came, 'parts', around(parts, -turn)))  38.8 us
    ppermute x9, waiting for transfers between devices, hidden_of(): lax.ppermute(outs[shift], 'row', around(rows, shift))  27.7 us
    pallas_call x9, Pallas kernels, pack(): pl.pallas_call(body, out_shape=jax.ShapeDtypeStruct((share, 2 * wide), ga...  18.2 us
    ppermute x9, starting transfers between devices, hidden_of(): lax.ppermute(outs[shift], 'row', around(rows, shift))  11.1 us
    unnamed x56, local copies, waits for them, and re-layouts  9.33 us
  transfers between devices with their start and end apart: 29, of which 11 were waited for; matrix products, arithmetic and copies ran while one was open for 0% of the time, Pallas kernels for 18%

profile of v7, /device:TPU:12, one launch (start us, length us, event | category | flops | bytes accessed | tf_op | source)
XLA Modules:
  0.0 322.7 jit_solution(9267022128258973743)
XLA Ops:
  6.5 0.7 all-gather.3.cloned.1.call-update
  7.3 0.0 all-gather.5.cloned.1.call-start
  7.3 2.2 pack.9.refs_2_
  9.5 2.7 collective-permute-start.1
  12.1 2.2 pack.10.refs_2_
  14.3 0.1 collective-permute-start
  14.4 63.3 %collective-permute-done.1.refs_3_.refs_0_ = bf16[512,768]{1,0:T(8,128)(2,1)S(1)} collective-permute-done((bf16[512,768]{1,0:T(8,128)(2,1)}, bf16[512,768]{1,0:T(8,128)(2,1)S(1)}, u32[]{:S(2)}, u32[]{:S(2)}) %collective-permute-start.1) | collective-permute-done | bytes 786464 | tf_op jit(solution)/shard_map/ppermute | solution.py:202
  77.7 0.5 collective-permute-start.3
  78.2 0.4 copy-done.16
  78.6 2.2 pack.11.refs_2_
  80.8 28.7 %collective-permute-start.2 = (bf16[512,768]{1,0:T(8,128)(2,1)}, bf16[512,768]{1,0:T(8,128)(2,1)S(1)}, u32[]{:S(2)}, u32[]{:S(2)}) collective-permute-start(bf16[512,768]{1,0:T(8,128)(2,1)} %pack.11.refs_2_), channel_id=1, source_target_pairs={{0,12},{4,0},{8,4},{12,8},{1,13},{5,1},{9,5},{13,9},{2,14},{6,2},{... | collective-permute-start | bytes 2359304 | tf_op jit(solution)/shard_map/ppermute | solution.py:202
  109.4 20.8 %collective-permute-done.refs_3_.refs_1_.refs_2_ = bf16[512,768]{1,0:T(8,128)(2,1)S(1)} collective-permute-done((bf16[512,768]{1,0:T(8,128)(2,1)}, bf16[512,768]{1,0:T(8,128)(2,1)S(1)}, u32[]{:S(2)}, u32[]{:S(2)}) %collective-permute-start) | collective-permute-done | bytes 786464 | tf_op jit(solution)/shard_map/ppermute | solution.py:202
  130.3 0.9 copy-done.1
  131.1 0.9 copy-done.17
  132.0 1.9 pack.12.refs_3_.refs_2_
  134.0 0.8 copy-done.3
  134.9 0.5 copy-done.2
  135.4 0.5 collective-permute-start.4
  135.9 1.5 collective-permute-start.5
  137.4 18.4 %collective-permute-done.4.refs_3_.refs_4_ = bf16[512,768]{1,0:T(8,128)(2,1)S(1)} collective-permute-done((bf16[512,768]{1,0:T(8,128)(2,1)S(1)}, bf16[512,768]{1,0:T(8,128)(2,1)S(1)}, u32[]{:S(2)}, u32[]{:S(2)}) %collective-permute-start.4) | collective-permute-done | bytes 786464 | tf_op jit(solution)/shard_map/ppermute | solution.py:208
  155.8 0.9 copy-done.18
  156.7 1.9 pack.13.refs_2_
  158.6 2.5 collective-permute-start.11
  161.1 0.5 collective-permute-start.10
  161.6 11.1 %collective-permute-done.5.refs_5_.refs_4_ = bf16[512,768]{1,0:T(8,128)(2,1)} collective-permute-done((bf16[512,768]{1,0:T(8,128)(2,1)}, bf16[512,768]{1,0:T(8,128)(2,1)}, u32[]{:S(2)}, u32[]{:S(2)}) %collective-permute-start.5) | collective-permute-done | bytes 786464 | tf_op jit(solution)/shard_map/ppermute | solution.py:208
  172.8 1.9 pack.14.refs_2_
  174.7 3.4 %collective-permute-start.13 = (bf16[512,512]{1,0:T(8,128)(2,1)}, bf16[512,512]{1,0:T(8,128)(2,1)S(1)}, u32[]{:S(2)}, u32[]{:S(2)}) collective-permute-start(bf16[512,512]{1,0:T(8,128)(2,1)} %pack.14.refs_2_), channel_id=1, source_target_pairs={{0,12},{4,0},{8,4},{12,8},{1,13},{5,1},{9,5},{13,9},{2,14},{6,2},{... | collective-permute-start | bytes 1572872 | tf_op jit(solution)/shard_map/ppermute | solution.py:202
  178.1 1.2 collective-permute-start.12
  179.3 4.6 %collective-permute-done.10.refs_1_.refs_4_ = bf16[512,512]{1,0:T(8,128)(2,1)S(1)} collective-permute-done((bf16[512,512]{1,0:T(8,128)(2,1)S(1)}, bf16[512,512]{1,0:T(8,128)(2,1)S(1)}, u32[]{:S(2)}, u32[]{:S(2)}) %collective-permute-start.10) | collective-permute-done | bytes 524320 | tf_op jit(solution)/shard_map/ppermute | solution.py:208
  183.9 0.8 copy-done.7
  184.7 1.9 pack.15.refs_2_
  186.6 0.1 collective-permute-start.18
  186.7 2.7 collective-permute-done.13.refs_4_.refs_3_
  189.5 1.0 collective-permute-start.14
  190.4 4.7 %collective-permute-done.12.refs_3_.refs_4_ = bf16[512,512]{1,0:T(8,128)(2,1)S(1)} collective-permute-done((bf16[512,512]{1,0:T(8,128)(2,1)S(1)}, bf16[512,512]{1,0:T(8,128)(2,1)S(1)}, u32[]{:S(2)}, u32[]{:S(2)}) %collective-permute-start.12) | collective-permute-done | bytes 524320 | tf_op jit(solution)/shard_map/ppermute | solution.py:208
  195.1 0.8 copy-done.9
  195.9 1.9 pack.16.refs_2_
  197.9 4.4 %collective-permute-start.20 = (bf16[512,512]{1,0:T(8,128)(2,1)}, bf16[512,512]{1,0:T(8,128)(2,1)S(1)}, u32[]{:S(2)}, u32[]{:S(2)}) collective-permute-start(bf16[512,512]{1,0:T(8,128)(2,1)} %pack.16.refs_2_), channel_id=1, source_target_pairs={{0,4},{4,8},{8,12},{12,0},{1,5},{5,9},{9,13},{13,1},{2,6},{6,10},{... | collective-permute-start | bytes 1572872 | tf_op jit(solution)/shard_map/ppermute | solution.py:202
  202.2 9.6 %collective-permute-done.18.refs_3_.refs_0_ = bf16[512,512]{1,0:T(8,128)(2,1)S(1)} collective-permute-done((bf16[512,512]{1,0:T(8,128)(2,1)}, bf16[512,512]{1,0:T(8,128)(2,1)S(1)}, u32[]{:S(2)}, u32[]{:S(2)}) %collective-permute-start.18) | collective-permute-done | bytes 524320 | tf_op jit(solution)/shard_map/ppermute | solution.py:202
  211.8 1.0 collective-permute-start.19
  212.8 0.8 copy-done.10
  213.6 2.0 pack.17
  215.5 12.8 %collective-permute-start.22 = (bf16[512,512]{1,0:T(8,128)(2,1)}, bf16[512,512]{1,0:T(8,128)(2,1)S(1)}, u32[]{:S(2)}, u32[]{:S(2)}) collective-permute-start(bf16[512,512]{1,0:T(8,128)(2,1)} %pack.17), channel_id=1, source_target_pairs={{0,12},{4,0},{8,4},{12,8},{1,13},{5,1},{9,5},{13,9},{2,14},{6,2},{... | collective-permute-start | bytes 1572872 | tf_op jit(solution)/shard_map/ppermute | solution.py:202
  228.3 16.6 %product.3 = (bf16[384,384]{1,0:T(8,128)(2,1)}, bf16[384,384]{1,0:T(8,128)(2,1)}, bf16[384,384]{1,0:T(8,128)(2,1)}, bf16[384,384]{1,0:T(8,128)(2,1)}) custom-call(bf16[1536,4096]{1,0:T(8,128)(2,1)} %all-gather.5.cloned.1.call-done.tokens_ref, bf16[1024,3584]{1,0:T(8,128)(2,1)} %gate_ref.5, bf16[1024,3584]{1,0:T(8,128)(2,1)} %up_ref.5, ...), custom_call_target="tpu_custom_call" | custom-call | flops 9663676416 | bytes 20054016 | tf_op jit(solution)/shard_map/product/pallas_call | solution.py:135
  245.0 0.1 collective-permute-start.6
  245.0 2.4 collective-permute-start.7
  247.4 0.8 copy-done.11
  248.2 1.1 collective-permute-start.21
  249.3 1.0 collective-permute-start.23
  250.3 11.9 %product.4 = (bf16[384,256]{1,0:T(8,128)(2,1)}, bf16[384,256]{1,0:T(8,128)(2,1)}, bf16[384,256]{1,0:T(8,128)(2,1)}, bf16[384,256]{1,0:T(8,128)(2,1)}) custom-call(bf16[1536,4096]{1,0:T(8,128)(2,1)} %all-gather.5.cloned.1.call-done.tokens_ref, bf16[1024,3584]{1,0:T(8,128)(2,1)} %gate_ref.5, bf16[1024,3584]{1,0:T(8,128)(2,1)} %up_ref.5, ...), custom_call_target="tpu_custom_call" | custom-call | flops 6442450944 | bytes 17563648 | tf_op jit(solution)/shard_map/product/pallas_call | solution.py:135
  262.2 1.4 collective-permute-start.15
  263.6 14.5 %collective-permute-done.7.refs_8_.refs_2_ = bf16[384,384]{1,0:T(8,128)(2,1)S(1)} collective-permute-done((bf16[384,384]{1,0:T(8,128)(2,1)}, bf16[384,384]{1,0:T(8,128)(2,1)S(1)}, u32[]{:S(2)}, u32[]{:S(2)}) %collective-permute-start.7) | collective-permute-done | bytes 294944 | tf_op jit(solution)/shard_map/ppermute | solution.py:214
  278.1 3.3 %collective-permute-start.16 = (bf16[384,256]{1,0:T(8,128)(2,1)}, bf16[384,256]{1,0:T(8,128)(2,1)S(1)}, u32[]{:S(2)}, u32[]{:S(2)}) collective-permute-start(bf16[384,256]{1,0:T(8,128)(2,1)} %get-tuple-element.23), channel_id=1, source_target_pairs={{0,8},{4,12},{8,0},{12,4},{1,9},{5,13},{9,1},{13,5},{2,10},{6,14},... | collective-permute-start | bytes 589832 | tf_op jit(solution)/shard_map/ppermute | solution.py:214
  281.4 0.7 copy-done.15
  282.1 0.2 copy-done.20
  282.2 0.2 copy-done.21
  282.4 12.0 %product.5 = (bf16[384,256]{1,0:T(8,128)(2,1)}, bf16[384,256]{1,0:T(8,128)(2,1)}, bf16[384,256]{1,0:T(8,128)(2,1)}, bf16[384,256]{1,0:T(8,128)(2,1)}) custom-call(bf16[1536,4096]{1,0:T(8,128)(2,1)} %all-gather.5.cloned.1.call-done.tokens_ref, bf16[1024,3584]{1,0:T(8,128)(2,1)} %gate_ref.5, bf16[1024,3584]{1,0:T(8,128)(2,1)} %up_ref.5, ...), custom_call_target="tpu_custom_call" | custom-call | flops 6442450944 | bytes 17563648 | tf_op jit(solution)/shard_map/product/pallas_call | solution.py:135
  294.4 2.0 collective-permute-start.24
  296.4 2.0 collective-permute-start.25
  298.5 11.1 %collective-permute-done.24.refs_9_ = bf16[384,256]{1,0:T(8,128)(2,1)S(1)} collective-permute-done((bf16[384,256]{1,0:T(8,128)(2,1)}, bf16[384,256]{1,0:T(8,128)(2,1)S(1)}, u32[]{:S(2)}, u32[]{:S(2)}) %collective-permute-start.24) | collective-permute-done | bytes 196640 | tf_op jit(solution)/shard_map/ppermute | solution.py:214
  309.6 2.1 collective-permute-done.25.refs_10_
  311.8 0.6 copy-done.26
  312.4 0.1 copy-done.27
  312.5 3.3 %place.1 = bf16[384,3584]{1,0:T(8,128)(2,1)} custom-call(bf16[384,384]{1,0:T(8,128)(2,1)} %get-tuple-element.17.refs_6_.refs_1_.refs_0_, bf16[384,384]{1,0:T(8,128)(2,1)} %copy-done.13, bf16[384,384]{1,0:T(8,128)(2,1)} %copy-done.14, bf16[384,384]{1,0:T(8,128)(2,1)} %copy-done.15, bf16[384,256]{1,0:T(8,128)(2,1)} %get-tuple-element.21.refs_6_.refs_4_, ...), custom_call_target="tpu_custom_call" | custom-call | bytes 5505024 | tf_op jit(solution)/shard_map/place/pallas_call | solution.py:170
  (68 shorter events, 0.2 us)
Async XLA Ops:
  6.5 127.5 %all-gather.3.cloned.1.call-start = ((), (), s32[]{:S(2)}) async-start(), calls=%async_computation | async-start | bytes 3932160 | tf_op jit(solution)/shard_map/all_gather | solution.py:188
  7.3 221.1 %all-gather.5.cloned.1.call-start = ((), (), s32[]{:S(2)}) async-start(), calls=%async_computation.1 | async-start | bytes 15728640 | tf_op jit(solution)/shard_map/all_gather | solution.py:224
  9.5 68.2 %collective-permute-start.1 = (bf16[512,768]{1,0:T(8,128)(2,1)}, bf16[512,768]{1,0:T(8,128)(2,1)S(1)}, u32[]{:S(2)}, u32[]{:S(2)}) collective-permute-start(bf16[512,768]{1,0:T(8,128)(2,1)} %pack.9.refs_2_), channel_id=1, source_target_pairs={{0,8},{4,12},{8,0},{12,4},{1,9},{5,13},{9,1},{13,5},{2,10},{6,14},... | collective-permute-start | bytes 2359304 | tf_op jit(solution)/shard_map/ppermute | solution.py:202
  14.3 116.0 %collective-permute-start = (bf16[512,768]{1,0:T(8,128)(2,1)}, bf16[512,768]{1,0:T(8,128)(2,1)S(1)}, u32[]{:S(2)}, u32[]{:S(2)}) collective-permute-start(bf16[512,768]{1,0:T(8,128)(2,1)} %pack.10.refs_2_), channel_id=1, source_target_pairs={{0,4},{4,8},{8,12},{12,0},{1,5},{5,9},{9,13},{13,1},{2,6},{6,10},{... | collective-permute-start | bytes 2359304 | tf_op jit(solution)/shard_map/ppermute | solution.py:202
  77.7 0.9 copy-start.16
  77.7 52.6 %collective-permute-start.3 = (bf16[512,768]{1,0:T(8,128)(2,1)S(1)}, bf16[512,768]{1,0:T(8,128)(2,1)S(1)}, u32[]{:S(2)}, u32[]{:S(2)}) collective-permute-start(bf16[512,768]{1,0:T(8,128)(2,1)S(1)} %collective-permute-done.1.refs_3_.refs_0_), channel_id=1, source_target_pairs={{0,16},{16,0},{1,17},{17,1},{2,18},{18,2},{3,19},{19,3},{4,20},{20... | collective-permute-start | bytes 2359304 | tf_op jit(solution)/shard_map/ppermute | solution.py:208
  80.8 53.2 %collective-permute-start.2 = (bf16[512,768]{1,0:T(8,128)(2,1)}, bf16[512,768]{1,0:T(8,128)(2,1)S(1)}, u32[]{:S(2)}, u32[]{:S(2)}) collective-permute-start(bf16[512,768]{1,0:T(8,128)(2,1)} %pack.11.refs_2_), channel_id=1, source_target_pairs={{0,12},{4,0},{8,4},{12,8},{1,13},{5,1},{9,5},{13,9},{2,14},{6,2},{... | collective-permute-start | bytes 2359304 | tf_op jit(solution)/shard_map/ppermute | solution.py:202
  130.3 0.9 copy-start.1
  131.1 0.9 copy-start.17
  134.0 1.4 copy-start.2
  134.0 3.4 %copy-start = (bf16[512,512]{1,0:T(8,128)(2,1)S(1)}, bf16[512,512]{1,0:T(8,128)(2,1)}, u32[]{:S(2)}) copy-start(bf16[512,512]{1,0:T(8,128)(2,1)} %pack.12.refs_3_.refs_2_) | copy-start | bytes 1572868
  134.0 0.9 copy-start.3
  135.4 20.4 %collective-permute-start.4 = (bf16[512,768]{1,0:T(8,128)(2,1)S(1)}, bf16[512,768]{1,0:T(8,128)(2,1)S(1)}, u32[]{:S(2)}, u32[]{:S(2)}) collective-permute-start(bf16[512,768]{1,0:T(8,128)(2,1)S(1)} %copy-done.2), channel_id=1, source_target_pairs={{0,16},{16,0},{1,17},{17,1},{2,18},{18,2},{3,19},{19,3},{4,20},{20... | collective-permute-start | bytes 2359304 | tf_op jit(solution)/shard_map/ppermute | solution.py:208
  135.9 36.9 %collective-permute-start.5 = (bf16[512,768]{1,0:T(8,128)(2,1)}, bf16[512,768]{1,0:T(8,128)(2,1)}, u32[]{:S(2)}, u32[]{:S(2)}) collective-permute-start(bf16[512,768]{1,0:T(8,128)(2,1)} %copy-done.3), channel_id=1, source_target_pairs={{0,16},{16,0},{1,17},{17,1},{2,18},{18,2},{3,19},{19,3},{4,20},{20... | collective-permute-start | bytes 2359304 | tf_op jit(solution)/shard_map/ppermute | solution.py:208
  137.4 23.7 %collective-permute-start.9 = (bf16[512,512]{1,0:T(8,128)(2,1)S(1)}, bf16[512,512]{1,0:T(8,128)(2,1)S(1)}, u32[]{:S(2)}, u32[]{:S(2)}) collective-permute-start(bf16[512,512]{1,0:T(8,128)(2,1)S(1)} %copy-done), channel_id=1, source_target_pairs={{0,8},{4,12},{8,0},{12,4},{1,9},{5,13},{9,1},{13,5},{2,10},{6,14},... | collective-permute-start | bytes 1572872 | tf_op jit(solution)/shard_map/ppermute | solution.py:202
  155.8 0.9 copy-start.18
  158.6 19.4 %collective-permute-start.11 = (bf16[512,512]{1,0:T(8,128)(2,1)}, bf16[512,512]{1,0:T(8,128)(2,1)S(1)}, u32[]{:S(2)}, u32[]{:S(2)}) collective-permute-start(bf16[512,512]{1,0:T(8,128)(2,1)} %pack.13.refs_2_), channel_id=1, source_target_pairs={{0,4},{4,8},{8,12},{12,0},{1,5},{5,9},{9,13},{13,1},{2,6},{6,10},{... | collective-permute-start | bytes 1572872 | tf_op jit(solution)/shard_map/ppermute | solution.py:202
  161.1 11.6 %copy-start.5 = (bf16[512,512]{1,0:T(8,128)(2,1)}, bf16[512,512]{1,0:T(8,128)(2,1)S(1)}, u32[]{:S(2)}) copy-start(bf16[512,512]{1,0:T(8,128)(2,1)S(1)} %collective-permute-done.9.refs_3_.refs_0_) | copy-start | bytes 1572868
  161.1 22.8 %collective-permute-start.10 = (bf16[512,512]{1,0:T(8,128)(2,1)S(1)}, bf16[512,512]{1,0:T(8,128)(2,1)S(1)}, u32[]{:S(2)}, u32[]{:S(2)}) collective-permute-start(bf16[512,512]{1,0:T(8,128)(2,1)S(1)} %collective-permute-done.9.refs_3_.refs_0_), channel_id=1, source_target_pairs={{0,16},{16,0},{1,17},{17,1},{2,18},{18,2},{3,19},{19,3},{4,20},{20... | collective-permute-start | bytes 1572872 | tf_op jit(solution)/shard_map/ppermute | solution.py:208
  174.7 14.7 %collective-permute-start.13 = (bf16[512,512]{1,0:T(8,128)(2,1)}, bf16[512,512]{1,0:T(8,128)(2,1)S(1)}, u32[]{:S(2)}, u32[]{:S(2)}) collective-permute-start(bf16[512,512]{1,0:T(8,128)(2,1)} %pack.14.refs_2_), channel_id=1, source_target_pairs={{0,12},{4,0},{8,4},{12,8},{1,13},{5,1},{9,5},{13,9},{2,14},{6,2},{... | collective-permute-start | bytes 1572872 | tf_op jit(solution)/shard_map/ppermute | solution.py:202
  178.1 5.8 %copy-start.6 = (bf16[512,512]{1,0:T(8,128)(2,1)}, bf16[512,512]{1,0:T(8,128)(2,1)S(1)}, u32[]{:S(2)}) copy-start(bf16[512,512]{1,0:T(8,128)(2,1)S(1)} %collective-permute-done.11.refs_2_.refs_3_) | copy-start | bytes 1572868
  178.1 17.0 %collective-permute-start.12 = (bf16[512,512]{1,0:T(8,128)(2,1)S(1)}, bf16[512,512]{1,0:T(8,128)(2,1)S(1)}, u32[]{:S(2)}, u32[]{:S(2)}) collective-permute-start(bf16[512,512]{1,0:T(8,128)(2,1)S(1)} %collective-permute-done.11.refs_2_.refs_3_), channel_id=1, source_target_pairs={{0,16},{16,0},{1,17},{17,1},{2,18},{18,2},{3,19},{19,3},{4,20},{20... | collective-permute-start | bytes 1572872 | tf_op jit(solution)/shard_map/ppermute | solution.py:208
  183.9 0.8 copy-start.7
  186.6 25.1 %collective-permute-start.18 = (bf16[512,512]{1,0:T(8,128)(2,1)}, bf16[512,512]{1,0:T(8,128)(2,1)S(1)}, u32[]{:S(2)}, u32[]{:S(2)}) collective-permute-start(bf16[512,512]{1,0:T(8,128)(2,1)} %pack.15.refs_2_), channel_id=1, source_target_pairs={{0,8},{4,12},{8,0},{12,4},{1,9},{5,13},{9,1},{13,5},{2,10},{6,14},... | collective-permute-start | bytes 1572872 | tf_op jit(solution)/shard_map/ppermute | solution.py:202
  189.4 5.7 %copy-start.8 = (bf16[512,512]{1,0:T(8,128)(2,1)}, bf16[512,512]{1,0:T(8,128)(2,1)S(1)}, u32[]{:S(2)}) copy-start(bf16[512,512]{1,0:T(8,128)(2,1)S(1)} %collective-permute-done.13.refs_4_.refs_3_) | copy-start | bytes 1572868
  189.5 23.3 %collective-permute-start.14 = (bf16[512,512]{1,0:T(8,128)(2,1)S(1)}, bf16[512,512]{1,0:T(8,128)(2,1)S(1)}, u32[]{:S(2)}, u32[]{:S(2)}) collective-permute-start(bf16[512,512]{1,0:T(8,128)(2,1)S(1)} %collective-permute-done.13.refs_4_.refs_3_), channel_id=1, source_target_pairs={{0,16},{16,0},{1,17},{17,1},{2,18},{18,2},{3,19},{19,3},{4,20},{20... | collective-permute-start | bytes 1572872 | tf_op jit(solution)/shard_map/ppermute | solution.py:208
  195.1 0.8 copy-start.9
  197.9 49.5 %collective-permute-start.20 = (bf16[512,512]{1,0:T(8,128)(2,1)}, bf16[512,512]{1,0:T(8,128)(2,1)S(1)}, u32[]{:S(2)}, u32[]{:S(2)}) collective-permute-start(bf16[512,512]{1,0:T(8,128)(2,1)} %pack.16.refs_2_), channel_id=1, source_target_pairs={{0,4},{4,8},{8,12},{12,0},{1,5},{5,9},{9,13},{13,1},{2,6},{6,10},{... | collective-permute-start | bytes 1572872 | tf_op jit(solution)/shard_map/ppermute | solution.py:202
  211.8 1.0 copy-start.4
  211.8 37.5 %collective-permute-start.19 = (bf16[512,512]{1,0:T(8,128)(2,1)S(1)}, bf16[512,512]{1,0:T(8,128)(2,1)S(1)}, u32[]{:S(2)}, u32[]{:S(2)}) collective-permute-start(bf16[512,512]{1,0:T(8,128)(2,1)S(1)} %collective-permute-done.18.refs_3_.refs_0_), channel_id=1, source_target_pairs={{0,16},{16,0},{1,17},{17,1},{2,18},{18,2},{3,19},{19,3},{4,20},{20... | collective-permute-start | bytes 1572872 | tf_op jit(solution)/shard_map/ppermute | solution.py:208
  212.8 0.8 copy-start.10
  215.5 32.7 %collective-permute-start.22 = (bf16[512,512]{1,0:T(8,128)(2,1)}, bf16[512,512]{1,0:T(8,128)(2,1)S(1)}, u32[]{:S(2)}, u32[]{:S(2)}) collective-permute-start(bf16[512,512]{1,0:T(8,128)(2,1)} %pack.17), channel_id=1, source_target_pairs={{0,12},{4,0},{8,4},{12,8},{1,13},{5,1},{9,5},{13,9},{2,14},{6,2},{... | collective-permute-start | bytes 1572872 | tf_op jit(solution)/shard_map/ppermute | solution.py:202
  245.0 17.3 %collective-permute-start.6 = (bf16[384,384]{1,0:T(8,128)(2,1)}, bf16[384,384]{1,0:T(8,128)(2,1)S(1)}, u32[]{:S(2)}, u32[]{:S(2)}) collective-permute-start(bf16[384,384]{1,0:T(8,128)(2,1)} %get-tuple-element.18), channel_id=1, source_target_pairs={{0,4},{4,8},{8,12},{12,0},{1,5},{5,9},{9,13},{13,1},{2,6},{6,10},{... | collective-permute-start | bytes 884744 | tf_op jit(solution)/shard_map/ppermute | solution.py:214
  245.0 33.0 %collective-permute-start.7 = (bf16[384,384]{1,0:T(8,128)(2,1)}, bf16[384,384]{1,0:T(8,128)(2,1)S(1)}, u32[]{:S(2)}, u32[]{:S(2)}) collective-permute-start(bf16[384,384]{1,0:T(8,128)(2,1)} %get-tuple-element.19), channel_id=1, source_target_pairs={{0,8},{4,12},{8,0},{12,4},{1,9},{5,13},{9,1},{13,5},{2,10},{6,14},... | collective-permute-start | bytes 884744 | tf_op jit(solution)/shard_map/ppermute | solution.py:214
  247.4 0.8 copy-start.11
  247.4 33.9 %collective-permute-start.8 = (bf16[384,384]{1,0:T(8,128)(2,1)}, bf16[384,384]{1,0:T(8,128)(2,1)S(1)}, u32[]{:S(2)}, u32[]{:S(2)}) collective-permute-start(bf16[384,384]{1,0:T(8,128)(2,1)} %get-tuple-element.20), channel_id=1, source_target_pairs={{0,12},{4,0},{8,4},{12,8},{1,13},{5,1},{9,5},{13,9},{2,14},{6,2},{... | collective-permute-start | bytes 884744 | tf_op jit(solution)/shard_map/ppermute | solution.py:214
  248.2 1.1 copy-start.12
  248.2 33.2 %collective-permute-start.21 = (bf16[512,512]{1,0:T(8,128)(2,1)}, bf16[512,512]{1,0:T(8,128)(2,1)S(1)}, u32[]{:S(2)}, u32[]{:S(2)}) collective-permute-start(bf16[512,512]{1,0:T(8,128)(2,1)} %hold.4.refs_2_), channel_id=1, source_target_pairs={{0,16},{16,0},{1,17},{17,1},{2,18},{18,2},{3,19},{19,3},{4,20},{20... | collective-permute-start | bytes 1572872 | tf_op jit(solution)/shard_map/ppermute | solution.py:208
  249.3 12.9 %copy-start.19 = (bf16[512,512]{1,0:T(8,128)(2,1)}, bf16[512,512]{1,0:T(8,128)(2,1)S(1)}, u32[]{:S(2)}) copy-start(bf16[512,512]{1,0:T(8,128)(2,1)S(1)} %collective-permute-done.19.refs_1_) | copy-start | bytes 1572868
  249.3 32.1 %collective-permute-start.23 = (bf16[512,512]{1,0:T(8,128)(2,1)}, bf16[512,512]{1,0:T(8,128)(2,1)S(1)}, u32[]{:S(2)}, u32[]{:S(2)}) collective-permute-start(bf16[512,512]{1,0:T(8,128)(2,1)} %hold.5.refs_4_), channel_id=1, source_target_pairs={{0,16},{16,0},{1,17},{17,1},{2,18},{18,2},{3,19},{19,3},{4,20},{20... | collective-permute-start | bytes 1572872 | tf_op jit(solution)/shard_map/ppermute | solution.py:208
  262.2 19.2 %copy-start.13 = (bf16[384,384]{1,0:T(8,128)(2,1)}, bf16[384,384]{1,0:T(8,128)(2,1)S(1)}, u32[]{:S(2)}) copy-start(bf16[384,384]{1,0:T(8,128)(2,1)S(1)} %collective-permute-done.6.refs_7_.refs_1_) | copy-start | bytes 884740
  262.2 36.2 %collective-permute-start.15 = (bf16[384,256]{1,0:T(8,128)(2,1)}, bf16[384,256]{1,0:T(8,128)(2,1)S(1)}, u32[]{:S(2)}, u32[]{:S(2)}) collective-permute-start(bf16[384,256]{1,0:T(8,128)(2,1)} %get-tuple-element.22), channel_id=1, source_target_pairs={{0,4},{4,8},{8,12},{12,0},{1,5},{5,9},{9,13},{13,1},{2,6},{6,10},{... | collective-permute-start | bytes 589832 | tf_op jit(solution)/shard_map/ppermute | solution.py:214
  278.1 3.3 %copy-start.14 = (bf16[384,384]{1,0:T(8,128)(2,1)}, bf16[384,384]{1,0:T(8,128)(2,1)S(1)}, u32[]{:S(2)}) copy-start(bf16[384,384]{1,0:T(8,128)(2,1)S(1)} %collective-permute-done.7.refs_8_.refs_2_) | copy-start | bytes 884740
  278.1 20.4 %collective-permute-start.16 = (bf16[384,256]{1,0:T(8,128)(2,1)}, bf16[384,256]{1,0:T(8,128)(2,1)S(1)}, u32[]{:S(2)}, u32[]{:S(2)}) collective-permute-start(bf16[384,256]{1,0:T(8,128)(2,1)} %get-tuple-element.23), channel_id=1, source_target_pairs={{0,8},{4,12},{8,0},{12,4},{1,9},{5,13},{9,1},{13,5},{2,10},{6,14},... | collective-permute-start | bytes 589832 | tf_op jit(solution)/shard_map/ppermute | solution.py:214
  281.3 0.7 copy-start.15
  281.4 17.1 %collective-permute-start.17 = (bf16[384,256]{1,0:T(8,128)(2,1)}, bf16[384,256]{1,0:T(8,128)(2,1)S(1)}, u32[]{:S(2)}, u32[]{:S(2)}) collective-permute-start(bf16[384,256]{1,0:T(8,128)(2,1)} %get-tuple-element.24), channel_id=1, source_target_pairs={{0,12},{4,0},{8,4},{12,8},{1,13},{5,1},{9,5},{13,9},{2,14},{6,2},{... | collective-permute-start | bytes 589832 | tf_op jit(solution)/shard_map/ppermute | solution.py:214
  281.4 0.9 copy-start.20
  281.4 1.0 copy-start.21
  294.4 15.2 %collective-permute-start.24 = (bf16[384,256]{1,0:T(8,128)(2,1)}, bf16[384,256]{1,0:T(8,128)(2,1)S(1)}, u32[]{:S(2)}, u32[]{:S(2)}) collective-permute-start(bf16[384,256]{1,0:T(8,128)(2,1)} %get-tuple-element.26), channel_id=1, source_target_pairs={{0,4},{4,8},{8,12},{12,0},{1,5},{5,9},{9,13},{13,1},{2,6},{6,10},{... | collective-permute-start | bytes 589832 | tf_op jit(solution)/shard_map/ppermute | solution.py:214
  296.4 15.3 %collective-permute-start.25 = (bf16[384,256]{1,0:T(8,128)(2,1)}, bf16[384,256]{1,0:T(8,128)(2,1)S(1)}, u32[]{:S(2)}, u32[]{:S(2)}) collective-permute-start(bf16[384,256]{1,0:T(8,128)(2,1)} %get-tuple-element.27), channel_id=1, source_target_pairs={{0,8},{4,12},{8,0},{12,4},{1,9},{5,13},{9,1},{13,5},{2,10},{6,14},... | collective-permute-start | bytes 589832 | tf_op jit(solution)/shard_map/ppermute | solution.py:214
  298.4 13.3 %copy-start.22 = (bf16[384,256]{1,0:T(8,128)(2,1)}, bf16[384,256]{1,0:T(8,128)(2,1)S(1)}, u32[]{:S(2)}) copy-start(bf16[384,256]{1,0:T(8,128)(2,1)S(1)} %collective-permute-done.15.refs_5_) | copy-start | bytes 589828
  298.4 13.3 %collective-permute-start.26 = (bf16[384,256]{1,0:T(8,128)(2,1)}, bf16[384,256]{1,0:T(8,128)(2,1)S(1)}, u32[]{:S(2)}, u32[]{:S(2)}) collective-permute-start(bf16[384,256]{1,0:T(8,128)(2,1)} %get-tuple-element.28), channel_id=1, source_target_pairs={{0,12},{4,0},{8,4},{12,8},{1,13},{5,1},{9,5},{13,9},{2,14},{6,2},{... | collective-permute-start | bytes 589832 | tf_op jit(solution)/shard_map/ppermute | solution.py:214
  298.4 13.3 %copy-start.23 = (bf16[384,256]{1,0:T(8,128)(2,1)}, bf16[384,256]{1,0:T(8,128)(2,1)S(1)}, u32[]{:S(2)}) copy-start(bf16[384,256]{1,0:T(8,128)(2,1)S(1)} %collective-permute-done.16.refs_6_) | copy-start | bytes 589828
  298.5 13.3 %copy-start.24 = (bf16[384,256]{1,0:T(8,128)(2,1)}, bf16[384,256]{1,0:T(8,128)(2,1)S(1)}, u32[]{:S(2)}) copy-start(bf16[384,256]{1,0:T(8,128)(2,1)S(1)} %collective-permute-done.17.refs_7_) | copy-start | bytes 589828
  309.6 2.1 copy-start.25
  311.7 0.7 copy-start.26
  311.7 0.7 copy-start.27
Sparse Core Ops, SparseCore 0:
  8.9 104.8 all-gather.2
  135.0 82.9 all-gather.4

commit v8 on v7

--- a/solution.py
+++ b/solution.py
@@ -79,11 +79,10 @@
     share, width, tiles = depth // parts, ff // rows, wide // LANES
     features = rows * depth
     order = by_distance(rows) + [0]
-    pieces = [(shift, turn) for shift in by_distance(rows) for turn in range(parts)]
 
     def body(tokens_ref, gate_ref, up_ref, *refs):
-        held_refs = refs[:len(pieces)]
-        outs = refs[len(pieces) + len(after):][:rows]
+        held_refs = refs[:len(held)]
+        outs = refs[len(held) + len(after):][:rows]
         stack, block, sems, block_sems = refs[-4:]
         z, y = lax.axis_index("row"), lax.axis_index("parts")
 
@@ -96,11 +95,13 @@
             )
 
         copies = []
-        for ref, (shift, turn) in zip(held_refs, pieces):
+        for ref, (shift, turn, begin, _) in zip(held_refs, held):
             came = lax.rem(z + rows - shift, rows)
             half = lax.rem(y + turn, parts)
             start = pl.multiple_of(came * depth + half * share, share)
-            copies.append(pltpu.make_async_copy(ref, stack.at[pl.ds(start, share), :], sems.at[len(copies)]))
+            copies.append(pltpu.make_async_copy(
+                ref.at[:, pl.ds(2 * (low - begin), 2 * wide)], stack.at[pl.ds(start, share), :], sems.at[len(copies)]
+            ))
         own = pl.multiple_of(z * depth, depth)
         for j in range(tiles):
             start = pl.multiple_of(z * width + low + j * LANES, LANES)
@@ -135,12 +136,12 @@
     return pl.pallas_call(
         body,
         out_shape=[jax.ShapeDtypeStruct((mine, wide), jnp.bfloat16)] * rows,
-        in_specs=[ANY] * (3 + len(pieces) + len(after)),
+        in_specs=[ANY] * (3 + len(held) + len(after)),
         out_specs=[pl.BlockSpec(memory_space=pltpu.VMEM)] * rows,
         scratch_shapes=[
             pltpu.VMEM((features, 2 * wide), gate_weight.dtype),
             pltpu.VMEM((2, mine, features), tokens.dtype),
-            pltpu.SemaphoreType.DMA((len(pieces) + 2 * tiles,)),
+            pltpu.SemaphoreType.DMA((len(held) + 2 * tiles,)),
             pltpu.SemaphoreType.DMA((2,)),
         ],
         compiler_params=pltpu.CompilerParams(vmem_limit_bytes=GRANT),
@@ -148,7 +149,7 @@
             flops=4 * rows * mine * features * wide, bytes_accessed=moved, transcendentals=rows * mine * wide
         ),
         name="product",
-    )(tokens, gate_weight, up_weight, *held, *after)
+    )(tokens, gate_weight, up_weight, *[value for *_, value in held], *after)
 
 
 def place(blocks, mine, ff):
@@ -187,26 +188,23 @@
 
     block_rows = lax.all_gather(tokens, "row", axis=0, tiled=True)
 
-    edges, total = [0], sum(PIECES)
+    edges = [0]
     for piece in range(len(PIECES)):
-        edge = units * sum(PIECES[:piece + 1]) // total * LANES
+        edge = units * sum(PIECES[:piece + 1]) // sum(PIECES) * LANES
         if edge > edges[-1]:
             edges.append(edge)
     spans = list(zip(edges[:-1], edges[1:]))
 
-    def weights_of(n):
-        low, high = spans[n]
-        for shift in by_distance(rows):
-            after = sent[-1:] + arrived[-2:-1] + swapped[-3:-2]
-            sent.append(pack(gate_weight, up_weight, shift, low, high - low, after))
-            arrived.append(lax.ppermute(sent[-1], "row", around(rows, shift)))
-            came = arrived[-1]
-            if done and len(sent) > len(spans) * (rows - 1) - 2:
-                came = hold(came, done)
-            held[n].append(came)
-            for turn in range(1, parts):
+    def weights(shift, low, high, users):
+        after = sent[-1:] + arrived[:len(sent) - 2][-1:] * (len(sent) > 2) + swapped[:len(sent) - 3][-1:] * (len(sent) > 3)
+        sent.append(pack(gate_weight, up_weight, shift, low, high - low, after))
+        arrived.append(lax.ppermute(sent[-1], "row", around(rows, shift)))
+        came = hold(arrived[-1], done) if done else arrived[-1]
+        for turn in range(parts):
+            if turn:
                 swapped.append(lax.ppermute(came, "parts", around(parts, -turn)))
-                held[n].append(swapped[-1])
+            for n in users:
+                held[n].append((shift, turn, low, swapped[-1] if turn else came))
 
     def hidden_of(n, after):
         low, high = spans[n]
@@ -217,14 +215,18 @@
         returned.append(back)
 
     last = len(spans) - 1
+    far, *near = by_distance(rows)
+    plan = [(far, 0, spans[max(last - 1, 0)][1], range(max(last, 1)))]
+    for n, (low, high) in enumerate(spans):
+        plan += [(shift, low, high, [n]) for shift in ([far] if 0 < n == last else []) + near]
     sent, arrived, swapped, done, returned, blocks = [], [], [], [], [], []
     held = [[] for _ in spans]
-    for n in range(last):
-        weights_of(n)
-    whole = lax.all_gather(hold(block_rows, arrived[1:3] + sent[3:4]), "col", axis=1, tiled=True)
-    if last:
-        hidden_of(0, [])
-    weights_of(last)
+    for step in plan:
+        if last and len(sent) == len(plan) - 2:
+            hidden_of(0, [])
+        weights(*step)
+        if len(sent) == min(3, len(plan)):
+            whole = lax.all_gather(hold(block_rows, arrived[:1] + sent[1:3]), "col", axis=1, tiled=True)
     for n in range(min(last, 1), last + 1):
         hidden_of(n, done[-1:] + (returned[n - 2] if n > 1 else []))
     return place(blocks, mine, ff)

time: 324 us -> 312 us (0.963)
  starting transfers between devices: 73.9 us -> 69.7 us
    ppermute x18 -> x16, starting transfers between devices: 62.7 us -> 48 us  [the longest x8 39.8 us: weights(): arrived.append(lax.ppermute(sent[-1], 'row', around(rows, shift)))]
    ppermute x9, starting transfers between devices: 11.1 us -> 21.6 us  [hidden_of(): lax.ppermute(outs[shift], 'row', around(rows, shift))]
    ppermute x9, waiting for transfers between devices: 27.7 us -> 18.1 us  [hidden_of(): lax.ppermute(outs[shift], 'row', around(rows, shift))]
    ppermute x18 -> x16, waiting for transfers between devices: 135 us -> 142 us  [the longest x8 140 us: weights(): arrived.append(lax.ppermute(sent[-1], 'row', around(rows, shift)))]
    unnamed x56 -> x48, local copies, waits for them, and re-layouts: 9.33 us -> 6.79 us
    pallas_call x9 -> x8, Pallas kernels: 18.2 us -> 16.6 us  [pack(): pl.pallas_call(body, out_shape=jax.ShapeDtypeStruct((share, 2 * wide), ga...]
  transfers between devices with their start and end apart: 29 -> 27, of which waited for: 11 -> 9; matrix products, arithmetic and copies ran while one was open for 0% -> 0% of each run, Pallas kernels for 18% -> 18%
where the time goes in v8:
time: 312 us; the launch traced here: 311 us
  waiting for transfers between devices  161 us (52%)
  starting transfers between devices  69.7 us (22%)
  Pallas kernels  60.5 us (19%)
  between operations  13.7 us (4%)
  local copies, waits for them, and re-layouts  6.79 us (2%)
    ppermute x8, waiting for transfers between devices, weights(): arrived.append(lax.ppermute(sent[-1], 'row', around(rows, shift)))  140 us
    pallas_call x3, Pallas kernels, product(): pl.pallas_call(body, out_shape=[jax.ShapeDtypeStruct((mine, wide), jnp.bf...  40.6 us
    ppermute x8, starting transfers between devices, weights(): arrived.append(lax.ppermute(sent[-1], 'row', around(rows, shift)))  39.8 us
    ppermute x9, starting transfers between devices, hidden_of(): lax.ppermute(outs[shift], 'row', around(rows, shift))  21.6 us
    ppermute x9, waiting for transfers between devices, hidden_of(): lax.ppermute(outs[shift], 'row', around(rows, shift))  18.1 us
    pallas_call x8, Pallas kernels, pack(): pl.pallas_call(body, out_shape=jax.ShapeDtypeStruct((share, 2 * wide), ga...  16.6 us
    ppermute x8, starting transfers between devices, weights(): swapped.append(lax.ppermute(came, 'parts', around(parts, -turn)))  8.2 us
    unnamed x48, local copies, waits for them, and re-layouts  6.79 us
  transfers between devices with their start and end apart: 27, of which 9 were waited for; matrix products, arithmetic and copies ran while one was open for 0% of the time, Pallas kernels for 18%

profile of v8, /device:TPU:12, one launch (start us, length us, event | category | flops | bytes accessed | tf_op | source)
XLA Modules:
  0.0 311.4 jit_solution(16017792299174968232)
XLA Ops:
  6.5 0.7 all-gather.3.cloned.1.call-update
  7.3 0.0 all-gather.5.cloned.1.call-start
  7.3 2.6 pack.8.refs_2_
  9.9 2.7 collective-permute-start
  12.5 2.2 pack.9.refs_2_
  14.7 2.2 pack.10.refs_3_.refs_2_
  16.9 102.6 %collective-permute-done.refs_1_.refs_0_.refs_3_ = bf16[512,1280]{1,0:T(8,128)(2,1)S(1)} collective-permute-done((bf16[512,1280]{1,0:T(8,128)(2,1)}, bf16[512,1280]{1,0:T(8,128)(2,1)S(1)}, u32[]{:S(2)}, u32[]{:S(2)}) %collective-permute-start) | collective-permute-done | bytes 1310752 | tf_op jit(solution)/shard_map/ppermute | solution.py:201
  119.5 1.1 copy-done
  120.5 0.0 all-gather.5.cloned.1.call-update
  120.5 1.1 copy-done.3
  121.6 0.0 collective-permute-start.2
  121.6 0.4 copy-done.1
  122.1 0.5 collective-permute-start.1
  122.6 1.6 collective-permute-start.4
  124.2 18.0 %collective-permute-done.2.refs_2_.refs_3_ = bf16[512,768]{1,0:T(8,128)(2,1)} collective-permute-done((bf16[512,768]{1,0:T(8,128)(2,1)S(1)}, bf16[512,768]{1,0:T(8,128)(2,1)}, u32[]{:S(2)}, u32[]{:S(2)}) %collective-permute-start.2) | collective-permute-done | bytes 786464 | tf_op jit(solution)/shard_map/ppermute | solution.py:201
  142.1 0.5 collective-permute-start.3
  142.7 2.0 pack.11.refs_2_
  144.6 17.7 %collective-permute-start.9 = (bf16[512,512]{1,0:T(8,128)(2,1)}, bf16[512,512]{1,0:T(8,128)(2,1)S(1)}, u32[]{:S(2)}, u32[]{:S(2)}) collective-permute-start(bf16[512,512]{1,0:T(8,128)(2,1)} %pack.11.refs_2_), channel_id=1, source_target_pairs={{0,4},{4,8},{8,12},{12,0},{1,5},{5,9},{9,13},{13,1},{2,6},{6,10},{... | collective-permute-start | bytes 1572872 | tf_op jit(solution)/shard_map/ppermute | solution.py:201
  162.3 0.0 collective-permute-done.4.refs_4_.refs_3_
  162.3 1.5 collective-permute-start.5
  163.9 5.5 %collective-permute-done.9.refs_2_.refs_3_ = bf16[512,512]{1,0:T(8,128)(2,1)S(1)} collective-permute-done((bf16[512,512]{1,0:T(8,128)(2,1)}, bf16[512,512]{1,0:T(8,128)(2,1)S(1)}, u32[]{:S(2)}, u32[]{:S(2)}) %collective-permute-start.9) | collective-permute-done | bytes 524320 | tf_op jit(solution)/shard_map/ppermute | solution.py:201
  169.3 1.5 collective-permute-start.10
  170.9 1.9 pack.12.refs_2_
  172.8 5.6 %collective-permute-start.11 = (bf16[512,512]{1,0:T(8,128)(2,1)}, bf16[512,512]{1,0:T(8,128)(2,1)S(1)}, u32[]{:S(2)}, u32[]{:S(2)}) collective-permute-start(bf16[512,512]{1,0:T(8,128)(2,1)} %pack.12.refs_2_), channel_id=1, source_target_pairs={{0,12},{4,0},{8,4},{12,8},{1,13},{5,1},{9,5},{13,9},{2,14},{6,2},{... | collective-permute-start | bytes 1572872 | tf_op jit(solution)/shard_map/ppermute | solution.py:201
  178.4 0.0 collective-permute-done.3.refs_3_.refs_4_
  178.4 0.9 copy-done.12
  179.3 1.9 pack.13.refs_2_
  181.3 4.3 %collective-permute-start.16 = (bf16[512,512]{1,0:T(8,128)(2,1)}, bf16[512,512]{1,0:T(8,128)(2,1)S(1)}, u32[]{:S(2)}, u32[]{:S(2)}) collective-permute-start(bf16[512,512]{1,0:T(8,128)(2,1)} %pack.13.refs_2_), channel_id=1, source_target_pairs={{0,8},{4,12},{8,0},{12,4},{1,9},{5,13},{9,1},{13,5},{2,10},{6,14},... | collective-permute-start | bytes 1572872 | tf_op jit(solution)/shard_map/ppermute | solution.py:201
  185.6 1.9 collective-permute-done.5.refs_5_.refs_4_
  187.5 1.9 pack.14.refs_2_
  189.5 7.9 %collective-permute-start.18 = (bf16[512,512]{1,0:T(8,128)(2,1)}, bf16[512,512]{1,0:T(8,128)(2,1)S(1)}, u32[]{:S(2)}, u32[]{:S(2)}) collective-permute-start(bf16[512,512]{1,0:T(8,128)(2,1)} %pack.14.refs_2_), channel_id=1, source_target_pairs={{0,4},{4,8},{8,12},{12,0},{1,5},{5,9},{9,13},{13,1},{2,6},{6,10},{... | collective-permute-start | bytes 1572872 | tf_op jit(solution)/shard_map/ppermute | solution.py:201
  197.3 0.4 collective-permute-done.10.refs_3_.refs_4_
  197.7 13.6 %collective-permute-done.11.refs_4_.refs_3_ = bf16[512,512]{1,0:T(8,128)(2,1)S(1)} collective-permute-done((bf16[512,512]{1,0:T(8,128)(2,1)}, bf16[512,512]{1,0:T(8,128)(2,1)S(1)}, u32[]{:S(2)}, u32[]{:S(2)}) %collective-permute-start.11) | collective-permute-done | bytes 524320 | tf_op jit(solution)/shard_map/ppermute | solution.py:201
  211.4 0.8 copy-done.6
  212.1 1.9 pack.15
  214.1 0.1 collective-permute-start.20
  214.1 0.3 collective-permute-start.12
  214.5 1.8 collective-permute-start.17
  216.2 16.7 %product.3 = (bf16[384,384]{1,0:T(8,128)(2,1)}, bf16[384,384]{1,0:T(8,128)(2,1)}, bf16[384,384]{1,0:T(8,128)(2,1)}, bf16[384,384]{1,0:T(8,128)(2,1)}) custom-call(bf16[1536,4096]{1,0:T(8,128)(2,1)} %all-gather.5.cloned.1.call-done.tokens_ref, bf16[1024,3584]{1,0:T(8,128)(2,1)} %gate_ref.5, bf16[1024,3584]{1,0:T(8,128)(2,1)} %up_ref.5, ...), custom_call_target="tpu_custom_call" | custom-call | flops 9663676416 | bytes 20054016 | tf_op jit(solution)/shard_map/product/pallas_call | solution.py:136
  232.9 6.3 %collective-permute-start.6 = (bf16[384,384]{1,0:T(8,128)(2,1)}, bf16[384,384]{1,0:T(8,128)(2,1)S(1)}, u32[]{:S(2)}, u32[]{:S(2)}) collective-permute-start(bf16[384,384]{1,0:T(8,128)(2,1)} %get-tuple-element.18), channel_id=1, source_target_pairs={{0,4},{4,8},{8,12},{12,0},{1,5},{5,9},{9,13},{13,1},{2,6},{6,10},{... | collective-permute-start | bytes 884744 | tf_op jit(solution)/shard_map/ppermute | solution.py:212
  239.2 0.0 collective-permute-done.18.refs_0_
  239.2 4.2 %collective-permute-start.7 = (bf16[384,384]{1,0:T(8,128)(2,1)}, bf16[384,384]{1,0:T(8,128)(2,1)S(1)}, u32[]{:S(2)}, u32[]{:S(2)}) collective-permute-start(bf16[384,384]{1,0:T(8,128)(2,1)} %get-tuple-element.19), channel_id=1, source_target_pairs={{0,8},{4,12},{8,0},{12,4},{1,9},{5,13},{9,1},{13,5},{2,10},{6,14},... | collective-permute-start | bytes 884744 | tf_op jit(solution)/shard_map/ppermute | solution.py:212
  243.4 0.1 collective-permute-start.8
  243.5 0.7 copy-done.8
  244.2 0.0 collective-permute-done.12.refs_5_
  244.2 1.8 collective-permute-start.19
  246.0 0.0 collective-permute-done.17.refs_1_
  246.0 0.3 collective-permute-start.21
  246.3 12.0 %product.4 = (bf16[384,256]{1,0:T(8,128)(2,1)}, bf16[384,256]{1,0:T(8,128)(2,1)}, bf16[384,256]{1,0:T(8,128)(2,1)}, bf16[384,256]{1,0:T(8,128)(2,1)}) custom-call(bf16[1536,4096]{1,0:T(8,128)(2,1)} %all-gather.5.cloned.1.call-done.tokens_ref, bf16[1024,3584]{1,0:T(8,128)(2,1)} %gate_ref.5, bf16[1024,3584]{1,0:T(8,128)(2,1)} %up_ref.5, ...), custom_call_target="tpu_custom_call" | custom-call | flops 6442450944 | bytes 17563648 | tf_op jit(solution)/shard_map/product/pallas_call | solution.py:136
  258.3 3.9 %collective-permute-start.13 = (bf16[384,256]{1,0:T(8,128)(2,1)}, bf16[384,256]{1,0:T(8,128)(2,1)S(1)}, u32[]{:S(2)}, u32[]{:S(2)}) collective-permute-start(bf16[384,256]{1,0:T(8,128)(2,1)} %get-tuple-element.22), channel_id=1, source_target_pairs={{0,4},{4,8},{8,12},{12,0},{1,5},{5,9},{9,13},{13,1},{2,6},{6,10},{... | collective-permute-start | bytes 589832 | tf_op jit(solution)/shard_map/ppermute | solution.py:212
  262.2 8.2 %collective-permute-done.7.refs_8_.refs_2_ = bf16[384,384]{1,0:T(8,128)(2,1)S(1)} collective-permute-done((bf16[384,384]{1,0:T(8,128)(2,1)}, bf16[384,384]{1,0:T(8,128)(2,1)S(1)}, u32[]{:S(2)}, u32[]{:S(2)}) %collective-permute-start.7) | collective-permute-done | bytes 294944 | tf_op jit(solution)/shard_map/ppermute | solution.py:212
  270.3 3.3 %collective-permute-start.14 = (bf16[384,256]{1,0:T(8,128)(2,1)}, bf16[384,256]{1,0:T(8,128)(2,1)S(1)}, u32[]{:S(2)}, u32[]{:S(2)}) collective-permute-start(bf16[384,256]{1,0:T(8,128)(2,1)} %get-tuple-element.23), channel_id=1, source_target_pairs={{0,8},{4,12},{8,0},{12,4},{1,9},{5,13},{9,1},{13,5},{2,10},{6,14},... | collective-permute-start | bytes 589832 | tf_op jit(solution)/shard_map/ppermute | solution.py:212
  273.6 0.0 copy-start.16
  273.7 0.6 copy-done.11
  274.3 0.2 copy-done.16
  274.5 0.2 copy-done.17
  274.7 12.0 %product.5 = (bf16[384,256]{1,0:T(8,128)(2,1)}, bf16[384,256]{1,0:T(8,128)(2,1)}, bf16[384,256]{1,0:T(8,128)(2,1)}, bf16[384,256]{1,0:T(8,128)(2,1)}) custom-call(bf16[1536,4096]{1,0:T(8,128)(2,1)} %all-gather.5.cloned.1.call-done.tokens_ref, bf16[1024,3584]{1,0:T(8,128)(2,1)} %gate_ref.5, bf16[1024,3584]{1,0:T(8,128)(2,1)} %up_ref.5, ...), custom_call_target="tpu_custom_call" | custom-call | flops 6442450944 | bytes 17563648 | tf_op jit(solution)/shard_map/product/pallas_call | solution.py:136
  286.7 2.0 collective-permute-start.22
  288.7 1.9 collective-permute-start.23
  290.6 7.8 %collective-permute-done.22.refs_9_ = bf16[384,256]{1,0:T(8,128)(2,1)S(1)} collective-permute-done((bf16[384,256]{1,0:T(8,128)(2,1)}, bf16[384,256]{1,0:T(8,128)(2,1)S(1)}, u32[]{:S(2)}, u32[]{:S(2)}) %collective-permute-start.22) | collective-permute-done | bytes 196640 | tf_op jit(solution)/shard_map/ppermute | solution.py:212
  298.4 2.1 collective-permute-done.23.refs_10_
  300.5 0.6 copy-done.22
  301.2 0.1 copy-done.23
  301.2 3.3 %place.1 = bf16[384,3584]{1,0:T(8,128)(2,1)} custom-call(bf16[384,384]{1,0:T(8,128)(2,1)} %get-tuple-element.17.refs_6_.refs_1_.refs_0_, bf16[384,384]{1,0:T(8,128)(2,1)} %copy-done.9, bf16[384,384]{1,0:T(8,128)(2,1)} %copy-done.10, bf16[384,384]{1,0:T(8,128)(2,1)} %copy-done.11, bf16[384,256]{1,0:T(8,128)(2,1)} %get-tuple-element.21.refs_6_.refs_4_, ...), custom_call_target="tpu_custom_call" | custom-call | bytes 5505024 | tf_op jit(solution)/shard_map/place/pallas_call | solution.py:171
  (55 shorter events, 0.1 us)
Async XLA Ops:
  6.5 112.9 %all-gather.3.cloned.1.call-start = ((), (), s32[]{:S(2)}) async-start(), calls=%async_computation | async-start | bytes 3932160 | tf_op jit(solution)/shard_map/all_gather | solution.py:189
  7.3 209.0 %all-gather.5.cloned.1.call-start = ((), (), s32[]{:S(2)}) async-start(), calls=%async_computation.1 | async-start | bytes 15728640 | tf_op jit(solution)/shard_map/all_gather | solution.py:229
  9.9 109.6 %collective-permute-start = (bf16[512,1280]{1,0:T(8,128)(2,1)}, bf16[512,1280]{1,0:T(8,128)(2,1)S(1)}, u32[]{:S(2)}, u32[]{:S(2)}) collective-permute-start(bf16[512,1280]{1,0:T(8,128)(2,1)} %pack.8.refs_2_), channel_id=1, source_target_pairs={{0,8},{4,12},{8,0},{12,4},{1,9},{5,13},{9,1},{13,5},{2,10},{6,14},... | collective-permute-start | bytes 3932168 | tf_op jit(solution)/shard_map/ppermute | solution.py:201
  119.5 1.1 copy-start
  120.5 1.1 copy-start.3
  120.5 1.6 copy-start.1
  120.5 2.1 copy-start.2
  121.6 20.5 %collective-permute-start.2 = (bf16[512,768]{1,0:T(8,128)(2,1)S(1)}, bf16[512,768]{1,0:T(8,128)(2,1)}, u32[]{:S(2)}, u32[]{:S(2)}) collective-permute-start(bf16[512,768]{1,0:T(8,128)(2,1)S(1)} %copy-done.3), channel_id=1, source_target_pairs={{0,4},{4,8},{8,12},{12,0},{1,5},{5,9},{9,13},{13,1},{2,6},{6,10},{... | collective-permute-start | bytes 2359304 | tf_op jit(solution)/shard_map/ppermute | solution.py:201
  122.1 48.8 %collective-permute-start.1 = (bf16[512,1280]{1,0:T(8,128)(2,1)S(1)}, bf16[512,1280]{1,0:T(8,128)(2,1)}, u32[]{:S(2)}, u32[]{:S(2)}) collective-permute-start(bf16[512,1280]{1,0:T(8,128)(2,1)S(1)} %copy-done.1), channel_id=1, source_target_pairs={{0,16},{16,0},{1,17},{17,1},{2,18},{18,2},{3,19},{19,3},{4,20},{20... | collective-permute-start | bytes 3932168 | tf_op jit(solution)/shard_map/ppermute | solution.py:205
  122.6 39.8 %collective-permute-start.4 = (bf16[512,768]{1,0:T(8,128)(2,1)S(1)}, bf16[512,768]{1,0:T(8,128)(2,1)}, u32[]{:S(2)}, u32[]{:S(2)}) collective-permute-start(bf16[512,768]{1,0:T(8,128)(2,1)S(1)} %copy-done.2), channel_id=1, source_target_pairs={{0,12},{4,0},{8,4},{12,8},{1,13},{5,1},{9,5},{13,9},{2,14},{6,2},{... | collective-permute-start | bytes 2359304 | tf_op jit(solution)/shard_map/ppermute | solution.py:201
  142.1 36.3 %collective-permute-start.3 = (bf16[512,768]{1,0:T(8,128)(2,1)}, bf16[512,768]{1,0:T(8,128)(2,1)S(1)}, u32[]{:S(2)}, u32[]{:S(2)}) collective-permute-start(bf16[512,768]{1,0:T(8,128)(2,1)} %collective-permute-done.2.refs_2_.refs_3_), channel_id=1, source_target_pairs={{0,16},{16,0},{1,17},{17,1},{2,18},{18,2},{3,19},{19,3},{4,20},{20... | collective-permute-start | bytes 2359304 | tf_op jit(solution)/shard_map/ppermute | solution.py:205
  144.6 24.7 %collective-permute-start.9 = (bf16[512,512]{1,0:T(8,128)(2,1)}, bf16[512,512]{1,0:T(8,128)(2,1)S(1)}, u32[]{:S(2)}, u32[]{:S(2)}) collective-permute-start(bf16[512,512]{1,0:T(8,128)(2,1)} %pack.11.refs_2_), channel_id=1, source_target_pairs={{0,4},{4,8},{8,12},{12,0},{1,5},{5,9},{9,13},{13,1},{2,6},{6,10},{... | collective-permute-start | bytes 1572872 | tf_op jit(solution)/shard_map/ppermute | solution.py:201
  162.3 25.2 %collective-permute-start.5 = (bf16[512,768]{1,0:T(8,128)(2,1)}, bf16[512,768]{1,0:T(8,128)(2,1)}, u32[]{:S(2)}, u32[]{:S(2)}) collective-permute-start(bf16[512,768]{1,0:T(8,128)(2,1)} %collective-permute-done.4.refs_4_.refs_3_), channel_id=1, source_target_pairs={{0,16},{16,0},{1,17},{17,1},{2,18},{18,2},{3,19},{19,3},{4,20},{20... | collective-permute-start | bytes 2359304 | tf_op jit(solution)/shard_map/ppermute | solution.py:205
  169.3 3.5 %copy-start.4 = (bf16[512,512]{1,0:T(8,128)(2,1)}, bf16[512,512]{1,0:T(8,128)(2,1)S(1)}, u32[]{:S(2)}) copy-start(bf16[512,512]{1,0:T(8,128)(2,1)S(1)} %collective-permute-done.9.refs_2_.refs_3_) | copy-start | bytes 1572868
  169.3 28.4 %collective-permute-start.10 = (bf16[512,512]{1,0:T(8,128)(2,1)S(1)}, bf16[512,512]{1,0:T(8,128)(2,1)S(1)}, u32[]{:S(2)}, u32[]{:S(2)}) collective-permute-start(bf16[512,512]{1,0:T(8,128)(2,1)S(1)} %collective-permute-done.9.refs_2_.refs_3_), channel_id=1, source_target_pairs={{0,16},{16,0},{1,17},{17,1},{2,18},{18,2},{3,19},{19,3},{4,20},{20... | collective-permute-start | bytes 1572872 | tf_op jit(solution)/shard_map/ppermute | solution.py:205
  172.8 38.5 %collective-permute-start.11 = (bf16[512,512]{1,0:T(8,128)(2,1)}, bf16[512,512]{1,0:T(8,128)(2,1)S(1)}, u32[]{:S(2)}, u32[]{:S(2)}) collective-permute-start(bf16[512,512]{1,0:T(8,128)(2,1)} %pack.12.refs_2_), channel_id=1, source_target_pairs={{0,12},{4,0},{8,4},{12,8},{1,13},{5,1},{9,5},{13,9},{2,14},{6,2},{... | collective-permute-start | bytes 1572872 | tf_op jit(solution)/shard_map/ppermute | solution.py:201
  178.4 0.9 copy-start.12
  181.3 33.2 %collective-permute-start.16 = (bf16[512,512]{1,0:T(8,128)(2,1)}, bf16[512,512]{1,0:T(8,128)(2,1)S(1)}, u32[]{:S(2)}, u32[]{:S(2)}) collective-permute-start(bf16[512,512]{1,0:T(8,128)(2,1)} %pack.13.refs_2_), channel_id=1, source_target_pairs={{0,8},{4,12},{8,0},{12,4},{1,9},{5,13},{9,1},{13,5},{2,10},{6,14},... | collective-permute-start | bytes 1572872 | tf_op jit(solution)/shard_map/ppermute | solution.py:201
  189.5 49.8 %collective-permute-start.18 = (bf16[512,512]{1,0:T(8,128)(2,1)}, bf16[512,512]{1,0:T(8,128)(2,1)S(1)}, u32[]{:S(2)}, u32[]{:S(2)}) collective-permute-start(bf16[512,512]{1,0:T(8,128)(2,1)} %pack.14.refs_2_), channel_id=1, source_target_pairs={{0,4},{4,8},{8,12},{12,0},{1,5},{5,9},{9,13},{13,1},{2,6},{6,10},{... | collective-permute-start | bytes 1572872 | tf_op jit(solution)/shard_map/ppermute | solution.py:201
  197.7 13.6 %copy-start.5 = (bf16[512,512]{1,0:T(8,128)(2,1)}, bf16[512,512]{1,0:T(8,128)(2,1)S(1)}, u32[]{:S(2)}) copy-start(bf16[512,512]{1,0:T(8,128)(2,1)S(1)} %collective-permute-done.10.refs_3_.refs_4_) | copy-start | bytes 1572868
  211.4 0.8 copy-start.6
  214.1 29.4 %collective-permute-start.20 = (bf16[512,512]{1,0:T(8,128)(2,1)}, bf16[512,512]{1,0:T(8,128)(2,1)S(1)}, u32[]{:S(2)}, u32[]{:S(2)}) collective-permute-start(bf16[512,512]{1,0:T(8,128)(2,1)} %pack.15), channel_id=1, source_target_pairs={{0,12},{4,0},{8,4},{12,8},{1,13},{5,1},{9,5},{13,9},{2,14},{6,2},{... | collective-permute-start | bytes 1572872 | tf_op jit(solution)/shard_map/ppermute | solution.py:201
  214.1 30.1 %collective-permute-start.12 = (bf16[512,512]{1,0:T(8,128)(2,1)}, bf16[512,512]{1,0:T(8,128)(2,1)S(1)}, u32[]{:S(2)}, u32[]{:S(2)}) collective-permute-start(bf16[512,512]{1,0:T(8,128)(2,1)} %copy-done.6), channel_id=1, source_target_pairs={{0,16},{16,0},{1,17},{17,1},{2,18},{18,2},{3,19},{19,3},{4,20},{20... | collective-permute-start | bytes 1572872 | tf_op jit(solution)/shard_map/ppermute | solution.py:205
  214.5 18.4 %copy-start.13 = (bf16[512,512]{1,0:T(8,128)(2,1)}, bf16[512,512]{1,0:T(8,128)(2,1)S(1)}, u32[]{:S(2)}) copy-start(bf16[512,512]{1,0:T(8,128)(2,1)S(1)} %collective-permute-done.16.refs_0_) | copy-start | bytes 1572868
  214.5 31.5 %collective-permute-start.17 = (bf16[512,512]{1,0:T(8,128)(2,1)S(1)}, bf16[512,512]{1,0:T(8,128)(2,1)S(1)}, u32[]{:S(2)}, u32[]{:S(2)}) collective-permute-start(bf16[512,512]{1,0:T(8,128)(2,1)S(1)} %collective-permute-done.16.refs_0_), channel_id=1, source_target_pairs={{0,16},{16,0},{1,17},{17,1},{2,18},{18,2},{3,19},{19,3},{4,20},{20... | collective-permute-start | bytes 1572872 | tf_op jit(solution)/shard_map/ppermute | solution.py:205
  232.9 25.4 %collective-permute-start.6 = (bf16[384,384]{1,0:T(8,128)(2,1)}, bf16[384,384]{1,0:T(8,128)(2,1)S(1)}, u32[]{:S(2)}, u32[]{:S(2)}) collective-permute-start(bf16[384,384]{1,0:T(8,128)(2,1)} %get-tuple-element.18), channel_id=1, source_target_pairs={{0,4},{4,8},{8,12},{12,0},{1,5},{5,9},{9,13},{13,1},{2,6},{6,10},{... | collective-permute-start | bytes 884744 | tf_op jit(solution)/shard_map/ppermute | solution.py:212
  239.2 4.2 %copy-start.7 = (bf16[512,512]{1,0:T(8,128)(2,1)}, bf16[512,512]{1,0:T(8,128)(2,1)S(1)}, u32[]{:S(2)}) copy-start(bf16[512,512]{1,0:T(8,128)(2,1)S(1)} %collective-permute-done.18.refs_0_) | copy-start | bytes 1572868
  239.2 31.1 %collective-permute-start.7 = (bf16[384,384]{1,0:T(8,128)(2,1)}, bf16[384,384]{1,0:T(8,128)(2,1)S(1)}, u32[]{:S(2)}, u32[]{:S(2)}) collective-permute-start(bf16[384,384]{1,0:T(8,128)(2,1)} %get-tuple-element.19), channel_id=1, source_target_pairs={{0,8},{4,12},{8,0},{12,4},{1,9},{5,13},{9,1},{13,5},{2,10},{6,14},... | collective-permute-start | bytes 884744 | tf_op jit(solution)/shard_map/ppermute | solution.py:212
  243.4 0.8 copy-start.8
  243.4 30.2 %collective-permute-start.8 = (bf16[384,384]{1,0:T(8,128)(2,1)}, bf16[384,384]{1,0:T(8,128)(2,1)S(1)}, u32[]{:S(2)}, u32[]{:S(2)}) collective-permute-start(bf16[384,384]{1,0:T(8,128)(2,1)} %get-tuple-element.20), channel_id=1, source_target_pairs={{0,12},{4,0},{8,4},{12,8},{1,13},{5,1},{9,5},{13,9},{2,14},{6,2},{... | collective-permute-start | bytes 884744 | tf_op jit(solution)/shard_map/ppermute | solution.py:212
  244.2 2.0 copy-start.15
  244.2 29.4 %collective-permute-start.19 = (bf16[512,512]{1,0:T(8,128)(2,1)}, bf16[512,512]{1,0:T(8,128)(2,1)S(1)}, u32[]{:S(2)}, u32[]{:S(2)}) collective-permute-start(bf16[512,512]{1,0:T(8,128)(2,1)} %hold.4.refs_2_), channel_id=1, source_target_pairs={{0,16},{16,0},{1,17},{17,1},{2,18},{18,2},{3,19},{19,3},{4,20},{20... | collective-permute-start | bytes 1572872 | tf_op jit(solution)/shard_map/ppermute | solution.py:205
  246.0 12.2 %copy-start.14 = (bf16[512,512]{1,0:T(8,128)(2,1)}, bf16[512,512]{1,0:T(8,128)(2,1)S(1)}, u32[]{:S(2)}) copy-start(bf16[512,512]{1,0:T(8,128)(2,1)S(1)} %collective-permute-done.17.refs_1_) | copy-start | bytes 1572868
  246.0 27.6 %collective-permute-start.21 = (bf16[512,512]{1,0:T(8,128)(2,1)}, bf16[512,512]{1,0:T(8,128)(2,1)S(1)}, u32[]{:S(2)}, u32[]{:S(2)}) collective-permute-start(bf16[512,512]{1,0:T(8,128)(2,1)} %hold.5.refs_4_), channel_id=1, source_target_pairs={{0,16},{16,0},{1,17},{17,1},{2,18},{18,2},{3,19},{19,3},{4,20},{20... | collective-permute-start | bytes 1572872 | tf_op jit(solution)/shard_map/ppermute | solution.py:205
  258.3 15.4 %copy-start.9 = (bf16[384,384]{1,0:T(8,128)(2,1)}, bf16[384,384]{1,0:T(8,128)(2,1)S(1)}, u32[]{:S(2)}) copy-start(bf16[384,384]{1,0:T(8,128)(2,1)S(1)} %collective-permute-done.6.refs_7_.refs_1_) | copy-start | bytes 884740
  258.3 32.2 %collective-permute-start.13 = (bf16[384,256]{1,0:T(8,128)(2,1)}, bf16[384,256]{1,0:T(8,128)(2,1)S(1)}, u32[]{:S(2)}, u32[]{:S(2)}) collective-permute-start(bf16[384,256]{1,0:T(8,128)(2,1)} %get-tuple-element.22), channel_id=1, source_target_pairs={{0,4},{4,8},{8,12},{12,0},{1,5},{5,9},{9,13},{13,1},{2,6},{6,10},{... | collective-permute-start | bytes 589832 | tf_op jit(solution)/shard_map/ppermute | solution.py:212
  270.3 3.3 %copy-start.10 = (bf16[384,384]{1,0:T(8,128)(2,1)}, bf16[384,384]{1,0:T(8,128)(2,1)S(1)}, u32[]{:S(2)}) copy-start(bf16[384,384]{1,0:T(8,128)(2,1)S(1)} %collective-permute-done.7.refs_8_.refs_2_) | copy-start | bytes 884740
  270.3 20.2 %collective-permute-start.14 = (bf16[384,256]{1,0:T(8,128)(2,1)}, bf16[384,256]{1,0:T(8,128)(2,1)S(1)}, u32[]{:S(2)}, u32[]{:S(2)}) collective-permute-start(bf16[384,256]{1,0:T(8,128)(2,1)} %get-tuple-element.23), channel_id=1, source_target_pairs={{0,8},{4,12},{8,0},{12,4},{1,9},{5,13},{9,1},{13,5},{2,10},{6,14},... | collective-permute-start | bytes 589832 | tf_op jit(solution)/shard_map/ppermute | solution.py:212
  273.6 0.7 copy-start.11
  273.6 16.9 %collective-permute-start.15 = (bf16[384,256]{1,0:T(8,128)(2,1)}, bf16[384,256]{1,0:T(8,128)(2,1)S(1)}, u32[]{:S(2)}, u32[]{:S(2)}) collective-permute-start(bf16[384,256]{1,0:T(8,128)(2,1)} %get-tuple-element.24), channel_id=1, source_target_pairs={{0,12},{4,0},{8,4},{12,8},{1,13},{5,1},{9,5},{13,9},{2,14},{6,2},{... | collective-permute-start | bytes 589832 | tf_op jit(solution)/shard_map/ppermute | solution.py:212
  273.6 0.9 copy-start.16
  273.7 1.1 copy-start.17
  286.7 11.7 %collective-permute-start.22 = (bf16[384,256]{1,0:T(8,128)(2,1)}, bf16[384,256]{1,0:T(8,128)(2,1)S(1)}, u32[]{:S(2)}, u32[]{:S(2)}) collective-permute-start(bf16[384,256]{1,0:T(8,128)(2,1)} %get-tuple-element.26), channel_id=1, source_target_pairs={{0,4},{4,8},{8,12},{12,0},{1,5},{5,9},{9,13},{13,1},{2,6},{6,10},{... | collective-permute-start | bytes 589832 | tf_op jit(solution)/shard_map/ppermute | solution.py:212
  288.7 11.8 %collective-permute-start.23 = (bf16[384,256]{1,0:T(8,128)(2,1)}, bf16[384,256]{1,0:T(8,128)(2,1)S(1)}, u32[]{:S(2)}, u32[]{:S(2)}) collective-permute-start(bf16[384,256]{1,0:T(8,128)(2,1)} %get-tuple-element.27), channel_id=1, source_target_pairs={{0,8},{4,12},{8,0},{12,4},{1,9},{5,13},{9,1},{13,5},{2,10},{6,14},... | collective-permute-start | bytes 589832 | tf_op jit(solution)/shard_map/ppermute | solution.py:212
  290.5 10.0 %copy-start.18 = (bf16[384,256]{1,0:T(8,128)(2,1)}, bf16[384,256]{1,0:T(8,128)(2,1)S(1)}, u32[]{:S(2)}) copy-start(bf16[384,256]{1,0:T(8,128)(2,1)S(1)} %collective-permute-done.13.refs_5_) | copy-start | bytes 589828
  290.5 10.0 %collective-permute-start.24 = (bf16[384,256]{1,0:T(8,128)(2,1)}, bf16[384,256]{1,0:T(8,128)(2,1)S(1)}, u32[]{:S(2)}, u32[]{:S(2)}) collective-permute-start(bf16[384,256]{1,0:T(8,128)(2,1)} %get-tuple-element.28), channel_id=1, source_target_pairs={{0,12},{4,0},{8,4},{12,8},{1,13},{5,1},{9,5},{13,9},{2,14},{6,2},{... | collective-permute-start | bytes 589832 | tf_op jit(solution)/shard_map/ppermute | solution.py:212
  290.6 10.0 %copy-start.19 = (bf16[384,256]{1,0:T(8,128)(2,1)}, bf16[384,256]{1,0:T(8,128)(2,1)S(1)}, u32[]{:S(2)}) copy-start(bf16[384,256]{1,0:T(8,128)(2,1)S(1)} %collective-permute-done.14.refs_6_) | copy-start | bytes 589828
  290.6 9.9 %copy-start.20 = (bf16[384,256]{1,0:T(8,128)(2,1)}, bf16[384,256]{1,0:T(8,128)(2,1)S(1)}, u32[]{:S(2)}) copy-start(bf16[384,256]{1,0:T(8,128)(2,1)S(1)} %collective-permute-done.15.refs_7_) | copy-start | bytes 589828
  298.4 2.1 copy-start.21
  300.5 0.7 copy-start.22
  300.5 0.8 copy-start.23
Sparse Core Ops, SparseCore 0:
  8.9 107.7 all-gather.2
  120.7 83.8 all-gather.4

commit v9 on v8

--- a/solution.py
+++ b/solution.py
@@ -94,43 +94,54 @@
                 block_sems.at[step % 2],
             )
 
-        copies = []
-        for ref, (shift, turn, begin, _) in zip(held_refs, held):
-            came = lax.rem(z + rows - shift, rows)
-            half = lax.rem(y + turn, parts)
-            start = pl.multiple_of(came * depth + half * share, share)
-            copies.append(pltpu.make_async_copy(
-                ref.at[:, pl.ds(2 * (low - begin), 2 * wide)], stack.at[pl.ds(start, share), :], sems.at[len(copies)]
-            ))
+        copies = [[] for _ in range(tiles)]
         own = pl.multiple_of(z * depth, depth)
         for j in range(tiles):
+            for ref, (shift, turn, begin, _) in zip(held_refs, held):
+                came = lax.rem(z + rows - shift, rows)
+                half = lax.rem(y + turn, parts)
+                start = pl.multiple_of(came * depth + half * share, share)
+                copies[j].append(pltpu.make_async_copy(
+                    ref.at[:, pl.ds(2 * (low - begin + j * LANES), 2 * LANES)],
+                    stack.at[pl.ds(start, share), pl.ds(2 * j * LANES, 2 * LANES)],
+                    sems.at[j, len(copies[j])],
+                ))
             start = pl.multiple_of(z * width + low + j * LANES, LANES)
             for g, weight in enumerate((gate_ref, up_ref)):
-                copies.append(pltpu.make_async_copy(
+                copies[j].append(pltpu.make_async_copy(
                     weight.at[:, pl.ds(start, LANES)],
                     stack.at[pl.ds(own, depth), pl.ds((2 * j + g) * LANES, LANES)],
-                    sems.at[len(copies)],
+                    sems.at[j, len(copies[j])],
                 ))
+
+        def tile(step, j):
+            both = jnp.dot(
+                block[step % 2],
+                stack[:, pl.ds(pl.multiple_of(j * 2 * LANES, 2 * LANES), 2 * LANES)],
+                preferred_element_type=jnp.float32,
+            )
+            gate, up = both[:, :LANES], both[:, LANES:]
+            outs[order[step]][:, pl.ds(pl.multiple_of(j * LANES, LANES), LANES)] = (
+                jax.nn.silu(gate) * up
+            ).astype(jnp.bfloat16)
+
+        def first_tiles():
+            for j in range(tiles):
+                for copy in copies[j]:
+                    copy.wait()
+                tile(0, j)
+
         fetch(0).start()
-        run_all(copies)
-        for step, shift in enumerate(order):
+        for copy in sum(copies, []):
+            copy.start()
+        for step in range(rows):
             fetch(step).wait()
             if step + 1 < rows:
                 fetch(step + 1).start()
-
-            def tile(j, carry, step=step, shift=shift):
-                both = jnp.dot(
-                    block[step % 2],
-                    stack[:, pl.ds(pl.multiple_of(j * 2 * LANES, 2 * LANES), 2 * LANES)],
-                    preferred_element_type=jnp.float32,
-                )
-                gate, up = both[:, :LANES], both[:, LANES:]
-                outs[shift][:, pl.ds(pl.multiple_of(j * LANES, LANES), LANES)] = (
-                    jax.nn.silu(gate) * up
-                ).astype(jnp.bfloat16)
-                return carry
-
-            lax.fori_loop(0, tiles, tile, 0)
+            if step:
+                lax.fori_loop(0, tiles, lambda j, carry, step=step: (tile(step, j), carry)[1], 0)
+            else:
+                first_tiles()
 
     moved = 2 * (rows * mine * features + features * 2 * wide + rows * mine * wide)
     return pl.pallas_call(
@@ -141,7 +152,7 @@
         scratch_shapes=[
             pltpu.VMEM((features, 2 * wide), gate_weight.dtype),
             pltpu.VMEM((2, mine, features), tokens.dtype),
-            pltpu.SemaphoreType.DMA((len(held) + 2 * tiles,)),
+            pltpu.SemaphoreType.DMA((tiles, len(held) + 2)),
             pltpu.SemaphoreType.DMA((2,)),
         ],
         compiler_params=pltpu.CompilerParams(vmem_limit_bytes=GRANT),
@@ -152,32 +163,43 @@
     )(tokens, gate_weight, up_weight, *[value for *_, value in held], *after)
 
 
-def place(blocks, mine, ff):
+def place(blocks, mine, ff, onto=None):
     rows = lax.axis_size("row")
     width = ff // rows
+    known = [] if onto is None else [onto]
 
     def body(*refs):
-        out, sems = refs[-2], refs[-1]
+        refs, out, slots, sems = refs[len(known):], refs[len(known) + len(blocks)], refs[-2 - len(blocks):-2], refs[-2:]
         z = lax.axis_index("row")
-        copies = []
-        for ref, (shift, low, value) in zip(refs, blocks):
+        loads, stores = [], []
+        for n, (ref, slot, (shift, low, value)) in enumerate(zip(refs, slots, blocks)):
             came = lax.rem(z + rows - shift, rows)
             start = pl.multiple_of(came * width + low, LANES)
-            copies.append(pltpu.make_async_copy(
-                ref, out.at[:, pl.ds(start, value.shape[1])], sems.at[len(copies)]
-            ))
-        run_all(copies)
-
+            loads.append(pltpu.make_async_copy(ref, slot, sems[0].at[n]))
+            stores.append(pltpu.make_async_copy(slot, out.at[:, pl.ds(start, value.shape[1])], sems[1].at[n]))
+        for load in loads:
+            load.start()
+        for load, store in zip(loads, stores):
+            load.wait()
+            store.start()
+        for store in stores:
+            store.wait()
+
+    values = [value for _, _, value in blocks]
     return pl.pallas_call(
         body,
         out_shape=jax.ShapeDtypeStruct((mine, ff), jnp.bfloat16),
-        in_specs=[ANY] * len(blocks),
-        out_specs=pl.BlockSpec(memory_space=pltpu.VMEM),
-        scratch_shapes=[pltpu.SemaphoreType.DMA((len(blocks),))],
+        in_specs=[ANY] * (len(known) + len(blocks)),
+        out_specs=ANY,
+        scratch_shapes=[pltpu.VMEM(value.shape, value.dtype) for value in values]
+        + [pltpu.SemaphoreType.DMA((len(blocks),))] * 2,
+        input_output_aliases={0: 0} if known else {},
         compiler_params=pltpu.CompilerParams(vmem_limit_bytes=GRANT),
-        cost_estimate=pl.CostEstimate(flops=0, bytes_accessed=4 * mine * ff, transcendentals=0),
+        cost_estimate=pl.CostEstimate(
+            flops=0, bytes_accessed=4 * sum(value.size for value in values), transcendentals=0
+        ),
         name="place",
-    )(*[value for _, _, value in blocks])
+    )(*known, *values)
 
 
 def in_tiles(tokens, gate_weight, up_weight):
@@ -218,7 +240,9 @@
     far, *near = by_distance(rows)
     plan = [(far, 0, spans[max(last - 1, 0)][1], range(max(last, 1)))]
     for n, (low, high) in enumerate(spans):
-        plan += [(shift, low, high, [n]) for shift in ([far] if 0 < n == last else []) + near]
+        plan += [(shift, low, high, [n]) for shift in near]
+        if n == 0 < last:
+            plan.append((far, *spans[last], [last]))
     sent, arrived, swapped, done, returned, blocks = [], [], [], [], [], []
     held = [[] for _ in spans]
     for step in plan:
@@ -229,7 +253,9 @@
             whole = lax.all_gather(hold(block_rows, arrived[:1] + sent[1:3]), "col", axis=1, tiled=True)
     for n in range(min(last, 1), last + 1):
         hidden_of(n, done[-1:] + (returned[n - 2] if n > 1 else []))
-    return place(blocks, mine, ff)
+    early = len(blocks) - rows if last else len(blocks)
+    out = place(blocks[:early], mine, ff)
+    return place(blocks[early:], mine, ff, out) if last else out
 
 
 def at_once(tokens, gate_weight, up_weight):

time: 312 us -> 311 us (level)
  starting transfers between devices: 69.7 us -> 59.7 us
  Pallas kernels: 60.5 us -> 66.6 us
    ppermute x9, starting transfers between devices: 21.6 us -> 13.9 us  [hidden_of(): lax.ppermute(outs[shift], 'row', around(rows, shift))]
    pallas_call x3, Pallas kernels: 40.6 us -> 45.7 us  [product(): pl.pallas_call(body, out_shape=[jax.ShapeDtypeStruct((mine, wide), jnp.bf...]
  transfers between devices with their start and end apart: 27 -> 27, of which waited for: 9 -> 10; matrix products, arithmetic and copies ran while one was open for 0% -> 0% of each run, Pallas kernels for 18% -> 21%
where the time goes in v9:
time: 311 us; the launch traced here: 310 us
  waiting for transfers between devices  162 us (52%)
  Pallas kernels  66.6 us (21%)
  starting transfers between devices  59.7 us (19%)
  between operations  13.7 us (4%)
  local copies, waits for them, and re-layouts  8.24 us (3%)
    ppermute x8, waiting for transfers between devices, weights(): arrived.append(lax.ppermute(sent[-1], 'row', around(rows, shift)))  142 us
    pallas_call x3, Pallas kernels, product(): pl.pallas_call(body, out_shape=[jax.ShapeDtypeStruct((mine, wide), jnp.bf...  45.7 us
    ppermute x8, starting transfers between devices, weights(): arrived.append(lax.ppermute(sent[-1], 'row', around(rows, shift)))  37.9 us
    ppermute x9, waiting for transfers between devices, hidden_of(): lax.ppermute(outs[shift], 'row', around(rows, shift))  19.2 us
    pallas_call x8, Pallas kernels, pack(): pl.pallas_call(body, out_shape=jax.ShapeDtypeStruct((share, 2 * wide), ga...  16.6 us
    ppermute x9, starting transfers between devices, hidden_of(): lax.ppermute(outs[shift], 'row', around(rows, shift))  13.9 us
    unnamed x48, local copies, waits for them, and re-layouts  8.24 us
    ppermute x8, starting transfers between devices, weights(): swapped.append(lax.ppermute(came, 'parts', around(parts, -turn)))  7.94 us
  transfers between devices with their start and end apart: 27, of which 10 were waited for; matrix products, arithmetic and copies ran while one was open for 0% of the time, Pallas kernels for 21%

profile of v9, /device:TPU:12, one launch (start us, length us, event | category | flops | bytes accessed | tf_op | source)
XLA Modules:
  0.0 310.3 jit_solution(15947912914776155271)
XLA Ops:
  6.5 0.7 all-gather.3.cloned.1.call-update
  7.3 0.0 all-gather.5.cloned.1.call-start
  7.3 2.6 pack.8.refs_2_
  9.9 2.7 collective-permute-start
  12.5 2.2 pack.9.refs_2_
  14.7 2.2 pack.10.refs_3_.refs_2_
  16.9 102.6 %collective-permute-done.refs_1_.refs_0_.refs_3_ = bf16[512,1280]{1,0:T(8,128)(2,1)S(1)} collective-permute-done((bf16[512,1280]{1,0:T(8,128)(2,1)}, bf16[512,1280]{1,0:T(8,128)(2,1)S(1)}, u32[]{:S(2)}, u32[]{:S(2)}) %collective-permute-start) | collective-permute-done | bytes 1310752 | tf_op jit(solution)/shard_map/ppermute | solution.py:223
  119.5 1.1 copy-done
  120.5 0.0 all-gather.5.cloned.1.call-update
  120.5 1.1 copy-done.3
  121.6 0.4 copy-done.1
  122.1 0.5 collective-permute-start.1
  122.6 1.6 collective-permute-start.4
  124.2 18.0 %collective-permute-done.2.refs_2_.refs_3_ = bf16[512,768]{1,0:T(8,128)(2,1)} collective-permute-done((bf16[512,768]{1,0:T(8,128)(2,1)S(1)}, bf16[512,768]{1,0:T(8,128)(2,1)}, u32[]{:S(2)}, u32[]{:S(2)}) %collective-permute-start.2) | collective-permute-done | bytes 786464 | tf_op jit(solution)/shard_map/ppermute | solution.py:223
  142.1 0.5 collective-permute-start.3
  142.7 1.9 pack.11.refs_2_
  144.6 19.3 %collective-permute-start.16 = (bf16[512,512]{1,0:T(8,128)(2,1)}, bf16[512,512]{1,0:T(8,128)(2,1)S(1)}, u32[]{:S(2)}, u32[]{:S(2)}) collective-permute-start(bf16[512,512]{1,0:T(8,128)(2,1)} %pack.11.refs_2_), channel_id=1, source_target_pairs={{0,8},{4,12},{8,0},{12,4},{1,9},{5,13},{9,1},{13,5},{2,10},{6,14},... | collective-permute-start | bytes 1572872 | tf_op jit(solution)/shard_map/ppermute | solution.py:223
  163.9 1.5 collective-permute-start.5
  165.4 14.2 %collective-permute-done.16.refs_3_.refs_0_ = bf16[512,512]{1,0:T(8,128)(2,1)S(1)} collective-permute-done((bf16[512,512]{1,0:T(8,128)(2,1)}, bf16[512,512]{1,0:T(8,128)(2,1)S(1)}, u32[]{:S(2)}, u32[]{:S(2)}) %collective-permute-start.16) | collective-permute-done | bytes 524320 | tf_op jit(solution)/shard_map/ppermute | solution.py:223
  179.6 0.5 collective-permute-start.17
  180.1 2.0 pack.12.refs_2_
  182.1 2.1 collective-permute-start.9
  184.2 0.9 copy-done.12
  185.1 1.9 pack.13.refs_2_
  187.0 2.0 collective-permute-start.11
  189.0 2.0 pack.14.refs_2_
  191.0 6.2 %collective-permute-start.18 = (bf16[512,512]{1,0:T(8,128)(2,1)}, bf16[512,512]{1,0:T(8,128)(2,1)S(1)}, u32[]{:S(2)}, u32[]{:S(2)}) collective-permute-start(bf16[512,512]{1,0:T(8,128)(2,1)} %pack.14.refs_2_), channel_id=1, source_target_pairs={{0,4},{4,8},{8,12},{12,0},{1,5},{5,9},{9,13},{13,1},{2,6},{6,10},{... | collective-permute-start | bytes 1572872 | tf_op jit(solution)/shard_map/ppermute | solution.py:223
  197.2 0.5 collective-permute-done.17.refs_4_.refs_1_
  197.7 1.3 collective-permute-done.9.refs_2_.refs_3_
  199.0 0.8 copy-done.6
  199.8 1.9 pack.15
  201.8 4.1 %collective-permute-start.20 = (bf16[512,512]{1,0:T(8,128)(2,1)}, bf16[512,512]{1,0:T(8,128)(2,1)S(1)}, u32[]{:S(2)}, u32[]{:S(2)}) collective-permute-start(bf16[512,512]{1,0:T(8,128)(2,1)} %pack.15), channel_id=1, source_target_pairs={{0,12},{4,0},{8,4},{12,8},{1,13},{5,1},{9,5},{13,9},{2,14},{6,2},{... | collective-permute-start | bytes 1572872 | tf_op jit(solution)/shard_map/ppermute | solution.py:223
  205.8 1.4 collective-permute-start.10
  207.2 5.5 %collective-permute-done.11.refs_4_ = bf16[512,512]{1,0:T(8,128)(2,1)S(1)} collective-permute-done((bf16[512,512]{1,0:T(8,128)(2,1)}, bf16[512,512]{1,0:T(8,128)(2,1)S(1)}, u32[]{:S(2)}, u32[]{:S(2)}) %collective-permute-start.11) | collective-permute-done | bytes 524320 | tf_op jit(solution)/shard_map/ppermute | solution.py:223
  212.7 1.5 collective-permute-start.12
  214.2 18.4 %product.3 = (bf16[384,384]{1,0:T(8,128)(2,1)}, bf16[384,384]{1,0:T(8,128)(2,1)}, bf16[384,384]{1,0:T(8,128)(2,1)}, bf16[384,384]{1,0:T(8,128)(2,1)}) custom-call(bf16[1536,4096]{1,0:T(8,128)(2,1)} %all-gather.5.cloned.1.call-done.tokens_ref, bf16[1024,3584]{1,0:T(8,128)(2,1)} %gate_ref.5, bf16[1024,3584]{1,0:T(8,128)(2,1)} %up_ref.5, ...), custom_call_target="tpu_custom_call" | custom-call | flops 9663676416 | bytes 20054016 | tf_op jit(solution)/shard_map/product/pallas_call | solution.py:147
  232.7 0.6 collective-permute-start.6
  233.2 3.4 %collective-permute-start.7 = (bf16[384,384]{1,0:T(8,128)(2,1)}, bf16[384,384]{1,0:T(8,128)(2,1)S(1)}, u32[]{:S(2)}, u32[]{:S(2)}) collective-permute-start(bf16[384,384]{1,0:T(8,128)(2,1)} %get-tuple-element.19), channel_id=1, source_target_pairs={{0,8},{4,12},{8,0},{12,4},{1,9},{5,13},{9,1},{13,5},{2,10},{6,14},... | collective-permute-start | bytes 884744 | tf_op jit(solution)/shard_map/ppermute | solution.py:234
  236.7 0.1 collective-permute-start.8
  236.7 0.7 copy-done.8
  237.5 0.6 collective-permute-start.19
  238.0 1.5 collective-permute-start.21
  239.5 13.6 %product.4 = (bf16[384,256]{1,0:T(8,128)(2,1)}, bf16[384,256]{1,0:T(8,128)(2,1)}, bf16[384,256]{1,0:T(8,128)(2,1)}, bf16[384,256]{1,0:T(8,128)(2,1)}) custom-call(bf16[1536,4096]{1,0:T(8,128)(2,1)} %all-gather.5.cloned.1.call-done.tokens_ref, bf16[1024,3584]{1,0:T(8,128)(2,1)} %gate_ref.5, bf16[1024,3584]{1,0:T(8,128)(2,1)} %up_ref.5, ...), custom_call_target="tpu_custom_call" | custom-call | flops 6442450944 | bytes 17563648 | tf_op jit(solution)/shard_map/product/pallas_call | solution.py:147
  253.2 0.3 collective-permute-done.6.refs_1_.refs_7_
  253.5 2.5 collective-permute-start.13
  256.0 10.3 %collective-permute-done.7.refs_2_.refs_8_ = bf16[384,384]{1,0:T(8,128)(2,1)S(1)} collective-permute-done((bf16[384,384]{1,0:T(8,128)(2,1)}, bf16[384,384]{1,0:T(8,128)(2,1)S(1)}, u32[]{:S(2)}, u32[]{:S(2)}) %collective-permute-start.7) | collective-permute-done | bytes 294944 | tf_op jit(solution)/shard_map/ppermute | solution.py:234
  266.3 3.3 %collective-permute-start.14 = (bf16[384,256]{1,0:T(8,128)(2,1)}, bf16[384,256]{1,0:T(8,128)(2,1)S(1)}, u32[]{:S(2)}, u32[]{:S(2)}) collective-permute-start(bf16[384,256]{1,0:T(8,128)(2,1)} %get-tuple-element.23), channel_id=1, source_target_pairs={{0,8},{4,12},{8,0},{12,4},{1,9},{5,13},{9,1},{13,5},{2,10},{6,14},... | collective-permute-start | bytes 589832 | tf_op jit(solution)/shard_map/ppermute | solution.py:234
  269.6 0.0 collective-permute-start.15
  269.6 0.0 copy-start.16
  269.6 0.7 copy-done.11
  270.3 0.2 copy-done.16
  270.5 0.2 copy-done.17
  270.6 13.6 %product.5 = (bf16[384,256]{1,0:T(8,128)(2,1)}, bf16[384,256]{1,0:T(8,128)(2,1)}, bf16[384,256]{1,0:T(8,128)(2,1)}, bf16[384,256]{1,0:T(8,128)(2,1)}) custom-call(bf16[1536,4096]{1,0:T(8,128)(2,1)} %all-gather.5.cloned.1.call-done.tokens_ref, bf16[1024,3584]{1,0:T(8,128)(2,1)} %gate_ref.5, bf16[1024,3584]{1,0:T(8,128)(2,1)} %up_ref.5, ...), custom_call_target="tpu_custom_call" | custom-call | flops 6442450944 | bytes 17563648 | tf_op jit(solution)/shard_map/product/pallas_call | solution.py:147
  284.2 2.0 collective-permute-start.22
  286.2 2.0 collective-permute-start.23
  288.3 0.6 copy-done.18
  288.9 0.1 copy-done.19
  289.0 0.7 copy-done.20
  289.7 2.4 place.2.refs_0_
  292.1 6.5 %collective-permute-done.22.refs_2_ = bf16[384,256]{1,0:T(8,128)(2,1)S(1)} collective-permute-done((bf16[384,256]{1,0:T(8,128)(2,1)}, bf16[384,256]{1,0:T(8,128)(2,1)S(1)}, u32[]{:S(2)}, u32[]{:S(2)}) %collective-permute-start.22) | collective-permute-done | bytes 196640 | tf_op jit(solution)/shard_map/ppermute | solution.py:234
  298.6 2.1 collective-permute-done.23.refs_3_
  300.7 0.7 copy-done.22
  301.4 0.1 copy-done.23
  301.5 2.0 place.3
  (56 shorter events, 0.1 us)
Async XLA Ops:
  6.5 112.9 %all-gather.3.cloned.1.call-start = ((), (), s32[]{:S(2)}) async-start(), calls=%async_computation | async-start | bytes 3932160 | tf_op jit(solution)/shard_map/all_gather | solution.py:211
  7.3 207.0 %all-gather.5.cloned.1.call-start = ((), (), s32[]{:S(2)}) async-start(), calls=%async_computation.1 | async-start | bytes 15728640 | tf_op jit(solution)/shard_map/all_gather | solution.py:253
  9.9 109.6 %collective-permute-start = (bf16[512,1280]{1,0:T(8,128)(2,1)}, bf16[512,1280]{1,0:T(8,128)(2,1)S(1)}, u32[]{:S(2)}, u32[]{:S(2)}) collective-permute-start(bf16[512,1280]{1,0:T(8,128)(2,1)} %pack.8.refs_2_), channel_id=1, source_target_pairs={{0,8},{4,12},{8,0},{12,4},{1,9},{5,13},{9,1},{13,5},{2,10},{6,14},... | collective-permute-start | bytes 3932168 | tf_op jit(solution)/shard_map/ppermute | solution.py:223
  119.5 1.1 copy-start
  120.5 1.1 copy-start.3
  120.5 1.6 copy-start.1
  120.5 2.1 copy-start.2
  121.6 20.5 %collective-permute-start.2 = (bf16[512,768]{1,0:T(8,128)(2,1)S(1)}, bf16[512,768]{1,0:T(8,128)(2,1)}, u32[]{:S(2)}, u32[]{:S(2)}) collective-permute-start(bf16[512,768]{1,0:T(8,128)(2,1)S(1)} %copy-done.3), channel_id=1, source_target_pairs={{0,4},{4,8},{8,12},{12,0},{1,5},{5,9},{9,13},{13,1},{2,6},{6,10},{... | collective-permute-start | bytes 2359304 | tf_op jit(solution)/shard_map/ppermute | solution.py:223
  122.1 58.0 %collective-permute-start.1 = (bf16[512,1280]{1,0:T(8,128)(2,1)S(1)}, bf16[512,1280]{1,0:T(8,128)(2,1)}, u32[]{:S(2)}, u32[]{:S(2)}) collective-permute-start(bf16[512,1280]{1,0:T(8,128)(2,1)S(1)} %copy-done.1), channel_id=1, source_target_pairs={{0,16},{16,0},{1,17},{17,1},{2,18},{18,2},{3,19},{19,3},{4,20},{20... | collective-permute-start | bytes 3932168 | tf_op jit(solution)/shard_map/ppermute | solution.py:227
  122.6 41.3 %collective-permute-start.4 = (bf16[512,768]{1,0:T(8,128)(2,1)S(1)}, bf16[512,768]{1,0:T(8,128)(2,1)}, u32[]{:S(2)}, u32[]{:S(2)}) collective-permute-start(bf16[512,768]{1,0:T(8,128)(2,1)S(1)} %copy-done.2), channel_id=1, source_target_pairs={{0,12},{4,0},{8,4},{12,8},{1,13},{5,1},{9,5},{13,9},{2,14},{6,2},{... | collective-permute-start | bytes 2359304 | tf_op jit(solution)/shard_map/ppermute | solution.py:223
  142.1 42.1 %collective-permute-start.3 = (bf16[512,768]{1,0:T(8,128)(2,1)}, bf16[512,768]{1,0:T(8,128)(2,1)S(1)}, u32[]{:S(2)}, u32[]{:S(2)}) collective-permute-start(bf16[512,768]{1,0:T(8,128)(2,1)} %collective-permute-done.2.refs_2_.refs_3_), channel_id=1, source_target_pairs={{0,16},{16,0},{1,17},{17,1},{2,18},{18,2},{3,19},{19,3},{4,20},{20... | collective-permute-start | bytes 2359304 | tf_op jit(solution)/shard_map/ppermute | solution.py:227
  144.6 35.0 %collective-permute-start.16 = (bf16[512,512]{1,0:T(8,128)(2,1)}, bf16[512,512]{1,0:T(8,128)(2,1)S(1)}, u32[]{:S(2)}, u32[]{:S(2)}) collective-permute-start(bf16[512,512]{1,0:T(8,128)(2,1)} %pack.11.refs_2_), channel_id=1, source_target_pairs={{0,8},{4,12},{8,0},{12,4},{1,9},{5,13},{9,1},{13,5},{2,10},{6,14},... | collective-permute-start | bytes 1572872 | tf_op jit(solution)/shard_map/ppermute | solution.py:223
  163.9 25.1 %collective-permute-start.5 = (bf16[512,768]{1,0:T(8,128)(2,1)}, bf16[512,768]{1,0:T(8,128)(2,1)}, u32[]{:S(2)}, u32[]{:S(2)}) collective-permute-start(bf16[512,768]{1,0:T(8,128)(2,1)} %collective-permute-done.4.refs_4_.refs_3_), channel_id=1, source_target_pairs={{0,16},{16,0},{1,17},{17,1},{2,18},{18,2},{3,19},{19,3},{4,20},{20... | collective-permute-start | bytes 2359304 | tf_op jit(solution)/shard_map/ppermute | solution.py:227
  179.6 2.5 copy-start.4
  179.6 18.1 %collective-permute-start.17 = (bf16[512,512]{1,0:T(8,128)(2,1)S(1)}, bf16[512,512]{1,0:T(8,128)(2,1)S(1)}, u32[]{:S(2)}, u32[]{:S(2)}) collective-permute-start(bf16[512,512]{1,0:T(8,128)(2,1)S(1)} %collective-permute-done.16.refs_3_.refs_0_), channel_id=1, source_target_pairs={{0,16},{16,0},{1,17},{17,1},{2,18},{18,2},{3,19},{19,3},{4,20},{20... | collective-permute-start | bytes 1572872 | tf_op jit(solution)/shard_map/ppermute | solution.py:227
  182.1 16.9 %collective-permute-start.9 = (bf16[512,512]{1,0:T(8,128)(2,1)}, bf16[512,512]{1,0:T(8,128)(2,1)S(1)}, u32[]{:S(2)}, u32[]{:S(2)}) collective-permute-start(bf16[512,512]{1,0:T(8,128)(2,1)} %pack.12.refs_2_), channel_id=1, source_target_pairs={{0,4},{4,8},{8,12},{12,0},{1,5},{5,9},{9,13},{13,1},{2,6},{6,10},{... | collective-permute-start | bytes 1572872 | tf_op jit(solution)/shard_map/ppermute | solution.py:223
  184.2 0.9 copy-start.12
  187.0 25.7 %collective-permute-start.11 = (bf16[512,512]{1,0:T(8,128)(2,1)}, bf16[512,512]{1,0:T(8,128)(2,1)S(1)}, u32[]{:S(2)}, u32[]{:S(2)}) collective-permute-start(bf16[512,512]{1,0:T(8,128)(2,1)} %pack.13.refs_2_), channel_id=1, source_target_pairs={{0,12},{4,0},{8,4},{12,8},{1,13},{5,1},{9,5},{13,9},{2,14},{6,2},{... | collective-permute-start | bytes 1572872 | tf_op jit(solution)/shard_map/ppermute | solution.py:223
  191.0 42.3 %collective-permute-start.18 = (bf16[512,512]{1,0:T(8,128)(2,1)}, bf16[512,512]{1,0:T(8,128)(2,1)S(1)}, u32[]{:S(2)}, u32[]{:S(2)}) collective-permute-start(bf16[512,512]{1,0:T(8,128)(2,1)} %pack.14.refs_2_), channel_id=1, source_target_pairs={{0,4},{4,8},{8,12},{12,0},{1,5},{5,9},{9,13},{13,1},{2,6},{6,10},{... | collective-permute-start | bytes 1572872 | tf_op jit(solution)/shard_map/ppermute | solution.py:223
  197.7 1.3 copy-start.5
  199.0 0.8 copy-start.6
  201.8 34.9 %collective-permute-start.20 = (bf16[512,512]{1,0:T(8,128)(2,1)}, bf16[512,512]{1,0:T(8,128)(2,1)S(1)}, u32[]{:S(2)}, u32[]{:S(2)}) collective-permute-start(bf16[512,512]{1,0:T(8,128)(2,1)} %pack.15), channel_id=1, source_target_pairs={{0,12},{4,0},{8,4},{12,8},{1,13},{5,1},{9,5},{13,9},{2,14},{6,2},{... | collective-permute-start | bytes 1572872 | tf_op jit(solution)/shard_map/ppermute | solution.py:223
  205.8 31.7 %collective-permute-start.10 = (bf16[512,512]{1,0:T(8,128)(2,1)}, bf16[512,512]{1,0:T(8,128)(2,1)S(1)}, u32[]{:S(2)}, u32[]{:S(2)}) collective-permute-start(bf16[512,512]{1,0:T(8,128)(2,1)} %copy-done.6), channel_id=1, source_target_pairs={{0,16},{16,0},{1,17},{17,1},{2,18},{18,2},{3,19},{19,3},{4,20},{20... | collective-permute-start | bytes 1572872 | tf_op jit(solution)/shard_map/ppermute | solution.py:227
  212.7 19.9 %copy-start.13 = (bf16[512,512]{1,0:T(8,128)(2,1)}, bf16[512,512]{1,0:T(8,128)(2,1)S(1)}, u32[]{:S(2)}) copy-start(bf16[512,512]{1,0:T(8,128)(2,1)S(1)} %collective-permute-done.11.refs_4_) | copy-start | bytes 1572868
  212.7 25.3 %collective-permute-start.12 = (bf16[512,512]{1,0:T(8,128)(2,1)S(1)}, bf16[512,512]{1,0:T(8,128)(2,1)S(1)}, u32[]{:S(2)}, u32[]{:S(2)}) collective-permute-start(bf16[512,512]{1,0:T(8,128)(2,1)S(1)} %collective-permute-done.11.refs_4_), channel_id=1, source_target_pairs={{0,16},{16,0},{1,17},{17,1},{2,18},{18,2},{3,19},{19,3},{4,20},{20... | collective-permute-start | bytes 1572872 | tf_op jit(solution)/shard_map/ppermute | solution.py:227
  232.7 20.8 %collective-permute-start.6 = (bf16[384,384]{1,0:T(8,128)(2,1)}, bf16[384,384]{1,0:T(8,128)(2,1)S(1)}, u32[]{:S(2)}, u32[]{:S(2)}) collective-permute-start(bf16[384,384]{1,0:T(8,128)(2,1)} %get-tuple-element.18), channel_id=1, source_target_pairs={{0,4},{4,8},{8,12},{12,0},{1,5},{5,9},{9,13},{13,1},{2,6},{6,10},{... | collective-permute-start | bytes 884744 | tf_op jit(solution)/shard_map/ppermute | solution.py:234
  233.2 3.4 %copy-start.7 = (bf16[512,512]{1,0:T(8,128)(2,1)}, bf16[512,512]{1,0:T(8,128)(2,1)S(1)}, u32[]{:S(2)}) copy-start(bf16[512,512]{1,0:T(8,128)(2,1)S(1)} %collective-permute-done.18.refs_0_) | copy-start | bytes 1572868
  233.2 33.1 %collective-permute-start.7 = (bf16[384,384]{1,0:T(8,128)(2,1)}, bf16[384,384]{1,0:T(8,128)(2,1)S(1)}, u32[]{:S(2)}, u32[]{:S(2)}) collective-permute-start(bf16[384,384]{1,0:T(8,128)(2,1)} %get-tuple-element.19), channel_id=1, source_target_pairs={{0,8},{4,12},{8,0},{12,4},{1,9},{5,13},{9,1},{13,5},{2,10},{6,14},... | collective-permute-start | bytes 884744 | tf_op jit(solution)/shard_map/ppermute | solution.py:234
  236.7 0.8 copy-start.8
  236.7 32.9 %collective-permute-start.8 = (bf16[384,384]{1,0:T(8,128)(2,1)}, bf16[384,384]{1,0:T(8,128)(2,1)S(1)}, u32[]{:S(2)}, u32[]{:S(2)}) collective-permute-start(bf16[384,384]{1,0:T(8,128)(2,1)} %get-tuple-element.20), channel_id=1, source_target_pairs={{0,12},{4,0},{8,4},{12,8},{1,13},{5,1},{9,5},{13,9},{2,14},{6,2},{... | collective-permute-start | bytes 884744 | tf_op jit(solution)/shard_map/ppermute | solution.py:234
  237.5 2.0 copy-start.14
  237.5 32.1 %collective-permute-start.19 = (bf16[512,512]{1,0:T(8,128)(2,1)}, bf16[512,512]{1,0:T(8,128)(2,1)S(1)}, u32[]{:S(2)}, u32[]{:S(2)}) collective-permute-start(bf16[512,512]{1,0:T(8,128)(2,1)} %hold.4.refs_2_), channel_id=1, source_target_pairs={{0,16},{16,0},{1,17},{17,1},{2,18},{18,2},{3,19},{19,3},{4,20},{20... | collective-permute-start | bytes 1572872 | tf_op jit(solution)/shard_map/ppermute | solution.py:227
  238.0 1.5 copy-start.15
  238.0 31.6 %collective-permute-start.21 = (bf16[512,512]{1,0:T(8,128)(2,1)}, bf16[512,512]{1,0:T(8,128)(2,1)S(1)}, u32[]{:S(2)}, u32[]{:S(2)}) collective-permute-start(bf16[512,512]{1,0:T(8,128)(2,1)} %hold.5.refs_4_), channel_id=1, source_target_pairs={{0,16},{16,0},{1,17},{17,1},{2,18},{18,2},{3,19},{19,3},{4,20},{20... | collective-permute-start | bytes 1572872 | tf_op jit(solution)/shard_map/ppermute | solution.py:227
  253.5 16.1 %copy-start.9 = (bf16[384,384]{1,0:T(8,128)(2,1)}, bf16[384,384]{1,0:T(8,128)(2,1)S(1)}, u32[]{:S(2)}) copy-start(bf16[384,384]{1,0:T(8,128)(2,1)S(1)} %collective-permute-done.6.refs_1_.refs_7_) | copy-start | bytes 884740
  253.5 34.8 %collective-permute-start.13 = (bf16[384,256]{1,0:T(8,128)(2,1)}, bf16[384,256]{1,0:T(8,128)(2,1)S(1)}, u32[]{:S(2)}, u32[]{:S(2)}) collective-permute-start(bf16[384,256]{1,0:T(8,128)(2,1)} %get-tuple-element.22), channel_id=1, source_target_pairs={{0,4},{4,8},{8,12},{12,0},{1,5},{5,9},{9,13},{13,1},{2,6},{6,10},{... | collective-permute-start | bytes 589832 | tf_op jit(solution)/shard_map/ppermute | solution.py:234
  266.3 3.3 %copy-start.10 = (bf16[384,384]{1,0:T(8,128)(2,1)}, bf16[384,384]{1,0:T(8,128)(2,1)S(1)}, u32[]{:S(2)}) copy-start(bf16[384,384]{1,0:T(8,128)(2,1)S(1)} %collective-permute-done.7.refs_2_.refs_8_) | copy-start | bytes 884740
  266.3 22.0 %collective-permute-start.14 = (bf16[384,256]{1,0:T(8,128)(2,1)}, bf16[384,256]{1,0:T(8,128)(2,1)S(1)}, u32[]{:S(2)}, u32[]{:S(2)}) collective-permute-start(bf16[384,256]{1,0:T(8,128)(2,1)} %get-tuple-element.23), channel_id=1, source_target_pairs={{0,8},{4,12},{8,0},{12,4},{1,9},{5,13},{9,1},{13,5},{2,10},{6,14},... | collective-permute-start | bytes 589832 | tf_op jit(solution)/shard_map/ppermute | solution.py:234
  269.6 0.7 copy-start.11
  269.6 18.7 %collective-permute-start.15 = (bf16[384,256]{1,0:T(8,128)(2,1)}, bf16[384,256]{1,0:T(8,128)(2,1)S(1)}, u32[]{:S(2)}, u32[]{:S(2)}) collective-permute-start(bf16[384,256]{1,0:T(8,128)(2,1)} %get-tuple-element.24), channel_id=1, source_target_pairs={{0,12},{4,0},{8,4},{12,8},{1,13},{5,1},{9,5},{13,9},{2,14},{6,2},{... | collective-permute-start | bytes 589832 | tf_op jit(solution)/shard_map/ppermute | solution.py:234
  269.6 0.9 copy-start.16
  269.6 1.0 copy-start.17
  284.2 14.4 %collective-permute-start.22 = (bf16[384,256]{1,0:T(8,128)(2,1)}, bf16[384,256]{1,0:T(8,128)(2,1)S(1)}, u32[]{:S(2)}, u32[]{:S(2)}) collective-permute-start(bf16[384,256]{1,0:T(8,128)(2,1)} %get-tuple-element.26), channel_id=1, source_target_pairs={{0,4},{4,8},{8,12},{12,0},{1,5},{5,9},{9,13},{13,1},{2,6},{6,10},{... | collective-permute-start | bytes 589832 | tf_op jit(solution)/shard_map/ppermute | solution.py:234
  286.2 14.5 %collective-permute-start.23 = (bf16[384,256]{1,0:T(8,128)(2,1)}, bf16[384,256]{1,0:T(8,128)(2,1)S(1)}, u32[]{:S(2)}, u32[]{:S(2)}) collective-permute-start(bf16[384,256]{1,0:T(8,128)(2,1)} %get-tuple-element.27), channel_id=1, source_target_pairs={{0,8},{4,12},{8,0},{12,4},{1,9},{5,13},{9,1},{13,5},{2,10},{6,14},... | collective-permute-start | bytes 589832 | tf_op jit(solution)/shard_map/ppermute | solution.py:234
  288.3 0.7 copy-start.18
  288.3 12.4 %collective-permute-start.24 = (bf16[384,256]{1,0:T(8,128)(2,1)}, bf16[384,256]{1,0:T(8,128)(2,1)S(1)}, u32[]{:S(2)}, u32[]{:S(2)}) collective-permute-start(bf16[384,256]{1,0:T(8,128)(2,1)} %get-tuple-element.28), channel_id=1, source_target_pairs={{0,12},{4,0},{8,4},{12,8},{1,13},{5,1},{9,5},{13,9},{2,14},{6,2},{... | collective-permute-start | bytes 589832 | tf_op jit(solution)/shard_map/ppermute | solution.py:234
  288.3 0.7 copy-start.19
  289.0 0.7 copy-start.20
  298.6 2.1 copy-start.21
  300.7 0.7 copy-start.22
  300.7 0.8 copy-start.23
Sparse Core Ops, SparseCore 0:
  8.9 107.7 all-gather.2
  120.7 83.8 all-gather.4

commit v10 on v8

--- a/solution.py
+++ b/solution.py
@@ -152,32 +152,86 @@
     )(tokens, gate_weight, up_weight, *[value for *_, value in held], *after)
 
 
-def place(blocks, mine, ff):
+def ordered(lower, upper, after):
+    rows = lax.axis_size("row")
+    mine, near = lower[0].shape
+
+    def body(*refs):
+        lower_refs, upper_refs = refs[:rows], refs[rows:2 * rows - 1]
+        out, slots, sems = refs[-3:]
+        z = lax.axis_index("row")
+        for here in range(rows):
+
+            @pl.when(z == here)
+            def _(here=here):
+                loads, stores = [], []
+                for row in range(rows):
+                    source = lower_refs[here - row] if row <= here else upper_refs[row - here - 1]
+                    loads.append(pltpu.make_async_copy(source, slots.at[row], sems.at[0, row]))
+                    stores.append(pltpu.make_async_copy(
+                        slots.at[row], out.at[pl.ds(row * mine, mine), :], sems.at[1, row]
+                    ))
+                for load in loads:
+                    load.start()
+                for load, store in zip(loads, stores):
+                    load.wait()
+                    store.start()
+                for store in stores:
+                    store.wait()
+
+    values = lower + upper[1:] + after
+    return pl.pallas_call(
+        body,
+        out_shape=jax.ShapeDtypeStruct((rows * mine, near), lower[0].dtype),
+        in_specs=[ANY] * len(values),
+        out_specs=ANY,
+        scratch_shapes=[
+            pltpu.VMEM((rows, mine, near), lower[0].dtype),
+            pltpu.SemaphoreType.DMA((2, rows)),
+        ],
+        compiler_params=pltpu.CompilerParams(vmem_limit_bytes=GRANT),
+        cost_estimate=pl.CostEstimate(flops=0, bytes_accessed=4 * rows * mine * near, transcendentals=0),
+        name="ordered",
+    )(*values)
+
+
+def place(blocks, mine, ff, onto=None):
     rows = lax.axis_size("row")
     width = ff // rows
+    known = [] if onto is None else [onto]
 
     def body(*refs):
-        out, sems = refs[-2], refs[-1]
+        refs, out, slots, sems = refs[len(known):], refs[len(known) + len(blocks)], refs[-2 - len(blocks):-2], refs[-2:]
         z = lax.axis_index("row")
-        copies = []
-        for ref, (shift, low, value) in zip(refs, blocks):
+        loads, stores = [], []
+        for n, (ref, slot, (shift, low, value)) in enumerate(zip(refs, slots, blocks)):
             came = lax.rem(z + rows - shift, rows)
             start = pl.multiple_of(came * width + low, LANES)
-            copies.append(pltpu.make_async_copy(
-                ref, out.at[:, pl.ds(start, value.shape[1])], sems.at[len(copies)]
-            ))
-        run_all(copies)
-
+            loads.append(pltpu.make_async_copy(ref, slot, sems[0].at[n]))
+            stores.append(pltpu.make_async_copy(slot, out.at[:, pl.ds(start, value.shape[1])], sems[1].at[n]))
+        for load in loads:
+            load.start()
+        for load, store in zip(loads, stores):
+            load.wait()
+            store.start()
+        for store in stores:
+            store.wait()
+
+    values = [value for _, _, value in blocks]
     return pl.pallas_call(
         body,
         out_shape=jax.ShapeDtypeStruct((mine, ff), jnp.bfloat16),
-        in_specs=[ANY] * len(blocks),
-        out_specs=pl.BlockSpec(memory_space=pltpu.VMEM),
-        scratch_shapes=[pltpu.SemaphoreType.DMA((len(blocks),))],
+        in_specs=[ANY] * (len(known) + len(blocks)),
+        out_specs=ANY,
+        scratch_shapes=[pltpu.VMEM(value.shape, value.dtype) for value in values]
+        + [pltpu.SemaphoreType.DMA((len(blocks),))] * 2,
+        input_output_aliases={0: 0} if known else {},
         compiler_params=pltpu.CompilerParams(vmem_limit_bytes=GRANT),
-        cost_estimate=pl.CostEstimate(flops=0, bytes_accessed=4 * mine * ff, transcendentals=0),
+        cost_estimate=pl.CostEstimate(
+            flops=0, bytes_accessed=4 * sum(value.size for value in values), transcendentals=0
+        ),
         name="place",
-    )(*[value for _, _, value in blocks])
+    )(*known, *values)
 
 
 def in_tiles(tokens, gate_weight, up_weight):
@@ -186,7 +240,10 @@
     width = ff // rows
     units = width // LANES
 
-    block_rows = lax.all_gather(tokens, "row", axis=0, tiled=True)
+    lower, upper = [tokens], [tokens]
+    for step in range(1, rows):
+        lower.append(lax.ppermute(lower[-1], "row", [(i, i + 1) for i in range(step - 1, rows - 1)]))
+        upper.append(lax.ppermute(upper[-1], "row", [(i, i - 1) for i in range(1, rows - step + 1)]))
 
     edges = [0]
     for piece in range(len(PIECES)):
@@ -218,18 +275,22 @@
     far, *near = by_distance(rows)
     plan = [(far, 0, spans[max(last - 1, 0)][1], range(max(last, 1)))]
     for n, (low, high) in enumerate(spans):
-        plan += [(shift, low, high, [n]) for shift in ([far] if 0 < n == last else []) + near]
+        plan += [(shift, low, high, [n]) for shift in near]
+        if n == 0 < last:
+            plan.append((far, *spans[last], [last]))
     sent, arrived, swapped, done, returned, blocks = [], [], [], [], [], []
     held = [[] for _ in spans]
     for step in plan:
-        if last and len(sent) == len(plan) - 2:
+        if last and len(sent) == max(len(plan) - 3, 3):
             hidden_of(0, [])
         weights(*step)
         if len(sent) == min(3, len(plan)):
-            whole = lax.all_gather(hold(block_rows, arrived[:1] + sent[1:3]), "col", axis=1, tiled=True)
+            whole = lax.all_gather(ordered(lower, upper, arrived[:1] + sent[1:3]), "col", axis=1, tiled=True)
     for n in range(min(last, 1), last + 1):
         hidden_of(n, done[-1:] + (returned[n - 2] if n > 1 else []))
-    return place(blocks, mine, ff)
+    early = len(blocks) - rows if last else len(blocks)
+    out = place(blocks[:early], mine, ff)
+    return place(blocks[early:], mine, ff, out) if last else out
 
 
 def at_once(tokens, gate_weight, up_weight):

time: 312 us -> 311 us (level)
  starting transfers between devices: 69.7 us -> 49.1 us
  waiting for transfers between devices: 161 us -> 174 us
  Pallas kernels: 60.5 us -> 64.5 us
    ppermute x0 -> x6, waiting for transfers between devices: none -> 79.8 us  [the longest x3 56.7 us: in_tiles(): lax.ppermute(lower[-1], 'row', [(i, i + 1) for i in range(step - 1, rows...]
    ppermute x8, waiting for transfers between devices: 140 us -> 71.2 us  [weights(): arrived.append(lax.ppermute(sent[-1], 'row', around(rows, shift)))]
    ppermute x8, starting transfers between devices: 39.8 us -> 9.05 us  [weights(): arrived.append(lax.ppermute(sent[-1], 'row', around(rows, shift)))]
    ppermute x0 -> x6, starting transfers between devices: none -> 13.5 us  [the longest x3 7.69 us: in_tiles(): lax.ppermute(lower[-1], 'row', [(i, i + 1) for i in range(step - 1, rows...]
    ppermute x9, starting transfers between devices: 21.6 us -> 17.4 us  [hidden_of(): lax.ppermute(outs[shift], 'row', around(rows, shift))]
    ppermute x8, waiting for transfers between devices: 2.33 us -> 6.31 us  [weights(): swapped.append(lax.ppermute(came, 'parts', around(parts, -turn)))]
    unnamed x48 -> x58, local copies, waits for them, and re-layouts: 6.79 us -> 8.61 us
  transfers between devices with their start and end apart: 27 -> 32, of which waited for: 9 -> 15; matrix products, arithmetic and copies ran while one was open for 0% -> 0% of each run, Pallas kernels for 18% -> 19%
where the time goes in v10:
time: 311 us; the launch traced here: 310 us
  waiting for transfers between devices  174 us (56%)
  Pallas kernels  64.5 us (21%)
  starting transfers between devices  49.1 us (16%)
  between operations  13.8 us (4%)
  local copies, waits for them, and re-layouts  8.61 us (3%)
    ppermute x8, waiting for transfers between devices, weights(): arrived.append(lax.ppermute(sent[-1], 'row', around(rows, shift)))  71.2 us
    ppermute x3, waiting for transfers between devices, in_tiles(): lax.ppermute(lower[-1], 'row', [(i, i + 1) for i in range(step - 1, rows...  56.7 us
    pallas_call x3, Pallas kernels, product(): pl.pallas_call(body, out_shape=[jax.ShapeDtypeStruct((mine, wide), jnp.bf...  40.6 us
    ppermute x3, waiting for transfers between devices, in_tiles(): lax.ppermute(upper[-1], 'row', [(i, i - 1) for i in range(1, rows - step...  23 us
    ppermute x9, starting transfers between devices, hidden_of(): lax.ppermute(outs[shift], 'row', around(rows, shift))  17.4 us
    pallas_call x8, Pallas kernels, pack(): pl.pallas_call(body, out_shape=jax.ShapeDtypeStruct((share, 2 * wide), ga...  16.7 us
    ppermute x9, waiting for transfers between devices, hidden_of(): lax.ppermute(outs[shift], 'row', around(rows, shift))  16.4 us
    ppermute x8, starting transfers between devices, weights(): swapped.append(lax.ppermute(came, 'parts', around(parts, -turn)))  9.17 us
  transfers between devices with their start and end apart: 32, of which 15 were waited for; matrix products, arithmetic and copies ran while one was open for 0% of the time, Pallas kernels for 19%

profile of v10, /device:TPU:12, one launch (start us, length us, event | category | flops | bytes accessed | tf_op | source)
XLA Modules:
  0.0 309.7 jit_solution(12218299283128537686)
XLA Ops:
  6.5 3.5 %collective-permute-start = (bf16[384,1024]{1,0:T(8,128)(2,1)}, bf16[384,1024]{1,0:T(8,128)(2,1)S(1)}, u32[]{:S(2)}, u32[]{:S(2)}) collective-permute-start(bf16[384,1024]{1,0:T(8,128)(2,1)} %refs_0_.12), channel_id=1, source_target_pairs={{0,4},{4,8},{8,12},{1,5},{5,9},{9,13},{2,6},{6,10},{10,14},{3,7},{... | collective-permute-start | bytes 2359304 | tf_op jit(solution)/shard_map/ppermute | solution.py:245
  10.0 2.4 collective-permute-start.3
  12.4 15.5 %collective-permute-done.refs_1_ = bf16[384,1024]{1,0:T(8,128)(2,1)S(1)} collective-permute-done((bf16[384,1024]{1,0:T(8,128)(2,1)}, bf16[384,1024]{1,0:T(8,128)(2,1)S(1)}, u32[]{:S(2)}, u32[]{:S(2)}) %collective-permute-start) | collective-permute-done | bytes 786464 | tf_op jit(solution)/shard_map/ppermute | solution.py:245
  27.9 3.5 %collective-permute-start.1 = (bf16[384,1024]{1,0:T(8,128)(2,1)S(1)}, bf16[384,1024]{1,0:T(8,128)(2,1)S(1)}, u32[]{:S(2)}, u32[]{:S(2)}) collective-permute-start(bf16[384,1024]{1,0:T(8,128)(2,1)S(1)} %collective-permute-done.refs_1_), channel_id=1, source_target_pairs={{4,8},{8,12},{5,9},{9,13},{6,10},{10,14},{7,11},{11,15},{20,24},{2... | collective-permute-start | bytes 2359304 | tf_op jit(solution)/shard_map/ppermute | solution.py:245
  31.5 2.1 collective-permute-start.4
  33.5 2.6 pack.8.refs_2_
  36.2 41.3 %collective-permute-done.1.refs_2_ = bf16[384,1024]{1,0:T(8,128)(2,1)S(1)} collective-permute-done((bf16[384,1024]{1,0:T(8,128)(2,1)S(1)}, bf16[384,1024]{1,0:T(8,128)(2,1)S(1)}, u32[]{:S(2)}, u32[]{:S(2)}) %collective-permute-start.1) | collective-permute-done | bytes 786464 | tf_op jit(solution)/shard_map/ppermute | solution.py:245
  77.5 0.7 collective-permute-start.2
  78.2 3.9 %collective-permute-done.4.refs_5_ = bf16[384,1024]{1,0:T(8,128)(2,1)} collective-permute-done((bf16[384,1024]{1,0:T(8,128)(2,1)S(1)}, bf16[384,1024]{1,0:T(8,128)(2,1)}, u32[]{:S(2)}, u32[]{:S(2)}) %collective-permute-start.4) | collective-permute-done | bytes 786464 | tf_op jit(solution)/shard_map/ppermute | solution.py:246
  82.0 1.3 collective-permute-start.5
  83.4 2.2 pack.9.refs_2_.refs_8_
  85.6 2.2 pack.10.refs_9_.refs_2_
  87.8 15.8 %collective-permute-done.6.refs_7_.refs_0_.refs_3_ = bf16[512,1280]{1,0:T(8,128)(2,1)S(1)} collective-permute-done((bf16[512,1280]{1,0:T(8,128)(2,1)}, bf16[512,1280]{1,0:T(8,128)(2,1)S(1)}, u32[]{:S(2)}, u32[]{:S(2)}) %collective-permute-start.6) | collective-permute-done | bytes 1310752 | tf_op jit(solution)/shard_map/ppermute | solution.py:258
  103.6 19.2 %collective-permute-done.5.refs_6_ = bf16[384,1024]{1,0:T(8,128)(2,1)S(1)} collective-permute-done((bf16[384,1024]{1,0:T(8,128)(2,1)}, bf16[384,1024]{1,0:T(8,128)(2,1)S(1)}, u32[]{:S(2)}, u32[]{:S(2)}) %collective-permute-start.5) | collective-permute-done | bytes 786464 | tf_op jit(solution)/shard_map/ppermute | solution.py:246
  122.8 0.9 copy-done.18
  123.7 2.8 ordered.1
  126.6 1.3 copy-done.1
  127.9 0.5 collective-permute-start.7
  128.4 2.4 collective-permute-start.10
  130.8 1.9 pack.11.refs_2_
  132.8 2.4 collective-permute-start.22
  135.2 14.2 %collective-permute-done.8.refs_2_.refs_3_ = bf16[512,768]{1,0:T(8,128)(2,1)} collective-permute-done((bf16[512,768]{1,0:T(8,128)(2,1)S(1)}, bf16[512,768]{1,0:T(8,128)(2,1)}, u32[]{:S(2)}, u32[]{:S(2)}) %collective-permute-start.8) | collective-permute-done | bytes 786464 | tf_op jit(solution)/shard_map/ppermute | solution.py:258
  149.3 1.5 collective-permute-start.9
  150.9 16.6 %collective-permute-done.10.refs_4_.refs_3_ = bf16[512,768]{1,0:T(8,128)(2,1)} collective-permute-done((bf16[512,768]{1,0:T(8,128)(2,1)S(1)}, bf16[512,768]{1,0:T(8,128)(2,1)}, u32[]{:S(2)}, u32[]{:S(2)}) %collective-permute-start.10) | collective-permute-done | bytes 786464 | tf_op jit(solution)/shard_map/ppermute | solution.py:258
  167.5 1.5 collective-permute-start.11
  169.0 14.9 %collective-permute-done.22.refs_3_.refs_0_ = bf16[512,512]{1,0:T(8,128)(2,1)S(1)} collective-permute-done((bf16[512,512]{1,0:T(8,128)(2,1)}, bf16[512,512]{1,0:T(8,128)(2,1)S(1)}, u32[]{:S(2)}, u32[]{:S(2)}) %collective-permute-start.22) | collective-permute-done | bytes 524320 | tf_op jit(solution)/shard_map/ppermute | solution.py:258
  183.9 1.5 collective-permute-start.23
  185.5 2.0 pack.12.refs_2_
  187.5 1.9 collective-permute-start.15
  189.3 0.9 copy-done.13
  190.2 1.9 pack.13.refs_2_
  192.1 1.9 collective-permute-start.17
  194.0 2.0 pack.14.refs_2_
  196.0 0.4 collective-permute-start.24
  196.4 6.3 %collective-permute-done.23.refs_4_.refs_1_ = bf16[512,512]{1,0:T(8,128)(2,1)S(1)} collective-permute-done((bf16[512,512]{1,0:T(8,128)(2,1)S(1)}, bf16[512,512]{1,0:T(8,128)(2,1)S(1)}, u32[]{:S(2)}, u32[]{:S(2)}) %collective-permute-start.23) | collective-permute-done | bytes 524320 | tf_op jit(solution)/shard_map/ppermute | solution.py:262
  202.7 8.8 %collective-permute-done.15.refs_2_.refs_3_ = bf16[512,512]{1,0:T(8,128)(2,1)S(1)} collective-permute-done((bf16[512,512]{1,0:T(8,128)(2,1)}, bf16[512,512]{1,0:T(8,128)(2,1)S(1)}, u32[]{:S(2)}, u32[]{:S(2)}) %collective-permute-start.15) | collective-permute-done | bytes 524320 | tf_op jit(solution)/shard_map/ppermute | solution.py:258
  211.5 0.8 copy-done.6
  212.3 1.9 pack.15
  214.3 0.7 collective-permute-start.16
  215.0 16.7 %product.3 = (bf16[384,384]{1,0:T(8,128)(2,1)}, bf16[384,384]{1,0:T(8,128)(2,1)}, bf16[384,384]{1,0:T(8,128)(2,1)}, bf16[384,384]{1,0:T(8,128)(2,1)}) custom-call(bf16[1536,4096]{1,0:T(8,128)(2,1)} %all-gather.2.cloned.1.call-done.tokens_ref, bf16[1024,3584]{1,0:T(8,128)(2,1)} %gate_ref.5, bf16[1024,3584]{1,0:T(8,128)(2,1)} %up_ref.5, ...), custom_call_target="tpu_custom_call" | custom-call | flops 9663676416 | bytes 20054016 | tf_op jit(solution)/shard_map/product/pallas_call | solution.py:136
  231.7 0.8 copy-done.9
  232.5 1.4 collective-permute-start.18
  233.9 2.9 collective-permute-start.12
  236.8 5.8 %collective-permute-start.13 = (bf16[384,384]{1,0:T(8,128)(2,1)}, bf16[384,384]{1,0:T(8,128)(2,1)S(1)}, u32[]{:S(2)}, u32[]{:S(2)}) collective-permute-start(bf16[384,384]{1,0:T(8,128)(2,1)} %get-tuple-element.19), channel_id=1, source_target_pairs={{0,8},{4,12},{8,0},{12,4},{1,9},{5,13},{9,1},{13,5},{2,10},{6,14},... | collective-permute-start | bytes 884744 | tf_op jit(solution)/shard_map/ppermute | solution.py:269
  242.6 0.8 collective-permute-done.26.refs_0_
  243.4 0.8 copy-done.8
  244.2 0.8 collective-permute-start.25
  245.0 1.2 collective-permute-start.27
  246.3 12.0 %product.4 = (bf16[384,256]{1,0:T(8,128)(2,1)}, bf16[384,256]{1,0:T(8,128)(2,1)}, bf16[384,256]{1,0:T(8,128)(2,1)}, bf16[384,256]{1,0:T(8,128)(2,1)}) custom-call(bf16[1536,4096]{1,0:T(8,128)(2,1)} %all-gather.2.cloned.1.call-done.tokens_ref, bf16[1024,3584]{1,0:T(8,128)(2,1)} %gate_ref.5, bf16[1024,3584]{1,0:T(8,128)(2,1)} %up_ref.5, ...), custom_call_target="tpu_custom_call" | custom-call | flops 6442450944 | bytes 17563648 | tf_op jit(solution)/shard_map/product/pallas_call | solution.py:136
  258.3 1.3 collective-permute-start.19
  259.6 7.1 %collective-permute-done.13.refs_2_.refs_8_ = bf16[384,384]{1,0:T(8,128)(2,1)S(1)} collective-permute-done((bf16[384,384]{1,0:T(8,128)(2,1)}, bf16[384,384]{1,0:T(8,128)(2,1)S(1)}, u32[]{:S(2)}, u32[]{:S(2)}) %collective-permute-start.13) | collective-permute-done | bytes 294944 | tf_op jit(solution)/shard_map/ppermute | solution.py:269
  266.7 3.4 %collective-permute-start.20 = (bf16[384,256]{1,0:T(8,128)(2,1)}, bf16[384,256]{1,0:T(8,128)(2,1)S(1)}, u32[]{:S(2)}, u32[]{:S(2)}) collective-permute-start(bf16[384,256]{1,0:T(8,128)(2,1)} %get-tuple-element.23), channel_id=1, source_target_pairs={{0,8},{4,12},{8,0},{12,4},{1,9},{5,13},{9,1},{13,5},{2,10},{6,14},... | collective-permute-start | bytes 589832 | tf_op jit(solution)/shard_map/ppermute | solution.py:269
  270.1 0.6 copy-done.12
  271.1 12.0 %product.5 = (bf16[384,256]{1,0:T(8,128)(2,1)}, bf16[384,256]{1,0:T(8,128)(2,1)}, bf16[384,256]{1,0:T(8,128)(2,1)}, bf16[384,256]{1,0:T(8,128)(2,1)}) custom-call(bf16[1536,4096]{1,0:T(8,128)(2,1)} %all-gather.2.cloned.1.call-done.tokens_ref, bf16[1024,3584]{1,0:T(8,128)(2,1)} %gate_ref.5, bf16[1024,3584]{1,0:T(8,128)(2,1)} %up_ref.5, ...), custom_call_target="tpu_custom_call" | custom-call | flops 6442450944 | bytes 17563648 | tf_op jit(solution)/shard_map/product/pallas_call | solution.py:136
  283.1 2.0 collective-permute-start.28
  285.1 2.0 collective-permute-start.29
  287.2 0.6 copy-done.23
  287.9 0.7 copy-done.25
  288.6 2.4 place.2.refs_0_
  290.9 5.2 %collective-permute-done.28.refs_2_ = bf16[384,256]{1,0:T(8,128)(2,1)S(1)} collective-permute-done((bf16[384,256]{1,0:T(8,128)(2,1)}, bf16[384,256]{1,0:T(8,128)(2,1)S(1)}, u32[]{:S(2)}, u32[]{:S(2)}) %collective-permute-start.28) | collective-permute-done | bytes 196640 | tf_op jit(solution)/shard_map/ppermute | solution.py:269
  296.1 2.1 collective-permute-done.29.refs_3_
  298.2 2.0 collective-permute-done.30.refs_4_
  300.2 0.7 copy-done.28
  300.9 2.0 place.3
  (76 shorter events, 0.7 us)
Async XLA Ops:
  6.5 208.5 %all-gather.2.cloned.1.call-start = ((), (), s32[]{:S(2)}) async-start(), calls=%async_computation | async-start | bytes 15728640 | tf_op jit(solution)/shard_map/all_gather | solution.py:288
  6.5 21.4 %collective-permute-start = (bf16[384,1024]{1,0:T(8,128)(2,1)}, bf16[384,1024]{1,0:T(8,128)(2,1)S(1)}, u32[]{:S(2)}, u32[]{:S(2)}) collective-permute-start(bf16[384,1024]{1,0:T(8,128)(2,1)} %refs_0_.12), channel_id=1, source_target_pairs={{0,4},{4,8},{8,12},{1,5},{5,9},{9,13},{2,6},{6,10},{10,14},{3,7},{... | collective-permute-start | bytes 2359304 | tf_op jit(solution)/shard_map/ppermute | solution.py:245
  10.0 21.4 %collective-permute-start.3 = (bf16[384,1024]{1,0:T(8,128)(2,1)}, bf16[384,1024]{1,0:T(8,128)(2,1)S(1)}, u32[]{:S(2)}, u32[]{:S(2)}) collective-permute-start(bf16[384,1024]{1,0:T(8,128)(2,1)} %refs_0_.12), channel_id=1, source_target_pairs={{4,0},{8,4},{12,8},{5,1},{9,5},{13,9},{6,2},{10,6},{14,10},{7,3},{... | collective-permute-start | bytes 2359304 | tf_op jit(solution)/shard_map/ppermute | solution.py:246
  27.9 8.2 %copy-start.14 = (bf16[384,1024]{1,0:T(8,128)(2,1)}, bf16[384,1024]{1,0:T(8,128)(2,1)S(1)}, u32[]{:S(2)}) copy-start(bf16[384,1024]{1,0:T(8,128)(2,1)S(1)} %collective-permute-done.refs_1_) | copy-start | bytes 2359300
  27.9 49.5 %collective-permute-start.1 = (bf16[384,1024]{1,0:T(8,128)(2,1)S(1)}, bf16[384,1024]{1,0:T(8,128)(2,1)S(1)}, u32[]{:S(2)}, u32[]{:S(2)}) collective-permute-start(bf16[384,1024]{1,0:T(8,128)(2,1)S(1)} %collective-permute-done.refs_1_), channel_id=1, source_target_pairs={{4,8},{8,12},{5,9},{9,13},{6,10},{10,14},{7,11},{11,15},{20,24},{2... | collective-permute-start | bytes 2359304 | tf_op jit(solution)/shard_map/ppermute | solution.py:245
  31.5 4.7 %copy-start.15 = (bf16[384,1024]{1,0:T(8,128)(2,1)}, bf16[384,1024]{1,0:T(8,128)(2,1)S(1)}, u32[]{:S(2)}) copy-start(bf16[384,1024]{1,0:T(8,128)(2,1)S(1)} %collective-permute-done.3.refs_4_) | copy-start | bytes 2359300
  31.5 50.6 %collective-permute-start.4 = (bf16[384,1024]{1,0:T(8,128)(2,1)S(1)}, bf16[384,1024]{1,0:T(8,128)(2,1)}, u32[]{:S(2)}, u32[]{:S(2)}) collective-permute-start(bf16[384,1024]{1,0:T(8,128)(2,1)S(1)} %collective-permute-done.3.refs_4_), channel_id=1, source_target_pairs={{4,0},{8,4},{5,1},{9,5},{6,2},{10,6},{7,3},{11,7},{20,16},{24,20},... | collective-permute-start | bytes 2359304 | tf_op jit(solution)/shard_map/ppermute | solution.py:246
  36.1 67.5 %collective-permute-start.6 = (bf16[512,1280]{1,0:T(8,128)(2,1)}, bf16[512,1280]{1,0:T(8,128)(2,1)S(1)}, u32[]{:S(2)}, u32[]{:S(2)}) collective-permute-start(bf16[512,1280]{1,0:T(8,128)(2,1)} %pack.8.refs_2_), channel_id=1, source_target_pairs={{0,8},{4,12},{8,0},{12,4},{1,9},{5,13},{9,1},{13,5},{2,10},{6,14},... | collective-permute-start | bytes 3932168 | tf_op jit(solution)/shard_map/ppermute | solution.py:258
  77.5 8.1 %copy-start.16 = (bf16[384,1024]{1,0:T(8,128)(2,1)}, bf16[384,1024]{1,0:T(8,128)(2,1)S(1)}, u32[]{:S(2)}) copy-start(bf16[384,1024]{1,0:T(8,128)(2,1)S(1)} %collective-permute-done.1.refs_2_) | copy-start | bytes 2359300
  77.5 26.2 %collective-permute-start.2 = (bf16[384,1024]{1,0:T(8,128)(2,1)S(1)}, bf16[384,1024]{1,0:T(8,128)(2,1)S(1)}, u32[]{:S(2)}, u32[]{:S(2)}) collective-permute-start(bf16[384,1024]{1,0:T(8,128)(2,1)S(1)} %collective-permute-done.1.refs_2_), channel_id=1, source_target_pairs={{8,12},{9,13},{10,14},{11,15},{24,28},{25,29},{26,30},{27,31}} | collective-permute-start | bytes 2359304 | tf_op jit(solution)/shard_map/ppermute | solution.py:245
  82.0 40.8 %collective-permute-start.5 = (bf16[384,1024]{1,0:T(8,128)(2,1)}, bf16[384,1024]{1,0:T(8,128)(2,1)S(1)}, u32[]{:S(2)}, u32[]{:S(2)}) collective-permute-start(bf16[384,1024]{1,0:T(8,128)(2,1)} %collective-permute-done.4.refs_5_), channel_id=1, source_target_pairs={{4,0},{5,1},{6,2},{7,3},{20,16},{21,17},{22,18},{23,19}} | collective-permute-start | bytes 2359304 | tf_op jit(solution)/shard_map/ppermute | solution.py:246
  103.6 19.2 %copy-start = (bf16[512,1280]{1,0:T(8,128)(2,1)}, bf16[512,1280]{1,0:T(8,128)(2,1)S(1)}, u32[]{:S(2)}) copy-start(bf16[512,1280]{1,0:T(8,128)(2,1)S(1)} %collective-permute-done.6.refs_7_.refs_0_.refs_3_) | copy-start | bytes 3932164
  103.6 19.2 %copy-start.17 = (bf16[384,1024]{1,0:T(8,128)(2,1)}, bf16[384,1024]{1,0:T(8,128)(2,1)S(1)}, u32[]{:S(2)}) copy-start(bf16[384,1024]{1,0:T(8,128)(2,1)S(1)} %collective-permute-done.2.refs_3_) | copy-start | bytes 2359300
  122.8 0.9 copy-start.18
  126.6 1.3 copy-start.1
  126.6 1.8 copy-start.3
  126.6 1.8 copy-start.2
  127.9 57.6 %collective-permute-start.7 = (bf16[512,1280]{1,0:T(8,128)(2,1)S(1)}, bf16[512,1280]{1,0:T(8,128)(2,1)}, u32[]{:S(2)}, u32[]{:S(2)}) collective-permute-start(bf16[512,1280]{1,0:T(8,128)(2,1)S(1)} %copy-done.1), channel_id=1, source_target_pairs={{0,16},{16,0},{1,17},{17,1},{2,18},{18,2},{3,19},{19,3},{4,20},{20... | collective-permute-start | bytes 3932168 | tf_op jit(solution)/shard_map/ppermute | solution.py:262
  128.4 20.9 %collective-permute-start.8 = (bf16[512,768]{1,0:T(8,128)(2,1)S(1)}, bf16[512,768]{1,0:T(8,128)(2,1)}, u32[]{:S(2)}, u32[]{:S(2)}) collective-permute-start(bf16[512,768]{1,0:T(8,128)(2,1)S(1)} %copy-done.3), channel_id=1, source_target_pairs={{0,4},{4,8},{8,12},{12,0},{1,5},{5,9},{9,13},{13,1},{2,6},{6,10},{... | collective-permute-start | bytes 2359304 | tf_op jit(solution)/shard_map/ppermute | solution.py:258
  128.4 39.1 %collective-permute-start.10 = (bf16[512,768]{1,0:T(8,128)(2,1)S(1)}, bf16[512,768]{1,0:T(8,128)(2,1)}, u32[]{:S(2)}, u32[]{:S(2)}) collective-permute-start(bf16[512,768]{1,0:T(8,128)(2,1)S(1)} %copy-done.2), channel_id=1, source_target_pairs={{0,12},{4,0},{8,4},{12,8},{1,13},{5,1},{9,5},{13,9},{2,14},{6,2},{... | collective-permute-start | bytes 2359304 | tf_op jit(solution)/shard_map/ppermute | solution.py:258
  132.8 51.2 %collective-permute-start.22 = (bf16[512,512]{1,0:T(8,128)(2,1)}, bf16[512,512]{1,0:T(8,128)(2,1)S(1)}, u32[]{:S(2)}, u32[]{:S(2)}) collective-permute-start(bf16[512,512]{1,0:T(8,128)(2,1)} %pack.11.refs_2_), channel_id=1, source_target_pairs={{0,8},{4,12},{8,0},{12,4},{1,9},{5,13},{9,1},{13,5},{2,10},{6,14},... | collective-permute-start | bytes 1572872 | tf_op jit(solution)/shard_map/ppermute | solution.py:258
  149.3 40.0 %collective-permute-start.9 = (bf16[512,768]{1,0:T(8,128)(2,1)}, bf16[512,768]{1,0:T(8,128)(2,1)S(1)}, u32[]{:S(2)}, u32[]{:S(2)}) collective-permute-start(bf16[512,768]{1,0:T(8,128)(2,1)} %collective-permute-done.8.refs_2_.refs_3_), channel_id=1, source_target_pairs={{0,16},{16,0},{1,17},{17,1},{2,18},{18,2},{3,19},{19,3},{4,20},{20... | collective-permute-start | bytes 2359304 | tf_op jit(solution)/shard_map/ppermute | solution.py:262
  167.5 26.6 %collective-permute-start.11 = (bf16[512,768]{1,0:T(8,128)(2,1)}, bf16[512,768]{1,0:T(8,128)(2,1)}, u32[]{:S(2)}, u32[]{:S(2)}) collective-permute-start(bf16[512,768]{1,0:T(8,128)(2,1)} %collective-permute-done.10.refs_4_.refs_3_), channel_id=1, source_target_pairs={{0,16},{16,0},{1,17},{17,1},{2,18},{18,2},{3,19},{19,3},{4,20},{20... | collective-permute-start | bytes 2359304 | tf_op jit(solution)/shard_map/ppermute | solution.py:262
  183.9 3.5 %copy-start.4 = (bf16[512,512]{1,0:T(8,128)(2,1)}, bf16[512,512]{1,0:T(8,128)(2,1)S(1)}, u32[]{:S(2)}) copy-start(bf16[512,512]{1,0:T(8,128)(2,1)S(1)} %collective-permute-done.22.refs_3_.refs_0_) | copy-start | bytes 1572868
  183.9 18.7 %collective-permute-start.23 = (bf16[512,512]{1,0:T(8,128)(2,1)S(1)}, bf16[512,512]{1,0:T(8,128)(2,1)S(1)}, u32[]{:S(2)}, u32[]{:S(2)}) collective-permute-start(bf16[512,512]{1,0:T(8,128)(2,1)S(1)} %collective-permute-done.22.refs_3_.refs_0_), channel_id=1, source_target_pairs={{0,16},{16,0},{1,17},{17,1},{2,18},{18,2},{3,19},{19,3},{4,20},{20... | collective-permute-start | bytes 1572872 | tf_op jit(solution)/shard_map/ppermute | solution.py:262
  187.5 24.0 %collective-permute-start.15 = (bf16[512,512]{1,0:T(8,128)(2,1)}, bf16[512,512]{1,0:T(8,128)(2,1)S(1)}, u32[]{:S(2)}, u32[]{:S(2)}) collective-permute-start(bf16[512,512]{1,0:T(8,128)(2,1)} %pack.12.refs_2_), channel_id=1, source_target_pairs={{0,4},{4,8},{8,12},{12,0},{1,5},{5,9},{9,13},{13,1},{2,6},{6,10},{... | collective-permute-start | bytes 1572872 | tf_op jit(solution)/shard_map/ppermute | solution.py:258
  189.3 0.9 copy-start.13
  192.1 39.6 %collective-permute-start.17 = (bf16[512,512]{1,0:T(8,128)(2,1)}, bf16[512,512]{1,0:T(8,128)(2,1)S(1)}, u32[]{:S(2)}, u32[]{:S(2)}) collective-permute-start(bf16[512,512]{1,0:T(8,128)(2,1)} %pack.13.refs_2_), channel_id=1, source_target_pairs={{0,12},{4,0},{8,4},{12,8},{1,13},{5,1},{9,5},{13,9},{2,14},{6,2},{... | collective-permute-start | bytes 1572872 | tf_op jit(solution)/shard_map/ppermute | solution.py:258
  196.0 40.8 %collective-permute-start.24 = (bf16[512,512]{1,0:T(8,128)(2,1)}, bf16[512,512]{1,0:T(8,128)(2,1)S(1)}, u32[]{:S(2)}, u32[]{:S(2)}) collective-permute-start(bf16[512,512]{1,0:T(8,128)(2,1)} %pack.14.refs_2_), channel_id=1, source_target_pairs={{0,4},{4,8},{8,12},{12,0},{1,5},{5,9},{9,13},{13,1},{2,6},{6,10},{... | collective-permute-start | bytes 1572872 | tf_op jit(solution)/shard_map/ppermute | solution.py:258
  202.7 8.8 %copy-start.5 = (bf16[512,512]{1,0:T(8,128)(2,1)}, bf16[512,512]{1,0:T(8,128)(2,1)S(1)}, u32[]{:S(2)}) copy-start(bf16[512,512]{1,0:T(8,128)(2,1)S(1)} %collective-permute-done.23.refs_4_.refs_1_) | copy-start | bytes 1572868
  211.4 0.8 copy-start.6
  214.2 29.2 %collective-permute-start.26 = (bf16[512,512]{1,0:T(8,128)(2,1)}, bf16[512,512]{1,0:T(8,128)(2,1)S(1)}, u32[]{:S(2)}, u32[]{:S(2)}) collective-permute-start(bf16[512,512]{1,0:T(8,128)(2,1)} %pack.15), channel_id=1, source_target_pairs={{0,12},{4,0},{8,4},{12,8},{1,13},{5,1},{9,5},{13,9},{2,14},{6,2},{... | collective-permute-start | bytes 1572872 | tf_op jit(solution)/shard_map/ppermute | solution.py:258
  214.3 29.9 %collective-permute-start.16 = (bf16[512,512]{1,0:T(8,128)(2,1)}, bf16[512,512]{1,0:T(8,128)(2,1)S(1)}, u32[]{:S(2)}, u32[]{:S(2)}) collective-permute-start(bf16[512,512]{1,0:T(8,128)(2,1)} %copy-done.6), channel_id=1, source_target_pairs={{0,16},{16,0},{1,17},{17,1},{2,18},{18,2},{3,19},{19,3},{4,20},{20... | collective-permute-start | bytes 1572872 | tf_op jit(solution)/shard_map/ppermute | solution.py:262
  231.7 0.8 copy-start.9
  232.5 12.5 %collective-permute-start.18 = (bf16[512,512]{1,0:T(8,128)(2,1)}, bf16[512,512]{1,0:T(8,128)(2,1)S(1)}, u32[]{:S(2)}, u32[]{:S(2)}) collective-permute-start(bf16[512,512]{1,0:T(8,128)(2,1)} %hold.3.refs_4_), channel_id=1, source_target_pairs={{0,16},{16,0},{1,17},{17,1},{2,18},{18,2},{3,19},{19,3},{4,20},{20... | collective-permute-start | bytes 1572872 | tf_op jit(solution)/shard_map/ppermute | solution.py:262
  233.9 24.4 %collective-permute-start.12 = (bf16[384,384]{1,0:T(8,128)(2,1)}, bf16[384,384]{1,0:T(8,128)(2,1)S(1)}, u32[]{:S(2)}, u32[]{:S(2)}) collective-permute-start(bf16[384,384]{1,0:T(8,128)(2,1)} %get-tuple-element.18), channel_id=1, source_target_pairs={{0,4},{4,8},{8,12},{12,0},{1,5},{5,9},{9,13},{13,1},{2,6},{6,10},{... | collective-permute-start | bytes 884744 | tf_op jit(solution)/shard_map/ppermute | solution.py:269
  236.8 5.8 %copy-start.7 = (bf16[512,512]{1,0:T(8,128)(2,1)}, bf16[512,512]{1,0:T(8,128)(2,1)S(1)}, u32[]{:S(2)}) copy-start(bf16[512,512]{1,0:T(8,128)(2,1)S(1)} %collective-permute-done.24.refs_0_) | copy-start | bytes 1572868
  236.8 29.9 %collective-permute-start.13 = (bf16[384,384]{1,0:T(8,128)(2,1)}, bf16[384,384]{1,0:T(8,128)(2,1)S(1)}, u32[]{:S(2)}, u32[]{:S(2)}) collective-permute-start(bf16[384,384]{1,0:T(8,128)(2,1)} %get-tuple-element.19), channel_id=1, source_target_pairs={{0,8},{4,12},{8,0},{12,4},{1,9},{5,13},{9,1},{13,5},{2,10},{6,14},... | collective-permute-start | bytes 884744 | tf_op jit(solution)/shard_map/ppermute | solution.py:269
  243.4 0.8 copy-start.8
  243.4 26.7 %collective-permute-start.14 = (bf16[384,384]{1,0:T(8,128)(2,1)}, bf16[384,384]{1,0:T(8,128)(2,1)S(1)}, u32[]{:S(2)}, u32[]{:S(2)}) collective-permute-start(bf16[384,384]{1,0:T(8,128)(2,1)} %get-tuple-element.20), channel_id=1, source_target_pairs={{0,12},{4,0},{8,4},{12,8},{1,13},{5,1},{9,5},{13,9},{2,14},{6,2},{... | collective-permute-start | bytes 884744 | tf_op jit(solution)/shard_map/ppermute | solution.py:269
  244.2 2.0 copy-start.19
  244.2 25.9 %collective-permute-start.25 = (bf16[512,512]{1,0:T(8,128)(2,1)}, bf16[512,512]{1,0:T(8,128)(2,1)S(1)}, u32[]{:S(2)}, u32[]{:S(2)}) collective-permute-start(bf16[512,512]{1,0:T(8,128)(2,1)} %hold.4.refs_2_), channel_id=1, source_target_pairs={{0,16},{16,0},{1,17},{17,1},{2,18},{18,2},{3,19},{19,3},{4,20},{20... | collective-permute-start | bytes 1572872 | tf_op jit(solution)/shard_map/ppermute | solution.py:262
  245.0 1.2 copy-start.22
  245.0 25.1 %collective-permute-start.27 = (bf16[512,512]{1,0:T(8,128)(2,1)}, bf16[512,512]{1,0:T(8,128)(2,1)S(1)}, u32[]{:S(2)}, u32[]{:S(2)}) collective-permute-start(bf16[512,512]{1,0:T(8,128)(2,1)} %hold.5.refs_4_), channel_id=1, source_target_pairs={{0,16},{16,0},{1,17},{17,1},{2,18},{18,2},{3,19},{19,3},{4,20},{20... | collective-permute-start | bytes 1572872 | tf_op jit(solution)/shard_map/ppermute | solution.py:262
  258.3 11.9 %copy-start.10 = (bf16[384,384]{1,0:T(8,128)(2,1)}, bf16[384,384]{1,0:T(8,128)(2,1)S(1)}, u32[]{:S(2)}) copy-start(bf16[384,384]{1,0:T(8,128)(2,1)S(1)} %collective-permute-done.12.refs_1_.refs_7_) | copy-start | bytes 884740
  258.3 28.9 %collective-permute-start.19 = (bf16[384,256]{1,0:T(8,128)(2,1)}, bf16[384,256]{1,0:T(8,128)(2,1)S(1)}, u32[]{:S(2)}, u32[]{:S(2)}) collective-permute-start(bf16[384,256]{1,0:T(8,128)(2,1)} %get-tuple-element.22), channel_id=1, source_target_pairs={{0,4},{4,8},{8,12},{12,0},{1,5},{5,9},{9,13},{13,1},{2,6},{6,10},{... | collective-permute-start | bytes 589832 | tf_op jit(solution)/shard_map/ppermute | solution.py:269
  266.7 3.4 %copy-start.11 = (bf16[384,384]{1,0:T(8,128)(2,1)}, bf16[384,384]{1,0:T(8,128)(2,1)S(1)}, u32[]{:S(2)}) copy-start(bf16[384,384]{1,0:T(8,128)(2,1)S(1)} %collective-permute-done.13.refs_2_.refs_8_) | copy-start | bytes 884740
  266.7 20.5 %collective-permute-start.20 = (bf16[384,256]{1,0:T(8,128)(2,1)}, bf16[384,256]{1,0:T(8,128)(2,1)S(1)}, u32[]{:S(2)}, u32[]{:S(2)}) collective-permute-start(bf16[384,256]{1,0:T(8,128)(2,1)} %get-tuple-element.23), channel_id=1, source_target_pairs={{0,8},{4,12},{8,0},{12,4},{1,9},{5,13},{9,1},{13,5},{2,10},{6,14},... | collective-permute-start | bytes 589832 | tf_op jit(solution)/shard_map/ppermute | solution.py:269
  270.1 0.7 copy-start.12
  270.1 17.1 %collective-permute-start.21 = (bf16[384,256]{1,0:T(8,128)(2,1)}, bf16[384,256]{1,0:T(8,128)(2,1)S(1)}, u32[]{:S(2)}, u32[]{:S(2)}) collective-permute-start(bf16[384,256]{1,0:T(8,128)(2,1)} %get-tuple-element.24), channel_id=1, source_target_pairs={{0,12},{4,0},{8,4},{12,8},{1,13},{5,1},{9,5},{13,9},{2,14},{6,2},{... | collective-permute-start | bytes 589832 | tf_op jit(solution)/shard_map/ppermute | solution.py:269
  270.1 0.9 copy-start.20
  270.1 1.0 copy-start.21
  283.1 13.0 %collective-permute-start.28 = (bf16[384,256]{1,0:T(8,128)(2,1)}, bf16[384,256]{1,0:T(8,128)(2,1)S(1)}, u32[]{:S(2)}, u32[]{:S(2)}) collective-permute-start(bf16[384,256]{1,0:T(8,128)(2,1)} %get-tuple-element.26), channel_id=1, source_target_pairs={{0,4},{4,8},{8,12},{12,0},{1,5},{5,9},{9,13},{13,1},{2,6},{6,10},{... | collective-permute-start | bytes 589832 | tf_op jit(solution)/shard_map/ppermute | solution.py:269
  285.1 13.2 %collective-permute-start.29 = (bf16[384,256]{1,0:T(8,128)(2,1)}, bf16[384,256]{1,0:T(8,128)(2,1)S(1)}, u32[]{:S(2)}, u32[]{:S(2)}) collective-permute-start(bf16[384,256]{1,0:T(8,128)(2,1)} %get-tuple-element.27), channel_id=1, source_target_pairs={{0,8},{4,12},{8,0},{12,4},{1,9},{5,13},{9,1},{13,5},{2,10},{6,14},... | collective-permute-start | bytes 589832 | tf_op jit(solution)/shard_map/ppermute | solution.py:269
  287.1 0.7 copy-start.23
  287.1 13.1 %collective-permute-start.30 = (bf16[384,256]{1,0:T(8,128)(2,1)}, bf16[384,256]{1,0:T(8,128)(2,1)S(1)}, u32[]{:S(2)}, u32[]{:S(2)}) collective-permute-start(bf16[384,256]{1,0:T(8,128)(2,1)} %get-tuple-element.28), channel_id=1, source_target_pairs={{0,12},{4,0},{8,4},{12,8},{1,13},{5,1},{9,5},{13,9},{2,14},{6,2},{... | collective-permute-start | bytes 589832 | tf_op jit(solution)/shard_map/ppermute | solution.py:269
  287.2 0.7 copy-start.24
  287.9 0.7 copy-start.25
  296.1 4.1 %copy-start.26 = (bf16[384,256]{1,0:T(8,128)(2,1)}, bf16[384,256]{1,0:T(8,128)(2,1)S(1)}, u32[]{:S(2)}) copy-start(bf16[384,256]{1,0:T(8,128)(2,1)S(1)} %collective-permute-done.28.refs_2_) | copy-start | bytes 589828
  298.2 2.0 copy-start.27
  300.2 0.7 copy-start.28
Sparse Core Ops, SparseCore 0:
  126.7 82.0 all-gather.1

commit v11 on v10

--- a/solution.py
+++ b/solution.py
@@ -78,21 +78,23 @@
     rows, parts = lax.axis_size("row"), lax.axis_size("parts")
     share, width, tiles = depth // parts, ff // rows, wide // LANES
     features = rows * depth
+    sources = by_step(rows)
     order = by_distance(rows) + [0]
 
-    def body(tokens_ref, gate_ref, up_ref, *refs):
+    def body(*refs):
+        token_refs, (gate_ref, up_ref), refs = refs[:rows], refs[rows:rows + 2], refs[rows + 2:]
         held_refs = refs[:len(held)]
         outs = refs[len(held) + len(after):][:rows]
         stack, block, sems, block_sems = refs[-4:]
         z, y = lax.axis_index("row"), lax.axis_index("parts")
 
+        def fetched(step, slot=0):
+            return pltpu.make_async_copy(token_refs[slot], block.at[step % 2], block_sems.at[step % 2])
+
         def fetch(step):
-            to = lax.rem(z + order[step], rows)
-            return pltpu.make_async_copy(
-                tokens_ref.at[pl.ds(pl.multiple_of(to * mine, mine), mine), :],
-                block.at[step % 2],
-                block_sems.at[step % 2],
-            )
+            for here in range(rows):
+                slot = sources[here].index((here + order[step]) % rows)
+                pl.when(z == here)(lambda slot=slot: fetched(step, slot).start())
 
         copies = []
         for ref, (shift, turn, begin, _) in zip(held_refs, held):
@@ -111,12 +113,12 @@
                     stack.at[pl.ds(own, depth), pl.ds((2 * j + g) * LANES, LANES)],
                     sems.at[len(copies)],
                 ))
-        fetch(0).start()
+        fetch(0)
         run_all(copies)
         for step, shift in enumerate(order):
-            fetch(step).wait()
+            fetched(step).wait()
             if step + 1 < rows:
-                fetch(step + 1).start()
+                fetch(step + 1)
 
             def tile(j, carry, step=step, shift=shift):
                 both = jnp.dot(
@@ -136,11 +138,11 @@
     return pl.pallas_call(
         body,
         out_shape=[jax.ShapeDtypeStruct((mine, wide), jnp.bfloat16)] * rows,
-        in_specs=[ANY] * (3 + len(held) + len(after)),
+        in_specs=[ANY] * (rows + 2 + len(held) + len(after)),
         out_specs=[pl.BlockSpec(memory_space=pltpu.VMEM)] * rows,
         scratch_shapes=[
             pltpu.VMEM((features, 2 * wide), gate_weight.dtype),
-            pltpu.VMEM((2, mine, features), tokens.dtype),
+            pltpu.VMEM((2, mine, features), tokens[0].dtype),
             pltpu.SemaphoreType.DMA((len(held) + 2 * tiles,)),
             pltpu.SemaphoreType.DMA((2,)),
         ],
@@ -149,50 +151,40 @@
             flops=4 * rows * mine * features * wide, bytes_accessed=moved, transcendentals=rows * mine * wide
         ),
         name="product",
-    )(tokens, gate_weight, up_weight, *[value for *_, value in held], *after)
-
-
-def ordered(lower, upper, after):
-    rows = lax.axis_size("row")
-    mine, near = lower[0].shape
-
-    def body(*refs):
-        lower_refs, upper_refs = refs[:rows], refs[rows:2 * rows - 1]
-        out, slots, sems = refs[-3:]
+    )(*tokens, gate_weight, up_weight, *[value for *_, value in held], *after)
+
+
+def by_step(rows):
+    sources = []
+    for z in range(rows):
+        above = [z + step for step in range(1, rows - z)]
+        below = [z - step for step in range(1, z + 1)]
+        sources.append([z] + (above + below if 2 * z < rows else below + above))
+    return sources
+
+
+def pick(choices, after):
+    rows, like = lax.axis_size("row"), choices[0][1]
+
+    def body(*refs):
+        out, sem = refs[-2:]
         z = lax.axis_index("row")
-        for here in range(rows):
-
-            @pl.when(z == here)
-            def _(here=here):
-                loads, stores = [], []
-                for row in range(rows):
-                    source = lower_refs[here - row] if row <= here else upper_refs[row - here - 1]
-                    loads.append(pltpu.make_async_copy(source, slots.at[row], sems.at[0, row]))
-                    stores.append(pltpu.make_async_copy(
-                        slots.at[row], out.at[pl.ds(row * mine, mine), :], sems.at[1, row]
-                    ))
-                for load in loads:
-                    load.start()
-                for load, store in zip(loads, stores):
-                    load.wait()
-                    store.start()
-                for store in stores:
-                    store.wait()
-
-    values = lower + upper[1:] + after
-    return pl.pallas_call(
-        body,
-        out_shape=jax.ShapeDtypeStruct((rows * mine, near), lower[0].dtype),
-        in_specs=[ANY] * len(values),
-        out_specs=ANY,
-        scratch_shapes=[
-            pltpu.VMEM((rows, mine, near), lower[0].dtype),
-            pltpu.SemaphoreType.DMA((2, rows)),
-        ],
+        copies = [pltpu.make_async_copy(ref, out, sem) for ref, _ in zip(refs, choices)]
+        for copy, (places, _) in zip(copies, choices):
+            for place in places:
+                pl.when(z == place)(copy.start)
+        copies[0].wait()
+
+    return pl.pallas_call(
+        body,
+        out_shape=jax.ShapeDtypeStruct(like.shape, like.dtype),
+        in_specs=[ANY] * (len(choices) + len(after)),
+        out_specs=pl.BlockSpec(memory_space=pltpu.VMEM),
+        scratch_shapes=[pltpu.SemaphoreType.DMA],
         compiler_params=pltpu.CompilerParams(vmem_limit_bytes=GRANT),
-        cost_estimate=pl.CostEstimate(flops=0, bytes_accessed=4 * rows * mine * near, transcendentals=0),
-        name="ordered",
-    )(*values)
+        cost_estimate=pl.CostEstimate(flops=0, bytes_accessed=4 * like.size, transcendentals=0),
+        name="pick",
+    )(*[value for _, value in choices], *after)
 
 
 def place(blocks, mine, ff, onto=None):
@@ -240,17 +232,29 @@
     width = ff // rows
     units = width // LANES
 
-    lower, upper = [tokens], [tokens]
-    for step in range(1, rows):
-        lower.append(lax.ppermute(lower[-1], "row", [(i, i + 1) for i in range(step - 1, rows - 1)]))
-        upper.append(lax.ppermute(upper[-1], "row", [(i, i - 1) for i in range(1, rows - step + 1)]))
-
     edges = [0]
     for piece in range(len(PIECES)):
         edge = units * sum(PIECES[:piece + 1]) // sum(PIECES) * LANES
         if edge > edges[-1]:
             edges.append(edge)
     spans = list(zip(edges[:-1], edges[1:]))
+
+    def tokens_of(before_last_step, before_last_gather):
+        lower, upper = [tokens], [tokens]
+        for step in range(1, rows):
+            if step > 1 and step == rows - 1:
+                lower[-1], upper[-1] = hold(lower[-1], before_last_step), hold(upper[-1], before_last_step)
+            lower.append(lax.ppermute(lower[-1], "row", [(i, i + 1) for i in range(step - 1, rows - 1)]))
+            upper.append(lax.ppermute(upper[-1], "row", [(i, i - 1) for i in range(1, rows - step + 1)]))
+        for slot in range(rows):
+            chosen = {}
+            for here, sources in enumerate(by_step(rows)):
+                chosen.setdefault(sources[slot] - here, []).append(here)
+            choices = [
+                (places, upper[offset] if offset > 0 else lower[-offset]) for offset, places in chosen.items()
+            ]
+            value = pick(choices, before_last_gather if slot == rows - 1 else []) if slot else tokens
+            whole.append(lax.all_gather(value, "col", axis=1, tiled=True))
 
     def weights(shift, low, high, users):
         after = sent[-1:] + arrived[:len(sent) - 2][-1:] * (len(sent) > 2) + swapped[:len(sent) - 3][-1:] * (len(sent) > 3)
@@ -273,19 +277,21 @@
 
     last = len(spans) - 1
     far, *near = by_distance(rows)
-    plan = [(far, 0, spans[max(last - 1, 0)][1], range(max(last, 1)))]
+    plan = [(far, *spans[n], [n]) for n in range(max(last, 1))]
+    ahead = len(plan)
     for n, (low, high) in enumerate(spans):
         plan += [(shift, low, high, [n]) for shift in near]
         if n == 0 < last:
             plan.append((far, *spans[last], [last]))
     sent, arrived, swapped, done, returned, blocks = [], [], [], [], [], []
     held = [[] for _ in spans]
+    whole = []
     for step in plan:
         if last and len(sent) == max(len(plan) - 3, 3):
             hidden_of(0, [])
         weights(*step)
-        if len(sent) == min(3, len(plan)):
-            whole = lax.all_gather(ordered(lower, upper, arrived[:1] + sent[1:3]), "col", axis=1, tiled=True)
+        if len(sent) == min(ahead + 2, len(plan)):
+            tokens_of(arrived[:1], arrived[1:ahead] + sent[ahead:])
     for n in range(min(last, 1), last + 1):
         hidden_of(n, done[-1:] + (returned[n - 2] if n > 1 else []))
     early = len(blocks) - rows if last else len(blocks)

time: 311 us -> 310 us (level)
  waiting for transfers between devices: 174 us -> 151 us
  starting transfers between devices: 49.1 us -> 66.7 us
  Pallas kernels: 64.5 us -> 69.1 us
    ppermute x6, waiting for transfers between devices: 79.8 us -> 34.3 us  [the longest x3 32.1 us: tokens_of(): lax.ppermute(upper[-1], 'row', [(i, i - 1) for i in range(1, rows - step...]
    ppermute x8 -> x9, starting transfers between devices: 9.05 us -> 28.4 us  [weights(): arrived.append(lax.ppermute(sent[-1], 'row', around(rows, shift)))]
    ppermute x8 -> x9, waiting for transfers between devices: 71.2 us -> 83.3 us  [weights(): arrived.append(lax.ppermute(sent[-1], 'row', around(rows, shift)))]
    ppermute x8 -> x9, waiting for transfers between devices: 6.31 us -> 15.7 us  [weights(): swapped.append(lax.ppermute(came, 'parts', around(parts, -turn)))]
    ppermute x9, starting transfers between devices: 17.4 us -> 13 us  [hidden_of(): lax.ppermute(outs[shift], 'row', around(rows, shift))]
    pallas_call x1 -> x3, Pallas kernels: 2.84 us -> 6.15 us  [pick(): pl.pallas_call(body, out_shape=jax.ShapeDtypeStruct(like.shape, like.dtyp...]
    pallas_call x8 -> x9, Pallas kernels: 16.7 us -> 18.4 us  [pack(): pl.pallas_call(body, out_shape=jax.ShapeDtypeStruct((share, 2 * wide), ga...]
    unnamed x58 -> x64, local copies, waits for them, and re-layouts: 8.61 us -> 9.07 us
  transfers between devices with their start and end apart: 32 -> 37, of which waited for: 15 -> 14; matrix products, arithmetic and copies ran while one was open for 0% -> 0% of each run, Pallas kernels for 19% -> 22%
where the time goes in v11:
time: 310 us; the launch traced here: 309 us
  waiting for transfers between devices  151 us (49%)
  Pallas kernels  69.1 us (22%)
  starting transfers between devices  66.7 us (22%)
  between operations  13.6 us (4%)
  local copies, waits for them, and re-layouts  9.07 us (3%)
    ppermute x9, waiting for transfers between devices, weights(): arrived.append(lax.ppermute(sent[-1], 'row', around(rows, shift)))  83.3 us
    pallas_call x3, Pallas kernels, product(): pl.pallas_call(body, out_shape=[jax.ShapeDtypeStruct((mine, wide), jnp.bf...  40.2 us
    ppermute x3, waiting for transfers between devices, tokens_of(): lax.ppermute(upper[-1], 'row', [(i, i - 1) for i in range(1, rows - step...  32.1 us
    ppermute x9, starting transfers between devices, weights(): arrived.append(lax.ppermute(sent[-1], 'row', around(rows, shift)))  28.4 us
    pallas_call x9, Pallas kernels, pack(): pl.pallas_call(body, out_shape=jax.ShapeDtypeStruct((share, 2 * wide), ga...  18.4 us
    ppermute x9, waiting for transfers between devices, hidden_of(): lax.ppermute(outs[shift], 'row', around(rows, shift))  16.6 us
    ppermute x9, waiting for transfers between devices, weights(): swapped.append(lax.ppermute(came, 'parts', around(parts, -turn)))  15.7 us
    ppermute x9, starting transfers between devices, hidden_of(): lax.ppermute(outs[shift], 'row', around(rows, shift))  13 us
  transfers between devices with their start and end apart: 37, of which 14 were waited for; matrix products, arithmetic and copies ran while one was open for 0% of the time, Pallas kernels for 22%

profile of v11, /device:TPU:12, one launch (start us, length us, event | category | flops | bytes accessed | tf_op | source)
XLA Modules:
  0.0 309.1 jit_solution(17835232039964125964)
XLA Ops:
  6.5 0.7 all-gather.5.cloned.1.call-update
  7.3 2.4 collective-permute-start
  9.7 3.5 %collective-permute-start.1 = (bf16[384,1024]{1,0:T(8,128)(2,1)}, bf16[384,1024]{1,0:T(8,128)(2,1)S(1)}, u32[]{:S(2)}, u32[]{:S(2)}) collective-permute-start(bf16[384,1024]{1,0:T(8,128)(2,1)} %param.3), channel_id=1, source_target_pairs={{0,4},{4,8},{8,12},{1,5},{5,9},{9,13},{2,6},{6,10},{10,14},{3,7},{... | collective-permute-start | bytes 2359304 | tf_op jit(solution)/shard_map/ppermute | solution.py:247
  13.2 15.5 %collective-permute-done.refs_0_.refs_2_ = bf16[384,1024]{1,0:T(8,128)(2,1)S(1)} collective-permute-done((bf16[384,1024]{1,0:T(8,128)(2,1)}, bf16[384,1024]{1,0:T(8,128)(2,1)S(1)}, u32[]{:S(2)}, u32[]{:S(2)}) %collective-permute-start) | collective-permute-done | bytes 786464 | tf_op jit(solution)/shard_map/ppermute | solution.py:248
  28.7 2.1 collective-permute-done.1.refs_1_
  30.8 0.9 copy-done.9
  31.7 2.0 pick.3
  33.8 2.3 pack.9.refs_2_
  36.1 2.7 collective-permute-start.3
  38.8 2.3 collective-permute-start.2
  41.1 4.4 %collective-permute-start.4 = (bf16[384,1024]{1,0:T(8,128)(2,1)S(1)}, bf16[384,1024]{1,0:T(8,128)(2,1)S(1)}, u32[]{:S(2)}, u32[]{:S(2)}) collective-permute-start(bf16[384,1024]{1,0:T(8,128)(2,1)S(1)} %copy-done.10), channel_id=1, source_target_pairs={{4,8},{8,12},{5,9},{9,13},{6,10},{10,14},{7,11},{11,15},{20,24},{2... | collective-permute-start | bytes 2359304 | tf_op jit(solution)/shard_map/ppermute | solution.py:247
  45.6 26.1 %collective-permute-done.3.refs_1_.refs_3_.refs_6_ = bf16[512,768]{1,0:T(8,128)(2,1)S(1)} collective-permute-done((bf16[512,768]{1,0:T(8,128)(2,1)}, bf16[512,768]{1,0:T(8,128)(2,1)S(1)}, u32[]{:S(2)}, u32[]{:S(2)}) %collective-permute-start.3) | collective-permute-done | bytes 786464 | tf_op jit(solution)/shard_map/ppermute | solution.py:262
  71.7 16.6 %collective-permute-done.2.refs_0_ = bf16[384,1024]{1,0:T(8,128)(2,1)} collective-permute-done((bf16[384,1024]{1,0:T(8,128)(2,1)S(1)}, bf16[384,1024]{1,0:T(8,128)(2,1)}, u32[]{:S(2)}, u32[]{:S(2)}) %collective-permute-start.2) | collective-permute-done | bytes 786464 | tf_op jit(solution)/shard_map/ppermute | solution.py:248
  88.4 0.9 copy-done.5
  89.3 2.1 pick.4
  91.4 2.2 collective-permute-start.5
  93.6 1.6 collective-permute-start.6
  95.2 2.0 pack.10.refs_2_
  97.3 2.2 pack.11.refs_2_.refs_5_
  99.4 2.3 pack.12.refs_6_.refs_2_
  101.8 18.8 %collective-permute-done.7.refs_4_.refs_3_.refs_6_ = bf16[512,512]{1,0:T(8,128)(2,1)S(1)} collective-permute-done((bf16[512,512]{1,0:T(8,128)(2,1)}, bf16[512,512]{1,0:T(8,128)(2,1)S(1)}, u32[]{:S(2)}, u32[]{:S(2)}) %collective-permute-start.7) | collective-permute-done | bytes 524320 | tf_op jit(solution)/shard_map/ppermute | solution.py:262
  120.5 0.8 copy-done.4
  121.4 2.0 pick.5
  123.4 0.6 collective-permute-start.8
  124.0 3.9 %collective-permute-start.9 = (bf16[512,768]{1,0:T(8,128)(2,1)S(1)}, bf16[512,768]{1,0:T(8,128)(2,1)}, u32[]{:S(2)}, u32[]{:S(2)}) collective-permute-start(bf16[512,768]{1,0:T(8,128)(2,1)S(1)} %copy-done.1), channel_id=1, source_target_pairs={{0,4},{4,8},{8,12},{12,0},{1,5},{5,9},{9,13},{13,1},{2,6},{6,10},{... | collective-permute-start | bytes 2359304 | tf_op jit(solution)/shard_map/ppermute | solution.py:262
  128.2 1.5 collective-permute-start.16
  129.8 14.3 %collective-permute-done.8.refs_7_.refs_4_ = bf16[512,768]{1,0:T(8,128)(2,1)} collective-permute-done((bf16[512,768]{1,0:T(8,128)(2,1)S(1)}, bf16[512,768]{1,0:T(8,128)(2,1)}, u32[]{:S(2)}, u32[]{:S(2)}) %collective-permute-start.8) | collective-permute-done | bytes 786464 | tf_op jit(solution)/shard_map/ppermute | solution.py:266
  144.1 1.9 pack.13.refs_2_
  146.0 6.0 %collective-permute-start.24 = (bf16[512,512]{1,0:T(8,128)(2,1)}, bf16[512,512]{1,0:T(8,128)(2,1)S(1)}, u32[]{:S(2)}, u32[]{:S(2)}) collective-permute-start(bf16[512,512]{1,0:T(8,128)(2,1)} %pack.13.refs_2_), channel_id=1, source_target_pairs={{0,8},{4,12},{8,0},{12,4},{1,9},{5,13},{9,1},{13,5},{2,10},{6,14},... | collective-permute-start | bytes 1572872 | tf_op jit(solution)/shard_map/ppermute | solution.py:262
  152.5 34.6 %collective-permute-done.11.refs_10_.refs_3_ = bf16[512,768]{1,0:T(8,128)(2,1)} collective-permute-done((bf16[512,768]{1,0:T(8,128)(2,1)S(1)}, bf16[512,768]{1,0:T(8,128)(2,1)}, u32[]{:S(2)}, u32[]{:S(2)}) %collective-permute-start.11) | collective-permute-done | bytes 786464 | tf_op jit(solution)/shard_map/ppermute | solution.py:262
  187.1 1.5 collective-permute-start.12
  188.7 0.8 copy-done.13
  189.5 1.9 pack.14.refs_2_
  191.5 0.6 collective-permute-start.25
  192.1 0.9 copy-done.21
  193.0 1.9 pack.15.refs_2_
  194.9 8.6 %collective-permute-start.19 = (bf16[512,512]{1,0:T(8,128)(2,1)}, bf16[512,512]{1,0:T(8,128)(2,1)S(1)}, u32[]{:S(2)}, u32[]{:S(2)}) collective-permute-start(bf16[512,512]{1,0:T(8,128)(2,1)} %pack.15.refs_2_), channel_id=1, source_target_pairs={{0,12},{4,0},{8,4},{12,8},{1,13},{5,1},{9,5},{13,9},{2,14},{6,2},{... | collective-permute-start | bytes 1572872 | tf_op jit(solution)/shard_map/ppermute | solution.py:262
  204.0 2.0 pack.16.refs_2_
  206.1 1.3 collective-permute-done.25.refs_4_.refs_7_
  207.4 0.8 copy-done.12
  208.2 1.9 pack.17
  210.1 6.7 %collective-permute-start.28 = (bf16[512,512]{1,0:T(8,128)(2,1)}, bf16[512,512]{1,0:T(8,128)(2,1)S(1)}, u32[]{:S(2)}, u32[]{:S(2)}) collective-permute-start(bf16[512,512]{1,0:T(8,128)(2,1)} %pack.17), channel_id=1, source_target_pairs={{0,12},{4,0},{8,4},{12,8},{1,13},{5,1},{9,5},{13,9},{2,14},{6,2},{... | collective-permute-start | bytes 1572872 | tf_op jit(solution)/shard_map/ppermute | solution.py:262
  216.8 16.6 %product.3 = (bf16[384,384]{1,0:T(8,128)(2,1)}, bf16[384,384]{1,0:T(8,128)(2,1)}, bf16[384,384]{1,0:T(8,128)(2,1)}, bf16[384,384]{1,0:T(8,128)(2,1)}) custom-call(bf16[384,4096]{1,0:T(8,128)(2,1)} %all-gather.5.cloned.1.call-done.refs_0_, bf16[384,4096]{1,0:T(8,128)(2,1)} %all-gather.7.cloned.1.call-done.refs_1_, ...), custom_call_target="tpu_custom_call" | custom-call | flops 9663676416 | bytes 20054016 | tf_op jit(solution)/shard_map/product/pallas_call | solution.py:138
  233.4 0.8 copy-done.17
  234.2 1.5 collective-permute-start.20
  235.8 2.6 collective-permute-start.14
  238.4 3.8 %collective-permute-done.28.refs_0_ = bf16[512,512]{1,0:T(8,128)(2,1)S(1)} collective-permute-done((bf16[512,512]{1,0:T(8,128)(2,1)}, bf16[512,512]{1,0:T(8,128)(2,1)S(1)}, u32[]{:S(2)}, u32[]{:S(2)}) %collective-permute-start.28) | collective-permute-done | bytes 524320 | tf_op jit(solution)/shard_map/ppermute | solution.py:262
  242.2 2.5 collective-permute-start.15
  245.4 1.5 collective-permute-start.29
  246.9 11.8 %product.4 = (bf16[384,256]{1,0:T(8,128)(2,1)}, bf16[384,256]{1,0:T(8,128)(2,1)}, bf16[384,256]{1,0:T(8,128)(2,1)}, bf16[384,256]{1,0:T(8,128)(2,1)}) custom-call(bf16[384,4096]{1,0:T(8,128)(2,1)} %all-gather.5.cloned.1.call-done.refs_0_, bf16[384,4096]{1,0:T(8,128)(2,1)} %all-gather.7.cloned.1.call-done.refs_1_, ...), custom_call_target="tpu_custom_call" | custom-call | flops 6442450944 | bytes 17563648 | tf_op jit(solution)/shard_map/product/pallas_call | solution.py:138
  259.1 8.0 %collective-permute-done.14.refs_2_.refs_14_ = bf16[384,384]{1,0:T(8,128)(2,1)S(1)} collective-permute-done((bf16[384,384]{1,0:T(8,128)(2,1)}, bf16[384,384]{1,0:T(8,128)(2,1)S(1)}, u32[]{:S(2)}, u32[]{:S(2)}) %collective-permute-start.14) | collective-permute-done | bytes 294944 | tf_op jit(solution)/shard_map/ppermute | solution.py:273
  267.1 3.4 %collective-permute-start.22 = (bf16[384,256]{1,0:T(8,128)(2,1)}, bf16[384,256]{1,0:T(8,128)(2,1)S(1)}, u32[]{:S(2)}, u32[]{:S(2)}) collective-permute-start(bf16[384,256]{1,0:T(8,128)(2,1)} %get-tuple-element.23), channel_id=1, source_target_pairs={{0,8},{4,12},{8,0},{12,4},{1,9},{5,13},{9,1},{13,5},{2,10},{6,14},... | collective-permute-start | bytes 589832 | tf_op jit(solution)/shard_map/ppermute | solution.py:273
  270.6 0.6 copy-done.20
  271.6 11.8 %product.5 = (bf16[384,256]{1,0:T(8,128)(2,1)}, bf16[384,256]{1,0:T(8,128)(2,1)}, bf16[384,256]{1,0:T(8,128)(2,1)}, bf16[384,256]{1,0:T(8,128)(2,1)}) custom-call(bf16[384,4096]{1,0:T(8,128)(2,1)} %all-gather.5.cloned.1.call-done.refs_0_, bf16[384,4096]{1,0:T(8,128)(2,1)} %all-gather.7.cloned.1.call-done.refs_1_, ...), custom_call_target="tpu_custom_call" | custom-call | flops 6442450944 | bytes 17563648 | tf_op jit(solution)/shard_map/product/pallas_call | solution.py:138
  283.4 2.0 collective-permute-start.30
  285.4 2.1 collective-permute-start.31
  287.5 0.6 copy-done.26
  288.3 0.7 copy-done.28
  288.9 2.4 place.2.refs_0_
  291.3 4.5 %collective-permute-done.30.refs_2_ = bf16[384,256]{1,0:T(8,128)(2,1)S(1)} collective-permute-done((bf16[384,256]{1,0:T(8,128)(2,1)}, bf16[384,256]{1,0:T(8,128)(2,1)S(1)}, u32[]{:S(2)}, u32[]{:S(2)}) %collective-permute-start.30) | collective-permute-done | bytes 196640 | tf_op jit(solution)/shard_map/ppermute | solution.py:273
  295.8 2.1 collective-permute-done.31.refs_3_
  297.9 1.9 collective-permute-done.32.refs_4_
  299.9 0.7 copy-done.31
  300.6 2.0 place.3
  (100 shorter events, 3.4 us)
Async XLA Ops:
  6.5 210.3 %all-gather.5.cloned.1.call-start = ((), (), s32[]{:S(2)}) async-start(), calls=%async_computation | async-start | bytes 3932160 | tf_op jit(solution)/shard_map/all_gather | solution.py:257
  7.3 209.5 %all-gather.7.cloned.1.call-start = ((), (), s32[]{:S(2)}) async-start(), calls=%async_computation.1 | async-start | bytes 3932160 | tf_op jit(solution)/shard_map/all_gather | solution.py:257
  7.3 21.4 %collective-permute-start = (bf16[384,1024]{1,0:T(8,128)(2,1)}, bf16[384,1024]{1,0:T(8,128)(2,1)S(1)}, u32[]{:S(2)}, u32[]{:S(2)}) collective-permute-start(bf16[384,1024]{1,0:T(8,128)(2,1)} %param.3), channel_id=1, source_target_pairs={{4,0},{8,4},{12,8},{5,1},{9,5},{13,9},{6,2},{10,6},{14,10},{7,3},{... | collective-permute-start | bytes 2359304 | tf_op jit(solution)/shard_map/ppermute | solution.py:248
  9.7 21.1 %collective-permute-start.1 = (bf16[384,1024]{1,0:T(8,128)(2,1)}, bf16[384,1024]{1,0:T(8,128)(2,1)S(1)}, u32[]{:S(2)}, u32[]{:S(2)}) collective-permute-start(bf16[384,1024]{1,0:T(8,128)(2,1)} %param.3), channel_id=1, source_target_pairs={{0,4},{4,8},{8,12},{1,5},{5,9},{9,13},{2,6},{6,10},{10,14},{3,7},{... | collective-permute-start | bytes 2359304 | tf_op jit(solution)/shard_map/ppermute | solution.py:247
  28.7 2.1 copy-start.7
  30.8 0.9 copy-start.9
  33.8 5.0 %copy-start.8 = (bf16[384,1024]{1,0:T(8,128)(2,1)S(1)}, bf16[384,1024]{1,0:T(8,128)(2,1)}, u32[]{:S(2)}) copy-start(bf16[384,1024]{1,0:T(8,128)(2,1)} %copy-done.7) | copy-start | bytes 2359300
  33.8 7.3 %copy-start.10 = (bf16[384,1024]{1,0:T(8,128)(2,1)S(1)}, bf16[384,1024]{1,0:T(8,128)(2,1)}, u32[]{:S(2)}) copy-start(bf16[384,1024]{1,0:T(8,128)(2,1)} %copy-done.9) | copy-start | bytes 2359300
  33.8 183.0 %all-gather.9.cloned.1.call-start = ((), (), s32[]{:S(2)}) async-start(), calls=%async_computation.2 | async-start | bytes 3932160 | tf_op jit(solution)/shard_map/all_gather | solution.py:257
  36.1 35.6 %collective-permute-start.3 = (bf16[512,768]{1,0:T(8,128)(2,1)}, bf16[512,768]{1,0:T(8,128)(2,1)S(1)}, u32[]{:S(2)}, u32[]{:S(2)}) collective-permute-start(bf16[512,768]{1,0:T(8,128)(2,1)} %pack.9.refs_2_), channel_id=1, source_target_pairs={{0,8},{4,12},{8,0},{12,4},{1,9},{5,13},{9,1},{13,5},{2,10},{6,14},... | collective-permute-start | bytes 2359304 | tf_op jit(solution)/shard_map/ppermute | solution.py:262
  38.8 49.5 %collective-permute-start.2 = (bf16[384,1024]{1,0:T(8,128)(2,1)S(1)}, bf16[384,1024]{1,0:T(8,128)(2,1)}, u32[]{:S(2)}, u32[]{:S(2)}) collective-permute-start(bf16[384,1024]{1,0:T(8,128)(2,1)S(1)} %copy-done.8), channel_id=1, source_target_pairs={{4,0},{8,4},{5,1},{9,5},{6,2},{10,6},{7,3},{11,7},{20,16},{24,20},... | collective-permute-start | bytes 2359304 | tf_op jit(solution)/shard_map/ppermute | solution.py:248
  41.1 47.2 %collective-permute-start.4 = (bf16[384,1024]{1,0:T(8,128)(2,1)S(1)}, bf16[384,1024]{1,0:T(8,128)(2,1)S(1)}, u32[]{:S(2)}, u32[]{:S(2)}) collective-permute-start(bf16[384,1024]{1,0:T(8,128)(2,1)S(1)} %copy-done.10), channel_id=1, source_target_pairs={{4,8},{8,12},{5,9},{9,13},{6,10},{10,14},{7,11},{11,15},{20,24},{2... | collective-permute-start | bytes 2359304 | tf_op jit(solution)/shard_map/ppermute | solution.py:247
  71.7 16.6 %copy-start.2 = (bf16[512,768]{1,0:T(8,128)(2,1)}, bf16[512,768]{1,0:T(8,128)(2,1)S(1)}, u32[]{:S(2)}) copy-start(bf16[512,768]{1,0:T(8,128)(2,1)S(1)} %collective-permute-done.3.refs_1_.refs_3_.refs_6_) | copy-start | bytes 2359300
  88.3 0.9 copy-start.5
  89.3 4.4 %copy-start.6 = (bf16[384,1024]{1,0:T(8,128)(2,1)S(1)}, bf16[384,1024]{1,0:T(8,128)(2,1)}, u32[]{:S(2)}) copy-start(bf16[384,1024]{1,0:T(8,128)(2,1)} %hold.6.refs_1_) | copy-start | bytes 2359300
  91.4 125.4 %all-gather.11.cloned.1.call-start = ((), (), s32[]{:S(2)}) async-start(), calls=%async_computation.3 | async-start | bytes 3932160 | tf_op jit(solution)/shard_map/all_gather | solution.py:257
  91.4 29.1 %collective-permute-start.5 = (bf16[384,1024]{1,0:T(8,128)(2,1)}, bf16[384,1024]{1,0:T(8,128)(2,1)}, u32[]{:S(2)}, u32[]{:S(2)}) collective-permute-start(bf16[384,1024]{1,0:T(8,128)(2,1)} %hold.5.refs_0_), channel_id=1, source_target_pairs={{4,0},{5,1},{6,2},{7,3},{20,16},{21,17},{22,18},{23,19}} | collective-permute-start | bytes 2359304 | tf_op jit(solution)/shard_map/ppermute | solution.py:248
  93.6 26.9 %collective-permute-start.6 = (bf16[384,1024]{1,0:T(8,128)(2,1)S(1)}, bf16[384,1024]{1,0:T(8,128)(2,1)}, u32[]{:S(2)}, u32[]{:S(2)}) collective-permute-start(bf16[384,1024]{1,0:T(8,128)(2,1)S(1)} %copy-done.6), channel_id=1, source_target_pairs={{8,12},{9,13},{10,14},{11,15},{24,28},{25,29},{26,30},{27,31}} | collective-permute-start | bytes 2359304 | tf_op jit(solution)/shard_map/ppermute | solution.py:247
  97.2 23.4 %collective-permute-start.7 = (bf16[512,512]{1,0:T(8,128)(2,1)}, bf16[512,512]{1,0:T(8,128)(2,1)S(1)}, u32[]{:S(2)}, u32[]{:S(2)}) collective-permute-start(bf16[512,512]{1,0:T(8,128)(2,1)} %pack.10.refs_2_), channel_id=1, source_target_pairs={{0,8},{4,12},{8,0},{12,4},{1,9},{5,13},{9,1},{13,5},{2,10},{6,14},... | collective-permute-start | bytes 1572872 | tf_op jit(solution)/shard_map/ppermute | solution.py:262
  101.7 21.7 %copy-start.3 = (bf16[512,768]{1,0:T(8,128)(2,1)S(1)}, bf16[512,768]{1,0:T(8,128)(2,1)}, u32[]{:S(2)}) copy-start(bf16[512,768]{1,0:T(8,128)(2,1)} %copy-done.2) | copy-start | bytes 2359300
  101.8 22.2 %copy-start.1 = (bf16[512,768]{1,0:T(8,128)(2,1)S(1)}, bf16[512,768]{1,0:T(8,128)(2,1)}, u32[]{:S(2)}) copy-start(bf16[512,768]{1,0:T(8,128)(2,1)} %pack.11.refs_2_.refs_5_) | copy-start | bytes 2359300
  101.8 26.1 %copy-start = (bf16[512,768]{1,0:T(8,128)(2,1)S(1)}, bf16[512,768]{1,0:T(8,128)(2,1)}, u32[]{:S(2)}) copy-start(bf16[512,768]{1,0:T(8,128)(2,1)} %pack.12.refs_6_.refs_2_) | copy-start | bytes 2359300
  120.5 0.8 copy-start.4
  123.4 20.6 %collective-permute-start.8 = (bf16[512,768]{1,0:T(8,128)(2,1)S(1)}, bf16[512,768]{1,0:T(8,128)(2,1)}, u32[]{:S(2)}, u32[]{:S(2)}) collective-permute-start(bf16[512,768]{1,0:T(8,128)(2,1)S(1)} %copy-done.3), channel_id=1, source_target_pairs={{0,16},{16,0},{1,17},{17,1},{2,18},{18,2},{3,19},{19,3},{4,20},{20... | collective-permute-start | bytes 2359304 | tf_op jit(solution)/shard_map/ppermute | solution.py:266
  124.0 28.0 %collective-permute-start.9 = (bf16[512,768]{1,0:T(8,128)(2,1)S(1)}, bf16[512,768]{1,0:T(8,128)(2,1)}, u32[]{:S(2)}, u32[]{:S(2)}) collective-permute-start(bf16[512,768]{1,0:T(8,128)(2,1)S(1)} %copy-done.1), channel_id=1, source_target_pairs={{0,4},{4,8},{8,12},{12,0},{1,5},{5,9},{9,13},{13,1},{2,6},{6,10},{... | collective-permute-start | bytes 2359304 | tf_op jit(solution)/shard_map/ppermute | solution.py:262
  127.9 59.3 %collective-permute-start.11 = (bf16[512,768]{1,0:T(8,128)(2,1)S(1)}, bf16[512,768]{1,0:T(8,128)(2,1)}, u32[]{:S(2)}, u32[]{:S(2)}) collective-permute-start(bf16[512,768]{1,0:T(8,128)(2,1)S(1)} %copy-done), channel_id=1, source_target_pairs={{0,12},{4,0},{8,4},{12,8},{1,13},{5,1},{9,5},{13,9},{2,14},{6,2},{... | collective-permute-start | bytes 2359304 | tf_op jit(solution)/shard_map/ppermute | solution.py:262
  128.2 60.4 %collective-permute-start.16 = (bf16[512,512]{1,0:T(8,128)(2,1)}, bf16[512,512]{1,0:T(8,128)(2,1)S(1)}, u32[]{:S(2)}, u32[]{:S(2)}) collective-permute-start(bf16[512,512]{1,0:T(8,128)(2,1)} %copy-done.4), channel_id=1, source_target_pairs={{0,16},{16,0},{1,17},{17,1},{2,18},{18,2},{3,19},{19,3},{4,20},{20... | collective-permute-start | bytes 1572872 | tf_op jit(solution)/shard_map/ppermute | solution.py:266
  146.0 45.5 %collective-permute-start.24 = (bf16[512,512]{1,0:T(8,128)(2,1)}, bf16[512,512]{1,0:T(8,128)(2,1)S(1)}, u32[]{:S(2)}, u32[]{:S(2)}) collective-permute-start(bf16[512,512]{1,0:T(8,128)(2,1)} %pack.13.refs_2_), channel_id=1, source_target_pairs={{0,8},{4,12},{8,0},{12,4},{1,9},{5,13},{9,1},{13,5},{2,10},{6,14},... | collective-permute-start | bytes 1572872 | tf_op jit(solution)/shard_map/ppermute | solution.py:262
  152.0 40.1 %collective-permute-start.10 = (bf16[512,768]{1,0:T(8,128)(2,1)}, bf16[512,768]{1,0:T(8,128)(2,1)S(1)}, u32[]{:S(2)}, u32[]{:S(2)}) collective-permute-start(bf16[512,768]{1,0:T(8,128)(2,1)} %collective-permute-done.9.refs_8_.refs_3_), channel_id=1, source_target_pairs={{0,16},{16,0},{1,17},{17,1},{2,18},{18,2},{3,19},{19,3},{4,20},{20... | collective-permute-start | bytes 2359304 | tf_op jit(solution)/shard_map/ppermute | solution.py:266
  187.1 16.9 %collective-permute-start.12 = (bf16[512,768]{1,0:T(8,128)(2,1)}, bf16[512,768]{1,0:T(8,128)(2,1)}, u32[]{:S(2)}, u32[]{:S(2)}) collective-permute-start(bf16[512,768]{1,0:T(8,128)(2,1)} %collective-permute-done.11.refs_10_.refs_3_), channel_id=1, source_target_pairs={{0,16},{16,0},{1,17},{17,1},{2,18},{18,2},{3,19},{19,3},{4,20},{20... | collective-permute-start | bytes 2359304 | tf_op jit(solution)/shard_map/ppermute | solution.py:266
  188.7 0.8 copy-start.13
  191.4 12.1 %collective-permute-start.17 = (bf16[512,512]{1,0:T(8,128)(2,1)}, bf16[512,512]{1,0:T(8,128)(2,1)S(1)}, u32[]{:S(2)}, u32[]{:S(2)}) collective-permute-start(bf16[512,512]{1,0:T(8,128)(2,1)} %pack.14.refs_2_), channel_id=1, source_target_pairs={{0,4},{4,8},{8,12},{12,0},{1,5},{5,9},{9,13},{13,1},{2,6},{6,10},{... | collective-permute-start | bytes 1572872 | tf_op jit(solution)/shard_map/ppermute | solution.py:262
  191.5 3.4 %copy-start.11 = (bf16[512,512]{1,0:T(8,128)(2,1)}, bf16[512,512]{1,0:T(8,128)(2,1)S(1)}, u32[]{:S(2)}) copy-start(bf16[512,512]{1,0:T(8,128)(2,1)S(1)} %collective-permute-done.24.refs_3_.refs_6_) | copy-start | bytes 1572868
  191.5 15.8 %collective-permute-start.25 = (bf16[512,512]{1,0:T(8,128)(2,1)S(1)}, bf16[512,512]{1,0:T(8,128)(2,1)S(1)}, u32[]{:S(2)}, u32[]{:S(2)}) collective-permute-start(bf16[512,512]{1,0:T(8,128)(2,1)S(1)} %collective-permute-done.24.refs_3_.refs_6_), channel_id=1, source_target_pairs={{0,16},{16,0},{1,17},{17,1},{2,18},{18,2},{3,19},{19,3},{4,20},{20... | collective-permute-start | bytes 1572872 | tf_op jit(solution)/shard_map/ppermute | solution.py:266
  192.1 0.9 copy-start.21
  194.9 38.5 %collective-permute-start.19 = (bf16[512,512]{1,0:T(8,128)(2,1)}, bf16[512,512]{1,0:T(8,128)(2,1)S(1)}, u32[]{:S(2)}, u32[]{:S(2)}) collective-permute-start(bf16[512,512]{1,0:T(8,128)(2,1)} %pack.15.refs_2_), channel_id=1, source_target_pairs={{0,12},{4,0},{8,4},{12,8},{1,13},{5,1},{9,5},{13,9},{2,14},{6,2},{... | collective-permute-start | bytes 1572872 | tf_op jit(solution)/shard_map/ppermute | solution.py:262
  203.5 2.5 copy-start.14
  203.5 41.2 %collective-permute-start.18 = (bf16[512,512]{1,0:T(8,128)(2,1)S(1)}, bf16[512,512]{1,0:T(8,128)(2,1)S(1)}, u32[]{:S(2)}, u32[]{:S(2)}) collective-permute-start(bf16[512,512]{1,0:T(8,128)(2,1)S(1)} %collective-permute-done.17.refs_8_.refs_3_), channel_id=1, source_target_pairs={{0,16},{16,0},{1,17},{17,1},{2,18},{18,2},{3,19},{19,3},{4,20},{20... | collective-permute-start | bytes 1572872 | tf_op jit(solution)/shard_map/ppermute | solution.py:266
  206.0 29.8 %collective-permute-start.26 = (bf16[512,512]{1,0:T(8,128)(2,1)}, bf16[512,512]{1,0:T(8,128)(2,1)S(1)}, u32[]{:S(2)}, u32[]{:S(2)}) collective-permute-start(bf16[512,512]{1,0:T(8,128)(2,1)} %pack.16.refs_2_), channel_id=1, source_target_pairs={{0,4},{4,8},{8,12},{12,0},{1,5},{5,9},{9,13},{13,1},{2,6},{6,10},{... | collective-permute-start | bytes 1572872 | tf_op jit(solution)/shard_map/ppermute | solution.py:262
  207.3 0.8 copy-start.12
  210.1 32.0 %collective-permute-start.28 = (bf16[512,512]{1,0:T(8,128)(2,1)}, bf16[512,512]{1,0:T(8,128)(2,1)S(1)}, u32[]{:S(2)}, u32[]{:S(2)}) collective-permute-start(bf16[512,512]{1,0:T(8,128)(2,1)} %pack.17), channel_id=1, source_target_pairs={{0,12},{4,0},{8,4},{12,8},{1,13},{5,1},{9,5},{13,9},{2,14},{6,2},{... | collective-permute-start | bytes 1572872 | tf_op jit(solution)/shard_map/ppermute | solution.py:262
  233.4 0.8 copy-start.17
  234.2 11.1 %collective-permute-start.20 = (bf16[512,512]{1,0:T(8,128)(2,1)}, bf16[512,512]{1,0:T(8,128)(2,1)S(1)}, u32[]{:S(2)}, u32[]{:S(2)}) collective-permute-start(bf16[512,512]{1,0:T(8,128)(2,1)} %hold.7.refs_10_), channel_id=1, source_target_pairs={{0,16},{16,0},{1,17},{17,1},{2,18},{18,2},{3,19},{19,3},{4,20},{20... | collective-permute-start | bytes 1572872 | tf_op jit(solution)/shard_map/ppermute | solution.py:266
  235.8 23.0 %collective-permute-start.13 = (bf16[384,384]{1,0:T(8,128)(2,1)}, bf16[384,384]{1,0:T(8,128)(2,1)S(1)}, u32[]{:S(2)}, u32[]{:S(2)}) collective-permute-start(bf16[384,384]{1,0:T(8,128)(2,1)} %get-tuple-element.18), channel_id=1, source_target_pairs={{0,4},{4,8},{8,12},{12,0},{1,5},{5,9},{9,13},{13,1},{2,6},{6,10},{... | collective-permute-start | bytes 884744 | tf_op jit(solution)/shard_map/ppermute | solution.py:273
  235.8 2.6 copy-start.16
  235.8 31.3 %collective-permute-start.14 = (bf16[384,384]{1,0:T(8,128)(2,1)}, bf16[384,384]{1,0:T(8,128)(2,1)S(1)}, u32[]{:S(2)}, u32[]{:S(2)}) collective-permute-start(bf16[384,384]{1,0:T(8,128)(2,1)} %get-tuple-element.19), channel_id=1, source_target_pairs={{0,8},{4,12},{8,0},{12,4},{1,9},{5,13},{9,1},{13,5},{2,10},{6,14},... | collective-permute-start | bytes 884744 | tf_op jit(solution)/shard_map/ppermute | solution.py:273
  242.2 2.5 copy-start.15
  242.2 28.4 %collective-permute-start.15 = (bf16[384,384]{1,0:T(8,128)(2,1)}, bf16[384,384]{1,0:T(8,128)(2,1)S(1)}, u32[]{:S(2)}, u32[]{:S(2)}) collective-permute-start(bf16[384,384]{1,0:T(8,128)(2,1)} %get-tuple-element.20), channel_id=1, source_target_pairs={{0,12},{4,0},{8,4},{12,8},{1,13},{5,1},{9,5},{13,9},{2,14},{6,2},{... | collective-permute-start | bytes 884744 | tf_op jit(solution)/shard_map/ppermute | solution.py:273
  244.7 2.2 copy-start.22
  244.7 25.9 %collective-permute-start.27 = (bf16[512,512]{1,0:T(8,128)(2,1)}, bf16[512,512]{1,0:T(8,128)(2,1)S(1)}, u32[]{:S(2)}, u32[]{:S(2)}) collective-permute-start(bf16[512,512]{1,0:T(8,128)(2,1)} %hold.8.refs_8_), channel_id=1, source_target_pairs={{0,16},{16,0},{1,17},{17,1},{2,18},{18,2},{3,19},{19,3},{4,20},{20... | collective-permute-start | bytes 1572872 | tf_op jit(solution)/shard_map/ppermute | solution.py:266
  245.4 1.5 copy-start.25
  245.4 25.2 %collective-permute-start.29 = (bf16[512,512]{1,0:T(8,128)(2,1)}, bf16[512,512]{1,0:T(8,128)(2,1)S(1)}, u32[]{:S(2)}, u32[]{:S(2)}) collective-permute-start(bf16[512,512]{1,0:T(8,128)(2,1)} %hold.9.refs_10_), channel_id=1, source_target_pairs={{0,16},{16,0},{1,17},{17,1},{2,18},{18,2},{3,19},{19,3},{4,20},{20... | collective-permute-start | bytes 1572872 | tf_op jit(solution)/shard_map/ppermute | solution.py:266
  258.8 11.8 %copy-start.18 = (bf16[384,384]{1,0:T(8,128)(2,1)}, bf16[384,384]{1,0:T(8,128)(2,1)S(1)}, u32[]{:S(2)}) copy-start(bf16[384,384]{1,0:T(8,128)(2,1)S(1)} %collective-permute-done.13.refs_1_.refs_13_) | copy-start | bytes 884740
  258.8 28.7 %collective-permute-start.21 = (bf16[384,256]{1,0:T(8,128)(2,1)}, bf16[384,256]{1,0:T(8,128)(2,1)S(1)}, u32[]{:S(2)}, u32[]{:S(2)}) collective-permute-start(bf16[384,256]{1,0:T(8,128)(2,1)} %get-tuple-element.22), channel_id=1, source_target_pairs={{0,4},{4,8},{8,12},{12,0},{1,5},{5,9},{9,13},{13,1},{2,6},{6,10},{... | collective-permute-start | bytes 589832 | tf_op jit(solution)/shard_map/ppermute | solution.py:273
  267.1 3.5 %copy-start.19 = (bf16[384,384]{1,0:T(8,128)(2,1)}, bf16[384,384]{1,0:T(8,128)(2,1)S(1)}, u32[]{:S(2)}) copy-start(bf16[384,384]{1,0:T(8,128)(2,1)S(1)} %collective-permute-done.14.refs_2_.refs_14_) | copy-start | bytes 884740
  267.1 20.4 %collective-permute-start.22 = (bf16[384,256]{1,0:T(8,128)(2,1)}, bf16[384,256]{1,0:T(8,128)(2,1)S(1)}, u32[]{:S(2)}, u32[]{:S(2)}) collective-permute-start(bf16[384,256]{1,0:T(8,128)(2,1)} %get-tuple-element.23), channel_id=1, source_target_pairs={{0,8},{4,12},{8,0},{12,4},{1,9},{5,13},{9,1},{13,5},{2,10},{6,14},... | collective-permute-start | bytes 589832 | tf_op jit(solution)/shard_map/ppermute | solution.py:273
  270.5 17.0 %collective-permute-start.23 = (bf16[384,256]{1,0:T(8,128)(2,1)}, bf16[384,256]{1,0:T(8,128)(2,1)S(1)}, u32[]{:S(2)}, u32[]{:S(2)}) collective-permute-start(bf16[384,256]{1,0:T(8,128)(2,1)} %get-tuple-element.24), channel_id=1, source_target_pairs={{0,12},{4,0},{8,4},{12,8},{1,13},{5,1},{9,5},{13,9},{2,14},{6,2},{... | collective-permute-start | bytes 589832 | tf_op jit(solution)/shard_map/ppermute | solution.py:273
  270.6 0.9 copy-start.23
  270.6 1.0 copy-start.24
  283.4 12.4 %collective-permute-start.30 = (bf16[384,256]{1,0:T(8,128)(2,1)}, bf16[384,256]{1,0:T(8,128)(2,1)S(1)}, u32[]{:S(2)}, u32[]{:S(2)}) collective-permute-start(bf16[384,256]{1,0:T(8,128)(2,1)} %get-tuple-element.26), channel_id=1, source_target_pairs={{0,4},{4,8},{8,12},{12,0},{1,5},{5,9},{9,13},{13,1},{2,6},{6,10},{... | collective-permute-start | bytes 589832 | tf_op jit(solution)/shard_map/ppermute | solution.py:273
  285.4 12.5 %collective-permute-start.31 = (bf16[384,256]{1,0:T(8,128)(2,1)}, bf16[384,256]{1,0:T(8,128)(2,1)S(1)}, u32[]{:S(2)}, u32[]{:S(2)}) collective-permute-start(bf16[384,256]{1,0:T(8,128)(2,1)} %get-tuple-element.27), channel_id=1, source_target_pairs={{0,8},{4,12},{8,0},{12,4},{1,9},{5,13},{9,1},{13,5},{2,10},{6,14},... | collective-permute-start | bytes 589832 | tf_op jit(solution)/shard_map/ppermute | solution.py:273
  287.5 12.4 %collective-permute-start.32 = (bf16[384,256]{1,0:T(8,128)(2,1)}, bf16[384,256]{1,0:T(8,128)(2,1)S(1)}, u32[]{:S(2)}, u32[]{:S(2)}) collective-permute-start(bf16[384,256]{1,0:T(8,128)(2,1)} %get-tuple-element.28), channel_id=1, source_target_pairs={{0,12},{4,0},{8,4},{12,8},{1,13},{5,1},{9,5},{13,9},{2,14},{6,2},{... | collective-permute-start | bytes 589832 | tf_op jit(solution)/shard_map/ppermute | solution.py:273
  295.8 4.0 %copy-start.29 = (bf16[384,256]{1,0:T(8,128)(2,1)}, bf16[384,256]{1,0:T(8,128)(2,1)S(1)}, u32[]{:S(2)}) copy-start(bf16[384,256]{1,0:T(8,128)(2,1)S(1)} %collective-permute-done.30.refs_2_) | copy-start | bytes 589828
  297.9 1.9 copy-start.30
  (5 other events, 3.5 us)
Sparse Core Ops, SparseCore 0:
  8.9 29.6 all-gather.4
  40.2 28.5 all-gather.6
  91.5 29.4 all-gather.8
  123.5 32.9 all-gather.10

commit v12 on v11

--- a/solution.py
+++ b/solution.py
@@ -239,11 +239,12 @@
             edges.append(edge)
     spans = list(zip(edges[:-1], edges[1:]))
 
-    def tokens_of(before_last_step, before_last_gather):
+    def tokens_of(before_last_gather):
         lower, upper = [tokens], [tokens]
         for step in range(1, rows):
-            if step > 1 and step == rows - 1:
-                lower[-1], upper[-1] = hold(lower[-1], before_last_step), hold(upper[-1], before_last_step)
+            if step > 1:
+                before = arrived[step - 2:step - 1] + sent[step - 1:step] + swapped[:step - 2][-1:]
+                lower[-1], upper[-1] = hold(lower[-1], before), hold(upper[-1], before)
             lower.append(lax.ppermute(lower[-1], "row", [(i, i + 1) for i in range(step - 1, rows - 1)]))
             upper.append(lax.ppermute(upper[-1], "row", [(i, i - 1) for i in range(1, rows - step + 1)]))
         for slot in range(rows):
@@ -257,7 +258,7 @@
             whole.append(lax.all_gather(value, "col", axis=1, tiled=True))
 
     def weights(shift, low, high, users):
-        after = sent[-1:] + arrived[:len(sent) - 2][-1:] * (len(sent) > 2) + swapped[:len(sent) - 3][-1:] * (len(sent) > 3)
+        after = sent[-1:]
         sent.append(pack(gate_weight, up_weight, shift, low, high - low, after))
         arrived.append(lax.ppermute(sent[-1], "row", around(rows, shift)))
         came = hold(arrived[-1], done) if done else arrived[-1]
@@ -277,21 +278,17 @@
 
     last = len(spans) - 1
     far, *near = by_distance(rows)
-    plan = [(far, *spans[n], [n]) for n in range(max(last, 1))]
-    ahead = len(plan)
-    for n, (low, high) in enumerate(spans):
-        plan += [(shift, low, high, [n]) for shift in near]
-        if n == 0 < last:
-            plan.append((far, *spans[last], [last]))
+    plan = [(far, low, high, [n]) for n, (low, high) in enumerate(spans)]
+    plan += [(shift, low, high, [n]) for n, (low, high) in enumerate(spans) for shift in near]
     sent, arrived, swapped, done, returned, blocks = [], [], [], [], [], []
     held = [[] for _ in spans]
     whole = []
     for step in plan:
-        if last and len(sent) == max(len(plan) - 3, 3):
+        if last and len(sent) == max(len(plan) - 2, 3):
             hidden_of(0, [])
         weights(*step)
-        if len(sent) == min(ahead + 2, len(plan)):
-            tokens_of(arrived[:1], arrived[1:ahead] + sent[ahead:])
+        if len(sent) == min(rows + 2, max(len(plan) - 2, 3)):
+            tokens_of(arrived[rows - 2:rows - 1] + sent[rows - 1:] + swapped[:rows - 2][-1:])
     for n in range(min(last, 1), last + 1):
         hidden_of(n, done[-1:] + (returned[n - 2] if n > 1 else []))
     early = len(blocks) - rows if last else len(blocks)

time: 310 us -> 326 us (1.052)
  waiting for transfers between devices: 151 us -> 174 us
  starting transfers between devices: 66.7 us -> 59.3 us
    ppermute x9, waiting for transfers between devices: 83.3 us -> 123 us  [weights(): arrived.append(lax.ppermute(sent[-1], 'row', around(rows, shift)))]
    ppermute x3, waiting for transfers between devices: 32.1 us -> 6.58 us  [tokens_of(): lax.ppermute(upper[-1], 'row', [(i, i - 1) for i in range(1, rows - step...]
    ppermute x9, starting transfers between devices: 28.4 us -> 10.2 us  [weights(): arrived.append(lax.ppermute(sent[-1], 'row', around(rows, shift)))]
    ppermute x3, waiting for transfers between devices: 2.13 us -> 16.8 us  [tokens_of(): lax.ppermute(lower[-1], 'row', [(i, i + 1) for i in range(step - 1, rows...]
    ppermute x3, starting transfers between devices: 6.85 us -> 15.4 us  [tokens_of(): lax.ppermute(upper[-1], 'row', [(i, i - 1) for i in range(1, rows - step...]
    ppermute x9, waiting for transfers between devices: 16.6 us -> 10.5 us  [hidden_of(): lax.ppermute(outs[shift], 'row', around(rows, shift))]
    unnamed x64 -> x62, local copies, waits for them, and re-layouts: 9.07 us -> 7.16 us
  transfers between devices with their start and end apart: 37 -> 37, of which waited for: 14 -> 16; matrix products, arithmetic and copies ran while one was open for 0% -> 0% of each run, Pallas kernels for 22% -> 21%
where the time goes in v12:
time: 326 us; the launch traced here: 324 us
  waiting for transfers between devices  174 us (53%)
  Pallas kernels  69.7 us (21%)
  starting transfers between devices  59.3 us (18%)
  between operations  13.6 us (4%)
  local copies, waits for them, and re-layouts  7.16 us (2%)
    ppermute x9, waiting for transfers between devices, weights(): arrived.append(lax.ppermute(sent[-1], 'row', around(rows, shift)))  123 us
    pallas_call x3, Pallas kernels, product(): pl.pallas_call(body, out_shape=[jax.ShapeDtypeStruct((mine, wide), jnp.bf...  40.2 us
    pallas_call x9, Pallas kernels, pack(): pl.pallas_call(body, out_shape=jax.ShapeDtypeStruct((share, 2 * wide), ga...  18.9 us
    ppermute x9, waiting for transfers between devices, weights(): swapped.append(lax.ppermute(came, 'parts', around(parts, -turn)))  16.8 us
    ppermute x3, waiting for transfers between devices, tokens_of(): lax.ppermute(lower[-1], 'row', [(i, i + 1) for i in range(step - 1, rows...  16.8 us
    ppermute x3, starting transfers between devices, tokens_of(): lax.ppermute(upper[-1], 'row', [(i, i - 1) for i in range(1, rows - step...  15.4 us
    ppermute x9, starting transfers between devices, hidden_of(): lax.ppermute(outs[shift], 'row', around(rows, shift))  15 us
    ppermute x9, waiting for transfers between devices, hidden_of(): lax.ppermute(outs[shift], 'row', around(rows, shift))  10.5 us
  transfers between devices with their start and end apart: 37, of which 16 were waited for; matrix products, arithmetic and copies ran while one was open for 0% of the time, Pallas kernels for 21%

profile of v12, /device:TPU:12, one launch (start us, length us, event | category | flops | bytes accessed | tf_op | source)
XLA Modules:
  0.0 324.1 jit_solution(10966129601440525594)
XLA Ops:
  6.5 0.7 all-gather.5.cloned.1.call-update
  7.3 2.2 pack.9.refs_2_
  9.5 2.7 collective-permute-start.1
  12.1 1.9 collective-permute-start.2
  14.1 4.0 %collective-permute-start = (bf16[384,1024]{1,0:T(8,128)(2,1)}, bf16[384,1024]{1,0:T(8,128)(2,1)S(1)}, u32[]{:S(2)}, u32[]{:S(2)}) collective-permute-start(bf16[384,1024]{1,0:T(8,128)(2,1)} %param.3), channel_id=1, source_target_pairs={{4,0},{8,4},{12,8},{5,1},{9,5},{13,9},{6,2},{10,6},{14,10},{7,3},{... | collective-permute-start | bytes 2359304 | tf_op jit(solution)/shard_map/ppermute | solution.py:249
  18.0 2.1 pack.10.refs_2_
  20.2 26.0 %collective-permute-done.1.refs_1_.refs_6_ = bf16[512,768]{1,0:T(8,128)(2,1)S(1)} collective-permute-done((bf16[512,768]{1,0:T(8,128)(2,1)}, bf16[512,768]{1,0:T(8,128)(2,1)S(1)}, u32[]{:S(2)}, u32[]{:S(2)}) %collective-permute-start.1) | collective-permute-done | bytes 786464 | tf_op jit(solution)/shard_map/ppermute | solution.py:263
  46.1 16.8 %collective-permute-done.2.refs_0_ = bf16[384,1024]{1,0:T(8,128)(2,1)S(1)} collective-permute-done((bf16[384,1024]{1,0:T(8,128)(2,1)}, bf16[384,1024]{1,0:T(8,128)(2,1)S(1)}, u32[]{:S(2)}, u32[]{:S(2)}) %collective-permute-start.2) | collective-permute-done | bytes 786464 | tf_op jit(solution)/shard_map/ppermute | solution.py:248
  62.9 0.9 copy-done.6
  63.8 0.9 copy-done.4
  64.7 2.1 pick.3
  66.9 5.2 %collective-permute-start.6 = (bf16[384,1024]{1,0:T(8,128)(2,1)S(1)}, bf16[384,1024]{1,0:T(8,128)(2,1)}, u32[]{:S(2)}, u32[]{:S(2)}) collective-permute-start(bf16[384,1024]{1,0:T(8,128)(2,1)S(1)} %copy-done.7), channel_id=1, source_target_pairs={{4,8},{8,12},{5,9},{9,13},{6,10},{10,14},{7,11},{11,15},{20,24},{2... | collective-permute-start | bytes 2359304 | tf_op jit(solution)/shard_map/ppermute | solution.py:248
  72.6 1.9 collective-permute-start.3
  74.6 2.1 pack.11.refs_2_
  76.8 33.9 %collective-permute-done.4.refs_1_.refs_6_ = bf16[512,512]{1,0:T(8,128)(2,1)S(1)} collective-permute-done((bf16[512,512]{1,0:T(8,128)(2,1)S(1)}, bf16[512,512]{1,0:T(8,128)(2,1)S(1)}, u32[]{:S(2)}, u32[]{:S(2)}) %collective-permute-start.4) | collective-permute-done | bytes 524320 | tf_op jit(solution)/shard_map/ppermute | solution.py:263
  110.6 0.8 copy-done.8
  111.5 2.1 pick.4
  113.7 1.6 collective-permute-start.8
  115.3 9.5 %collective-permute-start.7 = (bf16[384,1024]{1,0:T(8,128)(2,1)}, bf16[384,1024]{1,0:T(8,128)(2,1)}, u32[]{:S(2)}, u32[]{:S(2)}) collective-permute-start(bf16[384,1024]{1,0:T(8,128)(2,1)} %hold.8.refs_0_), channel_id=1, source_target_pairs={{4,0},{5,1},{6,2},{7,3},{20,16},{21,17},{22,18},{23,19}} | collective-permute-start | bytes 2359304 | tf_op jit(solution)/shard_map/ppermute | solution.py:249
  124.8 1.6 collective-permute-start.10
  126.3 2.5 pack.12.refs_2_.refs_5_
  128.8 2.2 pack.13.refs_2_.refs_6_
  131.0 2.0 pack.14.refs_7_.refs_2_
  133.0 11.7 %collective-permute-done.9.refs_4_.refs_6_ = bf16[512,512]{1,0:T(8,128)(2,1)S(1)} collective-permute-done((bf16[512,512]{1,0:T(8,128)(2,1)S(1)}, bf16[512,512]{1,0:T(8,128)(2,1)S(1)}, u32[]{:S(2)}, u32[]{:S(2)}) %collective-permute-start.9) | collective-permute-done | bytes 524320 | tf_op jit(solution)/shard_map/ppermute | solution.py:263
  144.7 6.6 %collective-permute-done.7.refs_0_ = bf16[384,1024]{1,0:T(8,128)(2,1)} collective-permute-done((bf16[384,1024]{1,0:T(8,128)(2,1)}, bf16[384,1024]{1,0:T(8,128)(2,1)}, u32[]{:S(2)}, u32[]{:S(2)}) %collective-permute-start.7) | collective-permute-done | bytes 786464 | tf_op jit(solution)/shard_map/ppermute | solution.py:249
  151.3 2.1 pick.5
  153.4 2.5 collective-permute-start.13
  156.0 33.8 %collective-permute-done.13.refs_10_ = bf16[512,768]{1,0:T(8,128)(2,1)} collective-permute-done((bf16[512,768]{1,0:T(8,128)(2,1)S(1)}, bf16[512,768]{1,0:T(8,128)(2,1)}, u32[]{:S(2)}, u32[]{:S(2)}) %collective-permute-start.13) | collective-permute-done | bytes 786464 | tf_op jit(solution)/shard_map/ppermute | solution.py:263
  189.7 1.5 collective-permute-start.14
  191.2 0.8 collective-permute-start.12
  192.0 1.9 pack.15.refs_2_
  194.0 2.3 collective-permute-start.20
  196.3 1.9 pack.16.refs_2_
  198.2 1.3 collective-permute-start.26
  199.5 2.0 pack.17
  201.4 6.1 %collective-permute-done.20.refs_10_ = bf16[512,512]{1,0:T(8,128)(2,1)S(1)} collective-permute-done((bf16[512,512]{1,0:T(8,128)(2,1)}, bf16[512,512]{1,0:T(8,128)(2,1)S(1)}, u32[]{:S(2)}, u32[]{:S(2)}) %collective-permute-start.20) | collective-permute-done | bytes 524320 | tf_op jit(solution)/shard_map/ppermute | solution.py:263
  207.6 1.4 collective-permute-start.28
  209.0 11.6 %collective-permute-done.18.refs_8_ = bf16[512,512]{1,0:T(8,128)(2,1)S(1)} collective-permute-done((bf16[512,512]{1,0:T(8,128)(2,1)S(1)}, bf16[512,512]{1,0:T(8,128)(2,1)S(1)}, u32[]{:S(2)}, u32[]{:S(2)}) %collective-permute-start.18) | collective-permute-done | bytes 524320 | tf_op jit(solution)/shard_map/ppermute | solution.py:263
  220.6 1.5 collective-permute-start.25
  222.6 4.8 %collective-permute-done.12.refs_9_ = bf16[512,768]{1,0:T(8,128)(2,1)} collective-permute-done((bf16[512,768]{1,0:T(8,128)(2,1)}, bf16[512,768]{1,0:T(8,128)(2,1)}, u32[]{:S(2)}, u32[]{:S(2)}) %collective-permute-start.12) | collective-permute-done | bytes 786464 | tf_op jit(solution)/shard_map/ppermute | solution.py:267
  227.4 1.5 collective-permute-start.19
  228.9 16.5 %product.3 = (bf16[384,384]{1,0:T(8,128)(2,1)}, bf16[384,384]{1,0:T(8,128)(2,1)}, bf16[384,384]{1,0:T(8,128)(2,1)}, bf16[384,384]{1,0:T(8,128)(2,1)}) custom-call(bf16[384,4096]{1,0:T(8,128)(2,1)} %all-gather.5.cloned.1.call-done.refs_0_, bf16[384,4096]{1,0:T(8,128)(2,1)} %all-gather.7.cloned.1.call-done.refs_1_, ...), custom_call_target="tpu_custom_call" | custom-call | flops 9663676416 | bytes 20054016 | tf_op jit(solution)/shard_map/product/pallas_call | solution.py:138
  245.5 0.8 copy-done.17
  246.8 0.8 copy-done.16
  247.6 1.5 collective-permute-start.27
  249.1 0.7 collective-permute-done.21.refs_11_
  249.9 11.2 %collective-permute-done.19.refs_9_ = bf16[512,512]{1,0:T(8,128)(2,1)} collective-permute-done((bf16[512,512]{1,0:T(8,128)(2,1)S(1)}, bf16[512,512]{1,0:T(8,128)(2,1)}, u32[]{:S(2)}, u32[]{:S(2)}) %collective-permute-start.19) | collective-permute-done | bytes 524320 | tf_op jit(solution)/shard_map/ppermute | solution.py:267
  261.1 2.5 collective-permute-start.17
  263.6 11.8 %product.4 = (bf16[384,256]{1,0:T(8,128)(2,1)}, bf16[384,256]{1,0:T(8,128)(2,1)}, bf16[384,256]{1,0:T(8,128)(2,1)}, bf16[384,256]{1,0:T(8,128)(2,1)}) custom-call(bf16[384,4096]{1,0:T(8,128)(2,1)} %all-gather.5.cloned.1.call-done.refs_0_, bf16[384,4096]{1,0:T(8,128)(2,1)} %all-gather.7.cloned.1.call-done.refs_1_, ...), custom_call_target="tpu_custom_call" | custom-call | flops 6442450944 | bytes 17563648 | tf_op jit(solution)/shard_map/product/pallas_call | solution.py:138
  275.5 1.7 collective-permute-start.22
  277.2 4.5 %collective-permute-done.16.refs_2_.refs_14_ = bf16[384,384]{1,0:T(8,128)(2,1)S(1)} collective-permute-done((bf16[384,384]{1,0:T(8,128)(2,1)}, bf16[384,384]{1,0:T(8,128)(2,1)S(1)}, u32[]{:S(2)}, u32[]{:S(2)}) %collective-permute-start.16) | collective-permute-done | bytes 294944 | tf_op jit(solution)/shard_map/ppermute | solution.py:274
  281.6 6.8 %collective-permute-start.23 = (bf16[384,256]{1,0:T(8,128)(2,1)}, bf16[384,256]{1,0:T(8,128)(2,1)S(1)}, u32[]{:S(2)}, u32[]{:S(2)}) collective-permute-start(bf16[384,256]{1,0:T(8,128)(2,1)} %get-tuple-element.23), channel_id=1, source_target_pairs={{0,8},{4,12},{8,0},{12,4},{1,9},{5,13},{9,1},{13,5},{2,10},{6,14},... | collective-permute-start | bytes 589832 | tf_op jit(solution)/shard_map/ppermute | solution.py:274
  288.6 0.7 copy-done.20
  289.4 11.8 %product.5 = (bf16[384,256]{1,0:T(8,128)(2,1)}, bf16[384,256]{1,0:T(8,128)(2,1)}, bf16[384,256]{1,0:T(8,128)(2,1)}, bf16[384,256]{1,0:T(8,128)(2,1)}) custom-call(bf16[384,4096]{1,0:T(8,128)(2,1)} %all-gather.5.cloned.1.call-done.refs_0_, bf16[384,4096]{1,0:T(8,128)(2,1)} %all-gather.7.cloned.1.call-done.refs_1_, ...), custom_call_target="tpu_custom_call" | custom-call | flops 6442450944 | bytes 17563648 | tf_op jit(solution)/shard_map/product/pallas_call | solution.py:138
  301.2 2.0 collective-permute-start.30
  303.2 2.0 collective-permute-start.31
  305.2 0.6 copy-done.25
  305.9 0.7 copy-done.27
  306.6 2.4 place.2.refs_0_
  309.0 2.5 collective-permute-done.30.refs_2_
  311.4 2.1 collective-permute-done.31.refs_3_
  313.5 1.4 collective-permute-done.32.refs_4_
  315.0 0.7 copy-done.30
  315.6 2.0 place.3
  (99 shorter events, 2.3 us)
Async XLA Ops:
  6.5 222.4 %all-gather.5.cloned.1.call-start = ((), (), s32[]{:S(2)}) async-start(), calls=%async_computation | async-start | bytes 3932160 | tf_op jit(solution)/shard_map/all_gather | solution.py:258
  7.3 221.6 %all-gather.7.cloned.1.call-start = ((), (), s32[]{:S(2)}) async-start(), calls=%async_computation.1 | async-start | bytes 3932160 | tf_op jit(solution)/shard_map/all_gather | solution.py:258
  9.5 36.6 %collective-permute-start.1 = (bf16[512,768]{1,0:T(8,128)(2,1)}, bf16[512,768]{1,0:T(8,128)(2,1)S(1)}, u32[]{:S(2)}, u32[]{:S(2)}) collective-permute-start(bf16[512,768]{1,0:T(8,128)(2,1)} %pack.9.refs_2_), channel_id=1, source_target_pairs={{0,8},{4,12},{8,0},{12,4},{1,9},{5,13},{9,1},{13,5},{2,10},{6,14},... | collective-permute-start | bytes 2359304 | tf_op jit(solution)/shard_map/ppermute | solution.py:263
  12.1 50.8 %collective-permute-start.2 = (bf16[384,1024]{1,0:T(8,128)(2,1)}, bf16[384,1024]{1,0:T(8,128)(2,1)S(1)}, u32[]{:S(2)}, u32[]{:S(2)}) collective-permute-start(bf16[384,1024]{1,0:T(8,128)(2,1)} %param.3), channel_id=1, source_target_pairs={{0,4},{4,8},{8,12},{1,5},{5,9},{9,13},{2,6},{6,10},{10,14},{3,7},{... | collective-permute-start | bytes 2359304 | tf_op jit(solution)/shard_map/ppermute | solution.py:248
  14.1 49.8 %collective-permute-start = (bf16[384,1024]{1,0:T(8,128)(2,1)}, bf16[384,1024]{1,0:T(8,128)(2,1)S(1)}, u32[]{:S(2)}, u32[]{:S(2)}) collective-permute-start(bf16[384,1024]{1,0:T(8,128)(2,1)} %param.3), channel_id=1, source_target_pairs={{4,0},{8,4},{12,8},{5,1},{9,5},{13,9},{6,2},{10,6},{14,10},{7,3},{... | collective-permute-start | bytes 2359304 | tf_op jit(solution)/shard_map/ppermute | solution.py:249
  46.1 16.8 %copy-start.11 = (bf16[512,768]{1,0:T(8,128)(2,1)}, bf16[512,768]{1,0:T(8,128)(2,1)S(1)}, u32[]{:S(2)}) copy-start(bf16[512,768]{1,0:T(8,128)(2,1)S(1)} %collective-permute-done.1.refs_1_.refs_6_) | copy-start | bytes 2359300
  62.9 0.9 copy-start.6
  63.8 3.1 copy-start.7
  63.8 8.3 %copy-start.12 = (bf16[512,768]{1,0:T(8,128)(2,1)S(1)}, bf16[512,768]{1,0:T(8,128)(2,1)}, u32[]{:S(2)}) copy-start(bf16[512,768]{1,0:T(8,128)(2,1)} %copy-done.11) | copy-start | bytes 2359300
  63.8 10.7 %copy-start.1 = (bf16[512,512]{1,0:T(8,128)(2,1)S(1)}, bf16[512,512]{1,0:T(8,128)(2,1)}, u32[]{:S(2)}) copy-start(bf16[512,512]{1,0:T(8,128)(2,1)} %pack.10.refs_2_) | copy-start | bytes 1572868
  63.8 0.9 copy-start.4
  64.7 7.9 %copy-start.5 = (bf16[384,1024]{1,0:T(8,128)(2,1)S(1)}, bf16[384,1024]{1,0:T(8,128)(2,1)}, u32[]{:S(2)}) copy-start(bf16[384,1024]{1,0:T(8,128)(2,1)} %hold.6.refs_0_.refs_2_) | copy-start | bytes 2359300
  66.9 162.0 %all-gather.9.cloned.1.call-start = ((), (), s32[]{:S(2)}) async-start(), calls=%async_computation.2 | async-start | bytes 3932160 | tf_op jit(solution)/shard_map/all_gather | solution.py:258
  66.9 43.7 %collective-permute-start.6 = (bf16[384,1024]{1,0:T(8,128)(2,1)S(1)}, bf16[384,1024]{1,0:T(8,128)(2,1)}, u32[]{:S(2)}, u32[]{:S(2)}) collective-permute-start(bf16[384,1024]{1,0:T(8,128)(2,1)S(1)} %copy-done.7), channel_id=1, source_target_pairs={{4,8},{8,12},{5,9},{9,13},{6,10},{10,14},{7,11},{11,15},{20,24},{2... | collective-permute-start | bytes 2359304 | tf_op jit(solution)/shard_map/ppermute | solution.py:248
  72.1 38.6 %collective-permute-start.5 = (bf16[512,768]{1,0:T(8,128)(2,1)S(1)}, bf16[512,768]{1,0:T(8,128)(2,1)}, u32[]{:S(2)}, u32[]{:S(2)}) collective-permute-start(bf16[512,768]{1,0:T(8,128)(2,1)S(1)} %copy-done.12), channel_id=1, source_target_pairs={{0,16},{16,0},{1,17},{17,1},{2,18},{18,2},{3,19},{19,3},{4,20},{20... | collective-permute-start | bytes 2359304 | tf_op jit(solution)/shard_map/ppermute | solution.py:267
  72.6 38.8 %collective-permute-start.3 = (bf16[384,1024]{1,0:T(8,128)(2,1)S(1)}, bf16[384,1024]{1,0:T(8,128)(2,1)}, u32[]{:S(2)}, u32[]{:S(2)}) collective-permute-start(bf16[384,1024]{1,0:T(8,128)(2,1)S(1)} %copy-done.5), channel_id=1, source_target_pairs={{4,0},{8,4},{5,1},{9,5},{6,2},{10,6},{7,3},{11,7},{20,16},{24,20},... | collective-permute-start | bytes 2359304 | tf_op jit(solution)/shard_map/ppermute | solution.py:249
  74.6 36.1 %collective-permute-start.4 = (bf16[512,512]{1,0:T(8,128)(2,1)S(1)}, bf16[512,512]{1,0:T(8,128)(2,1)S(1)}, u32[]{:S(2)}, u32[]{:S(2)}) collective-permute-start(bf16[512,512]{1,0:T(8,128)(2,1)S(1)} %copy-done.1), channel_id=1, source_target_pairs={{0,8},{4,12},{8,0},{12,4},{1,9},{5,13},{9,1},{13,5},{2,10},{6,14},... | collective-permute-start | bytes 1572872 | tf_op jit(solution)/shard_map/ppermute | solution.py:263
  110.6 0.8 copy-start.8
  111.5 13.3 %copy-start = (bf16[512,512]{1,0:T(8,128)(2,1)S(1)}, bf16[512,512]{1,0:T(8,128)(2,1)}, u32[]{:S(2)}) copy-start(bf16[512,512]{1,0:T(8,128)(2,1)} %pack.11.refs_2_) | copy-start | bytes 1572868
  111.5 13.3 %copy-start.9 = (bf16[512,512]{1,0:T(8,128)(2,1)S(1)}, bf16[512,512]{1,0:T(8,128)(2,1)}, u32[]{:S(2)}) copy-start(bf16[512,512]{1,0:T(8,128)(2,1)} %copy-done.8) | copy-start | bytes 1572868
  113.6 115.2 %all-gather.11.cloned.1.call-start = ((), (), s32[]{:S(2)}) async-start(), calls=%async_computation.3 | async-start | bytes 3932160 | tf_op jit(solution)/shard_map/all_gather | solution.py:258
  113.7 31.0 %collective-permute-start.8 = (bf16[384,1024]{1,0:T(8,128)(2,1)}, bf16[384,1024]{1,0:T(8,128)(2,1)}, u32[]{:S(2)}, u32[]{:S(2)}) collective-permute-start(bf16[384,1024]{1,0:T(8,128)(2,1)} %hold.9.refs_1_), channel_id=1, source_target_pairs={{8,12},{9,13},{10,14},{11,15},{24,28},{25,29},{26,30},{27,31}} | collective-permute-start | bytes 2359304 | tf_op jit(solution)/shard_map/ppermute | solution.py:248
  115.3 36.0 %collective-permute-start.7 = (bf16[384,1024]{1,0:T(8,128)(2,1)}, bf16[384,1024]{1,0:T(8,128)(2,1)}, u32[]{:S(2)}, u32[]{:S(2)}) collective-permute-start(bf16[384,1024]{1,0:T(8,128)(2,1)} %hold.8.refs_0_), channel_id=1, source_target_pairs={{4,0},{5,1},{6,2},{7,3},{20,16},{21,17},{22,18},{23,19}} | collective-permute-start | bytes 2359304 | tf_op jit(solution)/shard_map/ppermute | solution.py:249
  124.8 19.9 %collective-permute-start.9 = (bf16[512,512]{1,0:T(8,128)(2,1)S(1)}, bf16[512,512]{1,0:T(8,128)(2,1)S(1)}, u32[]{:S(2)}, u32[]{:S(2)}) collective-permute-start(bf16[512,512]{1,0:T(8,128)(2,1)S(1)} %copy-done), channel_id=1, source_target_pairs={{0,8},{4,12},{8,0},{12,4},{1,9},{5,13},{9,1},{13,5},{2,10},{6,14},... | collective-permute-start | bytes 1572872 | tf_op jit(solution)/shard_map/ppermute | solution.py:263
  124.8 19.9 %collective-permute-start.10 = (bf16[512,512]{1,0:T(8,128)(2,1)S(1)}, bf16[512,512]{1,0:T(8,128)(2,1)S(1)}, u32[]{:S(2)}, u32[]{:S(2)}) collective-permute-start(bf16[512,512]{1,0:T(8,128)(2,1)S(1)} %copy-done.9), channel_id=1, source_target_pairs={{0,16},{16,0},{1,17},{17,1},{2,18},{18,2},{3,19},{19,3},{4,20},{20... | collective-permute-start | bytes 1572872 | tf_op jit(solution)/shard_map/ppermute | solution.py:267
  133.0 20.4 %copy-start.3 = (bf16[512,768]{1,0:T(8,128)(2,1)S(1)}, bf16[512,768]{1,0:T(8,128)(2,1)}, u32[]{:S(2)}) copy-start(bf16[512,768]{1,0:T(8,128)(2,1)} %pack.13.refs_2_.refs_6_) | copy-start | bytes 2359300
  133.0 23.0 %copy-start.2 = (bf16[512,768]{1,0:T(8,128)(2,1)S(1)}, bf16[512,768]{1,0:T(8,128)(2,1)}, u32[]{:S(2)}) copy-start(bf16[512,768]{1,0:T(8,128)(2,1)} %pack.12.refs_2_.refs_5_) | copy-start | bytes 2359300
  144.7 6.6 %copy-start.13 = (bf16[512,512]{1,0:T(8,128)(2,1)}, bf16[512,512]{1,0:T(8,128)(2,1)S(1)}, u32[]{:S(2)}) copy-start(bf16[512,512]{1,0:T(8,128)(2,1)S(1)} %collective-permute-done.9.refs_4_.refs_6_) | copy-start | bytes 1572868
  144.7 6.6 %copy-start.15 = (bf16[512,512]{1,0:T(8,128)(2,1)}, bf16[512,512]{1,0:T(8,128)(2,1)S(1)}, u32[]{:S(2)}) copy-start(bf16[512,512]{1,0:T(8,128)(2,1)S(1)} %collective-permute-done.10.refs_8_.refs_7_) | copy-start | bytes 1572868
  153.4 42.8 %copy-start.10 = (bf16[512,512]{1,0:T(8,128)(2,1)S(1)}, bf16[512,512]{1,0:T(8,128)(2,1)}, u32[]{:S(2)}) copy-start(bf16[512,512]{1,0:T(8,128)(2,1)} %pack.14.refs_7_.refs_2_) | copy-start | bytes 1572868
  153.4 36.3 %collective-permute-start.13 = (bf16[512,768]{1,0:T(8,128)(2,1)S(1)}, bf16[512,768]{1,0:T(8,128)(2,1)}, u32[]{:S(2)}, u32[]{:S(2)}) collective-permute-start(bf16[512,768]{1,0:T(8,128)(2,1)S(1)} %copy-done.3), channel_id=1, source_target_pairs={{0,12},{4,0},{8,4},{12,8},{1,13},{5,1},{9,5},{13,9},{2,14},{6,2},{... | collective-permute-start | bytes 2359304 | tf_op jit(solution)/shard_map/ppermute | solution.py:263
  156.0 35.3 %collective-permute-start.11 = (bf16[512,768]{1,0:T(8,128)(2,1)S(1)}, bf16[512,768]{1,0:T(8,128)(2,1)}, u32[]{:S(2)}, u32[]{:S(2)}) collective-permute-start(bf16[512,768]{1,0:T(8,128)(2,1)S(1)} %copy-done.2), channel_id=1, source_target_pairs={{0,4},{4,8},{8,12},{12,0},{1,5},{5,9},{9,13},{13,1},{2,6},{6,10},{... | collective-permute-start | bytes 2359304 | tf_op jit(solution)/shard_map/ppermute | solution.py:263
  189.7 32.3 %collective-permute-start.14 = (bf16[512,768]{1,0:T(8,128)(2,1)}, bf16[512,768]{1,0:T(8,128)(2,1)}, u32[]{:S(2)}, u32[]{:S(2)}) collective-permute-start(bf16[512,768]{1,0:T(8,128)(2,1)} %collective-permute-done.13.refs_10_), channel_id=1, source_target_pairs={{0,16},{16,0},{1,17},{17,1},{2,18},{18,2},{3,19},{19,3},{4,20},{20... | collective-permute-start | bytes 2359304 | tf_op jit(solution)/shard_map/ppermute | solution.py:267
  191.2 36.2 %collective-permute-start.12 = (bf16[512,768]{1,0:T(8,128)(2,1)}, bf16[512,768]{1,0:T(8,128)(2,1)}, u32[]{:S(2)}, u32[]{:S(2)}) collective-permute-start(bf16[512,768]{1,0:T(8,128)(2,1)} %collective-permute-done.11.refs_8_), channel_id=1, source_target_pairs={{0,16},{16,0},{1,17},{17,1},{2,18},{18,2},{3,19},{19,3},{4,20},{20... | collective-permute-start | bytes 2359304 | tf_op jit(solution)/shard_map/ppermute | solution.py:267
  194.0 13.6 %collective-permute-start.20 = (bf16[512,512]{1,0:T(8,128)(2,1)}, bf16[512,512]{1,0:T(8,128)(2,1)S(1)}, u32[]{:S(2)}, u32[]{:S(2)}) collective-permute-start(bf16[512,512]{1,0:T(8,128)(2,1)} %pack.15.refs_2_), channel_id=1, source_target_pairs={{0,12},{4,0},{8,4},{12,8},{1,13},{5,1},{9,5},{13,9},{2,14},{6,2},{... | collective-permute-start | bytes 1572872 | tf_op jit(solution)/shard_map/ppermute | solution.py:263
  196.3 24.3 %collective-permute-start.18 = (bf16[512,512]{1,0:T(8,128)(2,1)S(1)}, bf16[512,512]{1,0:T(8,128)(2,1)S(1)}, u32[]{:S(2)}, u32[]{:S(2)}) collective-permute-start(bf16[512,512]{1,0:T(8,128)(2,1)S(1)} %copy-done.10), channel_id=1, source_target_pairs={{0,4},{4,8},{8,12},{12,0},{1,5},{5,9},{9,13},{13,1},{2,6},{6,10},{... | collective-permute-start | bytes 1572872 | tf_op jit(solution)/shard_map/ppermute | solution.py:263
  198.2 22.4 %copy-start.14 = (bf16[512,512]{1,0:T(8,128)(2,1)S(1)}, bf16[512,512]{1,0:T(8,128)(2,1)}, u32[]{:S(2)}) copy-start(bf16[512,512]{1,0:T(8,128)(2,1)} %copy-done.13) | copy-start | bytes 1572868
  198.2 48.6 %collective-permute-start.26 = (bf16[512,512]{1,0:T(8,128)(2,1)}, bf16[512,512]{1,0:T(8,128)(2,1)S(1)}, u32[]{:S(2)}, u32[]{:S(2)}) collective-permute-start(bf16[512,512]{1,0:T(8,128)(2,1)} %pack.16.refs_2_), channel_id=1, source_target_pairs={{0,4},{4,8},{8,12},{12,0},{1,5},{5,9},{9,13},{13,1},{2,6},{6,10},{... | collective-permute-start | bytes 1572872 | tf_op jit(solution)/shard_map/ppermute | solution.py:263
  207.6 37.9 %copy-start.22 = (bf16[512,512]{1,0:T(8,128)(2,1)}, bf16[512,512]{1,0:T(8,128)(2,1)S(1)}, u32[]{:S(2)}) copy-start(bf16[512,512]{1,0:T(8,128)(2,1)S(1)} %collective-permute-done.20.refs_10_) | copy-start | bytes 1572868
  207.6 37.9 %collective-permute-start.28 = (bf16[512,512]{1,0:T(8,128)(2,1)}, bf16[512,512]{1,0:T(8,128)(2,1)S(1)}, u32[]{:S(2)}, u32[]{:S(2)}) collective-permute-start(bf16[512,512]{1,0:T(8,128)(2,1)} %pack.17), channel_id=1, source_target_pairs={{0,12},{4,0},{8,4},{12,8},{1,13},{5,1},{9,5},{13,9},{2,14},{6,2},{... | collective-permute-start | bytes 1572872 | tf_op jit(solution)/shard_map/ppermute | solution.py:263
  220.6 24.9 %copy-start.23 = (bf16[512,512]{1,0:T(8,128)(2,1)}, bf16[512,512]{1,0:T(8,128)(2,1)S(1)}, u32[]{:S(2)}) copy-start(bf16[512,512]{1,0:T(8,128)(2,1)S(1)} %collective-permute-done.18.refs_8_) | copy-start | bytes 1572868
  220.6 40.5 %collective-permute-start.25 = (bf16[512,512]{1,0:T(8,128)(2,1)S(1)}, bf16[512,512]{1,0:T(8,128)(2,1)S(1)}, u32[]{:S(2)}, u32[]{:S(2)}) collective-permute-start(bf16[512,512]{1,0:T(8,128)(2,1)S(1)} %copy-done.14), channel_id=1, source_target_pairs={{0,16},{16,0},{1,17},{17,1},{2,18},{18,2},{3,19},{19,3},{4,20},{20... | collective-permute-start | bytes 1572872 | tf_op jit(solution)/shard_map/ppermute | solution.py:267
  222.0 27.8 %collective-permute-start.21 = (bf16[512,512]{1,0:T(8,128)(2,1)S(1)}, bf16[512,512]{1,0:T(8,128)(2,1)}, u32[]{:S(2)}, u32[]{:S(2)}) collective-permute-start(bf16[512,512]{1,0:T(8,128)(2,1)S(1)} %collective-permute-done.20.refs_10_), channel_id=1, source_target_pairs={{0,16},{16,0},{1,17},{17,1},{2,18},{18,2},{3,19},{19,3},{4,20},{20... | collective-permute-start | bytes 1572872 | tf_op jit(solution)/shard_map/ppermute | solution.py:267
  227.4 33.7 %collective-permute-start.19 = (bf16[512,512]{1,0:T(8,128)(2,1)S(1)}, bf16[512,512]{1,0:T(8,128)(2,1)}, u32[]{:S(2)}, u32[]{:S(2)}) collective-permute-start(bf16[512,512]{1,0:T(8,128)(2,1)S(1)} %collective-permute-done.18.refs_8_), channel_id=1, source_target_pairs={{0,16},{16,0},{1,17},{17,1},{2,18},{18,2},{3,19},{19,3},{4,20},{20... | collective-permute-start | bytes 1572872 | tf_op jit(solution)/shard_map/ppermute | solution.py:267
  245.5 0.8 copy-start.17
  246.3 42.2 %collective-permute-start.29 = (bf16[512,512]{1,0:T(8,128)(2,1)}, bf16[512,512]{1,0:T(8,128)(2,1)S(1)}, u32[]{:S(2)}, u32[]{:S(2)}) collective-permute-start(bf16[512,512]{1,0:T(8,128)(2,1)} %hold.11.refs_10_), channel_id=1, source_target_pairs={{0,16},{16,0},{1,17},{17,1},{2,18},{18,2},{3,19},{19,3},{4,20},{20... | collective-permute-start | bytes 1572872 | tf_op jit(solution)/shard_map/ppermute | solution.py:267
  246.8 0.8 copy-start.16
  247.6 40.9 %collective-permute-start.27 = (bf16[512,512]{1,0:T(8,128)(2,1)}, bf16[512,512]{1,0:T(8,128)(2,1)}, u32[]{:S(2)}, u32[]{:S(2)}) collective-permute-start(bf16[512,512]{1,0:T(8,128)(2,1)} %hold.10.refs_8_), channel_id=1, source_target_pairs={{0,16},{16,0},{1,17},{17,1},{2,18},{18,2},{3,19},{19,3},{4,20},{20... | collective-permute-start | bytes 1572872 | tf_op jit(solution)/shard_map/ppermute | solution.py:267
  249.9 25.6 %collective-permute-start.15 = (bf16[384,384]{1,0:T(8,128)(2,1)}, bf16[384,384]{1,0:T(8,128)(2,1)S(1)}, u32[]{:S(2)}, u32[]{:S(2)}) collective-permute-start(bf16[384,384]{1,0:T(8,128)(2,1)} %get-tuple-element.18), channel_id=1, source_target_pairs={{0,4},{4,8},{8,12},{12,0},{1,5},{5,9},{9,13},{13,1},{2,6},{6,10},{... | collective-permute-start | bytes 884744 | tf_op jit(solution)/shard_map/ppermute | solution.py:274
  261.1 20.5 %collective-permute-start.16 = (bf16[384,384]{1,0:T(8,128)(2,1)}, bf16[384,384]{1,0:T(8,128)(2,1)S(1)}, u32[]{:S(2)}, u32[]{:S(2)}) collective-permute-start(bf16[384,384]{1,0:T(8,128)(2,1)} %get-tuple-element.19), channel_id=1, source_target_pairs={{0,8},{4,12},{8,0},{12,4},{1,9},{5,13},{9,1},{13,5},{2,10},{6,14},... | collective-permute-start | bytes 884744 | tf_op jit(solution)/shard_map/ppermute | solution.py:274
  261.1 14.4 %copy-start.21 = (bf16[512,512]{1,0:T(8,128)(2,1)}, bf16[512,512]{1,0:T(8,128)(2,1)S(1)}, u32[]{:S(2)}) copy-start(bf16[512,512]{1,0:T(8,128)(2,1)S(1)} %collective-permute-done.25.refs_7_) | copy-start | bytes 1572868
  261.1 27.4 %collective-permute-start.17 = (bf16[384,384]{1,0:T(8,128)(2,1)}, bf16[384,384]{1,0:T(8,128)(2,1)S(1)}, u32[]{:S(2)}, u32[]{:S(2)}) collective-permute-start(bf16[384,384]{1,0:T(8,128)(2,1)} %get-tuple-element.20), channel_id=1, source_target_pairs={{0,12},{4,0},{8,4},{12,8},{1,13},{5,1},{9,5},{13,9},{2,14},{6,2},{... | collective-permute-start | bytes 884744 | tf_op jit(solution)/shard_map/ppermute | solution.py:274
  275.5 13.1 %copy-start.18 = (bf16[384,384]{1,0:T(8,128)(2,1)}, bf16[384,384]{1,0:T(8,128)(2,1)S(1)}, u32[]{:S(2)}) copy-start(bf16[384,384]{1,0:T(8,128)(2,1)S(1)} %collective-permute-done.15.refs_1_.refs_13_) | copy-start | bytes 884740
  275.5 29.7 %collective-permute-start.22 = (bf16[384,256]{1,0:T(8,128)(2,1)}, bf16[384,256]{1,0:T(8,128)(2,1)S(1)}, u32[]{:S(2)}, u32[]{:S(2)}) collective-permute-start(bf16[384,256]{1,0:T(8,128)(2,1)} %get-tuple-element.22), channel_id=1, source_target_pairs={{0,4},{4,8},{8,12},{12,0},{1,5},{5,9},{9,13},{13,1},{2,6},{6,10},{... | collective-permute-start | bytes 589832 | tf_op jit(solution)/shard_map/ppermute | solution.py:274
  281.6 6.9 %copy-start.19 = (bf16[384,384]{1,0:T(8,128)(2,1)}, bf16[384,384]{1,0:T(8,128)(2,1)S(1)}, u32[]{:S(2)}) copy-start(bf16[384,384]{1,0:T(8,128)(2,1)S(1)} %collective-permute-done.16.refs_2_.refs_14_) | copy-start | bytes 884740
  281.6 23.6 %collective-permute-start.23 = (bf16[384,256]{1,0:T(8,128)(2,1)}, bf16[384,256]{1,0:T(8,128)(2,1)S(1)}, u32[]{:S(2)}, u32[]{:S(2)}) collective-permute-start(bf16[384,256]{1,0:T(8,128)(2,1)} %get-tuple-element.23), channel_id=1, source_target_pairs={{0,8},{4,12},{8,0},{12,4},{1,9},{5,13},{9,1},{13,5},{2,10},{6,14},... | collective-permute-start | bytes 589832 | tf_op jit(solution)/shard_map/ppermute | solution.py:274
  288.5 0.7 copy-start.20
  288.5 16.7 %collective-permute-start.24 = (bf16[384,256]{1,0:T(8,128)(2,1)}, bf16[384,256]{1,0:T(8,128)(2,1)S(1)}, u32[]{:S(2)}, u32[]{:S(2)}) collective-permute-start(bf16[384,256]{1,0:T(8,128)(2,1)} %get-tuple-element.24), channel_id=1, source_target_pairs={{0,12},{4,0},{8,4},{12,8},{1,13},{5,1},{9,5},{13,9},{2,14},{6,2},{... | collective-permute-start | bytes 589832 | tf_op jit(solution)/shard_map/ppermute | solution.py:274
  288.5 0.9 copy-start.24
  301.2 10.2 %collective-permute-start.30 = (bf16[384,256]{1,0:T(8,128)(2,1)}, bf16[384,256]{1,0:T(8,128)(2,1)S(1)}, u32[]{:S(2)}, u32[]{:S(2)}) collective-permute-start(bf16[384,256]{1,0:T(8,128)(2,1)} %get-tuple-element.26), channel_id=1, source_target_pairs={{0,4},{4,8},{8,12},{12,0},{1,5},{5,9},{9,13},{13,1},{2,6},{6,10},{... | collective-permute-start | bytes 589832 | tf_op jit(solution)/shard_map/ppermute | solution.py:274
  303.2 10.3 %collective-permute-start.31 = (bf16[384,256]{1,0:T(8,128)(2,1)}, bf16[384,256]{1,0:T(8,128)(2,1)S(1)}, u32[]{:S(2)}, u32[]{:S(2)}) collective-permute-start(bf16[384,256]{1,0:T(8,128)(2,1)} %get-tuple-element.27), channel_id=1, source_target_pairs={{0,8},{4,12},{8,0},{12,4},{1,9},{5,13},{9,1},{13,5},{2,10},{6,14},... | collective-permute-start | bytes 589832 | tf_op jit(solution)/shard_map/ppermute | solution.py:274
  305.2 9.7 %collective-permute-start.32 = (bf16[384,256]{1,0:T(8,128)(2,1)}, bf16[384,256]{1,0:T(8,128)(2,1)S(1)}, u32[]{:S(2)}, u32[]{:S(2)}) collective-permute-start(bf16[384,256]{1,0:T(8,128)(2,1)} %get-tuple-element.28), channel_id=1, source_target_pairs={{0,12},{4,0},{8,4},{12,8},{1,13},{5,1},{9,5},{13,9},{2,14},{6,2},{... | collective-permute-start | bytes 589832 | tf_op jit(solution)/shard_map/ppermute | solution.py:274
  311.4 3.5 %copy-start.28 = (bf16[384,256]{1,0:T(8,128)(2,1)}, bf16[384,256]{1,0:T(8,128)(2,1)S(1)}, u32[]{:S(2)}) copy-start(bf16[384,256]{1,0:T(8,128)(2,1)S(1)} %collective-permute-done.30.refs_2_) | copy-start | bytes 589828
  313.5 1.4 copy-start.29
  (4 other events, 2.7 us)
Sparse Core Ops, SparseCore 0:
  8.9 29.6 all-gather.4
  67.0 29.4 all-gather.6
  113.8 32.8 all-gather.8
  153.5 28.6 all-gather.10

commit v13 on v10

--- a/solution.py
+++ b/solution.py
@@ -152,49 +152,6 @@
     )(tokens, gate_weight, up_weight, *[value for *_, value in held], *after)
 
 
-def ordered(lower, upper, after):
-    rows = lax.axis_size("row")
-    mine, near = lower[0].shape
-
-    def body(*refs):
-        lower_refs, upper_refs = refs[:rows], refs[rows:2 * rows - 1]
-        out, slots, sems = refs[-3:]
-        z = lax.axis_index("row")
-        for here in range(rows):
-
-            @pl.when(z == here)
-            def _(here=here):
-                loads, stores = [], []
-                for row in range(rows):
-                    source = lower_refs[here - row] if row <= here else upper_refs[row - here - 1]
-                    loads.append(pltpu.make_async_copy(source, slots.at[row], sems.at[0, row]))
-                    stores.append(pltpu.make_async_copy(
-                        slots.at[row], out.at[pl.ds(row * mine, mine), :], sems.at[1, row]
-                    ))
-                for load in loads:
-                    load.start()
-                for load, store in zip(loads, stores):
-                    load.wait()
-                    store.start()
-                for store in stores:
-                    store.wait()
-
-    values = lower + upper[1:] + after
-    return pl.pallas_call(
-        body,
-        out_shape=jax.ShapeDtypeStruct((rows * mine, near), lower[0].dtype),
-        in_specs=[ANY] * len(values),
-        out_specs=ANY,
-        scratch_shapes=[
-            pltpu.VMEM((rows, mine, near), lower[0].dtype),
-            pltpu.SemaphoreType.DMA((2, rows)),
-        ],
-        compiler_params=pltpu.CompilerParams(vmem_limit_bytes=GRANT),
-        cost_estimate=pl.CostEstimate(flops=0, bytes_accessed=4 * rows * mine * near, transcendentals=0),
-        name="ordered",
-    )(*values)
-
-
 def place(blocks, mine, ff, onto=None):
     rows = lax.axis_size("row")
     width = ff // rows
@@ -240,10 +197,7 @@
     width = ff // rows
     units = width // LANES
 
-    lower, upper = [tokens], [tokens]
-    for step in range(1, rows):
-        lower.append(lax.ppermute(lower[-1], "row", [(i, i + 1) for i in range(step - 1, rows - 1)]))
-        upper.append(lax.ppermute(upper[-1], "row", [(i, i - 1) for i in range(1, rows - step + 1)]))
+    block_rows = lax.all_gather(tokens, "row", axis=0, tiled=True)
 
     edges = [0]
     for piece in range(len(PIECES)):
@@ -285,7 +239,7 @@
             hidden_of(0, [])
         weights(*step)
         if len(sent) == min(3, len(plan)):
-            whole = lax.all_gather(ordered(lower, upper, arrived[:1] + sent[1:3]), "col", axis=1, tiled=True)
+            whole = lax.all_gather(hold(block_rows, arrived[:1] + sent[1:3]), "col", axis=1, tiled=True)
     for n in range(min(last, 1), last + 1):
         hidden_of(n, done[-1:] + (returned[n - 2] if n > 1 else []))
     early = len(blocks) - rows if last else len(blocks)

time: 311 us -> 307 us (0.987)
  waiting for transfers between devices: 174 us -> 167 us
  starting transfers between devices: 49.1 us -> 54.6 us
    ppermute x6 -> x0, waiting for transfers between devices: 79.8 us -> none  [the longest x3 56.7 us: in_tiles(): lax.ppermute(lower[-1], 'row', [(i, i + 1) for i in range(step - 1, rows...]
    ppermute x8, waiting for transfers between devices: 71.2 us -> 149 us  [weights(): arrived.append(lax.ppermute(sent[-1], 'row', around(rows, shift)))]
    ppermute x8, starting transfers between devices: 9.05 us -> 24.4 us  [weights(): arrived.append(lax.ppermute(sent[-1], 'row', around(rows, shift)))]
    ppermute x6 -> x0, starting transfers between devices: 13.5 us -> none  [the longest x3 7.69 us: in_tiles(): lax.ppermute(lower[-1], 'row', [(i, i + 1) for i in range(step - 1, rows...]
    ppermute x8, waiting for transfers between devices: 6.31 us -> 0.02 us  [weights(): swapped.append(lax.ppermute(came, 'parts', around(parts, -turn)))]
    ppermute x9, starting transfers between devices: 17.4 us -> 20.9 us  [hidden_of(): lax.ppermute(outs[shift], 'row', around(rows, shift))]
    unnamed x58 -> x48, local copies, waits for them, and re-layouts: 8.61 us -> 8.78 us
  transfers between devices with their start and end apart: 32 -> 27, of which waited for: 15 -> 9; matrix products, arithmetic and copies ran while one was open for 0% -> 0% of each run, Pallas kernels for 19% -> 19%
where the time goes in v13:
time: 307 us; the launch traced here: 306 us
  waiting for transfers between devices  167 us (54%)
  Pallas kernels  61.7 us (20%)
  starting transfers between devices  54.6 us (18%)
  between operations  13.7 us (4%)
  local copies, waits for them, and re-layouts  8.78 us (3%)
    ppermute x8, waiting for transfers between devices, weights(): arrived.append(lax.ppermute(sent[-1], 'row', around(rows, shift)))  149 us
    pallas_call x3, Pallas kernels, product(): pl.pallas_call(body, out_shape=[jax.ShapeDtypeStruct((mine, wide), jnp.bf...  40.6 us
    ppermute x8, starting transfers between devices, weights(): arrived.append(lax.ppermute(sent[-1], 'row', around(rows, shift)))  24.4 us
    ppermute x9, starting transfers between devices, hidden_of(): lax.ppermute(outs[shift], 'row', around(rows, shift))  20.9 us
    ppermute x9, waiting for transfers between devices, hidden_of(): lax.ppermute(outs[shift], 'row', around(rows, shift))  17.8 us
    pallas_call x8, Pallas kernels, pack(): pl.pallas_call(body, out_shape=jax.ShapeDtypeStruct((share, 2 * wide), ga...  16.7 us
    ppermute x8, starting transfers between devices, weights(): swapped.append(lax.ppermute(came, 'parts', around(parts, -turn)))  9.24 us
    unnamed x48, local copies, waits for them, and re-layouts  8.78 us
  transfers between devices with their start and end apart: 27, of which 9 were waited for; matrix products, arithmetic and copies ran while one was open for 0% of the time, Pallas kernels for 19%

profile of v13, /device:TPU:12, one launch (start us, length us, event | category | flops | bytes accessed | tf_op | source)
XLA Modules:
  0.0 306.2 jit_solution(3492147513341736376)
XLA Ops:
  6.5 0.7 all-gather.3.cloned.1.call-update
  7.3 0.0 all-gather.5.cloned.1.call-start
  7.3 2.6 pack.8.refs_2_
  9.9 2.7 collective-permute-start
  12.5 2.2 pack.9.refs_2_
  14.7 2.2 pack.10.refs_3_.refs_2_
  16.9 102.5 %collective-permute-done.refs_1_.refs_0_.refs_3_ = bf16[512,1280]{1,0:T(8,128)(2,1)S(1)} collective-permute-done((bf16[512,1280]{1,0:T(8,128)(2,1)}, bf16[512,1280]{1,0:T(8,128)(2,1)S(1)}, u32[]{:S(2)}, u32[]{:S(2)}) %collective-permute-start) | collective-permute-done | bytes 1310752 | tf_op jit(solution)/shard_map/ppermute | solution.py:212
  119.5 1.1 copy-done
  120.5 0.0 all-gather.5.cloned.1.call-update
  120.5 1.3 copy-done.1
  121.8 0.5 collective-permute-start.1
  122.3 0.0 collective-permute-start.2
  122.3 2.0 collective-permute-start.4
  124.4 1.9 pack.11.refs_2_
  126.3 3.3 %collective-permute-start.16 = (bf16[512,512]{1,0:T(8,128)(2,1)}, bf16[512,512]{1,0:T(8,128)(2,1)S(1)}, u32[]{:S(2)}, u32[]{:S(2)}) collective-permute-start(bf16[512,512]{1,0:T(8,128)(2,1)} %pack.11.refs_2_), channel_id=1, source_target_pairs={{0,8},{4,12},{8,0},{12,4},{1,9},{5,13},{9,1},{13,5},{2,10},{6,14},... | collective-permute-start | bytes 1572872 | tf_op jit(solution)/shard_map/ppermute | solution.py:212
  129.7 13.2 %collective-permute-done.2.refs_2_.refs_3_ = bf16[512,768]{1,0:T(8,128)(2,1)} collective-permute-done((bf16[512,768]{1,0:T(8,128)(2,1)S(1)}, bf16[512,768]{1,0:T(8,128)(2,1)}, u32[]{:S(2)}, u32[]{:S(2)}) %collective-permute-start.2) | collective-permute-done | bytes 786464 | tf_op jit(solution)/shard_map/ppermute | solution.py:212
  142.9 1.5 collective-permute-start.3
  144.4 17.0 %collective-permute-done.4.refs_4_.refs_3_ = bf16[512,768]{1,0:T(8,128)(2,1)} collective-permute-done((bf16[512,768]{1,0:T(8,128)(2,1)S(1)}, bf16[512,768]{1,0:T(8,128)(2,1)}, u32[]{:S(2)}, u32[]{:S(2)}) %collective-permute-start.4) | collective-permute-done | bytes 786464 | tf_op jit(solution)/shard_map/ppermute | solution.py:212
  161.4 1.6 collective-permute-start.5
  163.0 15.8 %collective-permute-done.16.refs_3_.refs_0_ = bf16[512,512]{1,0:T(8,128)(2,1)S(1)} collective-permute-done((bf16[512,512]{1,0:T(8,128)(2,1)}, bf16[512,512]{1,0:T(8,128)(2,1)S(1)}, u32[]{:S(2)}, u32[]{:S(2)}) %collective-permute-start.16) | collective-permute-done | bytes 524320 | tf_op jit(solution)/shard_map/ppermute | solution.py:212
  178.8 1.5 collective-permute-start.17
  180.3 0.0 collective-permute-done.1.refs_1_.refs_4_
  180.3 2.0 pack.12.refs_2_
  182.3 3.3 %collective-permute-start.9 = (bf16[512,512]{1,0:T(8,128)(2,1)}, bf16[512,512]{1,0:T(8,128)(2,1)S(1)}, u32[]{:S(2)}, u32[]{:S(2)}) collective-permute-start(bf16[512,512]{1,0:T(8,128)(2,1)} %pack.12.refs_2_), channel_id=1, source_target_pairs={{0,4},{4,8},{8,12},{12,0},{1,5},{5,9},{9,13},{13,1},{2,6},{6,10},{... | collective-permute-start | bytes 1572872 | tf_op jit(solution)/shard_map/ppermute | solution.py:212
  185.6 0.9 copy-done.13
  186.5 2.0 pack.13.refs_2_
  188.5 1.8 collective-permute-start.11
  190.3 1.9 pack.14.refs_2_
  192.3 8.4 %collective-permute-start.18 = (bf16[512,512]{1,0:T(8,128)(2,1)}, bf16[512,512]{1,0:T(8,128)(2,1)S(1)}, u32[]{:S(2)}, u32[]{:S(2)}) collective-permute-start(bf16[512,512]{1,0:T(8,128)(2,1)} %pack.14.refs_2_), channel_id=1, source_target_pairs={{0,4},{4,8},{8,12},{12,0},{1,5},{5,9},{9,13},{13,1},{2,6},{6,10},{... | collective-permute-start | bytes 1572872 | tf_op jit(solution)/shard_map/ppermute | solution.py:212
  200.6 0.0 collective-permute-done.17.refs_4_.refs_1_
  200.7 0.8 copy-done.5
  201.5 0.8 copy-done.6
  202.3 2.0 pack.15
  204.2 2.9 collective-permute-start.20
  207.1 0.5 collective-permute-start.10
  207.6 16.7 %product.3 = (bf16[384,384]{1,0:T(8,128)(2,1)}, bf16[384,384]{1,0:T(8,128)(2,1)}, bf16[384,384]{1,0:T(8,128)(2,1)}, bf16[384,384]{1,0:T(8,128)(2,1)}) custom-call(bf16[1536,4096]{1,0:T(8,128)(2,1)} %all-gather.5.cloned.1.call-done.tokens_ref, bf16[1024,3584]{1,0:T(8,128)(2,1)} %gate_ref.5, bf16[1024,3584]{1,0:T(8,128)(2,1)} %up_ref.5, ...), custom_call_target="tpu_custom_call" | custom-call | flops 9663676416 | bytes 20054016 | tf_op jit(solution)/shard_map/product/pallas_call | solution.py:136
  224.3 0.8 copy-done.9
  225.1 1.5 collective-permute-start.12
  226.6 3.3 %collective-permute-start.6 = (bf16[384,384]{1,0:T(8,128)(2,1)}, bf16[384,384]{1,0:T(8,128)(2,1)S(1)}, u32[]{:S(2)}, u32[]{:S(2)}) collective-permute-start(bf16[384,384]{1,0:T(8,128)(2,1)} %get-tuple-element.18), channel_id=1, source_target_pairs={{0,4},{4,8},{8,12},{12,0},{1,5},{5,9},{9,13},{13,1},{2,6},{6,10},{... | collective-permute-start | bytes 884744 | tf_op jit(solution)/shard_map/ppermute | solution.py:223
  229.9 6.3 %collective-permute-start.7 = (bf16[384,384]{1,0:T(8,128)(2,1)}, bf16[384,384]{1,0:T(8,128)(2,1)S(1)}, u32[]{:S(2)}, u32[]{:S(2)}) collective-permute-start(bf16[384,384]{1,0:T(8,128)(2,1)} %get-tuple-element.19), channel_id=1, source_target_pairs={{0,8},{4,12},{8,0},{12,4},{1,9},{5,13},{9,1},{13,5},{2,10},{6,14},... | collective-permute-start | bytes 884744 | tf_op jit(solution)/shard_map/ppermute | solution.py:223
  236.2 0.4 collective-permute-done.20.refs_0_
  236.6 1.8 collective-permute-start.8
  238.4 0.1 collective-permute-start.19
  238.5 1.9 collective-permute-start.21
  240.5 12.0 %product.4 = (bf16[384,256]{1,0:T(8,128)(2,1)}, bf16[384,256]{1,0:T(8,128)(2,1)}, bf16[384,256]{1,0:T(8,128)(2,1)}, bf16[384,256]{1,0:T(8,128)(2,1)}) custom-call(bf16[1536,4096]{1,0:T(8,128)(2,1)} %all-gather.5.cloned.1.call-done.tokens_ref, bf16[1024,3584]{1,0:T(8,128)(2,1)} %gate_ref.5, bf16[1024,3584]{1,0:T(8,128)(2,1)} %up_ref.5, ...), custom_call_target="tpu_custom_call" | custom-call | flops 6442450944 | bytes 17563648 | tf_op jit(solution)/shard_map/product/pallas_call | solution.py:136
  252.5 0.5 collective-permute-start.13
  253.0 6.8 %collective-permute-done.7.refs_2_.refs_8_ = bf16[384,384]{1,0:T(8,128)(2,1)S(1)} collective-permute-done((bf16[384,384]{1,0:T(8,128)(2,1)}, bf16[384,384]{1,0:T(8,128)(2,1)S(1)}, u32[]{:S(2)}, u32[]{:S(2)}) %collective-permute-start.7) | collective-permute-done | bytes 294944 | tf_op jit(solution)/shard_map/ppermute | solution.py:223
  259.8 3.3 %collective-permute-start.14 = (bf16[384,256]{1,0:T(8,128)(2,1)}, bf16[384,256]{1,0:T(8,128)(2,1)S(1)}, u32[]{:S(2)}, u32[]{:S(2)}) collective-permute-start(bf16[384,256]{1,0:T(8,128)(2,1)} %get-tuple-element.23), channel_id=1, source_target_pairs={{0,8},{4,12},{8,0},{12,4},{1,9},{5,13},{9,1},{13,5},{2,10},{6,14},... | collective-permute-start | bytes 589832 | tf_op jit(solution)/shard_map/ppermute | solution.py:223
  263.1 0.0 copy-start.15
  263.2 0.6 copy-done.12
  263.8 0.2 copy-done.15
  264.0 0.2 copy-done.16
  264.2 12.0 %product.5 = (bf16[384,256]{1,0:T(8,128)(2,1)}, bf16[384,256]{1,0:T(8,128)(2,1)}, bf16[384,256]{1,0:T(8,128)(2,1)}, bf16[384,256]{1,0:T(8,128)(2,1)}) custom-call(bf16[1536,4096]{1,0:T(8,128)(2,1)} %all-gather.5.cloned.1.call-done.tokens_ref, bf16[1024,3584]{1,0:T(8,128)(2,1)} %gate_ref.5, bf16[1024,3584]{1,0:T(8,128)(2,1)} %up_ref.5, ...), custom_call_target="tpu_custom_call" | custom-call | flops 6442450944 | bytes 17563648 | tf_op jit(solution)/shard_map/product/pallas_call | solution.py:136
  276.1 2.0 collective-permute-start.22
  278.1 3.8 %collective-permute-start.23 = (bf16[384,256]{1,0:T(8,128)(2,1)}, bf16[384,256]{1,0:T(8,128)(2,1)S(1)}, u32[]{:S(2)}, u32[]{:S(2)}) collective-permute-start(bf16[384,256]{1,0:T(8,128)(2,1)} %get-tuple-element.27), channel_id=1, source_target_pairs={{0,8},{4,12},{8,0},{12,4},{1,9},{5,13},{9,1},{13,5},{2,10},{6,14},... | collective-permute-start | bytes 589832 | tf_op jit(solution)/shard_map/ppermute | solution.py:223
  282.0 0.6 copy-done.18
  282.6 0.1 copy-done.19
  282.7 0.7 copy-done.20
  283.4 2.4 place.2.refs_0_
  285.7 6.5 %collective-permute-done.22.refs_2_ = bf16[384,256]{1,0:T(8,128)(2,1)S(1)} collective-permute-done((bf16[384,256]{1,0:T(8,128)(2,1)}, bf16[384,256]{1,0:T(8,128)(2,1)S(1)}, u32[]{:S(2)}, u32[]{:S(2)}) %collective-permute-start.22) | collective-permute-done | bytes 196640 | tf_op jit(solution)/shard_map/ppermute | solution.py:223
  292.2 2.5 collective-permute-done.23.refs_3_
  294.7 2.0 collective-permute-done.24.refs_4_
  296.7 0.7 copy-done.23
  297.4 2.0 place.3
  (57 shorter events, 0.1 us)
Async XLA Ops:
  6.5 112.9 %all-gather.3.cloned.1.call-start = ((), (), s32[]{:S(2)}) async-start(), calls=%async_computation | async-start | bytes 3932160 | tf_op jit(solution)/shard_map/all_gather | solution.py:200
  7.3 200.4 %all-gather.5.cloned.1.call-start = ((), (), s32[]{:S(2)}) async-start(), calls=%async_computation.1 | async-start | bytes 15728640 | tf_op jit(solution)/shard_map/all_gather | solution.py:242
  9.9 109.6 %collective-permute-start = (bf16[512,1280]{1,0:T(8,128)(2,1)}, bf16[512,1280]{1,0:T(8,128)(2,1)S(1)}, u32[]{:S(2)}, u32[]{:S(2)}) collective-permute-start(bf16[512,1280]{1,0:T(8,128)(2,1)} %pack.8.refs_2_), channel_id=1, source_target_pairs={{0,8},{4,12},{8,0},{12,4},{1,9},{5,13},{9,1},{13,5},{2,10},{6,14},... | collective-permute-start | bytes 3932168 | tf_op jit(solution)/shard_map/ppermute | solution.py:212
  119.5 1.1 copy-start
  120.5 1.3 copy-start.1
  120.5 1.8 copy-start.3
  120.5 1.8 copy-start.2
  121.8 58.5 %collective-permute-start.1 = (bf16[512,1280]{1,0:T(8,128)(2,1)S(1)}, bf16[512,1280]{1,0:T(8,128)(2,1)}, u32[]{:S(2)}, u32[]{:S(2)}) collective-permute-start(bf16[512,1280]{1,0:T(8,128)(2,1)S(1)} %copy-done.1), channel_id=1, source_target_pairs={{0,16},{16,0},{1,17},{17,1},{2,18},{18,2},{3,19},{19,3},{4,20},{20... | collective-permute-start | bytes 3932168 | tf_op jit(solution)/shard_map/ppermute | solution.py:216
  122.3 20.6 %collective-permute-start.2 = (bf16[512,768]{1,0:T(8,128)(2,1)S(1)}, bf16[512,768]{1,0:T(8,128)(2,1)}, u32[]{:S(2)}, u32[]{:S(2)}) collective-permute-start(bf16[512,768]{1,0:T(8,128)(2,1)S(1)} %copy-done.3), channel_id=1, source_target_pairs={{0,4},{4,8},{8,12},{12,0},{1,5},{5,9},{9,13},{13,1},{2,6},{6,10},{... | collective-permute-start | bytes 2359304 | tf_op jit(solution)/shard_map/ppermute | solution.py:212
  122.3 39.0 %collective-permute-start.4 = (bf16[512,768]{1,0:T(8,128)(2,1)S(1)}, bf16[512,768]{1,0:T(8,128)(2,1)}, u32[]{:S(2)}, u32[]{:S(2)}) collective-permute-start(bf16[512,768]{1,0:T(8,128)(2,1)S(1)} %copy-done.2), channel_id=1, source_target_pairs={{0,12},{4,0},{8,4},{12,8},{1,13},{5,1},{9,5},{13,9},{2,14},{6,2},{... | collective-permute-start | bytes 2359304 | tf_op jit(solution)/shard_map/ppermute | solution.py:212
  126.3 52.4 %collective-permute-start.16 = (bf16[512,512]{1,0:T(8,128)(2,1)}, bf16[512,512]{1,0:T(8,128)(2,1)S(1)}, u32[]{:S(2)}, u32[]{:S(2)}) collective-permute-start(bf16[512,512]{1,0:T(8,128)(2,1)} %pack.11.refs_2_), channel_id=1, source_target_pairs={{0,8},{4,12},{8,0},{12,4},{1,9},{5,13},{9,1},{13,5},{2,10},{6,14},... | collective-permute-start | bytes 1572872 | tf_op jit(solution)/shard_map/ppermute | solution.py:212
  142.9 42.7 %collective-permute-start.3 = (bf16[512,768]{1,0:T(8,128)(2,1)}, bf16[512,768]{1,0:T(8,128)(2,1)S(1)}, u32[]{:S(2)}, u32[]{:S(2)}) collective-permute-start(bf16[512,768]{1,0:T(8,128)(2,1)} %collective-permute-done.2.refs_2_.refs_3_), channel_id=1, source_target_pairs={{0,16},{16,0},{1,17},{17,1},{2,18},{18,2},{3,19},{19,3},{4,20},{20... | collective-permute-start | bytes 2359304 | tf_op jit(solution)/shard_map/ppermute | solution.py:216
  161.4 28.9 %collective-permute-start.5 = (bf16[512,768]{1,0:T(8,128)(2,1)}, bf16[512,768]{1,0:T(8,128)(2,1)}, u32[]{:S(2)}, u32[]{:S(2)}) collective-permute-start(bf16[512,768]{1,0:T(8,128)(2,1)} %collective-permute-done.4.refs_4_.refs_3_), channel_id=1, source_target_pairs={{0,16},{16,0},{1,17},{17,1},{2,18},{18,2},{3,19},{19,3},{4,20},{20... | collective-permute-start | bytes 2359304 | tf_op jit(solution)/shard_map/ppermute | solution.py:216
  178.8 3.5 %copy-start.4 = (bf16[512,512]{1,0:T(8,128)(2,1)}, bf16[512,512]{1,0:T(8,128)(2,1)S(1)}, u32[]{:S(2)}) copy-start(bf16[512,512]{1,0:T(8,128)(2,1)S(1)} %collective-permute-done.16.refs_3_.refs_0_) | copy-start | bytes 1572868
  178.8 21.9 %collective-permute-start.17 = (bf16[512,512]{1,0:T(8,128)(2,1)S(1)}, bf16[512,512]{1,0:T(8,128)(2,1)S(1)}, u32[]{:S(2)}, u32[]{:S(2)}) collective-permute-start(bf16[512,512]{1,0:T(8,128)(2,1)S(1)} %collective-permute-done.16.refs_3_.refs_0_), channel_id=1, source_target_pairs={{0,16},{16,0},{1,17},{17,1},{2,18},{18,2},{3,19},{19,3},{4,20},{20... | collective-permute-start | bytes 1572872 | tf_op jit(solution)/shard_map/ppermute | solution.py:216
  182.3 18.4 %collective-permute-start.9 = (bf16[512,512]{1,0:T(8,128)(2,1)}, bf16[512,512]{1,0:T(8,128)(2,1)S(1)}, u32[]{:S(2)}, u32[]{:S(2)}) collective-permute-start(bf16[512,512]{1,0:T(8,128)(2,1)} %pack.12.refs_2_), channel_id=1, source_target_pairs={{0,4},{4,8},{8,12},{12,0},{1,5},{5,9},{9,13},{13,1},{2,6},{6,10},{... | collective-permute-start | bytes 1572872 | tf_op jit(solution)/shard_map/ppermute | solution.py:212
  185.6 0.9 copy-start.13
  188.5 35.8 %collective-permute-start.11 = (bf16[512,512]{1,0:T(8,128)(2,1)}, bf16[512,512]{1,0:T(8,128)(2,1)S(1)}, u32[]{:S(2)}, u32[]{:S(2)}) collective-permute-start(bf16[512,512]{1,0:T(8,128)(2,1)} %pack.13.refs_2_), channel_id=1, source_target_pairs={{0,12},{4,0},{8,4},{12,8},{1,13},{5,1},{9,5},{13,9},{2,14},{6,2},{... | collective-permute-start | bytes 1572872 | tf_op jit(solution)/shard_map/ppermute | solution.py:212
  192.3 37.7 %collective-permute-start.18 = (bf16[512,512]{1,0:T(8,128)(2,1)}, bf16[512,512]{1,0:T(8,128)(2,1)S(1)}, u32[]{:S(2)}, u32[]{:S(2)}) collective-permute-start(bf16[512,512]{1,0:T(8,128)(2,1)} %pack.14.refs_2_), channel_id=1, source_target_pairs={{0,4},{4,8},{8,12},{12,0},{1,5},{5,9},{9,13},{13,1},{2,6},{6,10},{... | collective-permute-start | bytes 1572872 | tf_op jit(solution)/shard_map/ppermute | solution.py:212
  200.6 0.8 copy-start.5
  201.4 0.8 copy-start.6
  204.2 32.3 %collective-permute-start.20 = (bf16[512,512]{1,0:T(8,128)(2,1)}, bf16[512,512]{1,0:T(8,128)(2,1)S(1)}, u32[]{:S(2)}, u32[]{:S(2)}) collective-permute-start(bf16[512,512]{1,0:T(8,128)(2,1)} %pack.15), channel_id=1, source_target_pairs={{0,12},{4,0},{8,4},{12,8},{1,13},{5,1},{9,5},{13,9},{2,14},{6,2},{... | collective-permute-start | bytes 1572872 | tf_op jit(solution)/shard_map/ppermute | solution.py:212
  207.1 31.2 %collective-permute-start.10 = (bf16[512,512]{1,0:T(8,128)(2,1)}, bf16[512,512]{1,0:T(8,128)(2,1)S(1)}, u32[]{:S(2)}, u32[]{:S(2)}) collective-permute-start(bf16[512,512]{1,0:T(8,128)(2,1)} %copy-done.6), channel_id=1, source_target_pairs={{0,16},{16,0},{1,17},{17,1},{2,18},{18,2},{3,19},{19,3},{4,20},{20... | collective-permute-start | bytes 1572872 | tf_op jit(solution)/shard_map/ppermute | solution.py:216
  224.3 0.8 copy-start.9
  225.1 13.4 %collective-permute-start.12 = (bf16[512,512]{1,0:T(8,128)(2,1)}, bf16[512,512]{1,0:T(8,128)(2,1)S(1)}, u32[]{:S(2)}, u32[]{:S(2)}) collective-permute-start(bf16[512,512]{1,0:T(8,128)(2,1)} %hold.5.refs_4_), channel_id=1, source_target_pairs={{0,16},{16,0},{1,17},{17,1},{2,18},{18,2},{3,19},{19,3},{4,20},{20... | collective-permute-start | bytes 1572872 | tf_op jit(solution)/shard_map/ppermute | solution.py:216
  226.6 25.8 %collective-permute-start.6 = (bf16[384,384]{1,0:T(8,128)(2,1)}, bf16[384,384]{1,0:T(8,128)(2,1)S(1)}, u32[]{:S(2)}, u32[]{:S(2)}) collective-permute-start(bf16[384,384]{1,0:T(8,128)(2,1)} %get-tuple-element.18), channel_id=1, source_target_pairs={{0,4},{4,8},{8,12},{12,0},{1,5},{5,9},{9,13},{13,1},{2,6},{6,10},{... | collective-permute-start | bytes 884744 | tf_op jit(solution)/shard_map/ppermute | solution.py:223
  229.9 6.3 %copy-start.7 = (bf16[512,512]{1,0:T(8,128)(2,1)}, bf16[512,512]{1,0:T(8,128)(2,1)S(1)}, u32[]{:S(2)}) copy-start(bf16[512,512]{1,0:T(8,128)(2,1)S(1)} %collective-permute-done.18.refs_0_) | copy-start | bytes 1572868
  229.9 29.9 %collective-permute-start.7 = (bf16[384,384]{1,0:T(8,128)(2,1)}, bf16[384,384]{1,0:T(8,128)(2,1)S(1)}, u32[]{:S(2)}, u32[]{:S(2)}) collective-permute-start(bf16[384,384]{1,0:T(8,128)(2,1)} %get-tuple-element.19), channel_id=1, source_target_pairs={{0,8},{4,12},{8,0},{12,4},{1,9},{5,13},{9,1},{13,5},{2,10},{6,14},... | collective-permute-start | bytes 884744 | tf_op jit(solution)/shard_map/ppermute | solution.py:223
  236.6 1.8 copy-start.8
  236.6 26.5 %collective-permute-start.8 = (bf16[384,384]{1,0:T(8,128)(2,1)}, bf16[384,384]{1,0:T(8,128)(2,1)S(1)}, u32[]{:S(2)}, u32[]{:S(2)}) collective-permute-start(bf16[384,384]{1,0:T(8,128)(2,1)} %get-tuple-element.20), channel_id=1, source_target_pairs={{0,12},{4,0},{8,4},{12,8},{1,13},{5,1},{9,5},{13,9},{2,14},{6,2},{... | collective-permute-start | bytes 884744 | tf_op jit(solution)/shard_map/ppermute | solution.py:223
  238.4 2.1 copy-start.14
  238.4 24.8 %collective-permute-start.19 = (bf16[512,512]{1,0:T(8,128)(2,1)}, bf16[512,512]{1,0:T(8,128)(2,1)S(1)}, u32[]{:S(2)}, u32[]{:S(2)}) collective-permute-start(bf16[512,512]{1,0:T(8,128)(2,1)} %hold.6.refs_2_), channel_id=1, source_target_pairs={{0,16},{16,0},{1,17},{17,1},{2,18},{18,2},{3,19},{19,3},{4,20},{20... | collective-permute-start | bytes 1572872 | tf_op jit(solution)/shard_map/ppermute | solution.py:216
  238.5 1.9 copy-start.17
  238.5 24.6 %collective-permute-start.21 = (bf16[512,512]{1,0:T(8,128)(2,1)}, bf16[512,512]{1,0:T(8,128)(2,1)S(1)}, u32[]{:S(2)}, u32[]{:S(2)}) collective-permute-start(bf16[512,512]{1,0:T(8,128)(2,1)} %hold.7.refs_4_), channel_id=1, source_target_pairs={{0,16},{16,0},{1,17},{17,1},{2,18},{18,2},{3,19},{19,3},{4,20},{20... | collective-permute-start | bytes 1572872 | tf_op jit(solution)/shard_map/ppermute | solution.py:216
  252.4 10.7 %copy-start.10 = (bf16[384,384]{1,0:T(8,128)(2,1)}, bf16[384,384]{1,0:T(8,128)(2,1)S(1)}, u32[]{:S(2)}) copy-start(bf16[384,384]{1,0:T(8,128)(2,1)S(1)} %collective-permute-done.6.refs_1_.refs_7_) | copy-start | bytes 884740
  252.5 29.5 %collective-permute-start.13 = (bf16[384,256]{1,0:T(8,128)(2,1)}, bf16[384,256]{1,0:T(8,128)(2,1)S(1)}, u32[]{:S(2)}, u32[]{:S(2)}) collective-permute-start(bf16[384,256]{1,0:T(8,128)(2,1)} %get-tuple-element.22), channel_id=1, source_target_pairs={{0,4},{4,8},{8,12},{12,0},{1,5},{5,9},{9,13},{13,1},{2,6},{6,10},{... | collective-permute-start | bytes 589832 | tf_op jit(solution)/shard_map/ppermute | solution.py:223
  259.8 3.3 %copy-start.11 = (bf16[384,384]{1,0:T(8,128)(2,1)}, bf16[384,384]{1,0:T(8,128)(2,1)S(1)}, u32[]{:S(2)}) copy-start(bf16[384,384]{1,0:T(8,128)(2,1)S(1)} %collective-permute-done.7.refs_2_.refs_8_) | copy-start | bytes 884740
  259.8 22.1 %collective-permute-start.14 = (bf16[384,256]{1,0:T(8,128)(2,1)}, bf16[384,256]{1,0:T(8,128)(2,1)S(1)}, u32[]{:S(2)}, u32[]{:S(2)}) collective-permute-start(bf16[384,256]{1,0:T(8,128)(2,1)} %get-tuple-element.23), channel_id=1, source_target_pairs={{0,8},{4,12},{8,0},{12,4},{1,9},{5,13},{9,1},{13,5},{2,10},{6,14},... | collective-permute-start | bytes 589832 | tf_op jit(solution)/shard_map/ppermute | solution.py:223
  263.1 0.7 copy-start.12
  263.1 18.8 %collective-permute-start.15 = (bf16[384,256]{1,0:T(8,128)(2,1)}, bf16[384,256]{1,0:T(8,128)(2,1)S(1)}, u32[]{:S(2)}, u32[]{:S(2)}) collective-permute-start(bf16[384,256]{1,0:T(8,128)(2,1)} %get-tuple-element.24), channel_id=1, source_target_pairs={{0,12},{4,0},{8,4},{12,8},{1,13},{5,1},{9,5},{13,9},{2,14},{6,2},{... | collective-permute-start | bytes 589832 | tf_op jit(solution)/shard_map/ppermute | solution.py:223
  263.1 0.9 copy-start.15
  263.2 1.0 copy-start.16
  276.1 16.1 %collective-permute-start.22 = (bf16[384,256]{1,0:T(8,128)(2,1)}, bf16[384,256]{1,0:T(8,128)(2,1)S(1)}, u32[]{:S(2)}, u32[]{:S(2)}) collective-permute-start(bf16[384,256]{1,0:T(8,128)(2,1)} %get-tuple-element.26), channel_id=1, source_target_pairs={{0,4},{4,8},{8,12},{12,0},{1,5},{5,9},{9,13},{13,1},{2,6},{6,10},{... | collective-permute-start | bytes 589832 | tf_op jit(solution)/shard_map/ppermute | solution.py:223
  278.1 16.6 %collective-permute-start.23 = (bf16[384,256]{1,0:T(8,128)(2,1)}, bf16[384,256]{1,0:T(8,128)(2,1)S(1)}, u32[]{:S(2)}, u32[]{:S(2)}) collective-permute-start(bf16[384,256]{1,0:T(8,128)(2,1)} %get-tuple-element.27), channel_id=1, source_target_pairs={{0,8},{4,12},{8,0},{12,4},{1,9},{5,13},{9,1},{13,5},{2,10},{6,14},... | collective-permute-start | bytes 589832 | tf_op jit(solution)/shard_map/ppermute | solution.py:223
  281.9 0.7 copy-start.18
  281.9 14.8 %collective-permute-start.24 = (bf16[384,256]{1,0:T(8,128)(2,1)}, bf16[384,256]{1,0:T(8,128)(2,1)S(1)}, u32[]{:S(2)}, u32[]{:S(2)}) collective-permute-start(bf16[384,256]{1,0:T(8,128)(2,1)} %get-tuple-element.28), channel_id=1, source_target_pairs={{0,12},{4,0},{8,4},{12,8},{1,13},{5,1},{9,5},{13,9},{2,14},{6,2},{... | collective-permute-start | bytes 589832 | tf_op jit(solution)/shard_map/ppermute | solution.py:223
  281.9 0.7 copy-start.19
  282.7 0.7 copy-start.20
  292.2 4.5 %copy-start.21 = (bf16[384,256]{1,0:T(8,128)(2,1)}, bf16[384,256]{1,0:T(8,128)(2,1)S(1)}, u32[]{:S(2)}) copy-start(bf16[384,256]{1,0:T(8,128)(2,1)S(1)} %collective-permute-done.22.refs_2_) | copy-start | bytes 589828
  294.7 2.0 copy-start.22
  296.7 0.7 copy-start.23
Sparse Core Ops, SparseCore 0:
  8.9 107.7 all-gather.2
  120.7 83.8 all-gather.4

commit v14 on v13

--- a/solution.py
+++ b/solution.py
@@ -241,7 +241,7 @@
         if len(sent) == min(3, len(plan)):
             whole = lax.all_gather(hold(block_rows, arrived[:1] + sent[1:3]), "col", axis=1, tiled=True)
     for n in range(min(last, 1), last + 1):
-        hidden_of(n, done[-1:] + (returned[n - 2] if n > 1 else []))
+        hidden_of(n, done[-1:] + (returned[n - 2][:1] if n > 1 else []))
     early = len(blocks) - rows if last else len(blocks)
     out = place(blocks[:early], mine, ff)
     return place(blocks[early:], mine, ff, out) if last else out

time: 307 us -> 307 us (level)
  starting transfers between devices: 54.6 us -> 61.3 us
  waiting for transfers between devices: 167 us -> 162 us
    ppermute x9, waiting for transfers between devices: 17.8 us -> 11.1 us  [hidden_of(): lax.ppermute(outs[shift], 'row', around(rows, shift))]
    ppermute x9, starting transfers between devices: 20.9 us -> 27.6 us  [hidden_of(): lax.ppermute(outs[shift], 'row', around(rows, shift))]
  transfers between devices with their start and end apart: 27 -> 27, of which waited for: 9 -> 10; matrix products, arithmetic and copies ran while one was open for 0% -> 0% of each run, Pallas kernels for 19% -> 19%
where the time goes in v14:
time: 307 us; the launch traced here: 306 us
  waiting for transfers between devices  162 us (53%)
  Pallas kernels  61.6 us (20%)
  starting transfers between devices  61.3 us (20%)
  between operations  13.7 us (4%)
  local copies, waits for them, and re-layouts  7.74 us (3%)
    ppermute x8, waiting for transfers between devices, weights(): arrived.append(lax.ppermute(sent[-1], 'row', around(rows, shift)))  149 us
    pallas_call x3, Pallas kernels, product(): pl.pallas_call(body, out_shape=[jax.ShapeDtypeStruct((mine, wide), jnp.bf...  40.5 us
    ppermute x9, starting transfers between devices, hidden_of(): lax.ppermute(outs[shift], 'row', around(rows, shift))  27.6 us
    ppermute x8, starting transfers between devices, weights(): arrived.append(lax.ppermute(sent[-1], 'row', around(rows, shift)))  24.4 us
    pallas_call x8, Pallas kernels, pack(): pl.pallas_call(body, out_shape=jax.ShapeDtypeStruct((share, 2 * wide), ga...  16.7 us
    ppermute x9, waiting for transfers between devices, hidden_of(): lax.ppermute(outs[shift], 'row', around(rows, shift))  11.1 us
    ppermute x8, starting transfers between devices, weights(): swapped.append(lax.ppermute(came, 'parts', around(parts, -turn)))  9.24 us
    unnamed x48, local copies, waits for them, and re-layouts  7.74 us
  transfers between devices with their start and end apart: 27, of which 10 were waited for; matrix products, arithmetic and copies ran while one was open for 0% of the time, Pallas kernels for 19%

profile of v14, /device:TPU:12, one launch (start us, length us, event | category | flops | bytes accessed | tf_op | source)
XLA Modules:
  0.0 306.2 jit_solution(17785744710818483672)
XLA Ops:
  6.5 0.7 all-gather.3.cloned.1.call-update
  7.3 0.0 all-gather.5.cloned.1.call-start
  7.3 2.6 pack.8.refs_2_
  9.9 2.7 collective-permute-start
  12.5 2.2 pack.9.refs_2_
  14.7 2.2 pack.10.refs_3_.refs_2_
  16.9 102.5 %collective-permute-done.refs_1_.refs_0_.refs_3_ = bf16[512,1280]{1,0:T(8,128)(2,1)S(1)} collective-permute-done((bf16[512,1280]{1,0:T(8,128)(2,1)}, bf16[512,1280]{1,0:T(8,128)(2,1)S(1)}, u32[]{:S(2)}, u32[]{:S(2)}) %collective-permute-start) | collective-permute-done | bytes 1310752 | tf_op jit(solution)/shard_map/ppermute | solution.py:212
  119.5 1.1 copy-done
  120.5 0.0 all-gather.5.cloned.1.call-update
  120.5 1.3 copy-done.1
  121.8 0.5 collective-permute-start.1
  122.3 0.0 collective-permute-start.2
  122.3 2.0 collective-permute-start.4
  124.4 1.9 pack.11.refs_2_
  126.3 3.3 %collective-permute-start.16 = (bf16[512,512]{1,0:T(8,128)(2,1)}, bf16[512,512]{1,0:T(8,128)(2,1)S(1)}, u32[]{:S(2)}, u32[]{:S(2)}) collective-permute-start(bf16[512,512]{1,0:T(8,128)(2,1)} %pack.11.refs_2_), channel_id=1, source_target_pairs={{0,8},{4,12},{8,0},{12,4},{1,9},{5,13},{9,1},{13,5},{2,10},{6,14},... | collective-permute-start | bytes 1572872 | tf_op jit(solution)/shard_map/ppermute | solution.py:212
  129.7 13.2 %collective-permute-done.2.refs_2_.refs_3_ = bf16[512,768]{1,0:T(8,128)(2,1)} collective-permute-done((bf16[512,768]{1,0:T(8,128)(2,1)S(1)}, bf16[512,768]{1,0:T(8,128)(2,1)}, u32[]{:S(2)}, u32[]{:S(2)}) %collective-permute-start.2) | collective-permute-done | bytes 786464 | tf_op jit(solution)/shard_map/ppermute | solution.py:212
  142.9 1.5 collective-permute-start.3
  144.4 17.0 %collective-permute-done.4.refs_4_.refs_3_ = bf16[512,768]{1,0:T(8,128)(2,1)} collective-permute-done((bf16[512,768]{1,0:T(8,128)(2,1)S(1)}, bf16[512,768]{1,0:T(8,128)(2,1)}, u32[]{:S(2)}, u32[]{:S(2)}) %collective-permute-start.4) | collective-permute-done | bytes 786464 | tf_op jit(solution)/shard_map/ppermute | solution.py:212
  161.4 1.6 collective-permute-start.5
  163.0 15.8 %collective-permute-done.16.refs_3_.refs_0_ = bf16[512,512]{1,0:T(8,128)(2,1)S(1)} collective-permute-done((bf16[512,512]{1,0:T(8,128)(2,1)}, bf16[512,512]{1,0:T(8,128)(2,1)S(1)}, u32[]{:S(2)}, u32[]{:S(2)}) %collective-permute-start.16) | collective-permute-done | bytes 524320 | tf_op jit(solution)/shard_map/ppermute | solution.py:212
  178.8 1.5 collective-permute-start.17
  180.3 0.0 collective-permute-done.1.refs_1_.refs_4_
  180.3 2.0 pack.12.refs_2_
  182.3 3.3 %collective-permute-start.9 = (bf16[512,512]{1,0:T(8,128)(2,1)}, bf16[512,512]{1,0:T(8,128)(2,1)S(1)}, u32[]{:S(2)}, u32[]{:S(2)}) collective-permute-start(bf16[512,512]{1,0:T(8,128)(2,1)} %pack.12.refs_2_), channel_id=1, source_target_pairs={{0,4},{4,8},{8,12},{12,0},{1,5},{5,9},{9,13},{13,1},{2,6},{6,10},{... | collective-permute-start | bytes 1572872 | tf_op jit(solution)/shard_map/ppermute | solution.py:212
  185.6 0.0 collective-permute-done.3.refs_3_.refs_4_
  185.6 0.9 copy-done.11
  186.5 2.0 pack.13.refs_2_
  188.5 1.8 collective-permute-start.11
  190.3 1.9 pack.14.refs_2_
  192.3 8.4 %collective-permute-start.18 = (bf16[512,512]{1,0:T(8,128)(2,1)}, bf16[512,512]{1,0:T(8,128)(2,1)S(1)}, u32[]{:S(2)}, u32[]{:S(2)}) collective-permute-start(bf16[512,512]{1,0:T(8,128)(2,1)} %pack.14.refs_2_), channel_id=1, source_target_pairs={{0,4},{4,8},{8,12},{12,0},{1,5},{5,9},{9,13},{13,1},{2,6},{6,10},{... | collective-permute-start | bytes 1572872 | tf_op jit(solution)/shard_map/ppermute | solution.py:212
  200.6 0.0 collective-permute-done.17.refs_4_.refs_1_
  200.6 0.0 collective-permute-done.9.refs_2_.refs_3_
  200.7 0.8 copy-done.5
  201.5 0.8 copy-done.6
  202.3 2.0 pack.15
  204.2 2.9 collective-permute-start.20
  207.1 0.5 collective-permute-start.10
  207.6 16.7 %product.3 = (bf16[384,384]{1,0:T(8,128)(2,1)}, bf16[384,384]{1,0:T(8,128)(2,1)}, bf16[384,384]{1,0:T(8,128)(2,1)}, bf16[384,384]{1,0:T(8,128)(2,1)}) custom-call(bf16[1536,4096]{1,0:T(8,128)(2,1)} %all-gather.5.cloned.1.call-done.tokens_ref, bf16[1024,3584]{1,0:T(8,128)(2,1)} %gate_ref.5, bf16[1024,3584]{1,0:T(8,128)(2,1)} %up_ref.5, ...), custom_call_target="tpu_custom_call" | custom-call | flops 9663676416 | bytes 20054016 | tf_op jit(solution)/shard_map/product/pallas_call | solution.py:136
  224.3 0.8 copy-done.9
  225.1 1.5 collective-permute-start.12
  226.6 3.3 %collective-permute-start.6 = (bf16[384,384]{1,0:T(8,128)(2,1)}, bf16[384,384]{1,0:T(8,128)(2,1)S(1)}, u32[]{:S(2)}, u32[]{:S(2)}) collective-permute-start(bf16[384,384]{1,0:T(8,128)(2,1)} %get-tuple-element.18), channel_id=1, source_target_pairs={{0,4},{4,8},{8,12},{12,0},{1,5},{5,9},{9,13},{13,1},{2,6},{6,10},{... | collective-permute-start | bytes 884744 | tf_op jit(solution)/shard_map/ppermute | solution.py:223
  229.9 6.3 %collective-permute-start.7 = (bf16[384,384]{1,0:T(8,128)(2,1)}, bf16[384,384]{1,0:T(8,128)(2,1)S(1)}, u32[]{:S(2)}, u32[]{:S(2)}) collective-permute-start(bf16[384,384]{1,0:T(8,128)(2,1)} %get-tuple-element.19), channel_id=1, source_target_pairs={{0,8},{4,12},{8,0},{12,4},{1,9},{5,13},{9,1},{13,5},{2,10},{6,14},... | collective-permute-start | bytes 884744 | tf_op jit(solution)/shard_map/ppermute | solution.py:223
  236.2 0.4 collective-permute-done.20.refs_0_
  236.6 1.8 collective-permute-start.8
  238.4 0.1 collective-permute-start.19
  238.5 1.9 collective-permute-start.21
  240.5 12.0 %product.4 = (bf16[384,256]{1,0:T(8,128)(2,1)}, bf16[384,256]{1,0:T(8,128)(2,1)}, bf16[384,256]{1,0:T(8,128)(2,1)}, bf16[384,256]{1,0:T(8,128)(2,1)}) custom-call(bf16[1536,4096]{1,0:T(8,128)(2,1)} %all-gather.5.cloned.1.call-done.tokens_ref, bf16[1024,3584]{1,0:T(8,128)(2,1)} %gate_ref.5, bf16[1024,3584]{1,0:T(8,128)(2,1)} %up_ref.5, ...), custom_call_target="tpu_custom_call" | custom-call | flops 6442450944 | bytes 17563648 | tf_op jit(solution)/shard_map/product/pallas_call | solution.py:136
  252.5 0.5 collective-permute-start.13
  253.0 0.5 collective-permute-done.19.refs_3_
  253.5 8.8 %collective-permute-start.14 = (bf16[384,256]{1,0:T(8,128)(2,1)}, bf16[384,256]{1,0:T(8,128)(2,1)S(1)}, u32[]{:S(2)}, u32[]{:S(2)}) collective-permute-start(bf16[384,256]{1,0:T(8,128)(2,1)} %get-tuple-element.23), channel_id=1, source_target_pairs={{0,8},{4,12},{8,0},{12,4},{1,9},{5,13},{9,1},{13,5},{2,10},{6,14},... | collective-permute-start | bytes 589832 | tf_op jit(solution)/shard_map/ppermute | solution.py:223
  262.3 0.7 collective-permute-done.21.refs_5_
  262.9 3.8 %collective-permute-start.15 = (bf16[384,256]{1,0:T(8,128)(2,1)}, bf16[384,256]{1,0:T(8,128)(2,1)S(1)}, u32[]{:S(2)}, u32[]{:S(2)}) collective-permute-start(bf16[384,256]{1,0:T(8,128)(2,1)} %get-tuple-element.24), channel_id=1, source_target_pairs={{0,12},{4,0},{8,4},{12,8},{1,13},{5,1},{9,5},{13,9},{2,14},{6,2},{... | collective-permute-start | bytes 589832 | tf_op jit(solution)/shard_map/ppermute | solution.py:223
  266.8 11.9 %product.5 = (bf16[384,256]{1,0:T(8,128)(2,1)}, bf16[384,256]{1,0:T(8,128)(2,1)}, bf16[384,256]{1,0:T(8,128)(2,1)}, bf16[384,256]{1,0:T(8,128)(2,1)}) custom-call(bf16[1536,4096]{1,0:T(8,128)(2,1)} %all-gather.5.cloned.1.call-done.tokens_ref, bf16[1024,3584]{1,0:T(8,128)(2,1)} %gate_ref.5, bf16[1024,3584]{1,0:T(8,128)(2,1)} %up_ref.5, ...), custom_call_target="tpu_custom_call" | custom-call | flops 6442450944 | bytes 17563648 | tf_op jit(solution)/shard_map/product/pallas_call | solution.py:136
  278.7 0.1 collective-permute-start.22
  278.8 3.1 %collective-permute-start.23 = (bf16[384,256]{1,0:T(8,128)(2,1)}, bf16[384,256]{1,0:T(8,128)(2,1)S(1)}, u32[]{:S(2)}, u32[]{:S(2)}) collective-permute-start(bf16[384,256]{1,0:T(8,128)(2,1)} %get-tuple-element.27), channel_id=1, source_target_pairs={{0,8},{4,12},{8,0},{12,4},{1,9},{5,13},{9,1},{13,5},{2,10},{6,14},... | collective-permute-start | bytes 589832 | tf_op jit(solution)/shard_map/ppermute | solution.py:223
  281.9 0.6 copy-done.18
  282.6 0.1 copy-done.19
  282.6 0.7 copy-done.20
  283.3 2.4 place.2.refs_0_
  285.7 6.3 %collective-permute-done.22.refs_2_ = bf16[384,256]{1,0:T(8,128)(2,1)S(1)} collective-permute-done((bf16[384,256]{1,0:T(8,128)(2,1)}, bf16[384,256]{1,0:T(8,128)(2,1)S(1)}, u32[]{:S(2)}, u32[]{:S(2)}) %collective-permute-start.22) | collective-permute-done | bytes 196640 | tf_op jit(solution)/shard_map/ppermute | solution.py:223
  292.0 2.1 collective-permute-done.23.refs_3_
  294.1 2.6 collective-permute-done.24.refs_4_
  296.7 0.7 copy-done.23
  297.4 2.0 place.3
  (57 shorter events, 0.1 us)
Async XLA Ops:
  6.5 112.9 %all-gather.3.cloned.1.call-start = ((), (), s32[]{:S(2)}) async-start(), calls=%async_computation | async-start | bytes 3932160 | tf_op jit(solution)/shard_map/all_gather | solution.py:200
  7.3 200.4 %all-gather.5.cloned.1.call-start = ((), (), s32[]{:S(2)}) async-start(), calls=%async_computation.1 | async-start | bytes 15728640 | tf_op jit(solution)/shard_map/all_gather | solution.py:242
  9.9 109.6 %collective-permute-start = (bf16[512,1280]{1,0:T(8,128)(2,1)}, bf16[512,1280]{1,0:T(8,128)(2,1)S(1)}, u32[]{:S(2)}, u32[]{:S(2)}) collective-permute-start(bf16[512,1280]{1,0:T(8,128)(2,1)} %pack.8.refs_2_), channel_id=1, source_target_pairs={{0,8},{4,12},{8,0},{12,4},{1,9},{5,13},{9,1},{13,5},{2,10},{6,14},... | collective-permute-start | bytes 3932168 | tf_op jit(solution)/shard_map/ppermute | solution.py:212
  119.5 1.1 copy-start
  120.5 1.3 copy-start.1
  120.5 1.8 copy-start.3
  120.5 1.8 copy-start.2
  121.8 58.5 %collective-permute-start.1 = (bf16[512,1280]{1,0:T(8,128)(2,1)S(1)}, bf16[512,1280]{1,0:T(8,128)(2,1)}, u32[]{:S(2)}, u32[]{:S(2)}) collective-permute-start(bf16[512,1280]{1,0:T(8,128)(2,1)S(1)} %copy-done.1), channel_id=1, source_target_pairs={{0,16},{16,0},{1,17},{17,1},{2,18},{18,2},{3,19},{19,3},{4,20},{20... | collective-permute-start | bytes 3932168 | tf_op jit(solution)/shard_map/ppermute | solution.py:216
  122.3 20.6 %collective-permute-start.2 = (bf16[512,768]{1,0:T(8,128)(2,1)S(1)}, bf16[512,768]{1,0:T(8,128)(2,1)}, u32[]{:S(2)}, u32[]{:S(2)}) collective-permute-start(bf16[512,768]{1,0:T(8,128)(2,1)S(1)} %copy-done.3), channel_id=1, source_target_pairs={{0,4},{4,8},{8,12},{12,0},{1,5},{5,9},{9,13},{13,1},{2,6},{6,10},{... | collective-permute-start | bytes 2359304 | tf_op jit(solution)/shard_map/ppermute | solution.py:212
  122.3 39.0 %collective-permute-start.4 = (bf16[512,768]{1,0:T(8,128)(2,1)S(1)}, bf16[512,768]{1,0:T(8,128)(2,1)}, u32[]{:S(2)}, u32[]{:S(2)}) collective-permute-start(bf16[512,768]{1,0:T(8,128)(2,1)S(1)} %copy-done.2), channel_id=1, source_target_pairs={{0,12},{4,0},{8,4},{12,8},{1,13},{5,1},{9,5},{13,9},{2,14},{6,2},{... | collective-permute-start | bytes 2359304 | tf_op jit(solution)/shard_map/ppermute | solution.py:212
  126.3 52.4 %collective-permute-start.16 = (bf16[512,512]{1,0:T(8,128)(2,1)}, bf16[512,512]{1,0:T(8,128)(2,1)S(1)}, u32[]{:S(2)}, u32[]{:S(2)}) collective-permute-start(bf16[512,512]{1,0:T(8,128)(2,1)} %pack.11.refs_2_), channel_id=1, source_target_pairs={{0,8},{4,12},{8,0},{12,4},{1,9},{5,13},{9,1},{13,5},{2,10},{6,14},... | collective-permute-start | bytes 1572872 | tf_op jit(solution)/shard_map/ppermute | solution.py:212
  142.9 42.7 %collective-permute-start.3 = (bf16[512,768]{1,0:T(8,128)(2,1)}, bf16[512,768]{1,0:T(8,128)(2,1)S(1)}, u32[]{:S(2)}, u32[]{:S(2)}) collective-permute-start(bf16[512,768]{1,0:T(8,128)(2,1)} %collective-permute-done.2.refs_2_.refs_3_), channel_id=1, source_target_pairs={{0,16},{16,0},{1,17},{17,1},{2,18},{18,2},{3,19},{19,3},{4,20},{20... | collective-permute-start | bytes 2359304 | tf_op jit(solution)/shard_map/ppermute | solution.py:216
  161.4 28.9 %collective-permute-start.5 = (bf16[512,768]{1,0:T(8,128)(2,1)}, bf16[512,768]{1,0:T(8,128)(2,1)}, u32[]{:S(2)}, u32[]{:S(2)}) collective-permute-start(bf16[512,768]{1,0:T(8,128)(2,1)} %collective-permute-done.4.refs_4_.refs_3_), channel_id=1, source_target_pairs={{0,16},{16,0},{1,17},{17,1},{2,18},{18,2},{3,19},{19,3},{4,20},{20... | collective-permute-start | bytes 2359304 | tf_op jit(solution)/shard_map/ppermute | solution.py:216
  178.8 3.5 %copy-start.4 = (bf16[512,512]{1,0:T(8,128)(2,1)}, bf16[512,512]{1,0:T(8,128)(2,1)S(1)}, u32[]{:S(2)}) copy-start(bf16[512,512]{1,0:T(8,128)(2,1)S(1)} %collective-permute-done.16.refs_3_.refs_0_) | copy-start | bytes 1572868
  178.8 21.9 %collective-permute-start.17 = (bf16[512,512]{1,0:T(8,128)(2,1)S(1)}, bf16[512,512]{1,0:T(8,128)(2,1)S(1)}, u32[]{:S(2)}, u32[]{:S(2)}) collective-permute-start(bf16[512,512]{1,0:T(8,128)(2,1)S(1)} %collective-permute-done.16.refs_3_.refs_0_), channel_id=1, source_target_pairs={{0,16},{16,0},{1,17},{17,1},{2,18},{18,2},{3,19},{19,3},{4,20},{20... | collective-permute-start | bytes 1572872 | tf_op jit(solution)/shard_map/ppermute | solution.py:216
  182.3 18.4 %collective-permute-start.9 = (bf16[512,512]{1,0:T(8,128)(2,1)}, bf16[512,512]{1,0:T(8,128)(2,1)S(1)}, u32[]{:S(2)}, u32[]{:S(2)}) collective-permute-start(bf16[512,512]{1,0:T(8,128)(2,1)} %pack.12.refs_2_), channel_id=1, source_target_pairs={{0,4},{4,8},{8,12},{12,0},{1,5},{5,9},{9,13},{13,1},{2,6},{6,10},{... | collective-permute-start | bytes 1572872 | tf_op jit(solution)/shard_map/ppermute | solution.py:212
  185.6 0.9 copy-start.11
  188.5 35.8 %collective-permute-start.11 = (bf16[512,512]{1,0:T(8,128)(2,1)}, bf16[512,512]{1,0:T(8,128)(2,1)S(1)}, u32[]{:S(2)}, u32[]{:S(2)}) collective-permute-start(bf16[512,512]{1,0:T(8,128)(2,1)} %pack.13.refs_2_), channel_id=1, source_target_pairs={{0,12},{4,0},{8,4},{12,8},{1,13},{5,1},{9,5},{13,9},{2,14},{6,2},{... | collective-permute-start | bytes 1572872 | tf_op jit(solution)/shard_map/ppermute | solution.py:212
  192.3 37.7 %collective-permute-start.18 = (bf16[512,512]{1,0:T(8,128)(2,1)}, bf16[512,512]{1,0:T(8,128)(2,1)S(1)}, u32[]{:S(2)}, u32[]{:S(2)}) collective-permute-start(bf16[512,512]{1,0:T(8,128)(2,1)} %pack.14.refs_2_), channel_id=1, source_target_pairs={{0,4},{4,8},{8,12},{12,0},{1,5},{5,9},{9,13},{13,1},{2,6},{6,10},{... | collective-permute-start | bytes 1572872 | tf_op jit(solution)/shard_map/ppermute | solution.py:212
  200.6 0.8 copy-start.5
  201.4 0.8 copy-start.6
  204.2 32.3 %collective-permute-start.20 = (bf16[512,512]{1,0:T(8,128)(2,1)}, bf16[512,512]{1,0:T(8,128)(2,1)S(1)}, u32[]{:S(2)}, u32[]{:S(2)}) collective-permute-start(bf16[512,512]{1,0:T(8,128)(2,1)} %pack.15), channel_id=1, source_target_pairs={{0,12},{4,0},{8,4},{12,8},{1,13},{5,1},{9,5},{13,9},{2,14},{6,2},{... | collective-permute-start | bytes 1572872 | tf_op jit(solution)/shard_map/ppermute | solution.py:212
  207.1 31.2 %collective-permute-start.10 = (bf16[512,512]{1,0:T(8,128)(2,1)}, bf16[512,512]{1,0:T(8,128)(2,1)S(1)}, u32[]{:S(2)}, u32[]{:S(2)}) collective-permute-start(bf16[512,512]{1,0:T(8,128)(2,1)} %copy-done.6), channel_id=1, source_target_pairs={{0,16},{16,0},{1,17},{17,1},{2,18},{18,2},{3,19},{19,3},{4,20},{20... | collective-permute-start | bytes 1572872 | tf_op jit(solution)/shard_map/ppermute | solution.py:216
  224.3 0.8 copy-start.9
  225.1 13.4 %collective-permute-start.12 = (bf16[512,512]{1,0:T(8,128)(2,1)}, bf16[512,512]{1,0:T(8,128)(2,1)S(1)}, u32[]{:S(2)}, u32[]{:S(2)}) collective-permute-start(bf16[512,512]{1,0:T(8,128)(2,1)} %hold.5.refs_4_), channel_id=1, source_target_pairs={{0,16},{16,0},{1,17},{17,1},{2,18},{18,2},{3,19},{19,3},{4,20},{20... | collective-permute-start | bytes 1572872 | tf_op jit(solution)/shard_map/ppermute | solution.py:216
  226.6 25.8 %collective-permute-start.6 = (bf16[384,384]{1,0:T(8,128)(2,1)}, bf16[384,384]{1,0:T(8,128)(2,1)S(1)}, u32[]{:S(2)}, u32[]{:S(2)}) collective-permute-start(bf16[384,384]{1,0:T(8,128)(2,1)} %get-tuple-element.18), channel_id=1, source_target_pairs={{0,4},{4,8},{8,12},{12,0},{1,5},{5,9},{9,13},{13,1},{2,6},{6,10},{... | collective-permute-start | bytes 884744 | tf_op jit(solution)/shard_map/ppermute | solution.py:223
  229.9 6.3 %copy-start.7 = (bf16[512,512]{1,0:T(8,128)(2,1)}, bf16[512,512]{1,0:T(8,128)(2,1)S(1)}, u32[]{:S(2)}) copy-start(bf16[512,512]{1,0:T(8,128)(2,1)S(1)} %collective-permute-done.18.refs_0_) | copy-start | bytes 1572868
  229.9 48.7 %collective-permute-start.7 = (bf16[384,384]{1,0:T(8,128)(2,1)}, bf16[384,384]{1,0:T(8,128)(2,1)S(1)}, u32[]{:S(2)}, u32[]{:S(2)}) collective-permute-start(bf16[384,384]{1,0:T(8,128)(2,1)} %get-tuple-element.19), channel_id=1, source_target_pairs={{0,8},{4,12},{8,0},{12,4},{1,9},{5,13},{9,1},{13,5},{2,10},{6,14},... | collective-permute-start | bytes 884744 | tf_op jit(solution)/shard_map/ppermute | solution.py:223
  236.6 1.8 copy-start.8
  236.6 42.2 %collective-permute-start.8 = (bf16[384,384]{1,0:T(8,128)(2,1)}, bf16[384,384]{1,0:T(8,128)(2,1)S(1)}, u32[]{:S(2)}, u32[]{:S(2)}) collective-permute-start(bf16[384,384]{1,0:T(8,128)(2,1)} %get-tuple-element.20), channel_id=1, source_target_pairs={{0,12},{4,0},{8,4},{12,8},{1,13},{5,1},{9,5},{13,9},{2,14},{6,2},{... | collective-permute-start | bytes 884744 | tf_op jit(solution)/shard_map/ppermute | solution.py:223
  238.4 2.1 copy-start.12
  238.4 15.1 %collective-permute-start.19 = (bf16[512,512]{1,0:T(8,128)(2,1)}, bf16[512,512]{1,0:T(8,128)(2,1)S(1)}, u32[]{:S(2)}, u32[]{:S(2)}) collective-permute-start(bf16[512,512]{1,0:T(8,128)(2,1)} %hold.6.refs_2_), channel_id=1, source_target_pairs={{0,16},{16,0},{1,17},{17,1},{2,18},{18,2},{3,19},{19,3},{4,20},{20... | collective-permute-start | bytes 1572872 | tf_op jit(solution)/shard_map/ppermute | solution.py:216
  238.5 1.9 copy-start.14
  238.5 24.4 %collective-permute-start.21 = (bf16[512,512]{1,0:T(8,128)(2,1)}, bf16[512,512]{1,0:T(8,128)(2,1)S(1)}, u32[]{:S(2)}, u32[]{:S(2)}) collective-permute-start(bf16[512,512]{1,0:T(8,128)(2,1)} %hold.7.refs_4_), channel_id=1, source_target_pairs={{0,16},{16,0},{1,17},{17,1},{2,18},{18,2},{3,19},{19,3},{4,20},{20... | collective-permute-start | bytes 1572872 | tf_op jit(solution)/shard_map/ppermute | solution.py:216
  252.4 14.3 %copy-start.10 = (bf16[384,384]{1,0:T(8,128)(2,1)}, bf16[384,384]{1,0:T(8,128)(2,1)S(1)}, u32[]{:S(2)}) copy-start(bf16[384,384]{1,0:T(8,128)(2,1)S(1)} %collective-permute-done.6.refs_1_.refs_7_) | copy-start | bytes 884740
  252.5 29.4 %collective-permute-start.13 = (bf16[384,256]{1,0:T(8,128)(2,1)}, bf16[384,256]{1,0:T(8,128)(2,1)S(1)}, u32[]{:S(2)}, u32[]{:S(2)}) collective-permute-start(bf16[384,256]{1,0:T(8,128)(2,1)} %get-tuple-element.22), channel_id=1, source_target_pairs={{0,4},{4,8},{8,12},{12,0},{1,5},{5,9},{9,13},{13,1},{2,6},{6,10},{... | collective-permute-start | bytes 589832 | tf_op jit(solution)/shard_map/ppermute | solution.py:223
  253.5 13.3 %copy-start.13 = (bf16[512,512]{1,0:T(8,128)(2,1)}, bf16[512,512]{1,0:T(8,128)(2,1)S(1)}, u32[]{:S(2)}) copy-start(bf16[512,512]{1,0:T(8,128)(2,1)S(1)} %collective-permute-done.19.refs_3_) | copy-start | bytes 1572868
  253.5 28.4 %collective-permute-start.14 = (bf16[384,256]{1,0:T(8,128)(2,1)}, bf16[384,256]{1,0:T(8,128)(2,1)S(1)}, u32[]{:S(2)}, u32[]{:S(2)}) collective-permute-start(bf16[384,256]{1,0:T(8,128)(2,1)} %get-tuple-element.23), channel_id=1, source_target_pairs={{0,8},{4,12},{8,0},{12,4},{1,9},{5,13},{9,1},{13,5},{2,10},{6,14},... | collective-permute-start | bytes 589832 | tf_op jit(solution)/shard_map/ppermute | solution.py:223
  262.9 3.8 %copy-start.15 = (bf16[512,512]{1,0:T(8,128)(2,1)}, bf16[512,512]{1,0:T(8,128)(2,1)S(1)}, u32[]{:S(2)}) copy-start(bf16[512,512]{1,0:T(8,128)(2,1)S(1)} %collective-permute-done.21.refs_5_) | copy-start | bytes 1572868
  262.9 19.0 %collective-permute-start.15 = (bf16[384,256]{1,0:T(8,128)(2,1)}, bf16[384,256]{1,0:T(8,128)(2,1)S(1)}, u32[]{:S(2)}, u32[]{:S(2)}) collective-permute-start(bf16[384,256]{1,0:T(8,128)(2,1)} %get-tuple-element.24), channel_id=1, source_target_pairs={{0,12},{4,0},{8,4},{12,8},{1,13},{5,1},{9,5},{13,9},{2,14},{6,2},{... | collective-permute-start | bytes 589832 | tf_op jit(solution)/shard_map/ppermute | solution.py:223
  278.7 3.2 %copy-start.16 = (bf16[384,384]{1,0:T(8,128)(2,1)}, bf16[384,384]{1,0:T(8,128)(2,1)S(1)}, u32[]{:S(2)}) copy-start(bf16[384,384]{1,0:T(8,128)(2,1)S(1)} %collective-permute-done.7.refs_2_) | copy-start | bytes 884740
  278.7 13.3 %collective-permute-start.22 = (bf16[384,256]{1,0:T(8,128)(2,1)}, bf16[384,256]{1,0:T(8,128)(2,1)S(1)}, u32[]{:S(2)}, u32[]{:S(2)}) collective-permute-start(bf16[384,256]{1,0:T(8,128)(2,1)} %get-tuple-element.26), channel_id=1, source_target_pairs={{0,4},{4,8},{8,12},{12,0},{1,5},{5,9},{9,13},{13,1},{2,6},{6,10},{... | collective-permute-start | bytes 589832 | tf_op jit(solution)/shard_map/ppermute | solution.py:223
  278.8 3.2 %copy-start.17 = (bf16[384,384]{1,0:T(8,128)(2,1)}, bf16[384,384]{1,0:T(8,128)(2,1)S(1)}, u32[]{:S(2)}) copy-start(bf16[384,384]{1,0:T(8,128)(2,1)S(1)} %collective-permute-done.8.refs_3_) | copy-start | bytes 884740
  278.8 15.3 %collective-permute-start.23 = (bf16[384,256]{1,0:T(8,128)(2,1)}, bf16[384,256]{1,0:T(8,128)(2,1)S(1)}, u32[]{:S(2)}, u32[]{:S(2)}) collective-permute-start(bf16[384,256]{1,0:T(8,128)(2,1)} %get-tuple-element.27), channel_id=1, source_target_pairs={{0,8},{4,12},{8,0},{12,4},{1,9},{5,13},{9,1},{13,5},{2,10},{6,14},... | collective-permute-start | bytes 589832 | tf_op jit(solution)/shard_map/ppermute | solution.py:223
  281.9 0.7 copy-start.18
  281.9 14.9 %collective-permute-start.24 = (bf16[384,256]{1,0:T(8,128)(2,1)}, bf16[384,256]{1,0:T(8,128)(2,1)S(1)}, u32[]{:S(2)}, u32[]{:S(2)}) collective-permute-start(bf16[384,256]{1,0:T(8,128)(2,1)} %get-tuple-element.28), channel_id=1, source_target_pairs={{0,12},{4,0},{8,4},{12,8},{1,13},{5,1},{9,5},{13,9},{2,14},{6,2},{... | collective-permute-start | bytes 589832 | tf_op jit(solution)/shard_map/ppermute | solution.py:223
  281.9 0.7 copy-start.19
  282.6 0.7 copy-start.20
  292.0 4.7 %copy-start.21 = (bf16[384,256]{1,0:T(8,128)(2,1)}, bf16[384,256]{1,0:T(8,128)(2,1)S(1)}, u32[]{:S(2)}) copy-start(bf16[384,256]{1,0:T(8,128)(2,1)S(1)} %collective-permute-done.22.refs_2_) | copy-start | bytes 589828
  294.1 2.6 copy-start.22
  296.7 0.7 copy-start.23
Sparse Core Ops, SparseCore 0:
  8.9 107.7 all-gather.2
  120.7 83.8 all-gather.4

commit v15 on v14

--- a/solution.py
+++ b/solution.py
@@ -79,6 +79,7 @@
     share, width, tiles = depth // parts, ff // rows, wide // LANES
     features = rows * depth
     order = by_distance(rows) + [0]
+    group = 2 if rows % 2 == 0 else 1
 
     def body(tokens_ref, gate_ref, up_ref, *refs):
         held_refs = refs[:len(held)]
@@ -86,13 +87,12 @@
         stack, block, sems, block_sems = refs[-4:]
         z, y = lax.axis_index("row"), lax.axis_index("parts")
 
-        def fetch(step):
-            to = lax.rem(z + order[step], rows)
-            return pltpu.make_async_copy(
-                tokens_ref.at[pl.ds(pl.multiple_of(to * mine, mine), mine), :],
-                block.at[step % 2],
-                block_sems.at[step % 2],
-            )
+        fetches = []
+        for step, shift in enumerate(order):
+            first = pl.multiple_of(lax.rem(z + shift, rows) * mine, mine)
+            fetches.append(pltpu.make_async_copy(
+                tokens_ref.at[pl.ds(first, mine), :], block.at[pl.ds(step * mine, mine), :], block_sems.at[step]
+            ))
 
         copies = []
         for ref, (shift, turn, begin, _) in zip(held_refs, held):
@@ -111,23 +111,28 @@
                     stack.at[pl.ds(own, depth), pl.ds((2 * j + g) * LANES, LANES)],
                     sems.at[len(copies)],
                 ))
-        fetch(0).start()
-        run_all(copies)
-        for step, shift in enumerate(order):
-            fetch(step).wait()
-            if step + 1 < rows:
-                fetch(step + 1).start()
-
-            def tile(j, carry, step=step, shift=shift):
+        for fetch in fetches[:group]:
+            fetch.start()
+        for copy in copies + fetches[group:]:
+            copy.start()
+        for copy in copies:
+            copy.wait()
+        for first in range(0, rows, group):
+            for fetch in fetches[first:first + group]:
+                fetch.wait()
+
+            def tile(j, carry, first=first):
                 both = jnp.dot(
-                    block[step % 2],
+                    block[first * mine:(first + group) * mine],
                     stack[:, pl.ds(pl.multiple_of(j * 2 * LANES, 2 * LANES), 2 * LANES)],
                     preferred_element_type=jnp.float32,
                 )
                 gate, up = both[:, :LANES], both[:, LANES:]
-                outs[shift][:, pl.ds(pl.multiple_of(j * LANES, LANES), LANES)] = (
-                    jax.nn.silu(gate) * up
-                ).astype(jnp.bfloat16)
+                value = (jax.nn.silu(gate) * up).astype(jnp.bfloat16)
+                for n in range(group):
+                    outs[order[first + n]][:, pl.ds(pl.multiple_of(j * LANES, LANES), LANES)] = (
+                        value[n * mine:(n + 1) * mine]
+                    )
                 return carry
 
             lax.fori_loop(0, tiles, tile, 0)
@@ -140,9 +145,9 @@
         out_specs=[pl.BlockSpec(memory_space=pltpu.VMEM)] * rows,
         scratch_shapes=[
             pltpu.VMEM((features, 2 * wide), gate_weight.dtype),
-            pltpu.VMEM((2, mine, features), tokens.dtype),
+            pltpu.VMEM((rows * mine, features), tokens.dtype),
             pltpu.SemaphoreType.DMA((len(held) + 2 * tiles,)),
-            pltpu.SemaphoreType.DMA((2,)),
+            pltpu.SemaphoreType.DMA((rows,)),
         ],
         compiler_params=pltpu.CompilerParams(vmem_limit_bytes=GRANT),
         cost_estimate=pl.CostEstimate(
@@ -235,7 +240,7 @@
     sent, arrived, swapped, done, returned, blocks = [], [], [], [], [], []
     held = [[] for _ in spans]
     for step in plan:
-        if last and len(sent) == max(len(plan) - 3, 3):
+        if last and len(sent) == max(len(plan) - 2, 3):
             hidden_of(0, [])
         weights(*step)
         if len(sent) == min(3, len(plan)):

time: 307 us -> 304 us (level)
  starting transfers between devices: 61.3 us -> 57.8 us
    ppermute x9, starting transfers between devices: 27.6 us -> 11.9 us  [hidden_of(): lax.ppermute(outs[shift], 'row', around(rows, shift))]
    ppermute x8, starting transfers between devices: 24.4 us -> 37.9 us  [weights(): arrived.append(lax.ppermute(sent[-1], 'row', around(rows, shift)))]
    ppermute x8, waiting for transfers between devices: 149 us -> 141 us  [weights(): arrived.append(lax.ppermute(sent[-1], 'row', around(rows, shift)))]
    ppermute x8, waiting for transfers between devices: 1.16 us -> 5.82 us  [weights(): swapped.append(lax.ppermute(came, 'parts', around(parts, -turn)))]
    unnamed x48 -> x46, local copies, waits for them, and re-layouts: 7.74 us -> 7.13 us
  transfers between devices with their start and end apart: 27 -> 27, of which waited for: 10 -> 11; matrix products, arithmetic and copies ran while one was open for 0% -> 0% of each run, Pallas kernels for 19% -> 20%
where the time goes in v15:
time: 304 us
  waiting for transfers between devices  161 us (53%)
  Pallas kernels  64.1 us (21%)
  starting transfers between devices  57.8 us (19%)
  between operations  13.6 us (4%)
  local copies, waits for them, and re-layouts  7.13 us (2%)
    ppermute x8, waiting for transfers between devices, weights(): arrived.append(lax.ppermute(sent[-1], 'row', around(rows, shift)))  141 us
    pallas_call x3, Pallas kernels, product(): pl.pallas_call(body, out_shape=[jax.ShapeDtypeStruct((mine, wide), jnp.bf...  43.2 us
    ppermute x8, starting transfers between devices, weights(): arrived.append(lax.ppermute(sent[-1], 'row', around(rows, shift)))  37.9 us
    pallas_call x8, Pallas kernels, pack(): pl.pallas_call(body, out_shape=jax.ShapeDtypeStruct((share, 2 * wide), ga...  16.6 us
    ppermute x9, waiting for transfers between devices, hidden_of(): lax.ppermute(outs[shift], 'row', around(rows, shift))  12.9 us
    ppermute x9, starting transfers between devices, hidden_of(): lax.ppermute(outs[shift], 'row', around(rows, shift))  11.9 us
    ppermute x8, starting transfers between devices, weights(): swapped.append(lax.ppermute(came, 'parts', around(parts, -turn)))  7.93 us
    unnamed x46, local copies, waits for them, and re-layouts  7.13 us
  transfers between devices with their start and end apart: 27, of which 11 were waited for; matrix products, arithmetic and copies ran while one was open for 0% of the time, Pallas kernels for 20%

profile of v15, /device:TPU:12, one launch (start us, length us, event | category | flops | bytes accessed | tf_op | source)
XLA Modules:
  0.0 303.6 jit_solution(2388873496345579204)
XLA Ops:
  6.5 0.7 all-gather.3.cloned.1.call-update
  7.3 0.0 all-gather.5.cloned.1.call-start
  7.3 2.6 pack.8.refs_2_
  9.9 2.7 collective-permute-start
  12.5 2.2 pack.9.refs_2_
  14.7 2.2 pack.10.refs_3_.refs_2_
  16.9 102.6 %collective-permute-done.refs_1_.refs_0_.refs_3_ = bf16[512,1280]{1,0:T(8,128)(2,1)S(1)} collective-permute-done((bf16[512,1280]{1,0:T(8,128)(2,1)}, bf16[512,1280]{1,0:T(8,128)(2,1)S(1)}, u32[]{:S(2)}, u32[]{:S(2)}) %collective-permute-start) | collective-permute-done | bytes 1310752 | tf_op jit(solution)/shard_map/ppermute | solution.py:217
  119.5 1.1 copy-done
  120.5 0.0 all-gather.5.cloned.1.call-update
  120.5 1.1 copy-done.3
  121.6 0.0 collective-permute-start.2
  121.6 0.4 copy-done.1
  122.1 0.5 collective-permute-start.1
  122.6 1.6 collective-permute-start.4
  124.2 18.0 %collective-permute-done.2.refs_2_.refs_3_ = bf16[512,768]{1,0:T(8,128)(2,1)} collective-permute-done((bf16[512,768]{1,0:T(8,128)(2,1)S(1)}, bf16[512,768]{1,0:T(8,128)(2,1)}, u32[]{:S(2)}, u32[]{:S(2)}) %collective-permute-start.2) | collective-permute-done | bytes 786464 | tf_op jit(solution)/shard_map/ppermute | solution.py:217
  142.1 0.5 collective-permute-start.3
  142.7 1.9 pack.11.refs_2_
  144.6 19.3 %collective-permute-start.16 = (bf16[512,512]{1,0:T(8,128)(2,1)}, bf16[512,512]{1,0:T(8,128)(2,1)S(1)}, u32[]{:S(2)}, u32[]{:S(2)}) collective-permute-start(bf16[512,512]{1,0:T(8,128)(2,1)} %pack.11.refs_2_), channel_id=1, source_target_pairs={{0,8},{4,12},{8,0},{12,4},{1,9},{5,13},{9,1},{13,5},{2,10},{6,14},... | collective-permute-start | bytes 1572872 | tf_op jit(solution)/shard_map/ppermute | solution.py:217
  163.9 1.5 collective-permute-start.5
  165.4 14.2 %collective-permute-done.16.refs_3_.refs_0_ = bf16[512,512]{1,0:T(8,128)(2,1)S(1)} collective-permute-done((bf16[512,512]{1,0:T(8,128)(2,1)}, bf16[512,512]{1,0:T(8,128)(2,1)S(1)}, u32[]{:S(2)}, u32[]{:S(2)}) %collective-permute-start.16) | collective-permute-done | bytes 524320 | tf_op jit(solution)/shard_map/ppermute | solution.py:217
  179.6 0.5 collective-permute-start.17
  180.1 0.0 collective-permute-done.1.refs_1_.refs_4_
  180.1 2.0 pack.12.refs_2_
  182.1 2.1 collective-permute-start.9
  184.2 0.9 copy-done.10
  185.1 1.9 pack.13.refs_2_
  187.0 2.0 collective-permute-start.11
  189.0 0.0 collective-permute-done.5.refs_5_.refs_4_
  189.0 1.9 pack.14.refs_2_
  190.9 6.2 %collective-permute-start.18 = (bf16[512,512]{1,0:T(8,128)(2,1)}, bf16[512,512]{1,0:T(8,128)(2,1)S(1)}, u32[]{:S(2)}, u32[]{:S(2)}) collective-permute-start(bf16[512,512]{1,0:T(8,128)(2,1)} %pack.14.refs_2_), channel_id=1, source_target_pairs={{0,4},{4,8},{8,12},{12,0},{1,5},{5,9},{9,13},{13,1},{2,6},{6,10},{... | collective-permute-start | bytes 1572872 | tf_op jit(solution)/shard_map/ppermute | solution.py:217
  197.1 0.6 collective-permute-done.17.refs_4_.refs_1_
  197.7 1.3 collective-permute-done.9.refs_2_.refs_3_
  199.0 0.8 copy-done.6
  199.8 1.9 pack.15
  201.8 4.1 %collective-permute-start.20 = (bf16[512,512]{1,0:T(8,128)(2,1)}, bf16[512,512]{1,0:T(8,128)(2,1)S(1)}, u32[]{:S(2)}, u32[]{:S(2)}) collective-permute-start(bf16[512,512]{1,0:T(8,128)(2,1)} %pack.15), channel_id=1, source_target_pairs={{0,12},{4,0},{8,4},{12,8},{1,13},{5,1},{9,5},{13,9},{2,14},{6,2},{... | collective-permute-start | bytes 1572872 | tf_op jit(solution)/shard_map/ppermute | solution.py:217
  205.8 1.4 collective-permute-start.10
  207.2 5.5 %collective-permute-done.11.refs_4_ = bf16[512,512]{1,0:T(8,128)(2,1)S(1)} collective-permute-done((bf16[512,512]{1,0:T(8,128)(2,1)}, bf16[512,512]{1,0:T(8,128)(2,1)S(1)}, u32[]{:S(2)}, u32[]{:S(2)}) %collective-permute-start.11) | collective-permute-done | bytes 524320 | tf_op jit(solution)/shard_map/ppermute | solution.py:217
  212.7 1.5 collective-permute-start.12
  214.2 17.3 %product.3 = (bf16[384,384]{1,0:T(8,128)(2,1)}, bf16[384,384]{1,0:T(8,128)(2,1)}, bf16[384,384]{1,0:T(8,128)(2,1)}, bf16[384,384]{1,0:T(8,128)(2,1)}) custom-call(bf16[1536,4096]{1,0:T(8,128)(2,1)} %all-gather.5.cloned.1.call-done.tokens_ref, bf16[1024,3584]{1,0:T(8,128)(2,1)} %gate_ref.5, bf16[1024,3584]{1,0:T(8,128)(2,1)} %up_ref.5, ...), custom_call_target="tpu_custom_call" | custom-call | flops 9663676416 | bytes 20054016 | tf_op jit(solution)/shard_map/product/pallas_call | solution.py:141
  231.5 0.6 collective-permute-start.6
  232.1 0.0 collective-permute-done.18.refs_0_
  232.1 3.4 %collective-permute-start.7 = (bf16[384,384]{1,0:T(8,128)(2,1)}, bf16[384,384]{1,0:T(8,128)(2,1)}, u32[]{:S(2)}, u32[]{:S(2)}) collective-permute-start(bf16[384,384]{1,0:T(8,128)(2,1)} %get-tuple-element.19), channel_id=1, source_target_pairs={{0,8},{4,12},{8,0},{12,4},{1,9},{5,13},{9,1},{13,5},{2,10},{6,14},... | collective-permute-start | bytes 884744 | tf_op jit(solution)/shard_map/ppermute | solution.py:228
  235.5 0.0 collective-permute-done.20.refs_0_
  235.5 0.1 collective-permute-start.8
  235.6 0.7 copy-done.8
  236.3 0.6 collective-permute-start.19
  236.9 1.5 collective-permute-start.21
  238.3 13.0 %product.4 = (bf16[384,256]{1,0:T(8,128)(2,1)}, bf16[384,256]{1,0:T(8,128)(2,1)}, bf16[384,256]{1,0:T(8,128)(2,1)}, bf16[384,256]{1,0:T(8,128)(2,1)}) custom-call(bf16[1536,4096]{1,0:T(8,128)(2,1)} %all-gather.5.cloned.1.call-done.tokens_ref, bf16[1024,3584]{1,0:T(8,128)(2,1)} %gate_ref.5, bf16[1024,3584]{1,0:T(8,128)(2,1)} %up_ref.5, ...), custom_call_target="tpu_custom_call" | custom-call | flops 6442450944 | bytes 17563648 | tf_op jit(solution)/shard_map/product/pallas_call | solution.py:141
  251.3 1.0 collective-permute-done.6.refs_1_.refs_7_
  252.3 2.5 collective-permute-start.13
  254.9 0.4 collective-permute-start.14
  255.3 5.2 %collective-permute-done.21.refs_5_ = bf16[512,512]{1,0:T(8,128)(2,1)S(1)} collective-permute-done((bf16[512,512]{1,0:T(8,128)(2,1)}, bf16[512,512]{1,0:T(8,128)(2,1)S(1)}, u32[]{:S(2)}, u32[]{:S(2)}) %collective-permute-start.21) | collective-permute-done | bytes 524320 | tf_op jit(solution)/shard_map/ppermute | solution.py:221
  260.5 1.6 collective-permute-start.15
  262.1 12.9 %product.5 = (bf16[384,256]{1,0:T(8,128)(2,1)}, bf16[384,256]{1,0:T(8,128)(2,1)}, bf16[384,256]{1,0:T(8,128)(2,1)}, bf16[384,256]{1,0:T(8,128)(2,1)}) custom-call(bf16[1536,4096]{1,0:T(8,128)(2,1)} %all-gather.5.cloned.1.call-done.tokens_ref, bf16[1024,3584]{1,0:T(8,128)(2,1)} %gate_ref.5, bf16[1024,3584]{1,0:T(8,128)(2,1)} %up_ref.5, ...), custom_call_target="tpu_custom_call" | custom-call | flops 6442450944 | bytes 17563648 | tf_op jit(solution)/shard_map/product/pallas_call | solution.py:141
  275.0 0.5 collective-permute-start.22
  275.6 2.9 collective-permute-start.23
  278.5 0.7 copy-done.19
  279.2 0.7 copy-done.16
  279.9 2.4 place.2.refs_0_
  282.3 7.1 %collective-permute-done.22.refs_2_ = bf16[384,256]{1,0:T(8,128)(2,1)S(1)} collective-permute-done((bf16[384,256]{1,0:T(8,128)(2,1)}, bf16[384,256]{1,0:T(8,128)(2,1)S(1)}, u32[]{:S(2)}, u32[]{:S(2)}) %collective-permute-start.22) | collective-permute-done | bytes 196640 | tf_op jit(solution)/shard_map/ppermute | solution.py:228
  289.4 2.1 collective-permute-done.23.refs_3_
  291.5 2.6 collective-permute-done.24.refs_4_
  294.1 0.7 copy-done.22
  294.8 2.0 place.3
  (54 shorter events, 0.1 us)
Async XLA Ops:
  6.5 112.9 %all-gather.3.cloned.1.call-start = ((), (), s32[]{:S(2)}) async-start(), calls=%async_computation | async-start | bytes 3932160 | tf_op jit(solution)/shard_map/all_gather | solution.py:205
  7.3 207.0 %all-gather.5.cloned.1.call-start = ((), (), s32[]{:S(2)}) async-start(), calls=%async_computation.1 | async-start | bytes 15728640 | tf_op jit(solution)/shard_map/all_gather | solution.py:247
  9.9 109.6 %collective-permute-start = (bf16[512,1280]{1,0:T(8,128)(2,1)}, bf16[512,1280]{1,0:T(8,128)(2,1)S(1)}, u32[]{:S(2)}, u32[]{:S(2)}) collective-permute-start(bf16[512,1280]{1,0:T(8,128)(2,1)} %pack.8.refs_2_), channel_id=1, source_target_pairs={{0,8},{4,12},{8,0},{12,4},{1,9},{5,13},{9,1},{13,5},{2,10},{6,14},... | collective-permute-start | bytes 3932168 | tf_op jit(solution)/shard_map/ppermute | solution.py:217
  119.5 1.1 copy-start
  120.5 1.1 copy-start.3
  120.5 1.6 copy-start.1
  120.5 2.1 copy-start.2
  121.6 20.5 %collective-permute-start.2 = (bf16[512,768]{1,0:T(8,128)(2,1)S(1)}, bf16[512,768]{1,0:T(8,128)(2,1)}, u32[]{:S(2)}, u32[]{:S(2)}) collective-permute-start(bf16[512,768]{1,0:T(8,128)(2,1)S(1)} %copy-done.3), channel_id=1, source_target_pairs={{0,4},{4,8},{8,12},{12,0},{1,5},{5,9},{9,13},{13,1},{2,6},{6,10},{... | collective-permute-start | bytes 2359304 | tf_op jit(solution)/shard_map/ppermute | solution.py:217
  122.1 58.0 %collective-permute-start.1 = (bf16[512,1280]{1,0:T(8,128)(2,1)S(1)}, bf16[512,1280]{1,0:T(8,128)(2,1)}, u32[]{:S(2)}, u32[]{:S(2)}) collective-permute-start(bf16[512,1280]{1,0:T(8,128)(2,1)S(1)} %copy-done.1), channel_id=1, source_target_pairs={{0,16},{16,0},{1,17},{17,1},{2,18},{18,2},{3,19},{19,3},{4,20},{20... | collective-permute-start | bytes 3932168 | tf_op jit(solution)/shard_map/ppermute | solution.py:221
  122.6 41.3 %collective-permute-start.4 = (bf16[512,768]{1,0:T(8,128)(2,1)S(1)}, bf16[512,768]{1,0:T(8,128)(2,1)}, u32[]{:S(2)}, u32[]{:S(2)}) collective-permute-start(bf16[512,768]{1,0:T(8,128)(2,1)S(1)} %copy-done.2), channel_id=1, source_target_pairs={{0,12},{4,0},{8,4},{12,8},{1,13},{5,1},{9,5},{13,9},{2,14},{6,2},{... | collective-permute-start | bytes 2359304 | tf_op jit(solution)/shard_map/ppermute | solution.py:217
  142.1 42.1 %collective-permute-start.3 = (bf16[512,768]{1,0:T(8,128)(2,1)}, bf16[512,768]{1,0:T(8,128)(2,1)S(1)}, u32[]{:S(2)}, u32[]{:S(2)}) collective-permute-start(bf16[512,768]{1,0:T(8,128)(2,1)} %collective-permute-done.2.refs_2_.refs_3_), channel_id=1, source_target_pairs={{0,16},{16,0},{1,17},{17,1},{2,18},{18,2},{3,19},{19,3},{4,20},{20... | collective-permute-start | bytes 2359304 | tf_op jit(solution)/shard_map/ppermute | solution.py:221
  144.6 35.0 %collective-permute-start.16 = (bf16[512,512]{1,0:T(8,128)(2,1)}, bf16[512,512]{1,0:T(8,128)(2,1)S(1)}, u32[]{:S(2)}, u32[]{:S(2)}) collective-permute-start(bf16[512,512]{1,0:T(8,128)(2,1)} %pack.11.refs_2_), channel_id=1, source_target_pairs={{0,8},{4,12},{8,0},{12,4},{1,9},{5,13},{9,1},{13,5},{2,10},{6,14},... | collective-permute-start | bytes 1572872 | tf_op jit(solution)/shard_map/ppermute | solution.py:217
  163.9 25.1 %collective-permute-start.5 = (bf16[512,768]{1,0:T(8,128)(2,1)}, bf16[512,768]{1,0:T(8,128)(2,1)}, u32[]{:S(2)}, u32[]{:S(2)}) collective-permute-start(bf16[512,768]{1,0:T(8,128)(2,1)} %collective-permute-done.4.refs_4_.refs_3_), channel_id=1, source_target_pairs={{0,16},{16,0},{1,17},{17,1},{2,18},{18,2},{3,19},{19,3},{4,20},{20... | collective-permute-start | bytes 2359304 | tf_op jit(solution)/shard_map/ppermute | solution.py:221
  179.6 2.5 copy-start.4
  179.6 18.1 %collective-permute-start.17 = (bf16[512,512]{1,0:T(8,128)(2,1)S(1)}, bf16[512,512]{1,0:T(8,128)(2,1)S(1)}, u32[]{:S(2)}, u32[]{:S(2)}) collective-permute-start(bf16[512,512]{1,0:T(8,128)(2,1)S(1)} %collective-permute-done.16.refs_3_.refs_0_), channel_id=1, source_target_pairs={{0,16},{16,0},{1,17},{17,1},{2,18},{18,2},{3,19},{19,3},{4,20},{20... | collective-permute-start | bytes 1572872 | tf_op jit(solution)/shard_map/ppermute | solution.py:221
  182.1 16.9 %collective-permute-start.9 = (bf16[512,512]{1,0:T(8,128)(2,1)}, bf16[512,512]{1,0:T(8,128)(2,1)S(1)}, u32[]{:S(2)}, u32[]{:S(2)}) collective-permute-start(bf16[512,512]{1,0:T(8,128)(2,1)} %pack.12.refs_2_), channel_id=1, source_target_pairs={{0,4},{4,8},{8,12},{12,0},{1,5},{5,9},{9,13},{13,1},{2,6},{6,10},{... | collective-permute-start | bytes 1572872 | tf_op jit(solution)/shard_map/ppermute | solution.py:217
  184.2 0.9 copy-start.10
  187.0 25.7 %collective-permute-start.11 = (bf16[512,512]{1,0:T(8,128)(2,1)}, bf16[512,512]{1,0:T(8,128)(2,1)S(1)}, u32[]{:S(2)}, u32[]{:S(2)}) collective-permute-start(bf16[512,512]{1,0:T(8,128)(2,1)} %pack.13.refs_2_), channel_id=1, source_target_pairs={{0,12},{4,0},{8,4},{12,8},{1,13},{5,1},{9,5},{13,9},{2,14},{6,2},{... | collective-permute-start | bytes 1572872 | tf_op jit(solution)/shard_map/ppermute | solution.py:217
  190.9 41.1 %collective-permute-start.18 = (bf16[512,512]{1,0:T(8,128)(2,1)}, bf16[512,512]{1,0:T(8,128)(2,1)S(1)}, u32[]{:S(2)}, u32[]{:S(2)}) collective-permute-start(bf16[512,512]{1,0:T(8,128)(2,1)} %pack.14.refs_2_), channel_id=1, source_target_pairs={{0,4},{4,8},{8,12},{12,0},{1,5},{5,9},{9,13},{13,1},{2,6},{6,10},{... | collective-permute-start | bytes 1572872 | tf_op jit(solution)/shard_map/ppermute | solution.py:217
  197.7 1.3 copy-start.5
  199.0 0.8 copy-start.6
  201.8 33.7 %collective-permute-start.20 = (bf16[512,512]{1,0:T(8,128)(2,1)}, bf16[512,512]{1,0:T(8,128)(2,1)S(1)}, u32[]{:S(2)}, u32[]{:S(2)}) collective-permute-start(bf16[512,512]{1,0:T(8,128)(2,1)} %pack.15), channel_id=1, source_target_pairs={{0,12},{4,0},{8,4},{12,8},{1,13},{5,1},{9,5},{13,9},{2,14},{6,2},{... | collective-permute-start | bytes 1572872 | tf_op jit(solution)/shard_map/ppermute | solution.py:217
  205.8 30.4 %collective-permute-start.10 = (bf16[512,512]{1,0:T(8,128)(2,1)}, bf16[512,512]{1,0:T(8,128)(2,1)S(1)}, u32[]{:S(2)}, u32[]{:S(2)}) collective-permute-start(bf16[512,512]{1,0:T(8,128)(2,1)} %copy-done.6), channel_id=1, source_target_pairs={{0,16},{16,0},{1,17},{17,1},{2,18},{18,2},{3,19},{19,3},{4,20},{20... | collective-permute-start | bytes 1572872 | tf_op jit(solution)/shard_map/ppermute | solution.py:221
  212.7 18.7 %copy-start.11 = (bf16[512,512]{1,0:T(8,128)(2,1)}, bf16[512,512]{1,0:T(8,128)(2,1)S(1)}, u32[]{:S(2)}) copy-start(bf16[512,512]{1,0:T(8,128)(2,1)S(1)} %collective-permute-done.11.refs_4_) | copy-start | bytes 1572868
  212.7 24.1 %collective-permute-start.12 = (bf16[512,512]{1,0:T(8,128)(2,1)S(1)}, bf16[512,512]{1,0:T(8,128)(2,1)S(1)}, u32[]{:S(2)}, u32[]{:S(2)}) collective-permute-start(bf16[512,512]{1,0:T(8,128)(2,1)S(1)} %collective-permute-done.11.refs_4_), channel_id=1, source_target_pairs={{0,16},{16,0},{1,17},{17,1},{2,18},{18,2},{3,19},{19,3},{4,20},{20... | collective-permute-start | bytes 1572872 | tf_op jit(solution)/shard_map/ppermute | solution.py:221
  231.5 20.9 %collective-permute-start.6 = (bf16[384,384]{1,0:T(8,128)(2,1)}, bf16[384,384]{1,0:T(8,128)(2,1)S(1)}, u32[]{:S(2)}, u32[]{:S(2)}) collective-permute-start(bf16[384,384]{1,0:T(8,128)(2,1)} %get-tuple-element.18), channel_id=1, source_target_pairs={{0,4},{4,8},{8,12},{12,0},{1,5},{5,9},{9,13},{13,1},{2,6},{6,10},{... | collective-permute-start | bytes 884744 | tf_op jit(solution)/shard_map/ppermute | solution.py:228
  232.1 3.4 %copy-start.7 = (bf16[512,512]{1,0:T(8,128)(2,1)}, bf16[512,512]{1,0:T(8,128)(2,1)S(1)}, u32[]{:S(2)}) copy-start(bf16[512,512]{1,0:T(8,128)(2,1)S(1)} %collective-permute-done.18.refs_0_) | copy-start | bytes 1572868
  232.1 46.4 %collective-permute-start.7 = (bf16[384,384]{1,0:T(8,128)(2,1)}, bf16[384,384]{1,0:T(8,128)(2,1)}, u32[]{:S(2)}, u32[]{:S(2)}) collective-permute-start(bf16[384,384]{1,0:T(8,128)(2,1)} %get-tuple-element.19), channel_id=1, source_target_pairs={{0,8},{4,12},{8,0},{12,4},{1,9},{5,13},{9,1},{13,5},{2,10},{6,14},... | collective-permute-start | bytes 884744 | tf_op jit(solution)/shard_map/ppermute | solution.py:228
  235.5 0.8 copy-start.8
  235.5 43.0 %collective-permute-start.8 = (bf16[384,384]{1,0:T(8,128)(2,1)}, bf16[384,384]{1,0:T(8,128)(2,1)S(1)}, u32[]{:S(2)}, u32[]{:S(2)}) collective-permute-start(bf16[384,384]{1,0:T(8,128)(2,1)} %get-tuple-element.20), channel_id=1, source_target_pairs={{0,12},{4,0},{8,4},{12,8},{1,13},{5,1},{9,5},{13,9},{2,14},{6,2},{... | collective-permute-start | bytes 884744 | tf_op jit(solution)/shard_map/ppermute | solution.py:228
  236.3 2.0 copy-start.12
  236.3 18.6 %collective-permute-start.19 = (bf16[512,512]{1,0:T(8,128)(2,1)}, bf16[512,512]{1,0:T(8,128)(2,1)S(1)}, u32[]{:S(2)}, u32[]{:S(2)}) collective-permute-start(bf16[512,512]{1,0:T(8,128)(2,1)} %hold.4.refs_2_), channel_id=1, source_target_pairs={{0,16},{16,0},{1,17},{17,1},{2,18},{18,2},{3,19},{19,3},{4,20},{20... | collective-permute-start | bytes 1572872 | tf_op jit(solution)/shard_map/ppermute | solution.py:221
  236.9 1.5 copy-start.13
  236.9 23.6 %collective-permute-start.21 = (bf16[512,512]{1,0:T(8,128)(2,1)}, bf16[512,512]{1,0:T(8,128)(2,1)S(1)}, u32[]{:S(2)}, u32[]{:S(2)}) collective-permute-start(bf16[512,512]{1,0:T(8,128)(2,1)} %hold.5.refs_4_), channel_id=1, source_target_pairs={{0,16},{16,0},{1,17},{17,1},{2,18},{18,2},{3,19},{19,3},{4,20},{20... | collective-permute-start | bytes 1572872 | tf_op jit(solution)/shard_map/ppermute | solution.py:221
  252.3 9.7 %copy-start.9 = (bf16[384,384]{1,0:T(8,128)(2,1)}, bf16[384,384]{1,0:T(8,128)(2,1)S(1)}, u32[]{:S(2)}) copy-start(bf16[384,384]{1,0:T(8,128)(2,1)S(1)} %collective-permute-done.6.refs_1_.refs_7_) | copy-start | bytes 884740
  252.3 22.7 %collective-permute-start.13 = (bf16[384,256]{1,0:T(8,128)(2,1)}, bf16[384,256]{1,0:T(8,128)(2,1)S(1)}, u32[]{:S(2)}, u32[]{:S(2)}) collective-permute-start(bf16[384,256]{1,0:T(8,128)(2,1)} %get-tuple-element.22), channel_id=1, source_target_pairs={{0,4},{4,8},{8,12},{12,0},{1,5},{5,9},{9,13},{13,1},{2,6},{6,10},{... | collective-permute-start | bytes 589832 | tf_op jit(solution)/shard_map/ppermute | solution.py:228
  254.9 7.2 %copy-start.14 = (bf16[512,512]{1,0:T(8,128)(2,1)}, bf16[512,512]{1,0:T(8,128)(2,1)S(1)}, u32[]{:S(2)}) copy-start(bf16[512,512]{1,0:T(8,128)(2,1)S(1)} %collective-permute-done.19.refs_3_) | copy-start | bytes 1572868
  254.9 20.7 %collective-permute-start.14 = (bf16[384,256]{1,0:T(8,128)(2,1)}, bf16[384,256]{1,0:T(8,128)(2,1)S(1)}, u32[]{:S(2)}, u32[]{:S(2)}) collective-permute-start(bf16[384,256]{1,0:T(8,128)(2,1)} %get-tuple-element.23), channel_id=1, source_target_pairs={{0,8},{4,12},{8,0},{12,4},{1,9},{5,13},{9,1},{13,5},{2,10},{6,14},... | collective-permute-start | bytes 589832 | tf_op jit(solution)/shard_map/ppermute | solution.py:228
  260.5 1.6 copy-start.15
  260.5 18.0 %collective-permute-start.15 = (bf16[384,256]{1,0:T(8,128)(2,1)}, bf16[384,256]{1,0:T(8,128)(2,1)S(1)}, u32[]{:S(2)}, u32[]{:S(2)}) collective-permute-start(bf16[384,256]{1,0:T(8,128)(2,1)} %get-tuple-element.24), channel_id=1, source_target_pairs={{0,12},{4,0},{8,4},{12,8},{1,13},{5,1},{9,5},{13,9},{2,14},{6,2},{... | collective-permute-start | bytes 589832 | tf_op jit(solution)/shard_map/ppermute | solution.py:228
  275.0 3.5 %copy-start.17 = (bf16[384,256]{1,0:T(8,128)(2,1)}, bf16[384,256]{1,0:T(8,128)(2,1)S(1)}, u32[]{:S(2)}) copy-start(bf16[384,256]{1,0:T(8,128)(2,1)S(1)} %collective-permute-done.13.refs_5_) | copy-start | bytes 589828
  275.0 14.4 %collective-permute-start.22 = (bf16[384,256]{1,0:T(8,128)(2,1)}, bf16[384,256]{1,0:T(8,128)(2,1)S(1)}, u32[]{:S(2)}, u32[]{:S(2)}) collective-permute-start(bf16[384,256]{1,0:T(8,128)(2,1)} %get-tuple-element.26), channel_id=1, source_target_pairs={{0,4},{4,8},{8,12},{12,0},{1,5},{5,9},{9,13},{13,1},{2,6},{6,10},{... | collective-permute-start | bytes 589832 | tf_op jit(solution)/shard_map/ppermute | solution.py:228
  275.6 2.9 copy-start.18
  275.6 15.9 %collective-permute-start.23 = (bf16[384,256]{1,0:T(8,128)(2,1)}, bf16[384,256]{1,0:T(8,128)(2,1)S(1)}, u32[]{:S(2)}, u32[]{:S(2)}) collective-permute-start(bf16[384,256]{1,0:T(8,128)(2,1)} %get-tuple-element.27), channel_id=1, source_target_pairs={{0,8},{4,12},{8,0},{12,4},{1,9},{5,13},{9,1},{13,5},{2,10},{6,14},... | collective-permute-start | bytes 589832 | tf_op jit(solution)/shard_map/ppermute | solution.py:228
  278.5 0.7 copy-start.19
  278.5 15.6 %collective-permute-start.24 = (bf16[384,256]{1,0:T(8,128)(2,1)}, bf16[384,256]{1,0:T(8,128)(2,1)S(1)}, u32[]{:S(2)}, u32[]{:S(2)}) collective-permute-start(bf16[384,256]{1,0:T(8,128)(2,1)} %get-tuple-element.28), channel_id=1, source_target_pairs={{0,12},{4,0},{8,4},{12,8},{1,13},{5,1},{9,5},{13,9},{2,14},{6,2},{... | collective-permute-start | bytes 589832 | tf_op jit(solution)/shard_map/ppermute | solution.py:228
  279.2 0.7 copy-start.16
  289.4 4.7 %copy-start.20 = (bf16[384,256]{1,0:T(8,128)(2,1)}, bf16[384,256]{1,0:T(8,128)(2,1)S(1)}, u32[]{:S(2)}) copy-start(bf16[384,256]{1,0:T(8,128)(2,1)S(1)} %collective-permute-done.22.refs_2_) | copy-start | bytes 589828
  291.5 2.6 copy-start.21
  294.1 0.7 copy-start.22
Sparse Core Ops, SparseCore 0:
  8.9 107.7 all-gather.2
  120.7 83.8 all-gather.4

commit v16 on v11

--- a/solution.py
+++ b/solution.py
@@ -239,13 +239,12 @@
             edges.append(edge)
     spans = list(zip(edges[:-1], edges[1:]))
 
-    def tokens_of(before_last_step, before_last_gather):
+    def tokens_of():
         lower, upper = [tokens], [tokens]
         for step in range(1, rows):
-            if step > 1 and step == rows - 1:
-                lower[-1], upper[-1] = hold(lower[-1], before_last_step), hold(upper[-1], before_last_step)
             lower.append(lax.ppermute(lower[-1], "row", [(i, i + 1) for i in range(step - 1, rows - 1)]))
             upper.append(lax.ppermute(upper[-1], "row", [(i, i - 1) for i in range(1, rows - step + 1)]))
+        before = [[], sent[:1]] + [[]] * (rows - 3) + [arrived[:1] + sent[1:4]]
         for slot in range(rows):
             chosen = {}
             for here, sources in enumerate(by_step(rows)):
@@ -253,7 +252,7 @@
             choices = [
                 (places, upper[offset] if offset > 0 else lower[-offset]) for offset, places in chosen.items()
             ]
-            value = pick(choices, before_last_gather if slot == rows - 1 else []) if slot else tokens
+            value = pick(choices, before[slot]) if slot else tokens
             whole.append(lax.all_gather(value, "col", axis=1, tiled=True))
 
     def weights(shift, low, high, users):
@@ -277,8 +276,7 @@
 
     last = len(spans) - 1
     far, *near = by_distance(rows)
-    plan = [(far, *spans[n], [n]) for n in range(max(last, 1))]
-    ahead = len(plan)
+    plan = [(far, 0, spans[max(last - 1, 0)][1], range(max(last, 1)))]
     for n, (low, high) in enumerate(spans):
         plan += [(shift, low, high, [n]) for shift in near]
         if n == 0 < last:
@@ -287,13 +285,13 @@
     held = [[] for _ in spans]
     whole = []
     for step in plan:
-        if last and len(sent) == max(len(plan) - 3, 3):
+        if last and len(sent) == max(len(plan) - 2, 3):
             hidden_of(0, [])
         weights(*step)
-        if len(sent) == min(ahead + 2, len(plan)):
-            tokens_of(arrived[:1], arrived[1:ahead] + sent[ahead:])
+        if len(sent) == min(4, max(len(plan) - 2, 3)):
+            tokens_of()
     for n in range(min(last, 1), last + 1):
-        hidden_of(n, done[-1:] + (returned[n - 2] if n > 1 else []))
+        hidden_of(n, done[-1:] + (returned[n - 2][:1] if n > 1 else []))
     early = len(blocks) - rows if last else len(blocks)
     out = place(blocks[:early], mine, ff)
     return place(blocks[early:], mine, ff, out) if last else out

time: 310 us -> 303 us (0.977)
  starting transfers between devices: 66.7 us -> 60.4 us
    ppermute x9 -> x8, waiting for transfers between devices: 83.3 us -> 100 us  [weights(): arrived.append(lax.ppermute(sent[-1], 'row', around(rows, shift)))]
    ppermute x9 -> x8, starting transfers between devices: 28.4 us -> 15.8 us  [weights(): arrived.append(lax.ppermute(sent[-1], 'row', around(rows, shift)))]
    ppermute x9 -> x8, waiting for transfers between devices: 15.7 us -> 8.09 us  [weights(): swapped.append(lax.ppermute(came, 'parts', around(parts, -turn)))]
    ppermute x3, waiting for transfers between devices: 32.1 us -> 27.3 us  [tokens_of(): lax.ppermute(upper[-1], 'row', [(i, i - 1) for i in range(1, rows - step...]
    ppermute x9, waiting for transfers between devices: 16.6 us -> 12.3 us  [hidden_of(): lax.ppermute(outs[shift], 'row', around(rows, shift))]
    ppermute x9 -> x8, starting transfers between devices: 8.83 us -> 10.9 us  [weights(): swapped.append(lax.ppermute(came, 'parts', around(parts, -turn)))]
    pallas_call x9 -> x8, Pallas kernels: 18.4 us -> 16.6 us  [pack(): pl.pallas_call(body, out_shape=jax.ShapeDtypeStruct((share, 2 * wide), ga...]
    unnamed x64 -> x60, local copies, waits for them, and re-layouts: 9.07 us -> 7.69 us
  transfers between devices with their start and end apart: 37 -> 35, of which waited for: 14 -> 16; matrix products, arithmetic and copies ran while one was open for 0% -> 0% of each run, Pallas kernels for 22% -> 22%
where the time goes in v16:
time: 303 us; the launch traced here: 301 us
  waiting for transfers between devices  152 us (50%)
  Pallas kernels  67.5 us (22%)
  starting transfers between devices  60.4 us (20%)
  between operations  13.5 us (4%)
  local copies, waits for them, and re-layouts  7.69 us (3%)
    ppermute x8, waiting for transfers between devices, weights(): arrived.append(lax.ppermute(sent[-1], 'row', around(rows, shift)))  100 us
    pallas_call x3, Pallas kernels, product(): pl.pallas_call(body, out_shape=[jax.ShapeDtypeStruct((mine, wide), jnp.bf...  40.3 us
    ppermute x3, waiting for transfers between devices, tokens_of(): lax.ppermute(upper[-1], 'row', [(i, i - 1) for i in range(1, rows - step...  27.3 us
    pallas_call x8, Pallas kernels, pack(): pl.pallas_call(body, out_shape=jax.ShapeDtypeStruct((share, 2 * wide), ga...  16.6 us
    ppermute x8, starting transfers between devices, weights(): arrived.append(lax.ppermute(sent[-1], 'row', around(rows, shift)))  15.8 us
    ppermute x9, starting transfers between devices, hidden_of(): lax.ppermute(outs[shift], 'row', around(rows, shift))  15.7 us
    ppermute x9, waiting for transfers between devices, hidden_of(): lax.ppermute(outs[shift], 'row', around(rows, shift))  12.3 us
    ppermute x8, starting transfers between devices, weights(): swapped.append(lax.ppermute(came, 'parts', around(parts, -turn)))  10.9 us
  transfers between devices with their start and end apart: 35, of which 16 were waited for; matrix products, arithmetic and copies ran while one was open for 0% of the time, Pallas kernels for 22%

profile of v16, /device:TPU:12, one launch (start us, length us, event | category | flops | bytes accessed | tf_op | source)
XLA Modules:
  0.0 301.1 jit_solution(732009221417802403)
XLA Ops:
  7.3 2.4 collective-permute-start
  9.7 3.5 %collective-permute-start.1 = (bf16[384,1024]{1,0:T(8,128)(2,1)}, bf16[384,1024]{1,0:T(8,128)(2,1)S(1)}, u32[]{:S(2)}, u32[]{:S(2)}) collective-permute-start(bf16[384,1024]{1,0:T(8,128)(2,1)} %param.3), channel_id=1, source_target_pairs={{0,4},{4,8},{8,12},{1,5},{5,9},{9,13},{2,6},{6,10},{10,14},{3,7},{... | collective-permute-start | bytes 2359304 | tf_op jit(solution)/shard_map/ppermute | solution.py:245
  13.2 2.6 pack.8.refs_2_
  15.7 13.0 %collective-permute-done.refs_0_.refs_2_ = bf16[384,1024]{1,0:T(8,128)(2,1)S(1)} collective-permute-done((bf16[384,1024]{1,0:T(8,128)(2,1)}, bf16[384,1024]{1,0:T(8,128)(2,1)S(1)}, u32[]{:S(2)}, u32[]{:S(2)}) %collective-permute-start) | collective-permute-done | bytes 786464 | tf_op jit(solution)/shard_map/ppermute | solution.py:246
  28.7 2.1 collective-permute-done.1.refs_1_
  30.8 0.9 copy-done.7
  31.7 2.0 pick.3
  33.8 1.9 collective-permute-start.2
  35.7 4.0 %collective-permute-start.3 = (bf16[384,1024]{1,0:T(8,128)(2,1)}, bf16[384,1024]{1,0:T(8,128)(2,1)S(1)}, u32[]{:S(2)}, u32[]{:S(2)}) collective-permute-start(bf16[384,1024]{1,0:T(8,128)(2,1)} %copy-done.7), channel_id=1, source_target_pairs={{4,8},{8,12},{5,9},{9,13},{6,10},{10,14},{7,11},{11,15},{20,24},{2... | collective-permute-start | bytes 2359304 | tf_op jit(solution)/shard_map/ppermute | solution.py:245
  39.7 14.4 %collective-permute-done.2.refs_0_ = bf16[384,1024]{1,0:T(8,128)(2,1)S(1)} collective-permute-done((bf16[384,1024]{1,0:T(8,128)(2,1)}, bf16[384,1024]{1,0:T(8,128)(2,1)S(1)}, u32[]{:S(2)}, u32[]{:S(2)}) %collective-permute-start.2) | collective-permute-done | bytes 786464 | tf_op jit(solution)/shard_map/ppermute | solution.py:246
  54.1 1.3 collective-permute-done.3.refs_1_
  55.4 0.9 copy-done.17
  56.3 2.1 pick.4
  58.4 2.2 collective-permute-start.6
  60.6 4.6 %collective-permute-start.4 = (bf16[384,1024]{1,0:T(8,128)(2,1)}, bf16[384,1024]{1,0:T(8,128)(2,1)}, u32[]{:S(2)}, u32[]{:S(2)}) collective-permute-start(bf16[384,1024]{1,0:T(8,128)(2,1)} %copy-done.16), channel_id=1, source_target_pairs={{4,0},{5,1},{6,2},{7,3},{20,16},{21,17},{22,18},{23,19}} | collective-permute-start | bytes 2359304 | tf_op jit(solution)/shard_map/ppermute | solution.py:246
  65.2 1.6 collective-permute-start.5
  66.8 2.2 pack.9.refs_2_.refs_5_
  69.0 2.2 pack.10.refs_2_.refs_6_
  71.2 43.7 %collective-permute-done.6.refs_3_.refs_4_.refs_6_ = bf16[512,1280]{1,0:T(8,128)(2,1)S(1)} collective-permute-done((bf16[512,1280]{1,0:T(8,128)(2,1)S(1)}, bf16[512,1280]{1,0:T(8,128)(2,1)S(1)}, u32[]{:S(2)}, u32[]{:S(2)}) %collective-permute-start.6) | collective-permute-done | bytes 1310752 | tf_op jit(solution)/shard_map/ppermute | solution.py:261
  114.8 1.1 copy-done
  115.9 1.9 pack.11.refs_7_.refs_2_
  117.9 2.2 pick.5
  120.5 1.0 collective-permute-start.7
  121.4 2.0 collective-permute-start.10
  123.5 17.4 %collective-permute-done.8.refs_8_.refs_3_ = bf16[512,768]{1,0:T(8,128)(2,1)} collective-permute-done((bf16[512,768]{1,0:T(8,128)(2,1)S(1)}, bf16[512,768]{1,0:T(8,128)(2,1)}, u32[]{:S(2)}, u32[]{:S(2)}) %collective-permute-start.8) | collective-permute-done | bytes 786464 | tf_op jit(solution)/shard_map/ppermute | solution.py:261
  140.9 1.0 collective-permute-start.9
  141.8 1.8 collective-permute-start.22
  143.7 26.7 %collective-permute-done.10.refs_10_.refs_3_ = bf16[512,768]{1,0:T(8,128)(2,1)} collective-permute-done((bf16[512,768]{1,0:T(8,128)(2,1)S(1)}, bf16[512,768]{1,0:T(8,128)(2,1)}, u32[]{:S(2)}, u32[]{:S(2)}) %collective-permute-start.10) | collective-permute-done | bytes 786464 | tf_op jit(solution)/shard_map/ppermute | solution.py:261
  170.4 1.0 collective-permute-start.11
  171.4 6.9 %collective-permute-done.22.refs_3_.refs_6_ = bf16[512,512]{1,0:T(8,128)(2,1)S(1)} collective-permute-done((bf16[512,512]{1,0:T(8,128)(2,1)S(1)}, bf16[512,512]{1,0:T(8,128)(2,1)S(1)}, u32[]{:S(2)}, u32[]{:S(2)}) %collective-permute-start.22) | collective-permute-done | bytes 524320 | tf_op jit(solution)/shard_map/ppermute | solution.py:261
  178.3 1.0 collective-permute-start.23
  179.2 1.9 pack.12.refs_2_
  181.2 2.0 collective-permute-start.15
  183.2 0.9 copy-done.14
  184.1 2.0 pack.13.refs_2_
  186.1 2.0 collective-permute-start.17
  188.1 0.9 copy-done.15
  189.0 1.9 pack.14.refs_2_
  190.9 1.5 collective-permute-start.24
  192.4 3.2 %collective-permute-done.23.refs_4_.refs_7_ = bf16[512,512]{1,0:T(8,128)(2,1)S(1)} collective-permute-done((bf16[512,512]{1,0:T(8,128)(2,1)S(1)}, bf16[512,512]{1,0:T(8,128)(2,1)S(1)}, u32[]{:S(2)}, u32[]{:S(2)}) %collective-permute-start.23) | collective-permute-done | bytes 524320 | tf_op jit(solution)/shard_map/ppermute | solution.py:265
  195.7 2.5 collective-permute-done.15.refs_8_.refs_3_
  198.2 0.8 copy-done.10
  199.0 2.0 pack.15
  201.0 3.9 %collective-permute-start.26 = (bf16[512,512]{1,0:T(8,128)(2,1)}, bf16[512,512]{1,0:T(8,128)(2,1)S(1)}, u32[]{:S(2)}, u32[]{:S(2)}) collective-permute-start(bf16[512,512]{1,0:T(8,128)(2,1)} %pack.15), channel_id=1, source_target_pairs={{0,12},{4,0},{8,4},{12,8},{1,13},{5,1},{9,5},{13,9},{2,14},{6,2},{... | collective-permute-start | bytes 1572872 | tf_op jit(solution)/shard_map/ppermute | solution.py:261
  204.9 4.1 %collective-permute-start.16 = (bf16[512,512]{1,0:T(8,128)(2,1)}, bf16[512,512]{1,0:T(8,128)(2,1)S(1)}, u32[]{:S(2)}, u32[]{:S(2)}) collective-permute-start(bf16[512,512]{1,0:T(8,128)(2,1)} %copy-done.10), channel_id=1, source_target_pairs={{0,16},{16,0},{1,17},{17,1},{2,18},{18,2},{3,19},{19,3},{4,20},{20... | collective-permute-start | bytes 1572872 | tf_op jit(solution)/shard_map/ppermute | solution.py:265
  209.0 2.9 collective-permute-done.17.refs_10_
  211.9 0.8 collective-permute-start.18
  212.8 16.5 %product.3 = (bf16[384,384]{1,0:T(8,128)(2,1)}, bf16[384,384]{1,0:T(8,128)(2,1)}, bf16[384,384]{1,0:T(8,128)(2,1)}, bf16[384,384]{1,0:T(8,128)(2,1)}) custom-call(bf16[384,4096]{1,0:T(8,128)(2,1)} %all-gather.5.cloned.1.call-done.refs_0_, bf16[384,4096]{1,0:T(8,128)(2,1)} %all-gather.7.cloned.1.call-done.refs_1_, ...), custom_call_target="tpu_custom_call" | custom-call | flops 9663676416 | bytes 20054016 | tf_op jit(solution)/shard_map/product/pallas_call | solution.py:138
  229.9 5.3 %collective-permute-start.13 = (bf16[384,384]{1,0:T(8,128)(2,1)}, bf16[384,384]{1,0:T(8,128)(2,1)S(1)}, u32[]{:S(2)}, u32[]{:S(2)}) collective-permute-start(bf16[384,384]{1,0:T(8,128)(2,1)} %get-tuple-element.19), channel_id=1, source_target_pairs={{0,8},{4,12},{8,0},{12,4},{1,9},{5,13},{9,1},{13,5},{2,10},{6,14},... | collective-permute-start | bytes 884744 | tf_op jit(solution)/shard_map/ppermute | solution.py:272
  236.1 1.3 collective-permute-start.25
  238.1 11.9 %product.4 = (bf16[384,256]{1,0:T(8,128)(2,1)}, bf16[384,256]{1,0:T(8,128)(2,1)}, bf16[384,256]{1,0:T(8,128)(2,1)}, bf16[384,256]{1,0:T(8,128)(2,1)}) custom-call(bf16[384,4096]{1,0:T(8,128)(2,1)} %all-gather.5.cloned.1.call-done.refs_0_, bf16[384,4096]{1,0:T(8,128)(2,1)} %all-gather.7.cloned.1.call-done.refs_1_, ...), custom_call_target="tpu_custom_call" | custom-call | flops 6442450944 | bytes 17563648 | tf_op jit(solution)/shard_map/product/pallas_call | solution.py:138
  250.0 2.5 collective-permute-start.19
  252.5 1.4 collective-permute-start.20
  253.9 4.8 %collective-permute-done.27.refs_11_ = bf16[512,512]{1,0:T(8,128)(2,1)S(1)} collective-permute-done((bf16[512,512]{1,0:T(8,128)(2,1)}, bf16[512,512]{1,0:T(8,128)(2,1)S(1)}, u32[]{:S(2)}, u32[]{:S(2)}) %collective-permute-start.27) | collective-permute-done | bytes 524320 | tf_op jit(solution)/shard_map/ppermute | solution.py:265
  258.8 1.0 collective-permute-start.21
  259.8 11.9 %product.5 = (bf16[384,256]{1,0:T(8,128)(2,1)}, bf16[384,256]{1,0:T(8,128)(2,1)}, bf16[384,256]{1,0:T(8,128)(2,1)}, bf16[384,256]{1,0:T(8,128)(2,1)}) custom-call(bf16[384,4096]{1,0:T(8,128)(2,1)} %all-gather.5.cloned.1.call-done.refs_0_, bf16[384,4096]{1,0:T(8,128)(2,1)} %all-gather.7.cloned.1.call-done.refs_1_, ...), custom_call_target="tpu_custom_call" | custom-call | flops 6442450944 | bytes 17563648 | tf_op jit(solution)/shard_map/product/pallas_call | solution.py:138
  271.7 1.0 collective-permute-start.28
  272.7 3.4 %collective-permute-done.20.refs_6_ = bf16[384,256]{1,0:T(8,128)(2,1)S(1)} collective-permute-done((bf16[384,256]{1,0:T(8,128)(2,1)}, bf16[384,256]{1,0:T(8,128)(2,1)S(1)}, u32[]{:S(2)}, u32[]{:S(2)}) %collective-permute-start.20) | collective-permute-done | bytes 196640 | tf_op jit(solution)/shard_map/ppermute | solution.py:272
  276.1 3.8 %collective-permute-start.29 = (bf16[384,256]{1,0:T(8,128)(2,1)}, bf16[384,256]{1,0:T(8,128)(2,1)S(1)}, u32[]{:S(2)}, u32[]{:S(2)}) collective-permute-start(bf16[384,256]{1,0:T(8,128)(2,1)} %get-tuple-element.27), channel_id=1, source_target_pairs={{0,8},{4,12},{8,0},{12,4},{1,9},{5,13},{9,1},{13,5},{2,10},{6,14},... | collective-permute-start | bytes 589832 | tf_op jit(solution)/shard_map/ppermute | solution.py:272
  279.9 3.4 %collective-permute-done.21.refs_7_ = bf16[384,256]{1,0:T(8,128)(2,1)S(1)} collective-permute-done((bf16[384,256]{1,0:T(8,128)(2,1)}, bf16[384,256]{1,0:T(8,128)(2,1)S(1)}, u32[]{:S(2)}, u32[]{:S(2)}) %collective-permute-start.21) | collective-permute-done | bytes 196640 | tf_op jit(solution)/shard_map/ppermute | solution.py:272
  284.0 2.4 place.2.refs_0_
  286.4 2.2 collective-permute-done.29.refs_3_
  288.6 3.3 %collective-permute-done.30.refs_4_ = bf16[384,256]{1,0:T(8,128)(2,1)S(1)} collective-permute-done((bf16[384,256]{1,0:T(8,128)(2,1)}, bf16[384,256]{1,0:T(8,128)(2,1)S(1)}, u32[]{:S(2)}, u32[]{:S(2)}) %collective-permute-start.30) | collective-permute-done | bytes 196640 | tf_op jit(solution)/shard_map/ppermute | solution.py:272
  292.6 2.0 place.3
  (88 shorter events, 5.0 us)
Async XLA Ops:
  6.5 206.2 %all-gather.5.cloned.1.call-start = ((), (), s32[]{:S(2)}) async-start(), calls=%async_computation | async-start | bytes 3932160 | tf_op jit(solution)/shard_map/all_gather | solution.py:256
  7.3 205.5 %all-gather.7.cloned.1.call-start = ((), (), s32[]{:S(2)}) async-start(), calls=%async_computation.1 | async-start | bytes 3932160 | tf_op jit(solution)/shard_map/all_gather | solution.py:256
  7.3 21.4 %collective-permute-start = (bf16[384,1024]{1,0:T(8,128)(2,1)}, bf16[384,1024]{1,0:T(8,128)(2,1)S(1)}, u32[]{:S(2)}, u32[]{:S(2)}) collective-permute-start(bf16[384,1024]{1,0:T(8,128)(2,1)} %param.3), channel_id=1, source_target_pairs={{4,0},{8,4},{12,8},{5,1},{9,5},{13,9},{6,2},{10,6},{14,10},{7,3},{... | collective-permute-start | bytes 2359304 | tf_op jit(solution)/shard_map/ppermute | solution.py:246
  9.7 21.1 %collective-permute-start.1 = (bf16[384,1024]{1,0:T(8,128)(2,1)}, bf16[384,1024]{1,0:T(8,128)(2,1)S(1)}, u32[]{:S(2)}, u32[]{:S(2)}) collective-permute-start(bf16[384,1024]{1,0:T(8,128)(2,1)} %param.3), channel_id=1, source_target_pairs={{0,4},{4,8},{8,12},{1,5},{5,9},{9,13},{2,6},{6,10},{10,14},{3,7},{... | collective-permute-start | bytes 2359304 | tf_op jit(solution)/shard_map/ppermute | solution.py:245
  15.7 42.7 %copy-start.2 = (bf16[512,1280]{1,0:T(8,128)(2,1)S(1)}, bf16[512,1280]{1,0:T(8,128)(2,1)}, u32[]{:S(2)}) copy-start(bf16[512,1280]{1,0:T(8,128)(2,1)} %pack.8.refs_2_) | copy-start | bytes 3932164
  28.7 2.1 copy-start.6
  30.8 0.9 copy-start.7
  33.7 179.0 %all-gather.9.cloned.1.call-start = ((), (), s32[]{:S(2)}) async-start(), calls=%async_computation.2 | async-start | bytes 3932160 | tf_op jit(solution)/shard_map/all_gather | solution.py:256
  33.8 20.3 %collective-permute-start.2 = (bf16[384,1024]{1,0:T(8,128)(2,1)}, bf16[384,1024]{1,0:T(8,128)(2,1)S(1)}, u32[]{:S(2)}, u32[]{:S(2)}) collective-permute-start(bf16[384,1024]{1,0:T(8,128)(2,1)} %copy-done.6), channel_id=1, source_target_pairs={{4,0},{8,4},{5,1},{9,5},{6,2},{10,6},{7,3},{11,7},{20,16},{24,20},... | collective-permute-start | bytes 2359304 | tf_op jit(solution)/shard_map/ppermute | solution.py:246
  35.7 19.7 %collective-permute-start.3 = (bf16[384,1024]{1,0:T(8,128)(2,1)}, bf16[384,1024]{1,0:T(8,128)(2,1)S(1)}, u32[]{:S(2)}, u32[]{:S(2)}) collective-permute-start(bf16[384,1024]{1,0:T(8,128)(2,1)} %copy-done.7), channel_id=1, source_target_pairs={{4,8},{8,12},{5,9},{9,13},{6,10},{10,14},{7,11},{11,15},{20,24},{2... | collective-permute-start | bytes 2359304 | tf_op jit(solution)/shard_map/ppermute | solution.py:245
  54.1 1.3 copy-start.16
  55.4 0.9 copy-start.17
  58.4 154.4 %all-gather.11.cloned.1.call-start = ((), (), s32[]{:S(2)}) async-start(), calls=%async_computation.3 | async-start | bytes 3932160 | tf_op jit(solution)/shard_map/all_gather | solution.py:256
  58.4 56.4 %collective-permute-start.6 = (bf16[512,1280]{1,0:T(8,128)(2,1)S(1)}, bf16[512,1280]{1,0:T(8,128)(2,1)S(1)}, u32[]{:S(2)}, u32[]{:S(2)}) collective-permute-start(bf16[512,1280]{1,0:T(8,128)(2,1)S(1)} %copy-done.2), channel_id=1, source_target_pairs={{0,8},{4,12},{8,0},{12,4},{1,9},{5,13},{9,1},{13,5},{2,10},{6,14},... | collective-permute-start | bytes 3932168 | tf_op jit(solution)/shard_map/ppermute | solution.py:261
  60.6 57.3 %collective-permute-start.4 = (bf16[384,1024]{1,0:T(8,128)(2,1)}, bf16[384,1024]{1,0:T(8,128)(2,1)}, u32[]{:S(2)}, u32[]{:S(2)}) collective-permute-start(bf16[384,1024]{1,0:T(8,128)(2,1)} %copy-done.16), channel_id=1, source_target_pairs={{4,0},{5,1},{6,2},{7,3},{20,16},{21,17},{22,18},{23,19}} | collective-permute-start | bytes 2359304 | tf_op jit(solution)/shard_map/ppermute | solution.py:246
  65.2 52.7 %collective-permute-start.5 = (bf16[384,1024]{1,0:T(8,128)(2,1)}, bf16[384,1024]{1,0:T(8,128)(2,1)}, u32[]{:S(2)}, u32[]{:S(2)}) collective-permute-start(bf16[384,1024]{1,0:T(8,128)(2,1)} %copy-done.17), channel_id=1, source_target_pairs={{8,12},{9,13},{10,14},{11,15},{24,28},{25,29},{26,30},{27,31}} | collective-permute-start | bytes 2359304 | tf_op jit(solution)/shard_map/ppermute | solution.py:245
  114.8 1.1 copy-start
  117.8 2.3 copy-start.4
  117.8 2.6 copy-start.1
  117.9 3.6 %copy-start.3 = (bf16[512,768]{1,0:T(8,128)(2,1)S(1)}, bf16[512,768]{1,0:T(8,128)(2,1)}, u32[]{:S(2)}) copy-start(bf16[512,768]{1,0:T(8,128)(2,1)} %pack.10.refs_2_.refs_6_) | copy-start | bytes 2359300
  117.9 24.0 %copy-start.5 = (bf16[512,512]{1,0:T(8,128)(2,1)S(1)}, bf16[512,512]{1,0:T(8,128)(2,1)}, u32[]{:S(2)}) copy-start(bf16[512,512]{1,0:T(8,128)(2,1)} %pack.11.refs_7_.refs_2_) | copy-start | bytes 1572868
  120.1 20.7 %collective-permute-start.8 = (bf16[512,768]{1,0:T(8,128)(2,1)S(1)}, bf16[512,768]{1,0:T(8,128)(2,1)}, u32[]{:S(2)}, u32[]{:S(2)}) collective-permute-start(bf16[512,768]{1,0:T(8,128)(2,1)S(1)} %copy-done.4), channel_id=1, source_target_pairs={{0,4},{4,8},{8,12},{12,0},{1,5},{5,9},{9,13},{13,1},{2,6},{6,10},{... | collective-permute-start | bytes 2359304 | tf_op jit(solution)/shard_map/ppermute | solution.py:261
  120.5 58.8 %collective-permute-start.7 = (bf16[512,1280]{1,0:T(8,128)(2,1)S(1)}, bf16[512,1280]{1,0:T(8,128)(2,1)}, u32[]{:S(2)}, u32[]{:S(2)}) collective-permute-start(bf16[512,1280]{1,0:T(8,128)(2,1)S(1)} %copy-done.1), channel_id=1, source_target_pairs={{0,16},{16,0},{1,17},{17,1},{2,18},{18,2},{3,19},{19,3},{4,20},{20... | collective-permute-start | bytes 3932168 | tf_op jit(solution)/shard_map/ppermute | solution.py:265
  121.4 48.9 %collective-permute-start.10 = (bf16[512,768]{1,0:T(8,128)(2,1)S(1)}, bf16[512,768]{1,0:T(8,128)(2,1)}, u32[]{:S(2)}, u32[]{:S(2)}) collective-permute-start(bf16[512,768]{1,0:T(8,128)(2,1)S(1)} %copy-done.3), channel_id=1, source_target_pairs={{0,12},{4,0},{8,4},{12,8},{1,13},{5,1},{9,5},{13,9},{2,14},{6,2},{... | collective-permute-start | bytes 2359304 | tf_op jit(solution)/shard_map/ppermute | solution.py:261
  140.9 42.4 %collective-permute-start.9 = (bf16[512,768]{1,0:T(8,128)(2,1)}, bf16[512,768]{1,0:T(8,128)(2,1)S(1)}, u32[]{:S(2)}, u32[]{:S(2)}) collective-permute-start(bf16[512,768]{1,0:T(8,128)(2,1)} %collective-permute-done.8.refs_8_.refs_3_), channel_id=1, source_target_pairs={{0,16},{16,0},{1,17},{17,1},{2,18},{18,2},{3,19},{19,3},{4,20},{20... | collective-permute-start | bytes 2359304 | tf_op jit(solution)/shard_map/ppermute | solution.py:265
  141.8 36.4 %collective-permute-start.22 = (bf16[512,512]{1,0:T(8,128)(2,1)S(1)}, bf16[512,512]{1,0:T(8,128)(2,1)S(1)}, u32[]{:S(2)}, u32[]{:S(2)}) collective-permute-start(bf16[512,512]{1,0:T(8,128)(2,1)S(1)} %copy-done.5), channel_id=1, source_target_pairs={{0,8},{4,12},{8,0},{12,4},{1,9},{5,13},{9,1},{13,5},{2,10},{6,14},... | collective-permute-start | bytes 1572872 | tf_op jit(solution)/shard_map/ppermute | solution.py:261
  170.4 17.7 %collective-permute-start.11 = (bf16[512,768]{1,0:T(8,128)(2,1)}, bf16[512,768]{1,0:T(8,128)(2,1)S(1)}, u32[]{:S(2)}, u32[]{:S(2)}) collective-permute-start(bf16[512,768]{1,0:T(8,128)(2,1)} %collective-permute-done.10.refs_10_.refs_3_), channel_id=1, source_target_pairs={{0,16},{16,0},{1,17},{17,1},{2,18},{18,2},{3,19},{19,3},{4,20},{20... | collective-permute-start | bytes 2359304 | tf_op jit(solution)/shard_map/ppermute | solution.py:265
  178.3 2.9 copy-start.8
  178.3 17.4 %collective-permute-start.23 = (bf16[512,512]{1,0:T(8,128)(2,1)S(1)}, bf16[512,512]{1,0:T(8,128)(2,1)S(1)}, u32[]{:S(2)}, u32[]{:S(2)}) collective-permute-start(bf16[512,512]{1,0:T(8,128)(2,1)S(1)} %collective-permute-done.22.refs_3_.refs_6_), channel_id=1, source_target_pairs={{0,16},{16,0},{1,17},{17,1},{2,18},{18,2},{3,19},{19,3},{4,20},{20... | collective-permute-start | bytes 1572872 | tf_op jit(solution)/shard_map/ppermute | solution.py:265
  181.2 17.0 %collective-permute-start.15 = (bf16[512,512]{1,0:T(8,128)(2,1)}, bf16[512,512]{1,0:T(8,128)(2,1)S(1)}, u32[]{:S(2)}, u32[]{:S(2)}) collective-permute-start(bf16[512,512]{1,0:T(8,128)(2,1)} %pack.12.refs_2_), channel_id=1, source_target_pairs={{0,4},{4,8},{8,12},{12,0},{1,5},{5,9},{9,13},{13,1},{2,6},{6,10},{... | collective-permute-start | bytes 1572872 | tf_op jit(solution)/shard_map/ppermute | solution.py:261
  183.2 0.9 copy-start.14
  186.1 25.8 %collective-permute-start.17 = (bf16[512,512]{1,0:T(8,128)(2,1)}, bf16[512,512]{1,0:T(8,128)(2,1)S(1)}, u32[]{:S(2)}, u32[]{:S(2)}) collective-permute-start(bf16[512,512]{1,0:T(8,128)(2,1)} %pack.13.refs_2_), channel_id=1, source_target_pairs={{0,12},{4,0},{8,4},{12,8},{1,13},{5,1},{9,5},{13,9},{2,14},{6,2},{... | collective-permute-start | bytes 1572872 | tf_op jit(solution)/shard_map/ppermute | solution.py:261
  188.1 0.9 copy-start.15
  190.9 39.0 %collective-permute-start.24 = (bf16[512,512]{1,0:T(8,128)(2,1)}, bf16[512,512]{1,0:T(8,128)(2,1)S(1)}, u32[]{:S(2)}, u32[]{:S(2)}) collective-permute-start(bf16[512,512]{1,0:T(8,128)(2,1)} %pack.14.refs_2_), channel_id=1, source_target_pairs={{0,4},{4,8},{8,12},{12,0},{1,5},{5,9},{9,13},{13,1},{2,6},{6,10},{... | collective-permute-start | bytes 1572872 | tf_op jit(solution)/shard_map/ppermute | solution.py:261
  195.7 2.5 copy-start.9
  198.2 0.8 copy-start.10
  201.0 34.3 %collective-permute-start.26 = (bf16[512,512]{1,0:T(8,128)(2,1)}, bf16[512,512]{1,0:T(8,128)(2,1)S(1)}, u32[]{:S(2)}, u32[]{:S(2)}) collective-permute-start(bf16[512,512]{1,0:T(8,128)(2,1)} %pack.15), channel_id=1, source_target_pairs={{0,12},{4,0},{8,4},{12,8},{1,13},{5,1},{9,5},{13,9},{2,14},{6,2},{... | collective-permute-start | bytes 1572872 | tf_op jit(solution)/shard_map/ppermute | solution.py:261
  204.9 31.2 %collective-permute-start.16 = (bf16[512,512]{1,0:T(8,128)(2,1)}, bf16[512,512]{1,0:T(8,128)(2,1)S(1)}, u32[]{:S(2)}, u32[]{:S(2)}) collective-permute-start(bf16[512,512]{1,0:T(8,128)(2,1)} %copy-done.10), channel_id=1, source_target_pairs={{0,16},{16,0},{1,17},{17,1},{2,18},{18,2},{3,19},{19,3},{4,20},{20... | collective-permute-start | bytes 1572872 | tf_op jit(solution)/shard_map/ppermute | solution.py:265
  211.9 17.4 %copy-start.18 = (bf16[512,512]{1,0:T(8,128)(2,1)}, bf16[512,512]{1,0:T(8,128)(2,1)S(1)}, u32[]{:S(2)}) copy-start(bf16[512,512]{1,0:T(8,128)(2,1)S(1)} %collective-permute-done.17.refs_10_) | copy-start | bytes 1572868
  211.9 25.4 %collective-permute-start.18 = (bf16[512,512]{1,0:T(8,128)(2,1)S(1)}, bf16[512,512]{1,0:T(8,128)(2,1)S(1)}, u32[]{:S(2)}, u32[]{:S(2)}) collective-permute-start(bf16[512,512]{1,0:T(8,128)(2,1)S(1)} %collective-permute-done.17.refs_10_), channel_id=1, source_target_pairs={{0,16},{16,0},{1,17},{17,1},{2,18},{18,2},{3,19},{19,3},{4,20},{20... | collective-permute-start | bytes 1572872 | tf_op jit(solution)/shard_map/ppermute | solution.py:265
  229.3 20.7 %collective-permute-start.12 = (bf16[384,384]{1,0:T(8,128)(2,1)}, bf16[384,384]{1,0:T(8,128)(2,1)S(1)}, u32[]{:S(2)}, u32[]{:S(2)}) collective-permute-start(bf16[384,384]{1,0:T(8,128)(2,1)} %get-tuple-element.18), channel_id=1, source_target_pairs={{0,4},{4,8},{8,12},{12,0},{1,5},{5,9},{9,13},{13,1},{2,6},{6,10},{... | collective-permute-start | bytes 884744 | tf_op jit(solution)/shard_map/ppermute | solution.py:272
  229.9 5.3 %copy-start.11 = (bf16[512,512]{1,0:T(8,128)(2,1)}, bf16[512,512]{1,0:T(8,128)(2,1)S(1)}, u32[]{:S(2)}) copy-start(bf16[512,512]{1,0:T(8,128)(2,1)S(1)} %collective-permute-done.24.refs_0_) | copy-start | bytes 1572868
  229.9 53.3 %collective-permute-start.13 = (bf16[384,384]{1,0:T(8,128)(2,1)}, bf16[384,384]{1,0:T(8,128)(2,1)S(1)}, u32[]{:S(2)}, u32[]{:S(2)}) collective-permute-start(bf16[384,384]{1,0:T(8,128)(2,1)} %get-tuple-element.19), channel_id=1, source_target_pairs={{0,8},{4,12},{8,0},{12,4},{1,9},{5,13},{9,1},{13,5},{2,10},{6,14},... | collective-permute-start | bytes 884744 | tf_op jit(solution)/shard_map/ppermute | solution.py:272
  235.2 0.8 copy-start.12
  235.2 48.0 %collective-permute-start.14 = (bf16[384,384]{1,0:T(8,128)(2,1)}, bf16[384,384]{1,0:T(8,128)(2,1)}, u32[]{:S(2)}, u32[]{:S(2)}) collective-permute-start(bf16[384,384]{1,0:T(8,128)(2,1)} %get-tuple-element.20), channel_id=1, source_target_pairs={{0,12},{4,0},{8,4},{12,8},{1,13},{5,1},{9,5},{13,9},{2,14},{6,2},{... | collective-permute-start | bytes 884744 | tf_op jit(solution)/shard_map/ppermute | solution.py:272
  236.1 2.0 copy-start.19
  236.1 16.4 %collective-permute-start.25 = (bf16[512,512]{1,0:T(8,128)(2,1)}, bf16[512,512]{1,0:T(8,128)(2,1)S(1)}, u32[]{:S(2)}, u32[]{:S(2)}) collective-permute-start(bf16[512,512]{1,0:T(8,128)(2,1)} %hold.2.refs_8_), channel_id=1, source_target_pairs={{0,16},{16,0},{1,17},{17,1},{2,18},{18,2},{3,19},{19,3},{4,20},{20... | collective-permute-start | bytes 1572872 | tf_op jit(solution)/shard_map/ppermute | solution.py:265
  237.3 0.8 copy-start.20
  237.3 21.4 %collective-permute-start.27 = (bf16[512,512]{1,0:T(8,128)(2,1)}, bf16[512,512]{1,0:T(8,128)(2,1)S(1)}, u32[]{:S(2)}, u32[]{:S(2)}) collective-permute-start(bf16[512,512]{1,0:T(8,128)(2,1)} %hold.3.refs_10_), channel_id=1, source_target_pairs={{0,16},{16,0},{1,17},{17,1},{2,18},{18,2},{3,19},{19,3},{4,20},{20... | collective-permute-start | bytes 1572872 | tf_op jit(solution)/shard_map/ppermute | solution.py:265
  250.0 9.8 %copy-start.13 = (bf16[384,384]{1,0:T(8,128)(2,1)}, bf16[384,384]{1,0:T(8,128)(2,1)S(1)}, u32[]{:S(2)}) copy-start(bf16[384,384]{1,0:T(8,128)(2,1)S(1)} %collective-permute-done.12.refs_1_.refs_13_) | copy-start | bytes 884740
  250.0 21.7 %collective-permute-start.19 = (bf16[384,256]{1,0:T(8,128)(2,1)}, bf16[384,256]{1,0:T(8,128)(2,1)S(1)}, u32[]{:S(2)}, u32[]{:S(2)}) collective-permute-start(bf16[384,256]{1,0:T(8,128)(2,1)} %get-tuple-element.22), channel_id=1, source_target_pairs={{0,4},{4,8},{8,12},{12,0},{1,5},{5,9},{9,13},{13,1},{2,6},{6,10},{... | collective-permute-start | bytes 589832 | tf_op jit(solution)/shard_map/ppermute | solution.py:272
  252.5 7.3 %copy-start.21 = (bf16[512,512]{1,0:T(8,128)(2,1)}, bf16[512,512]{1,0:T(8,128)(2,1)S(1)}, u32[]{:S(2)}) copy-start(bf16[512,512]{1,0:T(8,128)(2,1)S(1)} %collective-permute-done.25.refs_9_) | copy-start | bytes 1572868
  252.5 23.6 %collective-permute-start.20 = (bf16[384,256]{1,0:T(8,128)(2,1)}, bf16[384,256]{1,0:T(8,128)(2,1)S(1)}, u32[]{:S(2)}, u32[]{:S(2)}) collective-permute-start(bf16[384,256]{1,0:T(8,128)(2,1)} %get-tuple-element.23), channel_id=1, source_target_pairs={{0,8},{4,12},{8,0},{12,4},{1,9},{5,13},{9,1},{13,5},{2,10},{6,14},... | collective-permute-start | bytes 589832 | tf_op jit(solution)/shard_map/ppermute | solution.py:272
  258.8 1.0 copy-start.22
  258.8 24.5 %collective-permute-start.21 = (bf16[384,256]{1,0:T(8,128)(2,1)}, bf16[384,256]{1,0:T(8,128)(2,1)S(1)}, u32[]{:S(2)}, u32[]{:S(2)}) collective-permute-start(bf16[384,256]{1,0:T(8,128)(2,1)} %get-tuple-element.24), channel_id=1, source_target_pairs={{0,12},{4,0},{8,4},{12,8},{1,13},{5,1},{9,5},{13,9},{2,14},{6,2},{... | collective-permute-start | bytes 589832 | tf_op jit(solution)/shard_map/ppermute | solution.py:272
  271.7 11.6 %copy-start.24 = (bf16[384,256]{1,0:T(8,128)(2,1)}, bf16[384,256]{1,0:T(8,128)(2,1)S(1)}, u32[]{:S(2)}) copy-start(bf16[384,256]{1,0:T(8,128)(2,1)S(1)} %collective-permute-done.19.refs_5_) | copy-start | bytes 589828
  271.7 14.7 %collective-permute-start.28 = (bf16[384,256]{1,0:T(8,128)(2,1)}, bf16[384,256]{1,0:T(8,128)(2,1)S(1)}, u32[]{:S(2)}, u32[]{:S(2)}) collective-permute-start(bf16[384,256]{1,0:T(8,128)(2,1)} %get-tuple-element.26), channel_id=1, source_target_pairs={{0,4},{4,8},{8,12},{12,0},{1,5},{5,9},{9,13},{13,1},{2,6},{6,10},{... | collective-permute-start | bytes 589832 | tf_op jit(solution)/shard_map/ppermute | solution.py:272
  276.1 7.2 %copy-start.25 = (bf16[384,256]{1,0:T(8,128)(2,1)}, bf16[384,256]{1,0:T(8,128)(2,1)S(1)}, u32[]{:S(2)}) copy-start(bf16[384,256]{1,0:T(8,128)(2,1)S(1)} %collective-permute-done.20.refs_6_) | copy-start | bytes 589828
  276.1 12.5 %collective-permute-start.29 = (bf16[384,256]{1,0:T(8,128)(2,1)}, bf16[384,256]{1,0:T(8,128)(2,1)S(1)}, u32[]{:S(2)}, u32[]{:S(2)}) collective-permute-start(bf16[384,256]{1,0:T(8,128)(2,1)} %get-tuple-element.27), channel_id=1, source_target_pairs={{0,8},{4,12},{8,0},{12,4},{1,9},{5,13},{9,1},{13,5},{2,10},{6,14},... | collective-permute-start | bytes 589832 | tf_op jit(solution)/shard_map/ppermute | solution.py:272
  283.3 8.6 %collective-permute-start.30 = (bf16[384,256]{1,0:T(8,128)(2,1)}, bf16[384,256]{1,0:T(8,128)(2,1)S(1)}, u32[]{:S(2)}, u32[]{:S(2)}) collective-permute-start(bf16[384,256]{1,0:T(8,128)(2,1)} %get-tuple-element.28), channel_id=1, source_target_pairs={{0,12},{4,0},{8,4},{12,8},{1,13},{5,1},{9,5},{13,9},{2,14},{6,2},{... | collective-permute-start | bytes 589832 | tf_op jit(solution)/shard_map/ppermute | solution.py:272
  283.3 0.8 copy-start.23
  286.4 5.5 %copy-start.27 = (bf16[384,256]{1,0:T(8,128)(2,1)}, bf16[384,256]{1,0:T(8,128)(2,1)S(1)}, u32[]{:S(2)}) copy-start(bf16[384,256]{1,0:T(8,128)(2,1)S(1)} %collective-permute-done.28.refs_2_) | copy-start | bytes 589828
  288.6 3.3 %copy-start.28 = (bf16[384,256]{1,0:T(8,128)(2,1)}, bf16[384,256]{1,0:T(8,128)(2,1)S(1)}, u32[]{:S(2)}) copy-start(bf16[384,256]{1,0:T(8,128)(2,1)S(1)} %collective-permute-done.29.refs_3_) | copy-start | bytes 589828
  291.9 0.7 copy-start.29
  (1 other events, 0.7 us)
Sparse Core Ops, SparseCore 0:
  8.9 29.6 all-gather.4
  40.2 28.5 all-gather.6
  70.3 28.5 all-gather.8
  120.2 30.4 all-gather.10

commit v17 on v16

--- a/solution.py
+++ b/solution.py
@@ -244,7 +244,8 @@
         for step in range(1, rows):
             lower.append(lax.ppermute(lower[-1], "row", [(i, i + 1) for i in range(step - 1, rows - 1)]))
             upper.append(lax.ppermute(upper[-1], "row", [(i, i - 1) for i in range(1, rows - step + 1)]))
-        before = [[], sent[:1]] + [[]] * (rows - 3) + [arrived[:1] + sent[1:4]]
+        z = lax.axis_index("row")
+        before = {1: sent[:1], rows - 1: arrived[:1] + sent[1:3]}
         for slot in range(rows):
             chosen = {}
             for here, sources in enumerate(by_step(rows)):
@@ -252,7 +253,14 @@
             choices = [
                 (places, upper[offset] if offset > 0 else lower[-offset]) for offset, places in chosen.items()
             ]
-            value = pick(choices, before[slot]) if slot else tokens
+            if len(choices) == 2:
+                (places, first), (_, second) = choices
+                here = sum([z == place for place in places[1:]], start=z == places[0])
+                value = jnp.where(here, first, second)
+            else:
+                value = pick(choices, []) if slot else tokens
+            if slot in before:
+                value = hold(value, before[slot])
             whole.append(lax.all_gather(value, "col", axis=1, tiled=True))
 
     def weights(shift, low, high, users):
@@ -269,8 +277,8 @@
     def hidden_of(n, after):
         low, high = spans[n]
         outs = product(whole, gate_weight, up_weight, held[n], low, high - low, mine, after)
-        back = [lax.ppermute(outs[shift], "row", around(rows, shift)) for shift in range(1, rows)]
-        blocks.extend((shift, low, value) for shift, value in enumerate([outs[0]] + back))
+        back = [lax.ppermute(outs[shift], "row", around(rows, shift)) for shift in by_distance(rows)]
+        blocks.extend((shift, low, value) for shift, value in zip([0] + by_distance(rows), [outs[0]] + back))
         done.append(outs[0])
         returned.append(back)
 
@@ -288,7 +296,7 @@
         if last and len(sent) == max(len(plan) - 2, 3):
             hidden_of(0, [])
         weights(*step)
-        if len(sent) == min(4, max(len(plan) - 2, 3)):
+        if len(sent) == min(3, max(len(plan) - 2, 3)):
             tokens_of()
     for n in range(min(last, 1), last + 1):
         hidden_of(n, done[-1:] + (returned[n - 2][:1] if n > 1 else []))

time: 303 us -> 299 us (0.987)
  starting transfers between devices: 60.4 us -> 52.9 us
  Pallas kernels: 67.5 us -> 63.3 us
    ppermute x3, waiting for transfers between devices: 27.3 us -> 35.7 us  [tokens_of(): lax.ppermute(upper[-1], 'row', [(i, i - 1) for i in range(1, rows - step...]
    ppermute x8, waiting for transfers between devices: 100 us -> 95.5 us  [weights(): arrived.append(lax.ppermute(sent[-1], 'row', around(rows, shift)))]
    pallas_call x3 -> x1, Pallas kernels: 6.27 us -> 2.08 us  [pick(): pl.pallas_call(body, out_shape=jax.ShapeDtypeStruct(like.shape, like.dtyp...]
    ppermute x8, starting transfers between devices: 15.8 us -> 11.8 us  [weights(): arrived.append(lax.ppermute(sent[-1], 'row', around(rows, shift)))]
    ppermute x8, starting transfers between devices: 10.9 us -> 7.71 us  [weights(): swapped.append(lax.ppermute(came, 'parts', around(parts, -turn)))]
    unnamed x60 -> x58, local copies, waits for them, and re-layouts: 7.69 us -> 8.77 us
  transfers between devices with their start and end apart: 35 -> 35, of which waited for: 16 -> 18; matrix products, arithmetic and copies ran while one was open for 0% -> 1% of each run, Pallas kernels for 22% -> 21%
where the time goes in v17:
time: 299 us; the launch traced here: 296 us
  waiting for transfers between devices  155 us (52%)
  Pallas kernels  63.3 us (21%)
  starting transfers between devices  52.9 us (18%)
  between operations  13.5 us (5%)
  local copies, waits for them, and re-layouts  8.77 us (3%)
    ppermute x8, waiting for transfers between devices, weights(): arrived.append(lax.ppermute(sent[-1], 'row', around(rows, shift)))  95.5 us
    pallas_call x3, Pallas kernels, product(): pl.pallas_call(body, out_shape=[jax.ShapeDtypeStruct((mine, wide), jnp.bf...  40.3 us
    ppermute x3, waiting for transfers between devices, tokens_of(): lax.ppermute(upper[-1], 'row', [(i, i - 1) for i in range(1, rows - step...  35.7 us
    pallas_call x8, Pallas kernels, pack(): pl.pallas_call(body, out_shape=jax.ShapeDtypeStruct((share, 2 * wide), ga...  16.7 us
    ppermute x9, starting transfers between devices, hidden_of(): lax.ppermute(outs[shift], 'row', around(rows, shift))  16.2 us
    ppermute x9, waiting for transfers between devices, hidden_of(): lax.ppermute(outs[shift], 'row', around(rows, shift))  12.5 us
    ppermute x8, starting transfers between devices, weights(): arrived.append(lax.ppermute(sent[-1], 'row', around(rows, shift)))  11.8 us
    ppermute x3, starting transfers between devices, tokens_of(): lax.ppermute(lower[-1], 'row', [(i, i + 1) for i in range(step - 1, rows...  9.05 us
  transfers between devices with their start and end apart: 35, of which 18 were waited for; matrix products, arithmetic and copies ran while one was open for 1% of the time, Pallas kernels for 21%

profile of v17, /device:TPU:12, one launch (start us, length us, event | category | flops | bytes accessed | tf_op | source)
XLA Modules:
  0.0 295.6 jit_solution(4667612782443603254)
XLA Ops:
  7.3 2.4 collective-permute-start
  9.7 3.5 %collective-permute-start.1 = (bf16[384,1024]{1,0:T(8,128)(2,1)}, bf16[384,1024]{1,0:T(8,128)(2,1)S(1)}, u32[]{:S(2)}, u32[]{:S(2)}) collective-permute-start(bf16[384,1024]{1,0:T(8,128)(2,1)} %param.3), channel_id=1, source_target_pairs={{0,4},{4,8},{8,12},{1,5},{5,9},{9,13},{2,6},{6,10},{10,14},{3,7},{... | collective-permute-start | bytes 2359304 | tf_op jit(solution)/shard_map/ppermute | solution.py:245
  13.2 2.6 pack.8.refs_1_.refs_2_
  15.7 13.0 %collective-permute-done.refs_2_ = bf16[384,1024]{1,0:T(8,128)(2,1)S(1)} collective-permute-done((bf16[384,1024]{1,0:T(8,128)(2,1)}, bf16[384,1024]{1,0:T(8,128)(2,1)S(1)}, u32[]{:S(2)}, u32[]{:S(2)}) %collective-permute-start) | collective-permute-done | bytes 786464 | tf_op jit(solution)/shard_map/ppermute | solution.py:246
  28.7 2.1 collective-permute-done.1.refs_1_
  30.8 1.1 broadcast_select_fusion.1.refs_0_
  31.9 2.1 collective-permute-start.2
  34.0 4.0 %collective-permute-start.3 = (bf16[384,1024]{1,0:T(8,128)(2,1)S(1)}, bf16[384,1024]{1,0:T(8,128)(2,1)S(1)}, u32[]{:S(2)}, u32[]{:S(2)}) collective-permute-start(bf16[384,1024]{1,0:T(8,128)(2,1)S(1)} %collective-permute-done.1.refs_1_), channel_id=1, source_target_pairs={{4,8},{8,12},{5,9},{9,13},{6,10},{10,14},{7,11},{11,15},{20,24},{2... | collective-permute-start | bytes 2359304 | tf_op jit(solution)/shard_map/ppermute | solution.py:245
  38.0 14.1 %collective-permute-done.2 = bf16[384,1024]{1,0:T(8,128)(2,1)S(1)} collective-permute-done((bf16[384,1024]{1,0:T(8,128)(2,1)S(1)}, bf16[384,1024]{1,0:T(8,128)(2,1)S(1)}, u32[]{:S(2)}, u32[]{:S(2)}) %collective-permute-start.2) | collective-permute-done | bytes 786464 | tf_op jit(solution)/shard_map/ppermute | solution.py:246
  52.2 1.2 collective-permute-done.3
  53.4 0.9 copy-done.14
  54.3 1.0 broadcast_select_fusion
  55.3 2.3 collective-permute-start.6
  57.6 3.7 %collective-permute-start.4 = (bf16[384,1024]{1,0:T(8,128)(2,1)}, bf16[384,1024]{1,0:T(8,128)(2,1)S(1)}, u32[]{:S(2)}, u32[]{:S(2)}) collective-permute-start(bf16[384,1024]{1,0:T(8,128)(2,1)} %copy-done.13), channel_id=1, source_target_pairs={{4,0},{5,1},{6,2},{7,3},{20,16},{21,17},{22,18},{23,19}} | collective-permute-start | bytes 2359304 | tf_op jit(solution)/shard_map/ppermute | solution.py:246
  61.3 1.6 collective-permute-start.5
  62.9 2.2 pack.9.refs_2_
  65.1 2.2 pack.10.refs_3_.refs_2_
  67.2 8.6 %collective-permute-done.4.refs_0_ = bf16[384,1024]{1,0:T(8,128)(2,1)S(1)} collective-permute-done((bf16[384,1024]{1,0:T(8,128)(2,1)}, bf16[384,1024]{1,0:T(8,128)(2,1)S(1)}, u32[]{:S(2)}, u32[]{:S(2)}) %collective-permute-start.4) | collective-permute-done | bytes 786464 | tf_op jit(solution)/shard_map/ppermute | solution.py:246
  75.9 0.9 copy-done.15
  76.8 2.1 pick.1.refs_0_
  78.9 33.0 %collective-permute-done.6.refs_1_.refs_6_.refs_3_ = bf16[512,1280]{1,0:T(8,128)(2,1)S(1)} collective-permute-done((bf16[512,1280]{1,0:T(8,128)(2,1)S(1)}, bf16[512,1280]{1,0:T(8,128)(2,1)S(1)}, u32[]{:S(2)}, u32[]{:S(2)}) %collective-permute-start.6) | collective-permute-done | bytes 1310752 | tf_op jit(solution)/shard_map/ppermute | solution.py:269
  111.8 1.1 copy-done
  112.9 1.1 copy-done.3
  114.3 1.0 collective-permute-start.7
  115.3 1.9 collective-permute-start.10
  117.2 17.5 %collective-permute-done.8.refs_8_.refs_3_ = bf16[512,768]{1,0:T(8,128)(2,1)} collective-permute-done((bf16[512,768]{1,0:T(8,128)(2,1)S(1)}, bf16[512,768]{1,0:T(8,128)(2,1)}, u32[]{:S(2)}, u32[]{:S(2)}) %collective-permute-start.8) | collective-permute-done | bytes 786464 | tf_op jit(solution)/shard_map/ppermute | solution.py:269
  134.7 1.0 collective-permute-start.9
  135.7 1.9 pack.11.refs_2_
  137.6 1.9 collective-permute-start.22
  139.5 24.8 %collective-permute-done.10.refs_10_.refs_3_ = bf16[512,768]{1,0:T(8,128)(2,1)} collective-permute-done((bf16[512,768]{1,0:T(8,128)(2,1)S(1)}, bf16[512,768]{1,0:T(8,128)(2,1)}, u32[]{:S(2)}, u32[]{:S(2)}) %collective-permute-start.10) | collective-permute-done | bytes 786464 | tf_op jit(solution)/shard_map/ppermute | solution.py:269
  164.3 1.0 collective-permute-start.11
  165.3 7.0 %collective-permute-done.22.refs_3_.refs_6_ = bf16[512,512]{1,0:T(8,128)(2,1)S(1)} collective-permute-done((bf16[512,512]{1,0:T(8,128)(2,1)}, bf16[512,512]{1,0:T(8,128)(2,1)S(1)}, u32[]{:S(2)}, u32[]{:S(2)}) %collective-permute-start.22) | collective-permute-done | bytes 524320 | tf_op jit(solution)/shard_map/ppermute | solution.py:269
  172.3 1.0 collective-permute-start.23
  173.3 1.1 copy-done.4
  174.3 1.9 pack.12.refs_2_
  176.3 1.9 collective-permute-start.15
  178.2 2.0 pack.13.refs_2_
  180.2 1.9 collective-permute-start.17
  182.3 1.9 pack.14.refs_2_
  184.2 1.5 collective-permute-start.24
  185.7 4.1 %collective-permute-done.23.refs_4_.refs_7_ = bf16[512,512]{1,0:T(8,128)(2,1)S(1)} collective-permute-done((bf16[512,512]{1,0:T(8,128)(2,1)S(1)}, bf16[512,512]{1,0:T(8,128)(2,1)S(1)}, u32[]{:S(2)}, u32[]{:S(2)}) %collective-permute-start.23) | collective-permute-done | bytes 524320 | tf_op jit(solution)/shard_map/ppermute | solution.py:273
  189.8 10.6 %collective-permute-done.15.refs_8_.refs_3_ = bf16[512,512]{1,0:T(8,128)(2,1)S(1)} collective-permute-done((bf16[512,512]{1,0:T(8,128)(2,1)}, bf16[512,512]{1,0:T(8,128)(2,1)S(1)}, u32[]{:S(2)}, u32[]{:S(2)}) %collective-permute-start.15) | collective-permute-done | bytes 524320 | tf_op jit(solution)/shard_map/ppermute | solution.py:269
  201.2 2.0 pack.15
  203.2 0.9 collective-permute-start.16
  204.1 2.7 collective-permute-done.17.refs_10_
  206.8 0.8 collective-permute-start.18
  207.6 16.5 %product.3 = (bf16[384,384]{1,0:T(8,128)(2,1)}, bf16[384,384]{1,0:T(8,128)(2,1)}, bf16[384,384]{1,0:T(8,128)(2,1)}, bf16[384,384]{1,0:T(8,128)(2,1)}) custom-call(bf16[384,4096]{1,0:T(8,128)(2,1)} %all-gather.5.cloned.1.call-done.refs_0_, bf16[384,4096]{1,0:T(8,128)(2,1)} %all-gather.7.cloned.1.call-done.refs_1_, ...), custom_call_target="tpu_custom_call" | custom-call | flops 9663676416 | bytes 20054016 | tf_op jit(solution)/shard_map/product/pallas_call | solution.py:138
  224.2 2.5 collective-permute-start.12
  226.7 2.8 collective-permute-start.13
  230.3 1.2 collective-permute-start.25
  232.3 11.8 %product.4 = (bf16[384,256]{1,0:T(8,128)(2,1)}, bf16[384,256]{1,0:T(8,128)(2,1)}, bf16[384,256]{1,0:T(8,128)(2,1)}, bf16[384,256]{1,0:T(8,128)(2,1)}) custom-call(bf16[384,4096]{1,0:T(8,128)(2,1)} %all-gather.5.cloned.1.call-done.refs_0_, bf16[384,4096]{1,0:T(8,128)(2,1)} %all-gather.7.cloned.1.call-done.refs_1_, ...), custom_call_target="tpu_custom_call" | custom-call | flops 6442450944 | bytes 17563648 | tf_op jit(solution)/shard_map/product/pallas_call | solution.py:138
  244.2 3.5 %collective-permute-start.19 = (bf16[384,256]{1,0:T(8,128)(2,1)}, bf16[384,256]{1,0:T(8,128)(2,1)S(1)}, u32[]{:S(2)}, u32[]{:S(2)}) collective-permute-start(bf16[384,256]{1,0:T(8,128)(2,1)} %get-tuple-element.22), channel_id=1, source_target_pairs={{0,8},{4,12},{8,0},{12,4},{1,9},{5,13},{9,1},{13,5},{2,10},{6,14},... | collective-permute-start | bytes 589832 | tf_op jit(solution)/shard_map/ppermute | solution.py:280
  247.7 2.9 collective-permute-start.20
  250.5 3.0 %collective-permute-done.27.refs_11_ = bf16[512,512]{1,0:T(8,128)(2,1)S(1)} collective-permute-done((bf16[512,512]{1,0:T(8,128)(2,1)}, bf16[512,512]{1,0:T(8,128)(2,1)S(1)}, u32[]{:S(2)}, u32[]{:S(2)}) %collective-permute-start.27) | collective-permute-done | bytes 524320 | tf_op jit(solution)/shard_map/ppermute | solution.py:273
  253.6 1.0 collective-permute-start.21
  254.6 11.9 %product.5 = (bf16[384,256]{1,0:T(8,128)(2,1)}, bf16[384,256]{1,0:T(8,128)(2,1)}, bf16[384,256]{1,0:T(8,128)(2,1)}, bf16[384,256]{1,0:T(8,128)(2,1)}) custom-call(bf16[384,4096]{1,0:T(8,128)(2,1)} %all-gather.5.cloned.1.call-done.refs_0_, bf16[384,4096]{1,0:T(8,128)(2,1)} %all-gather.7.cloned.1.call-done.refs_1_, ...), custom_call_target="tpu_custom_call" | custom-call | flops 6442450944 | bytes 17563648 | tf_op jit(solution)/shard_map/product/pallas_call | solution.py:138
  266.5 1.0 collective-permute-start.28
  267.5 2.0 collective-permute-done.20.refs_6_
  269.5 2.5 collective-permute-start.29
  272.0 6.1 %collective-permute-done.21.refs_7_ = bf16[384,256]{1,0:T(8,128)(2,1)S(1)} collective-permute-done((bf16[384,256]{1,0:T(8,128)(2,1)}, bf16[384,256]{1,0:T(8,128)(2,1)S(1)}, u32[]{:S(2)}, u32[]{:S(2)}) %collective-permute-start.21) | collective-permute-done | bytes 196640 | tf_op jit(solution)/shard_map/ppermute | solution.py:280
  279.7 2.4 place.2.refs_0_
  282.1 1.4 collective-permute-done.29.refs_3_
  283.5 3.0 %collective-permute-done.30.refs_4_ = bf16[384,256]{1,0:T(8,128)(2,1)S(1)} collective-permute-done((bf16[384,256]{1,0:T(8,128)(2,1)}, bf16[384,256]{1,0:T(8,128)(2,1)S(1)}, u32[]{:S(2)}, u32[]{:S(2)}) %collective-permute-start.30) | collective-permute-done | bytes 196640 | tf_op jit(solution)/shard_map/ppermute | solution.py:280
  287.1 2.0 place.3
  (88 shorter events, 6.1 us)
Async XLA Ops:
  6.5 201.1 %all-gather.5.cloned.1.call-start = ((), (), s32[]{:S(2)}) async-start(), calls=%async_computation | async-start | bytes 3932160 | tf_op jit(solution)/shard_map/all_gather | solution.py:264
  7.3 200.4 %all-gather.7.cloned.1.call-start = ((), (), s32[]{:S(2)}) async-start(), calls=%async_computation.1 | async-start | bytes 3932160 | tf_op jit(solution)/shard_map/all_gather | solution.py:264
  7.3 21.4 %collective-permute-start = (bf16[384,1024]{1,0:T(8,128)(2,1)}, bf16[384,1024]{1,0:T(8,128)(2,1)S(1)}, u32[]{:S(2)}, u32[]{:S(2)}) collective-permute-start(bf16[384,1024]{1,0:T(8,128)(2,1)} %param.3), channel_id=1, source_target_pairs={{4,0},{8,4},{12,8},{5,1},{9,5},{13,9},{6,2},{10,6},{14,10},{7,3},{... | collective-permute-start | bytes 2359304 | tf_op jit(solution)/shard_map/ppermute | solution.py:246
  9.7 21.1 %collective-permute-start.1 = (bf16[384,1024]{1,0:T(8,128)(2,1)}, bf16[384,1024]{1,0:T(8,128)(2,1)S(1)}, u32[]{:S(2)}, u32[]{:S(2)}) collective-permute-start(bf16[384,1024]{1,0:T(8,128)(2,1)} %param.3), channel_id=1, source_target_pairs={{0,4},{4,8},{8,12},{1,5},{5,9},{9,13},{2,6},{6,10},{10,14},{3,7},{... | collective-permute-start | bytes 2359304 | tf_op jit(solution)/shard_map/ppermute | solution.py:245
  28.7 26.6 %copy-start.5 = (bf16[384,1024]{1,0:T(8,128)(2,1)}, bf16[384,1024]{1,0:T(8,128)(2,1)S(1)}, u32[]{:S(2)}) copy-start(bf16[384,1024]{1,0:T(8,128)(2,1)S(1)} %collective-permute-done.refs_2_) | copy-start | bytes 2359300
  30.8 24.5 %copy-start.6 = (bf16[384,1024]{1,0:T(8,128)(2,1)}, bf16[384,1024]{1,0:T(8,128)(2,1)S(1)}, u32[]{:S(2)}) copy-start(bf16[384,1024]{1,0:T(8,128)(2,1)S(1)} %collective-permute-done.1.refs_1_) | copy-start | bytes 2359300
  31.9 23.5 %copy-start.1 = (bf16[512,1280]{1,0:T(8,128)(2,1)S(1)}, bf16[512,1280]{1,0:T(8,128)(2,1)}, u32[]{:S(2)}) copy-start(bf16[512,1280]{1,0:T(8,128)(2,1)} %pack.8.refs_1_.refs_2_) | copy-start | bytes 3932164
  31.9 175.7 %all-gather.9.cloned.1.call-start = ((), (), s32[]{:S(2)}) async-start(), calls=%async_computation.2 | async-start | bytes 3932160 | tf_op jit(solution)/shard_map/all_gather | solution.py:264
  31.9 20.2 %collective-permute-start.2 = (bf16[384,1024]{1,0:T(8,128)(2,1)S(1)}, bf16[384,1024]{1,0:T(8,128)(2,1)S(1)}, u32[]{:S(2)}, u32[]{:S(2)}) collective-permute-start(bf16[384,1024]{1,0:T(8,128)(2,1)S(1)} %collective-permute-done.refs_2_), channel_id=1, source_target_pairs={{4,0},{8,4},{5,1},{9,5},{6,2},{10,6},{7,3},{11,7},{20,16},{24,20},... | collective-permute-start | bytes 2359304 | tf_op jit(solution)/shard_map/ppermute | solution.py:246
  34.0 19.4 %collective-permute-start.3 = (bf16[384,1024]{1,0:T(8,128)(2,1)S(1)}, bf16[384,1024]{1,0:T(8,128)(2,1)S(1)}, u32[]{:S(2)}, u32[]{:S(2)}) collective-permute-start(bf16[384,1024]{1,0:T(8,128)(2,1)S(1)} %collective-permute-done.1.refs_1_), channel_id=1, source_target_pairs={{4,8},{8,12},{5,9},{9,13},{6,10},{10,14},{7,11},{11,15},{20,24},{2... | collective-permute-start | bytes 2359304 | tf_op jit(solution)/shard_map/ppermute | solution.py:245
  52.2 1.2 copy-start.13
  53.4 0.9 copy-start.14
  55.3 152.4 %all-gather.11.cloned.1.call-start = ((), (), s32[]{:S(2)}) async-start(), calls=%async_computation.3 | async-start | bytes 3932160 | tf_op jit(solution)/shard_map/all_gather | solution.py:264
  55.3 56.5 %collective-permute-start.6 = (bf16[512,1280]{1,0:T(8,128)(2,1)S(1)}, bf16[512,1280]{1,0:T(8,128)(2,1)S(1)}, u32[]{:S(2)}, u32[]{:S(2)}) collective-permute-start(bf16[512,1280]{1,0:T(8,128)(2,1)S(1)} %copy-done.1), channel_id=1, source_target_pairs={{0,8},{4,12},{8,0},{12,4},{1,9},{5,13},{9,1},{13,5},{2,10},{6,14},... | collective-permute-start | bytes 3932168 | tf_op jit(solution)/shard_map/ppermute | solution.py:269
  57.6 18.3 %collective-permute-start.4 = (bf16[384,1024]{1,0:T(8,128)(2,1)}, bf16[384,1024]{1,0:T(8,128)(2,1)S(1)}, u32[]{:S(2)}, u32[]{:S(2)}) collective-permute-start(bf16[384,1024]{1,0:T(8,128)(2,1)} %copy-done.13), channel_id=1, source_target_pairs={{4,0},{5,1},{6,2},{7,3},{20,16},{21,17},{22,18},{23,19}} | collective-permute-start | bytes 2359304 | tf_op jit(solution)/shard_map/ppermute | solution.py:246
  61.3 14.6 %collective-permute-start.5 = (bf16[384,1024]{1,0:T(8,128)(2,1)}, bf16[384,1024]{1,0:T(8,128)(2,1)}, u32[]{:S(2)}, u32[]{:S(2)}) collective-permute-start(bf16[384,1024]{1,0:T(8,128)(2,1)} %copy-done.14), channel_id=1, source_target_pairs={{8,12},{9,13},{10,14},{11,15},{24,28},{25,29},{26,30},{27,31}} | collective-permute-start | bytes 2359304 | tf_op jit(solution)/shard_map/ppermute | solution.py:245
  75.9 0.9 copy-start.15
  78.9 36.4 %copy-start.2 = (bf16[512,768]{1,0:T(8,128)(2,1)S(1)}, bf16[512,768]{1,0:T(8,128)(2,1)}, u32[]{:S(2)}) copy-start(bf16[512,768]{1,0:T(8,128)(2,1)} %pack.10.refs_3_.refs_2_) | copy-start | bytes 2359300
  111.8 1.1 copy-start
  112.9 1.1 copy-start.3
  114.0 20.7 %collective-permute-start.8 = (bf16[512,768]{1,0:T(8,128)(2,1)S(1)}, bf16[512,768]{1,0:T(8,128)(2,1)}, u32[]{:S(2)}, u32[]{:S(2)}) collective-permute-start(bf16[512,768]{1,0:T(8,128)(2,1)S(1)} %copy-done.3), channel_id=1, source_target_pairs={{0,4},{4,8},{8,12},{12,0},{1,5},{5,9},{9,13},{13,1},{2,6},{6,10},{... | collective-permute-start | bytes 2359304 | tf_op jit(solution)/shard_map/ppermute | solution.py:269
  114.3 59.0 %collective-permute-start.7 = (bf16[512,1280]{1,0:T(8,128)(2,1)}, bf16[512,1280]{1,0:T(8,128)(2,1)S(1)}, u32[]{:S(2)}, u32[]{:S(2)}) collective-permute-start(bf16[512,1280]{1,0:T(8,128)(2,1)} %copy-done), channel_id=1, source_target_pairs={{0,16},{16,0},{1,17},{17,1},{2,18},{18,2},{3,19},{19,3},{4,20},{20... | collective-permute-start | bytes 3932168 | tf_op jit(solution)/shard_map/ppermute | solution.py:273
  115.3 49.0 %collective-permute-start.10 = (bf16[512,768]{1,0:T(8,128)(2,1)S(1)}, bf16[512,768]{1,0:T(8,128)(2,1)}, u32[]{:S(2)}, u32[]{:S(2)}) collective-permute-start(bf16[512,768]{1,0:T(8,128)(2,1)S(1)} %copy-done.2), channel_id=1, source_target_pairs={{0,12},{4,0},{8,4},{12,8},{1,13},{5,1},{9,5},{13,9},{2,14},{6,2},{... | collective-permute-start | bytes 2359304 | tf_op jit(solution)/shard_map/ppermute | solution.py:269
  134.7 43.6 %collective-permute-start.9 = (bf16[512,768]{1,0:T(8,128)(2,1)}, bf16[512,768]{1,0:T(8,128)(2,1)}, u32[]{:S(2)}, u32[]{:S(2)}) collective-permute-start(bf16[512,768]{1,0:T(8,128)(2,1)} %collective-permute-done.8.refs_8_.refs_3_), channel_id=1, source_target_pairs={{0,16},{16,0},{1,17},{17,1},{2,18},{18,2},{3,19},{19,3},{4,20},{20... | collective-permute-start | bytes 2359304 | tf_op jit(solution)/shard_map/ppermute | solution.py:273
  137.6 34.7 %collective-permute-start.22 = (bf16[512,512]{1,0:T(8,128)(2,1)}, bf16[512,512]{1,0:T(8,128)(2,1)S(1)}, u32[]{:S(2)}, u32[]{:S(2)}) collective-permute-start(bf16[512,512]{1,0:T(8,128)(2,1)} %pack.11.refs_2_), channel_id=1, source_target_pairs={{0,8},{4,12},{8,0},{12,4},{1,9},{5,13},{9,1},{13,5},{2,10},{6,14},... | collective-permute-start | bytes 1572872 | tf_op jit(solution)/shard_map/ppermute | solution.py:269
  164.3 18.0 %collective-permute-start.11 = (bf16[512,768]{1,0:T(8,128)(2,1)}, bf16[512,768]{1,0:T(8,128)(2,1)}, u32[]{:S(2)}, u32[]{:S(2)}) collective-permute-start(bf16[512,768]{1,0:T(8,128)(2,1)} %collective-permute-done.10.refs_10_.refs_3_), channel_id=1, source_target_pairs={{0,16},{16,0},{1,17},{17,1},{2,18},{18,2},{3,19},{19,3},{4,20},{20... | collective-permute-start | bytes 2359304 | tf_op jit(solution)/shard_map/ppermute | solution.py:273
  172.3 7.9 %copy-start.7 = (bf16[512,512]{1,0:T(8,128)(2,1)}, bf16[512,512]{1,0:T(8,128)(2,1)S(1)}, u32[]{:S(2)}) copy-start(bf16[512,512]{1,0:T(8,128)(2,1)S(1)} %collective-permute-done.22.refs_3_.refs_6_) | copy-start | bytes 1572868
  172.3 17.5 %collective-permute-start.23 = (bf16[512,512]{1,0:T(8,128)(2,1)S(1)}, bf16[512,512]{1,0:T(8,128)(2,1)S(1)}, u32[]{:S(2)}, u32[]{:S(2)}) collective-permute-start(bf16[512,512]{1,0:T(8,128)(2,1)S(1)} %collective-permute-done.22.refs_3_.refs_6_), channel_id=1, source_target_pairs={{0,16},{16,0},{1,17},{17,1},{2,18},{18,2},{3,19},{19,3},{4,20},{20... | collective-permute-start | bytes 1572872 | tf_op jit(solution)/shard_map/ppermute | solution.py:273
  173.3 1.1 copy-start.4
  176.3 24.1 %collective-permute-start.15 = (bf16[512,512]{1,0:T(8,128)(2,1)}, bf16[512,512]{1,0:T(8,128)(2,1)S(1)}, u32[]{:S(2)}, u32[]{:S(2)}) collective-permute-start(bf16[512,512]{1,0:T(8,128)(2,1)} %pack.12.refs_2_), channel_id=1, source_target_pairs={{0,4},{4,8},{8,12},{12,0},{1,5},{5,9},{9,13},{13,1},{2,6},{6,10},{... | collective-permute-start | bytes 1572872 | tf_op jit(solution)/shard_map/ppermute | solution.py:269
  180.2 26.6 %collective-permute-start.17 = (bf16[512,512]{1,0:T(8,128)(2,1)}, bf16[512,512]{1,0:T(8,128)(2,1)S(1)}, u32[]{:S(2)}, u32[]{:S(2)}) collective-permute-start(bf16[512,512]{1,0:T(8,128)(2,1)} %pack.13.refs_2_), channel_id=1, source_target_pairs={{0,12},{4,0},{8,4},{12,8},{1,13},{5,1},{9,5},{13,9},{2,14},{6,2},{... | collective-permute-start | bytes 1572872 | tf_op jit(solution)/shard_map/ppermute | solution.py:269
  184.2 42.4 %collective-permute-start.24 = (bf16[512,512]{1,0:T(8,128)(2,1)}, bf16[512,512]{1,0:T(8,128)(2,1)S(1)}, u32[]{:S(2)}, u32[]{:S(2)}) collective-permute-start(bf16[512,512]{1,0:T(8,128)(2,1)} %pack.14.refs_2_), channel_id=1, source_target_pairs={{0,4},{4,8},{8,12},{12,0},{1,5},{5,9},{9,13},{13,1},{2,6},{6,10},{... | collective-permute-start | bytes 1572872 | tf_op jit(solution)/shard_map/ppermute | solution.py:269
  189.8 10.6 %copy-start.8 = (bf16[512,512]{1,0:T(8,128)(2,1)}, bf16[512,512]{1,0:T(8,128)(2,1)S(1)}, u32[]{:S(2)}) copy-start(bf16[512,512]{1,0:T(8,128)(2,1)S(1)} %collective-permute-done.23.refs_4_.refs_7_) | copy-start | bytes 1572868
  200.4 0.8 copy-start.9
  203.1 26.3 %collective-permute-start.26 = (bf16[512,512]{1,0:T(8,128)(2,1)}, bf16[512,512]{1,0:T(8,128)(2,1)S(1)}, u32[]{:S(2)}, u32[]{:S(2)}) collective-permute-start(bf16[512,512]{1,0:T(8,128)(2,1)} %pack.15), channel_id=1, source_target_pairs={{0,12},{4,0},{8,4},{12,8},{1,13},{5,1},{9,5},{13,9},{2,14},{6,2},{... | collective-permute-start | bytes 1572872 | tf_op jit(solution)/shard_map/ppermute | solution.py:269
  203.2 27.1 %collective-permute-start.16 = (bf16[512,512]{1,0:T(8,128)(2,1)}, bf16[512,512]{1,0:T(8,128)(2,1)S(1)}, u32[]{:S(2)}, u32[]{:S(2)}) collective-permute-start(bf16[512,512]{1,0:T(8,128)(2,1)} %copy-done.9), channel_id=1, source_target_pairs={{0,16},{16,0},{1,17},{17,1},{2,18},{18,2},{3,19},{19,3},{4,20},{20... | collective-permute-start | bytes 1572872 | tf_op jit(solution)/shard_map/ppermute | solution.py:273
  206.8 17.4 %copy-start.16 = (bf16[512,512]{1,0:T(8,128)(2,1)}, bf16[512,512]{1,0:T(8,128)(2,1)S(1)}, u32[]{:S(2)}) copy-start(bf16[512,512]{1,0:T(8,128)(2,1)S(1)} %collective-permute-done.17.refs_10_) | copy-start | bytes 1572868
  206.8 24.7 %collective-permute-start.18 = (bf16[512,512]{1,0:T(8,128)(2,1)S(1)}, bf16[512,512]{1,0:T(8,128)(2,1)S(1)}, u32[]{:S(2)}, u32[]{:S(2)}) collective-permute-start(bf16[512,512]{1,0:T(8,128)(2,1)S(1)} %collective-permute-done.17.refs_10_), channel_id=1, source_target_pairs={{0,16},{16,0},{1,17},{17,1},{2,18},{18,2},{3,19},{19,3},{4,20},{20... | collective-permute-start | bytes 1572872 | tf_op jit(solution)/shard_map/ppermute | solution.py:273
  224.2 20.0 %collective-permute-start.12 = (bf16[384,384]{1,0:T(8,128)(2,1)}, bf16[384,384]{1,0:T(8,128)(2,1)S(1)}, u32[]{:S(2)}, u32[]{:S(2)}) collective-permute-start(bf16[384,384]{1,0:T(8,128)(2,1)} %get-tuple-element.18), channel_id=1, source_target_pairs={{0,8},{4,12},{8,0},{12,4},{1,9},{5,13},{9,1},{13,5},{2,10},{6,14},... | collective-permute-start | bytes 884744 | tf_op jit(solution)/shard_map/ppermute | solution.py:280
  226.7 2.8 copy-start.10
  226.7 51.5 %collective-permute-start.13 = (bf16[384,384]{1,0:T(8,128)(2,1)}, bf16[384,384]{1,0:T(8,128)(2,1)S(1)}, u32[]{:S(2)}, u32[]{:S(2)}) collective-permute-start(bf16[384,384]{1,0:T(8,128)(2,1)} %get-tuple-element.19), channel_id=1, source_target_pairs={{0,4},{4,8},{8,12},{12,0},{1,5},{5,9},{9,13},{13,1},{2,6},{6,10},{... | collective-permute-start | bytes 884744 | tf_op jit(solution)/shard_map/ppermute | solution.py:280
  229.4 0.8 copy-start.11
  229.4 48.7 %collective-permute-start.14 = (bf16[384,384]{1,0:T(8,128)(2,1)}, bf16[384,384]{1,0:T(8,128)(2,1)S(1)}, u32[]{:S(2)}, u32[]{:S(2)}) collective-permute-start(bf16[384,384]{1,0:T(8,128)(2,1)} %get-tuple-element.20), channel_id=1, source_target_pairs={{0,12},{4,0},{8,4},{12,8},{1,13},{5,1},{9,5},{13,9},{2,14},{6,2},{... | collective-permute-start | bytes 884744 | tf_op jit(solution)/shard_map/ppermute | solution.py:280
  230.3 2.0 copy-start.17
  230.3 17.4 %collective-permute-start.25 = (bf16[512,512]{1,0:T(8,128)(2,1)}, bf16[512,512]{1,0:T(8,128)(2,1)S(1)}, u32[]{:S(2)}, u32[]{:S(2)}) collective-permute-start(bf16[512,512]{1,0:T(8,128)(2,1)} %hold.6.refs_8_), channel_id=1, source_target_pairs={{0,16},{16,0},{1,17},{17,1},{2,18},{18,2},{3,19},{19,3},{4,20},{20... | collective-permute-start | bytes 1572872 | tf_op jit(solution)/shard_map/ppermute | solution.py:273
  231.5 0.8 copy-start.18
  231.5 22.0 %collective-permute-start.27 = (bf16[512,512]{1,0:T(8,128)(2,1)}, bf16[512,512]{1,0:T(8,128)(2,1)S(1)}, u32[]{:S(2)}, u32[]{:S(2)}) collective-permute-start(bf16[512,512]{1,0:T(8,128)(2,1)} %hold.7.refs_10_), channel_id=1, source_target_pairs={{0,16},{16,0},{1,17},{17,1},{2,18},{18,2},{3,19},{19,3},{4,20},{20... | collective-permute-start | bytes 1572872 | tf_op jit(solution)/shard_map/ppermute | solution.py:273
  244.2 10.4 %copy-start.12 = (bf16[384,384]{1,0:T(8,128)(2,1)}, bf16[384,384]{1,0:T(8,128)(2,1)S(1)}, u32[]{:S(2)}) copy-start(bf16[384,384]{1,0:T(8,128)(2,1)S(1)} %collective-permute-done.12.refs_1_.refs_13_) | copy-start | bytes 884740
  244.2 22.3 %collective-permute-start.19 = (bf16[384,256]{1,0:T(8,128)(2,1)}, bf16[384,256]{1,0:T(8,128)(2,1)S(1)}, u32[]{:S(2)}, u32[]{:S(2)}) collective-permute-start(bf16[384,256]{1,0:T(8,128)(2,1)} %get-tuple-element.22), channel_id=1, source_target_pairs={{0,8},{4,12},{8,0},{12,4},{1,9},{5,13},{9,1},{13,5},{2,10},{6,14},... | collective-permute-start | bytes 589832 | tf_op jit(solution)/shard_map/ppermute | solution.py:280
  247.7 6.9 %copy-start.19 = (bf16[512,512]{1,0:T(8,128)(2,1)}, bf16[512,512]{1,0:T(8,128)(2,1)S(1)}, u32[]{:S(2)}) copy-start(bf16[512,512]{1,0:T(8,128)(2,1)S(1)} %collective-permute-done.25.refs_9_) | copy-start | bytes 1572868
  247.7 21.9 %collective-permute-start.20 = (bf16[384,256]{1,0:T(8,128)(2,1)}, bf16[384,256]{1,0:T(8,128)(2,1)S(1)}, u32[]{:S(2)}, u32[]{:S(2)}) collective-permute-start(bf16[384,256]{1,0:T(8,128)(2,1)} %get-tuple-element.23), channel_id=1, source_target_pairs={{0,4},{4,8},{8,12},{12,0},{1,5},{5,9},{9,13},{13,1},{2,6},{6,10},{... | collective-permute-start | bytes 589832 | tf_op jit(solution)/shard_map/ppermute | solution.py:280
  253.6 1.0 copy-start.20
  253.6 24.6 %collective-permute-start.21 = (bf16[384,256]{1,0:T(8,128)(2,1)}, bf16[384,256]{1,0:T(8,128)(2,1)S(1)}, u32[]{:S(2)}, u32[]{:S(2)}) collective-permute-start(bf16[384,256]{1,0:T(8,128)(2,1)} %get-tuple-element.24), channel_id=1, source_target_pairs={{0,12},{4,0},{8,4},{12,8},{1,13},{5,1},{9,5},{13,9},{2,14},{6,2},{... | collective-permute-start | bytes 589832 | tf_op jit(solution)/shard_map/ppermute | solution.py:280
  266.5 11.7 %copy-start.23 = (bf16[384,256]{1,0:T(8,128)(2,1)}, bf16[384,256]{1,0:T(8,128)(2,1)S(1)}, u32[]{:S(2)}) copy-start(bf16[384,256]{1,0:T(8,128)(2,1)S(1)} %collective-permute-done.19.refs_5_) | copy-start | bytes 589828
  266.5 15.5 %collective-permute-start.28 = (bf16[384,256]{1,0:T(8,128)(2,1)}, bf16[384,256]{1,0:T(8,128)(2,1)S(1)}, u32[]{:S(2)}, u32[]{:S(2)}) collective-permute-start(bf16[384,256]{1,0:T(8,128)(2,1)} %get-tuple-element.26), channel_id=1, source_target_pairs={{0,8},{4,12},{8,0},{12,4},{1,9},{5,13},{9,1},{13,5},{2,10},{6,14},... | collective-permute-start | bytes 589832 | tf_op jit(solution)/shard_map/ppermute | solution.py:280
  269.5 8.7 %copy-start.24 = (bf16[384,256]{1,0:T(8,128)(2,1)}, bf16[384,256]{1,0:T(8,128)(2,1)S(1)}, u32[]{:S(2)}) copy-start(bf16[384,256]{1,0:T(8,128)(2,1)S(1)} %collective-permute-done.20.refs_6_) | copy-start | bytes 589828
  269.5 13.9 %collective-permute-start.29 = (bf16[384,256]{1,0:T(8,128)(2,1)}, bf16[384,256]{1,0:T(8,128)(2,1)S(1)}, u32[]{:S(2)}, u32[]{:S(2)}) collective-permute-start(bf16[384,256]{1,0:T(8,128)(2,1)} %get-tuple-element.27), channel_id=1, source_target_pairs={{0,4},{4,8},{8,12},{12,0},{1,5},{5,9},{9,13},{13,1},{2,6},{6,10},{... | collective-permute-start | bytes 589832 | tf_op jit(solution)/shard_map/ppermute | solution.py:280
  278.2 0.7 copy-start.25
  278.2 8.3 %collective-permute-start.30 = (bf16[384,256]{1,0:T(8,128)(2,1)}, bf16[384,256]{1,0:T(8,128)(2,1)S(1)}, u32[]{:S(2)}, u32[]{:S(2)}) collective-permute-start(bf16[384,256]{1,0:T(8,128)(2,1)} %get-tuple-element.28), channel_id=1, source_target_pairs={{0,12},{4,0},{8,4},{12,8},{1,13},{5,1},{9,5},{13,9},{2,14},{6,2},{... | collective-permute-start | bytes 589832 | tf_op jit(solution)/shard_map/ppermute | solution.py:280
  278.2 0.8 copy-start.21
  279.0 0.7 copy-start.22
  282.1 4.4 %copy-start.26 = (bf16[384,256]{1,0:T(8,128)(2,1)}, bf16[384,256]{1,0:T(8,128)(2,1)S(1)}, u32[]{:S(2)}) copy-start(bf16[384,256]{1,0:T(8,128)(2,1)S(1)} %collective-permute-done.28.refs_2_) | copy-start | bytes 589828
  283.4 3.0 %copy-start.27 = (bf16[384,256]{1,0:T(8,128)(2,1)}, bf16[384,256]{1,0:T(8,128)(2,1)S(1)}, u32[]{:S(2)}) copy-start(bf16[384,256]{1,0:T(8,128)(2,1)S(1)} %collective-permute-done.29.refs_3_) | copy-start | bytes 589828
  286.4 0.7 copy-start.28
Sparse Core Ops, SparseCore 0:
  8.9 29.6 all-gather.4
  40.2 28.5 all-gather.6
  70.3 28.5 all-gather.8
  113.0 30.4 all-gather.10

commit v18 on v17

--- a/solution.py
+++ b/solution.py
@@ -264,7 +264,7 @@
             whole.append(lax.all_gather(value, "col", axis=1, tiled=True))
 
     def weights(shift, low, high, users):
-        after = sent[-1:] + arrived[:len(sent) - 2][-1:] * (len(sent) > 2) + swapped[:len(sent) - 3][-1:] * (len(sent) > 3)
+        after = sent[-1:] + arrived[:len(sent) - 2][-1:] * (len(sent) > 2) + swapped[:len(sent) - 3][-1:] * (len(sent) > 4)
         sent.append(pack(gate_weight, up_weight, shift, low, high - low, after))
         arrived.append(lax.ppermute(sent[-1], "row", around(rows, shift)))
         came = hold(arrived[-1], done) if done else arrived[-1]

time: 299 us -> 303 us (1.013)
  waiting for transfers between devices: 155 us -> 160 us
    ppermute x8, waiting for transfers between devices: 7.3 us -> 23.7 us  [weights(): swapped.append(lax.ppermute(came, 'parts', around(parts, -turn)))]
    ppermute x8, waiting for transfers between devices: 95.5 us -> 85.5 us  [weights(): arrived.append(lax.ppermute(sent[-1], 'row', around(rows, shift)))]
    unnamed x58 -> x54, local copies, waits for them, and re-layouts: 8.77 us -> 8.97 us
  transfers between devices with their start and end apart: 35 -> 35, of which waited for: 18 -> 15; matrix products, arithmetic and copies ran while one was open for 1% -> 1% of each run, Pallas kernels for 21% -> 20%
where the time goes in v18:
time: 303 us; the launch traced here: 301 us
  waiting for transfers between devices  160 us (53%)
  Pallas kernels  63.2 us (21%)
  starting transfers between devices  52.7 us (17%)
  between operations  13.5 us (4%)
  local copies, waits for them, and re-layouts  8.97 us (3%)
    ppermute x8, waiting for transfers between devices, weights(): arrived.append(lax.ppermute(sent[-1], 'row', around(rows, shift)))  85.5 us
    pallas_call x3, Pallas kernels, product(): pl.pallas_call(body, out_shape=[jax.ShapeDtypeStruct((mine, wide), jnp.bf...  40.1 us
    ppermute x3, waiting for transfers between devices, tokens_of(): lax.ppermute(upper[-1], 'row', [(i, i - 1) for i in range(1, rows - step...  35.7 us
    ppermute x8, waiting for transfers between devices, weights(): swapped.append(lax.ppermute(came, 'parts', around(parts, -turn)))  23.7 us
    pallas_call x8, Pallas kernels, pack(): pl.pallas_call(body, out_shape=jax.ShapeDtypeStruct((share, 2 * wide), ga...  16.6 us
    ppermute x9, starting transfers between devices, hidden_of(): lax.ppermute(outs[shift], 'row', around(rows, shift))  14.8 us
    ppermute x8, starting transfers between devices, weights(): arrived.append(lax.ppermute(sent[-1], 'row', around(rows, shift)))  12.5 us
    ppermute x9, waiting for transfers between devices, hidden_of(): lax.ppermute(outs[shift], 'row', around(rows, shift))  11.2 us
  transfers between devices with their start and end apart: 35, of which 15 were waited for; matrix products, arithmetic and copies ran while one was open for 1% of the time, Pallas kernels for 20%

profile of v18, /device:TPU:12, one launch (start us, length us, event | category | flops | bytes accessed | tf_op | source)
XLA Modules:
  0.0 300.8 jit_solution(14371657373219506769)
XLA Ops:
  6.5 0.7 all-gather.5.cloned.1.call-update
  7.3 2.4 collective-permute-start
  9.7 3.5 %collective-permute-start.1 = (bf16[384,1024]{1,0:T(8,128)(2,1)}, bf16[384,1024]{1,0:T(8,128)(2,1)S(1)}, u32[]{:S(2)}, u32[]{:S(2)}) collective-permute-start(bf16[384,1024]{1,0:T(8,128)(2,1)} %param.3), channel_id=1, source_target_pairs={{0,4},{4,8},{8,12},{1,5},{5,9},{9,13},{2,6},{6,10},{10,14},{3,7},{... | collective-permute-start | bytes 2359304 | tf_op jit(solution)/shard_map/ppermute | solution.py:245
  13.2 2.6 pack.8.refs_1_.refs_2_
  15.7 13.0 %collective-permute-done.refs_2_ = bf16[384,1024]{1,0:T(8,128)(2,1)S(1)} collective-permute-done((bf16[384,1024]{1,0:T(8,128)(2,1)}, bf16[384,1024]{1,0:T(8,128)(2,1)S(1)}, u32[]{:S(2)}, u32[]{:S(2)}) %collective-permute-start) | collective-permute-done | bytes 786464 | tf_op jit(solution)/shard_map/ppermute | solution.py:246
  28.7 2.1 collective-permute-done.1.refs_1_
  30.8 1.1 broadcast_select_fusion.1.refs_0_
  32.0 2.1 collective-permute-start.2
  34.0 4.0 %collective-permute-start.3 = (bf16[384,1024]{1,0:T(8,128)(2,1)S(1)}, bf16[384,1024]{1,0:T(8,128)(2,1)S(1)}, u32[]{:S(2)}, u32[]{:S(2)}) collective-permute-start(bf16[384,1024]{1,0:T(8,128)(2,1)S(1)} %collective-permute-done.1.refs_1_), channel_id=1, source_target_pairs={{4,8},{8,12},{5,9},{9,13},{6,10},{10,14},{7,11},{11,15},{20,24},{2... | collective-permute-start | bytes 2359304 | tf_op jit(solution)/shard_map/ppermute | solution.py:245
  38.0 14.1 %collective-permute-done.2 = bf16[384,1024]{1,0:T(8,128)(2,1)S(1)} collective-permute-done((bf16[384,1024]{1,0:T(8,128)(2,1)S(1)}, bf16[384,1024]{1,0:T(8,128)(2,1)S(1)}, u32[]{:S(2)}, u32[]{:S(2)}) %collective-permute-start.2) | collective-permute-done | bytes 786464 | tf_op jit(solution)/shard_map/ppermute | solution.py:246
  52.2 1.2 collective-permute-done.3
  53.4 0.9 copy-done.15
  54.3 1.0 broadcast_select_fusion
  55.4 2.3 collective-permute-start.6
  57.7 3.7 %collective-permute-start.4 = (bf16[384,1024]{1,0:T(8,128)(2,1)}, bf16[384,1024]{1,0:T(8,128)(2,1)S(1)}, u32[]{:S(2)}, u32[]{:S(2)}) collective-permute-start(bf16[384,1024]{1,0:T(8,128)(2,1)} %copy-done.14), channel_id=1, source_target_pairs={{4,0},{5,1},{6,2},{7,3},{20,16},{21,17},{22,18},{23,19}} | collective-permute-start | bytes 2359304 | tf_op jit(solution)/shard_map/ppermute | solution.py:246
  61.3 1.6 collective-permute-start.5
  62.9 2.2 pack.9.refs_2_
  65.1 2.2 pack.10.refs_3_.refs_2_
  67.3 8.7 %collective-permute-done.4.refs_0_ = bf16[384,1024]{1,0:T(8,128)(2,1)S(1)} collective-permute-done((bf16[384,1024]{1,0:T(8,128)(2,1)}, bf16[384,1024]{1,0:T(8,128)(2,1)S(1)}, u32[]{:S(2)}, u32[]{:S(2)}) %collective-permute-start.4) | collective-permute-done | bytes 786464 | tf_op jit(solution)/shard_map/ppermute | solution.py:246
  75.9 0.9 copy-done.16
  76.8 2.1 pick.1.refs_0_
  78.9 33.0 %collective-permute-done.6.refs_1_.refs_6_.refs_3_ = bf16[512,1280]{1,0:T(8,128)(2,1)S(1)} collective-permute-done((bf16[512,1280]{1,0:T(8,128)(2,1)S(1)}, bf16[512,1280]{1,0:T(8,128)(2,1)S(1)}, u32[]{:S(2)}, u32[]{:S(2)}) %collective-permute-start.6) | collective-permute-done | bytes 1310752 | tf_op jit(solution)/shard_map/ppermute | solution.py:269
  111.9 1.1 copy-done
  113.0 1.1 copy-done.3
  114.4 1.9 collective-permute-start.10
  116.3 18.4 %collective-permute-done.8.refs_8_.refs_3_ = bf16[512,768]{1,0:T(8,128)(2,1)} collective-permute-done((bf16[512,768]{1,0:T(8,128)(2,1)S(1)}, bf16[512,768]{1,0:T(8,128)(2,1)}, u32[]{:S(2)}, u32[]{:S(2)}) %collective-permute-start.8) | collective-permute-done | bytes 786464 | tf_op jit(solution)/shard_map/ppermute | solution.py:269
  134.7 1.0 collective-permute-start.9
  135.7 1.0 collective-permute-start.7
  136.8 2.0 pack.11.refs_2_
  138.7 1.9 collective-permute-start.22
  140.7 34.1 %collective-permute-done.10.refs_10_.refs_3_ = bf16[512,768]{1,0:T(8,128)(2,1)} collective-permute-done((bf16[512,768]{1,0:T(8,128)(2,1)S(1)}, bf16[512,768]{1,0:T(8,128)(2,1)}, u32[]{:S(2)}, u32[]{:S(2)}) %collective-permute-start.10) | collective-permute-done | bytes 786464 | tf_op jit(solution)/shard_map/ppermute | solution.py:269
  174.7 1.0 collective-permute-start.11
  175.7 1.9 pack.12.refs_2_
  177.8 0.9 copy-done.13
  178.7 2.0 pack.13.refs_2_
  180.6 2.1 collective-permute-start.17
  182.7 1.1 collective-permute-start.23
  183.8 16.7 %collective-permute-done.11.refs_11_.refs_4_ = bf16[512,768]{1,0:T(8,128)(2,1)} collective-permute-done((bf16[512,768]{1,0:T(8,128)(2,1)}, bf16[512,768]{1,0:T(8,128)(2,1)}, u32[]{:S(2)}, u32[]{:S(2)}) %collective-permute-start.11) | collective-permute-done | bytes 786464 | tf_op jit(solution)/shard_map/ppermute | solution.py:273
  200.5 1.9 pack.14.refs_2_
  202.5 1.1 collective-permute-start.16
  203.6 1.0 collective-permute-start.18
  204.6 7.0 %collective-permute-done.23.refs_4_.refs_7_ = bf16[512,512]{1,0:T(8,128)(2,1)S(1)} collective-permute-done((bf16[512,512]{1,0:T(8,128)(2,1)S(1)}, bf16[512,512]{1,0:T(8,128)(2,1)S(1)}, u32[]{:S(2)}, u32[]{:S(2)}) %collective-permute-start.23) | collective-permute-done | bytes 524320 | tf_op jit(solution)/shard_map/ppermute | solution.py:273
  211.6 0.8 copy-done.7
  212.4 1.9 pack.15
  214.3 3.9 %collective-permute-start.26 = (bf16[512,512]{1,0:T(8,128)(2,1)}, bf16[512,512]{1,0:T(8,128)(2,1)S(1)}, u32[]{:S(2)}, u32[]{:S(2)}) collective-permute-start(bf16[512,512]{1,0:T(8,128)(2,1)} %pack.15), channel_id=1, source_target_pairs={{0,12},{4,0},{8,4},{12,8},{1,13},{5,1},{9,5},{13,9},{2,14},{6,2},{... | collective-permute-start | bytes 1572872 | tf_op jit(solution)/shard_map/ppermute | solution.py:269
  218.3 1.0 copy-done.11
  219.3 16.5 %product.3 = (bf16[384,384]{1,0:T(8,128)(2,1)}, bf16[384,384]{1,0:T(8,128)(2,1)}, bf16[384,384]{1,0:T(8,128)(2,1)}, bf16[384,384]{1,0:T(8,128)(2,1)}) custom-call(bf16[384,4096]{1,0:T(8,128)(2,1)} %all-gather.5.cloned.1.call-done.refs_0_, bf16[384,4096]{1,0:T(8,128)(2,1)} %all-gather.7.cloned.1.call-done.refs_1_, ...), custom_call_target="tpu_custom_call" | custom-call | flops 9663676416 | bytes 20054016 | tf_op jit(solution)/shard_map/product/pallas_call | solution.py:138
  235.9 1.5 collective-permute-start.13
  238.2 1.0 collective-permute-start.25
  239.2 1.0 collective-permute-start.27
  240.2 11.8 %product.4 = (bf16[384,256]{1,0:T(8,128)(2,1)}, bf16[384,256]{1,0:T(8,128)(2,1)}, bf16[384,256]{1,0:T(8,128)(2,1)}, bf16[384,256]{1,0:T(8,128)(2,1)}) custom-call(bf16[384,4096]{1,0:T(8,128)(2,1)} %all-gather.5.cloned.1.call-done.refs_0_, bf16[384,4096]{1,0:T(8,128)(2,1)} %all-gather.7.cloned.1.call-done.refs_1_, ...), custom_call_target="tpu_custom_call" | custom-call | flops 6442450944 | bytes 17563648 | tf_op jit(solution)/shard_map/product/pallas_call | solution.py:138
  252.1 1.1 collective-permute-done.12.refs_1_.refs_13_
  253.2 3.1 %collective-permute-start.19 = (bf16[384,256]{1,0:T(8,128)(2,1)}, bf16[384,256]{1,0:T(8,128)(2,1)S(1)}, u32[]{:S(2)}, u32[]{:S(2)}) collective-permute-start(bf16[384,256]{1,0:T(8,128)(2,1)} %get-tuple-element.22), channel_id=1, source_target_pairs={{0,8},{4,12},{8,0},{12,4},{1,9},{5,13},{9,1},{13,5},{2,10},{6,14},... | collective-permute-start | bytes 589832 | tf_op jit(solution)/shard_map/ppermute | solution.py:280
  256.3 1.6 collective-permute-start.20
  257.9 2.1 collective-permute-start.21
  260.0 11.8 %product.5 = (bf16[384,256]{1,0:T(8,128)(2,1)}, bf16[384,256]{1,0:T(8,128)(2,1)}, bf16[384,256]{1,0:T(8,128)(2,1)}, bf16[384,256]{1,0:T(8,128)(2,1)}) custom-call(bf16[384,4096]{1,0:T(8,128)(2,1)} %all-gather.5.cloned.1.call-done.refs_0_, bf16[384,4096]{1,0:T(8,128)(2,1)} %all-gather.7.cloned.1.call-done.refs_1_, ...), custom_call_target="tpu_custom_call" | custom-call | flops 6442450944 | bytes 17563648 | tf_op jit(solution)/shard_map/product/pallas_call | solution.py:138
  271.8 2.2 collective-permute-done.19.refs_5_
  274.0 3.4 %collective-permute-start.28 = (bf16[384,256]{1,0:T(8,128)(2,1)}, bf16[384,256]{1,0:T(8,128)(2,1)S(1)}, u32[]{:S(2)}, u32[]{:S(2)}) collective-permute-start(bf16[384,256]{1,0:T(8,128)(2,1)} %get-tuple-element.26), channel_id=1, source_target_pairs={{0,8},{4,12},{8,0},{12,4},{1,9},{5,13},{9,1},{13,5},{2,10},{6,14},... | collective-permute-start | bytes 589832 | tf_op jit(solution)/shard_map/ppermute | solution.py:280
  277.4 5.1 %collective-permute-done.20.refs_6_ = bf16[384,256]{1,0:T(8,128)(2,1)S(1)} collective-permute-done((bf16[384,256]{1,0:T(8,128)(2,1)}, bf16[384,256]{1,0:T(8,128)(2,1)S(1)}, u32[]{:S(2)}, u32[]{:S(2)}) %collective-permute-start.20) | collective-permute-done | bytes 196640 | tf_op jit(solution)/shard_map/ppermute | solution.py:280
  282.5 2.4 collective-permute-start.29
  286.4 2.4 place.2.refs_0_
  288.8 1.7 collective-permute-done.29.refs_3_
  290.5 1.1 collective-permute-done.30.refs_4_
  292.3 2.0 place.3
  (84 shorter events, 3.7 us)
Async XLA Ops:
  6.5 211.7 %all-gather.5.cloned.1.call-start = ((), (), s32[]{:S(2)}) async-start(), calls=%async_computation | async-start | bytes 3932160 | tf_op jit(solution)/shard_map/all_gather | solution.py:264
  7.3 211.0 %all-gather.7.cloned.1.call-start = ((), (), s32[]{:S(2)}) async-start(), calls=%async_computation.1 | async-start | bytes 3932160 | tf_op jit(solution)/shard_map/all_gather | solution.py:264
  7.3 21.4 %collective-permute-start = (bf16[384,1024]{1,0:T(8,128)(2,1)}, bf16[384,1024]{1,0:T(8,128)(2,1)S(1)}, u32[]{:S(2)}, u32[]{:S(2)}) collective-permute-start(bf16[384,1024]{1,0:T(8,128)(2,1)} %param.3), channel_id=1, source_target_pairs={{4,0},{8,4},{12,8},{5,1},{9,5},{13,9},{6,2},{10,6},{14,10},{7,3},{... | collective-permute-start | bytes 2359304 | tf_op jit(solution)/shard_map/ppermute | solution.py:246
  9.7 21.1 %collective-permute-start.1 = (bf16[384,1024]{1,0:T(8,128)(2,1)}, bf16[384,1024]{1,0:T(8,128)(2,1)S(1)}, u32[]{:S(2)}, u32[]{:S(2)}) collective-permute-start(bf16[384,1024]{1,0:T(8,128)(2,1)} %param.3), channel_id=1, source_target_pairs={{0,4},{4,8},{8,12},{1,5},{5,9},{9,13},{2,6},{6,10},{10,14},{3,7},{... | collective-permute-start | bytes 2359304 | tf_op jit(solution)/shard_map/ppermute | solution.py:245
  28.7 26.6 %copy-start.4 = (bf16[384,1024]{1,0:T(8,128)(2,1)}, bf16[384,1024]{1,0:T(8,128)(2,1)S(1)}, u32[]{:S(2)}) copy-start(bf16[384,1024]{1,0:T(8,128)(2,1)S(1)} %collective-permute-done.refs_2_) | copy-start | bytes 2359300
  30.8 24.5 %copy-start.5 = (bf16[384,1024]{1,0:T(8,128)(2,1)}, bf16[384,1024]{1,0:T(8,128)(2,1)S(1)}, u32[]{:S(2)}) copy-start(bf16[384,1024]{1,0:T(8,128)(2,1)S(1)} %collective-permute-done.1.refs_1_) | copy-start | bytes 2359300
  31.9 23.5 %copy-start.1 = (bf16[512,1280]{1,0:T(8,128)(2,1)S(1)}, bf16[512,1280]{1,0:T(8,128)(2,1)}, u32[]{:S(2)}) copy-start(bf16[512,1280]{1,0:T(8,128)(2,1)} %pack.8.refs_1_.refs_2_) | copy-start | bytes 3932164
  31.9 186.4 %all-gather.9.cloned.1.call-start = ((), (), s32[]{:S(2)}) async-start(), calls=%async_computation.2 | async-start | bytes 3932160 | tf_op jit(solution)/shard_map/all_gather | solution.py:264
  32.0 20.2 %collective-permute-start.2 = (bf16[384,1024]{1,0:T(8,128)(2,1)S(1)}, bf16[384,1024]{1,0:T(8,128)(2,1)S(1)}, u32[]{:S(2)}, u32[]{:S(2)}) collective-permute-start(bf16[384,1024]{1,0:T(8,128)(2,1)S(1)} %collective-permute-done.refs_2_), channel_id=1, source_target_pairs={{4,0},{8,4},{5,1},{9,5},{6,2},{10,6},{7,3},{11,7},{20,16},{24,20},... | collective-permute-start | bytes 2359304 | tf_op jit(solution)/shard_map/ppermute | solution.py:246
  34.0 19.4 %collective-permute-start.3 = (bf16[384,1024]{1,0:T(8,128)(2,1)S(1)}, bf16[384,1024]{1,0:T(8,128)(2,1)S(1)}, u32[]{:S(2)}, u32[]{:S(2)}) collective-permute-start(bf16[384,1024]{1,0:T(8,128)(2,1)S(1)} %collective-permute-done.1.refs_1_), channel_id=1, source_target_pairs={{4,8},{8,12},{5,9},{9,13},{6,10},{10,14},{7,11},{11,15},{20,24},{2... | collective-permute-start | bytes 2359304 | tf_op jit(solution)/shard_map/ppermute | solution.py:245
  52.2 1.2 copy-start.14
  53.4 0.9 copy-start.15
  55.3 163.0 %all-gather.11.cloned.1.call-start = ((), (), s32[]{:S(2)}) async-start(), calls=%async_computation.3 | async-start | bytes 3932160 | tf_op jit(solution)/shard_map/all_gather | solution.py:264
  55.4 56.5 %collective-permute-start.6 = (bf16[512,1280]{1,0:T(8,128)(2,1)S(1)}, bf16[512,1280]{1,0:T(8,128)(2,1)S(1)}, u32[]{:S(2)}, u32[]{:S(2)}) collective-permute-start(bf16[512,1280]{1,0:T(8,128)(2,1)S(1)} %copy-done.1), channel_id=1, source_target_pairs={{0,8},{4,12},{8,0},{12,4},{1,9},{5,13},{9,1},{13,5},{2,10},{6,14},... | collective-permute-start | bytes 3932168 | tf_op jit(solution)/shard_map/ppermute | solution.py:269
  57.7 18.3 %collective-permute-start.4 = (bf16[384,1024]{1,0:T(8,128)(2,1)}, bf16[384,1024]{1,0:T(8,128)(2,1)S(1)}, u32[]{:S(2)}, u32[]{:S(2)}) collective-permute-start(bf16[384,1024]{1,0:T(8,128)(2,1)} %copy-done.14), channel_id=1, source_target_pairs={{4,0},{5,1},{6,2},{7,3},{20,16},{21,17},{22,18},{23,19}} | collective-permute-start | bytes 2359304 | tf_op jit(solution)/shard_map/ppermute | solution.py:246
  61.3 14.6 %collective-permute-start.5 = (bf16[384,1024]{1,0:T(8,128)(2,1)}, bf16[384,1024]{1,0:T(8,128)(2,1)}, u32[]{:S(2)}, u32[]{:S(2)}) collective-permute-start(bf16[384,1024]{1,0:T(8,128)(2,1)} %copy-done.15), channel_id=1, source_target_pairs={{8,12},{9,13},{10,14},{11,15},{24,28},{25,29},{26,30},{27,31}} | collective-permute-start | bytes 2359304 | tf_op jit(solution)/shard_map/ppermute | solution.py:245
  75.9 0.9 copy-start.16
  78.9 35.4 %copy-start.2 = (bf16[512,768]{1,0:T(8,128)(2,1)S(1)}, bf16[512,768]{1,0:T(8,128)(2,1)}, u32[]{:S(2)}) copy-start(bf16[512,768]{1,0:T(8,128)(2,1)} %pack.10.refs_3_.refs_2_) | copy-start | bytes 2359300
  111.9 1.1 copy-start
  112.9 1.1 copy-start.3
  114.1 20.7 %collective-permute-start.8 = (bf16[512,768]{1,0:T(8,128)(2,1)S(1)}, bf16[512,768]{1,0:T(8,128)(2,1)}, u32[]{:S(2)}, u32[]{:S(2)}) collective-permute-start(bf16[512,768]{1,0:T(8,128)(2,1)S(1)} %copy-done.3), channel_id=1, source_target_pairs={{0,4},{4,8},{8,12},{12,0},{1,5},{5,9},{9,13},{13,1},{2,6},{6,10},{... | collective-permute-start | bytes 2359304 | tf_op jit(solution)/shard_map/ppermute | solution.py:269
  114.4 60.4 %collective-permute-start.10 = (bf16[512,768]{1,0:T(8,128)(2,1)S(1)}, bf16[512,768]{1,0:T(8,128)(2,1)}, u32[]{:S(2)}, u32[]{:S(2)}) collective-permute-start(bf16[512,768]{1,0:T(8,128)(2,1)S(1)} %copy-done.2), channel_id=1, source_target_pairs={{0,12},{4,0},{8,4},{12,8},{1,13},{5,1},{9,5},{13,9},{2,14},{6,2},{... | collective-permute-start | bytes 2359304 | tf_op jit(solution)/shard_map/ppermute | solution.py:269
  134.7 43.0 %collective-permute-start.9 = (bf16[512,768]{1,0:T(8,128)(2,1)}, bf16[512,768]{1,0:T(8,128)(2,1)S(1)}, u32[]{:S(2)}, u32[]{:S(2)}) collective-permute-start(bf16[512,768]{1,0:T(8,128)(2,1)} %collective-permute-done.8.refs_8_.refs_3_), channel_id=1, source_target_pairs={{0,16},{16,0},{1,17},{17,1},{2,18},{18,2},{3,19},{19,3},{4,20},{20... | collective-permute-start | bytes 2359304 | tf_op jit(solution)/shard_map/ppermute | solution.py:273
  135.7 82.6 %collective-permute-start.7 = (bf16[512,1280]{1,0:T(8,128)(2,1)}, bf16[512,1280]{1,0:T(8,128)(2,1)S(1)}, u32[]{:S(2)}, u32[]{:S(2)}) collective-permute-start(bf16[512,1280]{1,0:T(8,128)(2,1)} %copy-done), channel_id=1, source_target_pairs={{0,16},{16,0},{1,17},{17,1},{2,18},{18,2},{3,19},{19,3},{4,20},{20... | collective-permute-start | bytes 3932168 | tf_op jit(solution)/shard_map/ppermute | solution.py:273
  138.7 44.0 %collective-permute-start.22 = (bf16[512,512]{1,0:T(8,128)(2,1)}, bf16[512,512]{1,0:T(8,128)(2,1)S(1)}, u32[]{:S(2)}, u32[]{:S(2)}) collective-permute-start(bf16[512,512]{1,0:T(8,128)(2,1)} %pack.11.refs_2_), channel_id=1, source_target_pairs={{0,8},{4,12},{8,0},{12,4},{1,9},{5,13},{9,1},{13,5},{2,10},{6,14},... | collective-permute-start | bytes 1572872 | tf_op jit(solution)/shard_map/ppermute | solution.py:269
  174.7 25.7 %collective-permute-start.11 = (bf16[512,768]{1,0:T(8,128)(2,1)}, bf16[512,768]{1,0:T(8,128)(2,1)}, u32[]{:S(2)}, u32[]{:S(2)}) collective-permute-start(bf16[512,768]{1,0:T(8,128)(2,1)} %collective-permute-done.10.refs_10_.refs_3_), channel_id=1, source_target_pairs={{0,16},{16,0},{1,17},{17,1},{2,18},{18,2},{3,19},{19,3},{4,20},{20... | collective-permute-start | bytes 2359304 | tf_op jit(solution)/shard_map/ppermute | solution.py:273
  177.7 24.8 %collective-permute-start.15 = (bf16[512,512]{1,0:T(8,128)(2,1)}, bf16[512,512]{1,0:T(8,128)(2,1)S(1)}, u32[]{:S(2)}, u32[]{:S(2)}) collective-permute-start(bf16[512,512]{1,0:T(8,128)(2,1)} %pack.12.refs_2_), channel_id=1, source_target_pairs={{0,4},{4,8},{8,12},{12,0},{1,5},{5,9},{9,13},{13,1},{2,6},{6,10},{... | collective-permute-start | bytes 1572872 | tf_op jit(solution)/shard_map/ppermute | solution.py:269
  177.8 0.9 copy-start.13
  180.6 22.9 %collective-permute-start.17 = (bf16[512,512]{1,0:T(8,128)(2,1)}, bf16[512,512]{1,0:T(8,128)(2,1)}, u32[]{:S(2)}, u32[]{:S(2)}) collective-permute-start(bf16[512,512]{1,0:T(8,128)(2,1)} %pack.13.refs_2_), channel_id=1, source_target_pairs={{0,12},{4,0},{8,4},{12,8},{1,13},{5,1},{9,5},{13,9},{2,14},{6,2},{... | collective-permute-start | bytes 1572872 | tf_op jit(solution)/shard_map/ppermute | solution.py:269
  182.7 17.8 %copy-start.6 = (bf16[512,512]{1,0:T(8,128)(2,1)}, bf16[512,512]{1,0:T(8,128)(2,1)S(1)}, u32[]{:S(2)}) copy-start(bf16[512,512]{1,0:T(8,128)(2,1)S(1)} %collective-permute-done.22.refs_3_.refs_6_) | copy-start | bytes 1572868
  182.7 28.9 %collective-permute-start.23 = (bf16[512,512]{1,0:T(8,128)(2,1)S(1)}, bf16[512,512]{1,0:T(8,128)(2,1)S(1)}, u32[]{:S(2)}, u32[]{:S(2)}) collective-permute-start(bf16[512,512]{1,0:T(8,128)(2,1)S(1)} %collective-permute-done.22.refs_3_.refs_6_), channel_id=1, source_target_pairs={{0,16},{16,0},{1,17},{17,1},{2,18},{18,2},{3,19},{19,3},{4,20},{20... | collective-permute-start | bytes 1572872 | tf_op jit(solution)/shard_map/ppermute | solution.py:273
  202.4 33.5 %collective-permute-start.24 = (bf16[512,512]{1,0:T(8,128)(2,1)}, bf16[512,512]{1,0:T(8,128)(2,1)S(1)}, u32[]{:S(2)}, u32[]{:S(2)}) collective-permute-start(bf16[512,512]{1,0:T(8,128)(2,1)} %pack.14.refs_2_), channel_id=1, source_target_pairs={{0,4},{4,8},{8,12},{12,0},{1,5},{5,9},{9,13},{13,1},{2,6},{6,10},{... | collective-permute-start | bytes 1572872 | tf_op jit(solution)/shard_map/ppermute | solution.py:269
  202.5 9.1 %copy-start.8 = (bf16[512,512]{1,0:T(8,128)(2,1)}, bf16[512,512]{1,0:T(8,128)(2,1)S(1)}, u32[]{:S(2)}) copy-start(bf16[512,512]{1,0:T(8,128)(2,1)S(1)} %collective-permute-done.15.refs_8_.refs_3_) | copy-start | bytes 1572868
  202.5 35.7 %collective-permute-start.16 = (bf16[512,512]{1,0:T(8,128)(2,1)S(1)}, bf16[512,512]{1,0:T(8,128)(2,1)}, u32[]{:S(2)}, u32[]{:S(2)}) collective-permute-start(bf16[512,512]{1,0:T(8,128)(2,1)S(1)} %collective-permute-done.15.refs_8_.refs_3_), channel_id=1, source_target_pairs={{0,16},{16,0},{1,17},{17,1},{2,18},{18,2},{3,19},{19,3},{4,20},{20... | collective-permute-start | bytes 1572872 | tf_op jit(solution)/shard_map/ppermute | solution.py:273
  203.6 35.6 %collective-permute-start.18 = (bf16[512,512]{1,0:T(8,128)(2,1)}, bf16[512,512]{1,0:T(8,128)(2,1)}, u32[]{:S(2)}, u32[]{:S(2)}) collective-permute-start(bf16[512,512]{1,0:T(8,128)(2,1)} %collective-permute-done.17.refs_10_), channel_id=1, source_target_pairs={{0,16},{16,0},{1,17},{17,1},{2,18},{18,2},{3,19},{19,3},{4,20},{20... | collective-permute-start | bytes 1572872 | tf_op jit(solution)/shard_map/ppermute | solution.py:273
  211.6 0.8 copy-start.7
  214.3 23.1 %collective-permute-start.26 = (bf16[512,512]{1,0:T(8,128)(2,1)}, bf16[512,512]{1,0:T(8,128)(2,1)S(1)}, u32[]{:S(2)}, u32[]{:S(2)}) collective-permute-start(bf16[512,512]{1,0:T(8,128)(2,1)} %pack.15), channel_id=1, source_target_pairs={{0,12},{4,0},{8,4},{12,8},{1,13},{5,1},{9,5},{13,9},{2,14},{6,2},{... | collective-permute-start | bytes 1572872 | tf_op jit(solution)/shard_map/ppermute | solution.py:269
  218.3 1.1 copy-start.11
  235.8 17.3 %collective-permute-start.12 = (bf16[384,384]{1,0:T(8,128)(2,1)}, bf16[384,384]{1,0:T(8,128)(2,1)S(1)}, u32[]{:S(2)}, u32[]{:S(2)}) collective-permute-start(bf16[384,384]{1,0:T(8,128)(2,1)} %get-tuple-element.18), channel_id=1, source_target_pairs={{0,8},{4,12},{8,0},{12,4},{1,9},{5,13},{9,1},{13,5},{2,10},{6,14},... | collective-permute-start | bytes 884744 | tf_op jit(solution)/shard_map/ppermute | solution.py:280
  235.9 1.5 copy-start.9
  235.9 48.9 %collective-permute-start.13 = (bf16[384,384]{1,0:T(8,128)(2,1)}, bf16[384,384]{1,0:T(8,128)(2,1)S(1)}, u32[]{:S(2)}, u32[]{:S(2)}) collective-permute-start(bf16[384,384]{1,0:T(8,128)(2,1)} %get-tuple-element.19), channel_id=1, source_target_pairs={{0,4},{4,8},{8,12},{12,0},{1,5},{5,9},{9,13},{13,1},{2,6},{6,10},{... | collective-permute-start | bytes 884744 | tf_op jit(solution)/shard_map/ppermute | solution.py:280
  237.4 0.8 copy-start.10
  237.4 47.5 %collective-permute-start.14 = (bf16[384,384]{1,0:T(8,128)(2,1)}, bf16[384,384]{1,0:T(8,128)(2,1)S(1)}, u32[]{:S(2)}, u32[]{:S(2)}) collective-permute-start(bf16[384,384]{1,0:T(8,128)(2,1)} %get-tuple-element.20), channel_id=1, source_target_pairs={{0,12},{4,0},{8,4},{12,8},{1,13},{5,1},{9,5},{13,9},{2,14},{6,2},{... | collective-permute-start | bytes 884744 | tf_op jit(solution)/shard_map/ppermute | solution.py:280
  238.2 18.1 %collective-permute-start.25 = (bf16[512,512]{1,0:T(8,128)(2,1)}, bf16[512,512]{1,0:T(8,128)(2,1)S(1)}, u32[]{:S(2)}, u32[]{:S(2)}) collective-permute-start(bf16[512,512]{1,0:T(8,128)(2,1)} %hold.6.refs_8_), channel_id=1, source_target_pairs={{0,16},{16,0},{1,17},{17,1},{2,18},{18,2},{3,19},{19,3},{4,20},{20... | collective-permute-start | bytes 1572872 | tf_op jit(solution)/shard_map/ppermute | solution.py:273
  239.2 18.7 %collective-permute-start.27 = (bf16[512,512]{1,0:T(8,128)(2,1)}, bf16[512,512]{1,0:T(8,128)(2,1)S(1)}, u32[]{:S(2)}, u32[]{:S(2)}) collective-permute-start(bf16[512,512]{1,0:T(8,128)(2,1)} %hold.7.refs_10_), channel_id=1, source_target_pairs={{0,16},{16,0},{1,17},{17,1},{2,18},{18,2},{3,19},{19,3},{4,20},{20... | collective-permute-start | bytes 1572872 | tf_op jit(solution)/shard_map/ppermute | solution.py:273
  253.2 6.8 %copy-start.12 = (bf16[384,384]{1,0:T(8,128)(2,1)}, bf16[384,384]{1,0:T(8,128)(2,1)S(1)}, u32[]{:S(2)}) copy-start(bf16[384,384]{1,0:T(8,128)(2,1)S(1)} %collective-permute-done.12.refs_1_.refs_13_) | copy-start | bytes 884740
  253.2 20.9 %collective-permute-start.19 = (bf16[384,256]{1,0:T(8,128)(2,1)}, bf16[384,256]{1,0:T(8,128)(2,1)S(1)}, u32[]{:S(2)}, u32[]{:S(2)}) collective-permute-start(bf16[384,256]{1,0:T(8,128)(2,1)} %get-tuple-element.22), channel_id=1, source_target_pairs={{0,8},{4,12},{8,0},{12,4},{1,9},{5,13},{9,1},{13,5},{2,10},{6,14},... | collective-permute-start | bytes 589832 | tf_op jit(solution)/shard_map/ppermute | solution.py:280
  256.3 3.7 %copy-start.17 = (bf16[512,512]{1,0:T(8,128)(2,1)}, bf16[512,512]{1,0:T(8,128)(2,1)S(1)}, u32[]{:S(2)}) copy-start(bf16[512,512]{1,0:T(8,128)(2,1)S(1)} %collective-permute-done.25.refs_9_) | copy-start | bytes 1572868
  256.3 26.2 %collective-permute-start.20 = (bf16[384,256]{1,0:T(8,128)(2,1)}, bf16[384,256]{1,0:T(8,128)(2,1)S(1)}, u32[]{:S(2)}, u32[]{:S(2)}) collective-permute-start(bf16[384,256]{1,0:T(8,128)(2,1)} %get-tuple-element.23), channel_id=1, source_target_pairs={{0,4},{4,8},{8,12},{12,0},{1,5},{5,9},{9,13},{13,1},{2,6},{6,10},{... | collective-permute-start | bytes 589832 | tf_op jit(solution)/shard_map/ppermute | solution.py:280
  257.9 2.1 copy-start.18
  257.9 26.9 %collective-permute-start.21 = (bf16[384,256]{1,0:T(8,128)(2,1)}, bf16[384,256]{1,0:T(8,128)(2,1)S(1)}, u32[]{:S(2)}, u32[]{:S(2)}) collective-permute-start(bf16[384,256]{1,0:T(8,128)(2,1)} %get-tuple-element.24), channel_id=1, source_target_pairs={{0,12},{4,0},{8,4},{12,8},{1,13},{5,1},{9,5},{13,9},{2,14},{6,2},{... | collective-permute-start | bytes 589832 | tf_op jit(solution)/shard_map/ppermute | solution.py:280
  274.0 10.9 %copy-start.21 = (bf16[384,256]{1,0:T(8,128)(2,1)}, bf16[384,256]{1,0:T(8,128)(2,1)S(1)}, u32[]{:S(2)}) copy-start(bf16[384,256]{1,0:T(8,128)(2,1)S(1)} %collective-permute-done.19.refs_5_) | copy-start | bytes 589828
  274.0 14.7 %collective-permute-start.28 = (bf16[384,256]{1,0:T(8,128)(2,1)}, bf16[384,256]{1,0:T(8,128)(2,1)S(1)}, u32[]{:S(2)}, u32[]{:S(2)}) collective-permute-start(bf16[384,256]{1,0:T(8,128)(2,1)} %get-tuple-element.26), channel_id=1, source_target_pairs={{0,8},{4,12},{8,0},{12,4},{1,9},{5,13},{9,1},{13,5},{2,10},{6,14},... | collective-permute-start | bytes 589832 | tf_op jit(solution)/shard_map/ppermute | solution.py:280
  282.5 2.4 copy-start.22
  282.5 8.0 %collective-permute-start.29 = (bf16[384,256]{1,0:T(8,128)(2,1)}, bf16[384,256]{1,0:T(8,128)(2,1)S(1)}, u32[]{:S(2)}, u32[]{:S(2)}) collective-permute-start(bf16[384,256]{1,0:T(8,128)(2,1)} %get-tuple-element.27), channel_id=1, source_target_pairs={{0,4},{4,8},{8,12},{12,0},{1,5},{5,9},{9,13},{13,1},{2,6},{6,10},{... | collective-permute-start | bytes 589832 | tf_op jit(solution)/shard_map/ppermute | solution.py:280
  284.9 0.7 copy-start.23
  284.9 6.7 %collective-permute-start.30 = (bf16[384,256]{1,0:T(8,128)(2,1)}, bf16[384,256]{1,0:T(8,128)(2,1)S(1)}, u32[]{:S(2)}, u32[]{:S(2)}) collective-permute-start(bf16[384,256]{1,0:T(8,128)(2,1)} %get-tuple-element.28), channel_id=1, source_target_pairs={{0,12},{4,0},{8,4},{12,8},{1,13},{5,1},{9,5},{13,9},{2,14},{6,2},{... | collective-permute-start | bytes 589832 | tf_op jit(solution)/shard_map/ppermute | solution.py:280
  284.9 0.8 copy-start.19
  285.7 0.7 copy-start.20
  288.8 2.8 copy-start.24
  290.5 1.1 copy-start.25
  291.6 0.7 copy-start.26
Sparse Core Ops, SparseCore 0:
  8.9 29.6 all-gather.4
  40.2 28.5 all-gather.6
  70.3 28.5 all-gather.8
  113.1 30.4 all-gather.10

commit v19 on v17

--- a/solution.py
+++ b/solution.py
@@ -5,7 +5,7 @@
 from jax.experimental.pallas import tpu as pltpu
 from jax.sharding import PartitionSpec as P
 
-PIECES = (3, 2, 2)
+PIECES = (4, 2, 1)
 GRANT = 60 * 2**20
 LANES = 128
 ANY = pl.BlockSpec(memory_space=pl.ANY)

time: 299 us -> 316 us (1.057)
  starting transfers between devices: 52.9 us -> 65.3 us
  Pallas kernels: 63.3 us -> 67.1 us
    ppermute x8, waiting for transfers between devices: 7.3 us -> 23.7 us  [weights(): swapped.append(lax.ppermute(came, 'parts', around(parts, -turn)))]
    ppermute x9, starting transfers between devices: 16.2 us -> 24.6 us  [hidden_of(): lax.ppermute(outs[shift], 'row', around(rows, shift))]
    ppermute x8, waiting for transfers between devices: 95.5 us -> 88.4 us  [weights(): arrived.append(lax.ppermute(sent[-1], 'row', around(rows, shift)))]
    ppermute x9, waiting for transfers between devices: 12.5 us -> 7.07 us  [hidden_of(): lax.ppermute(outs[shift], 'row', around(rows, shift))]
    pallas_call x3, Pallas kernels: 40.3 us -> 44.3 us  [product(): pl.pallas_call(body, out_shape=[jax.ShapeDtypeStruct((mine, wide), jnp.bf...]
    unnamed x58 -> x54, local copies, waits for them, and re-layouts: 8.77 us -> 8.44 us
  transfers between devices with their start and end apart: 35 -> 35, of which waited for: 18 -> 15; matrix products, arithmetic and copies ran while one was open for 1% -> 1% of each run, Pallas kernels for 21% -> 21%
where the time goes in v19:
time: 316 us; the launch traced here: 314 us
  waiting for transfers between devices  158 us (50%)
  Pallas kernels  67.1 us (21%)
  starting transfers between devices  65.3 us (21%)
  between operations  13.5 us (4%)
  local copies, waits for them, and re-layouts  8.44 us (3%)
    ppermute x8, waiting for transfers between devices, weights(): arrived.append(lax.ppermute(sent[-1], 'row', around(rows, shift)))  88.4 us
    pallas_call x3, Pallas kernels, product(): pl.pallas_call(body, out_shape=[jax.ShapeDtypeStruct((mine, wide), jnp.bf...  44.3 us
    ppermute x3, waiting for transfers between devices, tokens_of(): lax.ppermute(upper[-1], 'row', [(i, i - 1) for i in range(1, rows - step...  34.4 us
    ppermute x9, starting transfers between devices, hidden_of(): lax.ppermute(outs[shift], 'row', around(rows, shift))  24.6 us
    ppermute x8, waiting for transfers between devices, weights(): swapped.append(lax.ppermute(came, 'parts', around(parts, -turn)))  23.7 us
    pallas_call x8, Pallas kernels, pack(): pl.pallas_call(body, out_shape=jax.ShapeDtypeStruct((share, 2 * wide), ga...  16.4 us
    ppermute x8, starting transfers between devices, weights(): arrived.append(lax.ppermute(sent[-1], 'row', around(rows, shift)))  14.8 us
    ppermute x3, starting transfers between devices, tokens_of(): lax.ppermute(lower[-1], 'row', [(i, i + 1) for i in range(step - 1, rows...  9.04 us
  transfers between devices with their start and end apart: 35, of which 15 were waited for; matrix products, arithmetic and copies ran while one was open for 1% of the time, Pallas kernels for 21%

profile of v19, /device:TPU:12, one launch (start us, length us, event | category | flops | bytes accessed | tf_op | source)
XLA Modules:
  0.0 314.0 jit_solution(4496966982702919310)
XLA Ops:
  6.5 0.7 all-gather.5.cloned.1.call-update
  7.3 2.4 collective-permute-start
  9.7 3.5 %collective-permute-start.1 = (bf16[384,1024]{1,0:T(8,128)(2,1)}, bf16[384,1024]{1,0:T(8,128)(2,1)S(1)}, u32[]{:S(2)}, u32[]{:S(2)}) collective-permute-start(bf16[384,1024]{1,0:T(8,128)(2,1)} %param.3), channel_id=1, source_target_pairs={{0,4},{4,8},{8,12},{1,5},{5,9},{9,13},{2,6},{6,10},{10,14},{3,7},{... | collective-permute-start | bytes 2359304 | tf_op jit(solution)/shard_map/ppermute | solution.py:245
  13.2 2.7 pack.8.refs_1_.refs_2_
  15.9 12.8 %collective-permute-done.refs_2_ = bf16[384,1024]{1,0:T(8,128)(2,1)S(1)} collective-permute-done((bf16[384,1024]{1,0:T(8,128)(2,1)}, bf16[384,1024]{1,0:T(8,128)(2,1)S(1)}, u32[]{:S(2)}, u32[]{:S(2)}) %collective-permute-start) | collective-permute-done | bytes 786464 | tf_op jit(solution)/shard_map/ppermute | solution.py:246
  28.7 2.1 collective-permute-done.1.refs_1_
  30.8 1.1 broadcast_select_fusion.1.refs_0_
  31.9 2.1 collective-permute-start.2
  34.0 4.0 %collective-permute-start.3 = (bf16[384,1024]{1,0:T(8,128)(2,1)S(1)}, bf16[384,1024]{1,0:T(8,128)(2,1)S(1)}, u32[]{:S(2)}, u32[]{:S(2)}) collective-permute-start(bf16[384,1024]{1,0:T(8,128)(2,1)S(1)} %collective-permute-done.1.refs_1_), channel_id=1, source_target_pairs={{4,8},{8,12},{5,9},{9,13},{6,10},{10,14},{7,11},{11,15},{20,24},{2... | collective-permute-start | bytes 2359304 | tf_op jit(solution)/shard_map/ppermute | solution.py:245
  38.0 14.1 %collective-permute-done.2 = bf16[384,1024]{1,0:T(8,128)(2,1)S(1)} collective-permute-done((bf16[384,1024]{1,0:T(8,128)(2,1)S(1)}, bf16[384,1024]{1,0:T(8,128)(2,1)S(1)}, u32[]{:S(2)}, u32[]{:S(2)}) %collective-permute-start.2) | collective-permute-done | bytes 786464 | tf_op jit(solution)/shard_map/ppermute | solution.py:246
  52.2 1.2 collective-permute-done.3
  53.4 0.9 copy-done.13
  54.3 1.0 broadcast_select_fusion
  55.4 2.3 collective-permute-start.6
  57.6 4.5 %collective-permute-start.4 = (bf16[384,1024]{1,0:T(8,128)(2,1)}, bf16[384,1024]{1,0:T(8,128)(2,1)}, u32[]{:S(2)}, u32[]{:S(2)}) collective-permute-start(bf16[384,1024]{1,0:T(8,128)(2,1)} %copy-done.12), channel_id=1, source_target_pairs={{4,0},{5,1},{6,2},{7,3},{20,16},{21,17},{22,18},{23,19}} | collective-permute-start | bytes 2359304 | tf_op jit(solution)/shard_map/ppermute | solution.py:246
  62.2 1.5 collective-permute-start.5
  63.7 2.3 pack.9.refs_2_
  66.1 2.4 pack.10.refs_3_.refs_2_
  68.4 7.5 %collective-permute-done.4.refs_0_ = bf16[384,1024]{1,0:T(8,128)(2,1)} collective-permute-done((bf16[384,1024]{1,0:T(8,128)(2,1)}, bf16[384,1024]{1,0:T(8,128)(2,1)}, u32[]{:S(2)}, u32[]{:S(2)}) %collective-permute-start.4) | collective-permute-done | bytes 786464 | tf_op jit(solution)/shard_map/ppermute | solution.py:246
  75.9 2.1 pick.1.refs_0_
  78.0 45.1 %collective-permute-done.6.refs_1_.refs_6_.refs_3_ = bf16[512,1536]{1,0:T(8,128)(2,1)S(1)} collective-permute-done((bf16[512,1536]{1,0:T(8,128)(2,1)S(1)}, bf16[512,1536]{1,0:T(8,128)(2,1)S(1)}, u32[]{:S(2)}, u32[]{:S(2)}) %collective-permute-start.6) | collective-permute-done | bytes 1572896 | tf_op jit(solution)/shard_map/ppermute | solution.py:269
  123.1 1.1 copy-done
  124.6 0.9 copy-done.2
  125.5 2.2 collective-permute-start.10
  127.7 1.0 collective-permute-start.7
  128.6 22.2 %collective-permute-done.8.refs_8_.refs_3_ = bf16[512,1024]{1,0:T(8,128)(2,1)} collective-permute-done((bf16[512,1024]{1,0:T(8,128)(2,1)}, bf16[512,1024]{1,0:T(8,128)(2,1)}, u32[]{:S(2)}, u32[]{:S(2)}) %collective-permute-start.8) | collective-permute-done | bytes 1048608 | tf_op jit(solution)/shard_map/ppermute | solution.py:269
  150.8 1.0 collective-permute-start.9
  151.8 21.2 %collective-permute-done.10.refs_10_.refs_3_ = bf16[512,1024]{1,0:T(8,128)(2,1)} collective-permute-done((bf16[512,1024]{1,0:T(8,128)(2,1)S(1)}, bf16[512,1024]{1,0:T(8,128)(2,1)}, u32[]{:S(2)}, u32[]{:S(2)}) %collective-permute-start.10) | collective-permute-done | bytes 1048608 | tf_op jit(solution)/shard_map/ppermute | solution.py:269
  172.9 0.8 collective-permute-start.11
  173.8 1.7 pack.11.refs_2_
  175.5 2.2 collective-permute-start.22
  177.7 1.2 copy-done.3
  178.8 2.0 pack.12.refs_2_
  180.8 1.8 collective-permute-start.15
  182.6 5.1 %collective-permute-done.9.refs_9_.refs_4_ = bf16[512,1024]{1,0:T(8,128)(2,1)} collective-permute-done((bf16[512,1024]{1,0:T(8,128)(2,1)}, bf16[512,1024]{1,0:T(8,128)(2,1)}, u32[]{:S(2)}, u32[]{:S(2)}) %collective-permute-start.9) | collective-permute-done | bytes 1048608 | tf_op jit(solution)/shard_map/ppermute | solution.py:273
  187.7 1.9 pack.13.refs_2_
  189.7 2.8 collective-permute-start.17
  192.5 1.0 collective-permute-start.23
  193.4 16.8 %collective-permute-done.11.refs_11_.refs_4_ = bf16[512,1024]{1,0:T(8,128)(2,1)} collective-permute-done((bf16[512,1024]{1,0:T(8,128)(2,1)}, bf16[512,1024]{1,0:T(8,128)(2,1)}, u32[]{:S(2)}, u32[]{:S(2)}) %collective-permute-start.11) | collective-permute-done | bytes 1048608 | tf_op jit(solution)/shard_map/ppermute | solution.py:273
  210.2 1.7 pack.14.refs_2_
  212.6 1.8 collective-permute-done.23.refs_4_.refs_7_
  214.4 0.7 copy-done.9
  215.1 0.8 copy-done.6
  215.9 1.7 pack.15
  217.6 2.5 collective-permute-start.26
  220.1 1.0 collective-permute-start.16
  221.1 1.0 collective-permute-start.18
  222.1 21.7 %product.3 = (bf16[384,512]{1,0:T(8,128)(2,1)}, bf16[384,512]{1,0:T(8,128)(2,1)}, bf16[384,512]{1,0:T(8,128)(2,1)}, bf16[384,512]{1,0:T(8,128)(2,1)}) custom-call(bf16[384,4096]{1,0:T(8,128)(2,1)} %all-gather.5.cloned.1.call-done.refs_0_, bf16[384,4096]{1,0:T(8,128)(2,1)} %all-gather.7.cloned.1.call-done.refs_1_, ...), custom_call_target="tpu_custom_call" | custom-call | flops 12884901888 | bytes 22544384 | tf_op jit(solution)/shard_map/product/pallas_call | solution.py:138
  244.3 2.8 collective-permute-start.13
  247.8 1.0 collective-permute-start.25
  248.8 1.0 collective-permute-start.27
  249.8 11.8 %product.4 = (bf16[384,256]{1,0:T(8,128)(2,1)}, bf16[384,256]{1,0:T(8,128)(2,1)}, bf16[384,256]{1,0:T(8,128)(2,1)}, bf16[384,256]{1,0:T(8,128)(2,1)}) custom-call(bf16[384,4096]{1,0:T(8,128)(2,1)} %all-gather.5.cloned.1.call-done.refs_0_, bf16[384,4096]{1,0:T(8,128)(2,1)} %all-gather.7.cloned.1.call-done.refs_1_, ...), custom_call_target="tpu_custom_call" | custom-call | flops 6442450944 | bytes 17563648 | tf_op jit(solution)/shard_map/product/pallas_call | solution.py:138
  261.7 1.6 collective-permute-start.19
  263.4 1.8 collective-permute-start.20
  265.1 12.2 %collective-permute-start.21 = (bf16[384,256]{1,0:T(8,128)(2,1)}, bf16[384,256]{1,0:T(8,128)(2,1)S(1)}, u32[]{:S(2)}, u32[]{:S(2)}) collective-permute-start(bf16[384,256]{1,0:T(8,128)(2,1)} %get-tuple-element.24), channel_id=1, source_target_pairs={{0,12},{4,0},{8,4},{12,8},{1,13},{5,1},{9,5},{13,9},{2,14},{6,2},{... | collective-permute-start | bytes 589832 | tf_op jit(solution)/shard_map/ppermute | solution.py:280
  277.4 10.7 %product.5 = (bf16[384,128]{1,0:T(8,128)(2,1)}, bf16[384,128]{1,0:T(8,128)(2,1)}, bf16[384,128]{1,0:T(8,128)(2,1)}, bf16[384,128]{1,0:T(8,128)(2,1)}) custom-call(bf16[384,4096]{1,0:T(8,128)(2,1)} %all-gather.5.cloned.1.call-done.refs_0_, bf16[384,4096]{1,0:T(8,128)(2,1)} %all-gather.7.cloned.1.call-done.refs_1_, ...), custom_call_target="tpu_custom_call" | custom-call | flops 3221225472 | bytes 15073280 | tf_op jit(solution)/shard_map/product/pallas_call | solution.py:138
  288.1 1.3 collective-permute-done.19.refs_5_
  289.3 3.3 %collective-permute-start.28 = (bf16[384,128]{1,0:T(8,128)(2,1)}, bf16[384,128]{1,0:T(8,128)(2,1)S(1)}, u32[]{:S(2)}, u32[]{:S(2)}) collective-permute-start(bf16[384,128]{1,0:T(8,128)(2,1)} %get-tuple-element.26), channel_id=1, source_target_pairs={{0,8},{4,12},{8,0},{12,4},{1,9},{5,13},{9,1},{13,5},{2,10},{6,14},... | collective-permute-start | bytes 294920 | tf_op jit(solution)/shard_map/ppermute | solution.py:280
  292.6 2.9 collective-permute-done.20.refs_6_
  295.5 2.5 collective-permute-start.29
  298.0 2.2 collective-permute-done.21.refs_7_
  301.0 0.7 copy-done.18
  301.8 2.5 place.2.refs_0_
  305.7 1.7 place.3
  (84 shorter events, 4.5 us)
Async XLA Ops:
  6.5 215.6 %all-gather.5.cloned.1.call-start = ((), (), s32[]{:S(2)}) async-start(), calls=%async_computation | async-start | bytes 3932160 | tf_op jit(solution)/shard_map/all_gather | solution.py:264
  7.3 214.9 %all-gather.7.cloned.1.call-start = ((), (), s32[]{:S(2)}) async-start(), calls=%async_computation.1 | async-start | bytes 3932160 | tf_op jit(solution)/shard_map/all_gather | solution.py:264
  7.3 21.4 %collective-permute-start = (bf16[384,1024]{1,0:T(8,128)(2,1)}, bf16[384,1024]{1,0:T(8,128)(2,1)S(1)}, u32[]{:S(2)}, u32[]{:S(2)}) collective-permute-start(bf16[384,1024]{1,0:T(8,128)(2,1)} %param.3), channel_id=1, source_target_pairs={{4,0},{8,4},{12,8},{5,1},{9,5},{13,9},{6,2},{10,6},{14,10},{7,3},{... | collective-permute-start | bytes 2359304 | tf_op jit(solution)/shard_map/ppermute | solution.py:246
  9.7 21.1 %collective-permute-start.1 = (bf16[384,1024]{1,0:T(8,128)(2,1)}, bf16[384,1024]{1,0:T(8,128)(2,1)S(1)}, u32[]{:S(2)}, u32[]{:S(2)}) collective-permute-start(bf16[384,1024]{1,0:T(8,128)(2,1)} %param.3), channel_id=1, source_target_pairs={{0,4},{4,8},{8,12},{1,5},{5,9},{9,13},{2,6},{6,10},{10,14},{3,7},{... | collective-permute-start | bytes 2359304 | tf_op jit(solution)/shard_map/ppermute | solution.py:245
  28.7 3.3 %copy-start.4 = (bf16[384,1024]{1,0:T(8,128)(2,1)}, bf16[384,1024]{1,0:T(8,128)(2,1)S(1)}, u32[]{:S(2)}) copy-start(bf16[384,1024]{1,0:T(8,128)(2,1)S(1)} %collective-permute-done.refs_2_) | copy-start | bytes 2359300
  30.8 3.2 %copy-start.5 = (bf16[384,1024]{1,0:T(8,128)(2,1)}, bf16[384,1024]{1,0:T(8,128)(2,1)S(1)}, u32[]{:S(2)}) copy-start(bf16[384,1024]{1,0:T(8,128)(2,1)S(1)} %collective-permute-done.1.refs_1_) | copy-start | bytes 2359300
  31.9 23.5 %copy-start.1 = (bf16[512,1536]{1,0:T(8,128)(2,1)S(1)}, bf16[512,1536]{1,0:T(8,128)(2,1)}, u32[]{:S(2)}) copy-start(bf16[512,1536]{1,0:T(8,128)(2,1)} %pack.8.refs_1_.refs_2_) | copy-start | bytes 4718596
  31.9 190.2 %all-gather.9.cloned.1.call-start = ((), (), s32[]{:S(2)}) async-start(), calls=%async_computation.2 | async-start | bytes 3932160 | tf_op jit(solution)/shard_map/all_gather | solution.py:264
  31.9 20.2 %collective-permute-start.2 = (bf16[384,1024]{1,0:T(8,128)(2,1)S(1)}, bf16[384,1024]{1,0:T(8,128)(2,1)S(1)}, u32[]{:S(2)}, u32[]{:S(2)}) collective-permute-start(bf16[384,1024]{1,0:T(8,128)(2,1)S(1)} %collective-permute-done.refs_2_), channel_id=1, source_target_pairs={{4,0},{8,4},{5,1},{9,5},{6,2},{10,6},{7,3},{11,7},{20,16},{24,20},... | collective-permute-start | bytes 2359304 | tf_op jit(solution)/shard_map/ppermute | solution.py:246
  34.0 19.4 %collective-permute-start.3 = (bf16[384,1024]{1,0:T(8,128)(2,1)S(1)}, bf16[384,1024]{1,0:T(8,128)(2,1)S(1)}, u32[]{:S(2)}, u32[]{:S(2)}) collective-permute-start(bf16[384,1024]{1,0:T(8,128)(2,1)S(1)} %collective-permute-done.1.refs_1_), channel_id=1, source_target_pairs={{4,8},{8,12},{5,9},{9,13},{6,10},{10,14},{7,11},{11,15},{20,24},{2... | collective-permute-start | bytes 2359304 | tf_op jit(solution)/shard_map/ppermute | solution.py:245
  52.2 1.2 copy-start.12
  53.4 0.9 copy-start.13
  55.3 166.8 %all-gather.11.cloned.1.call-start = ((), (), s32[]{:S(2)}) async-start(), calls=%async_computation.3 | async-start | bytes 3932160 | tf_op jit(solution)/shard_map/all_gather | solution.py:264
  55.4 67.7 %collective-permute-start.6 = (bf16[512,1536]{1,0:T(8,128)(2,1)S(1)}, bf16[512,1536]{1,0:T(8,128)(2,1)S(1)}, u32[]{:S(2)}, u32[]{:S(2)}) collective-permute-start(bf16[512,1536]{1,0:T(8,128)(2,1)S(1)} %copy-done.1), channel_id=1, source_target_pairs={{0,8},{4,12},{8,0},{12,4},{1,9},{5,13},{9,1},{13,5},{2,10},{6,14},... | collective-permute-start | bytes 4718600 | tf_op jit(solution)/shard_map/ppermute | solution.py:269
  57.6 18.3 %collective-permute-start.4 = (bf16[384,1024]{1,0:T(8,128)(2,1)}, bf16[384,1024]{1,0:T(8,128)(2,1)}, u32[]{:S(2)}, u32[]{:S(2)}) collective-permute-start(bf16[384,1024]{1,0:T(8,128)(2,1)} %copy-done.12), channel_id=1, source_target_pairs={{4,0},{5,1},{6,2},{7,3},{20,16},{21,17},{22,18},{23,19}} | collective-permute-start | bytes 2359304 | tf_op jit(solution)/shard_map/ppermute | solution.py:246
  62.2 13.8 %collective-permute-start.5 = (bf16[384,1024]{1,0:T(8,128)(2,1)}, bf16[384,1024]{1,0:T(8,128)(2,1)}, u32[]{:S(2)}, u32[]{:S(2)}) collective-permute-start(bf16[384,1024]{1,0:T(8,128)(2,1)} %copy-done.13), channel_id=1, source_target_pairs={{8,12},{9,13},{10,14},{11,15},{24,28},{25,29},{26,30},{27,31}} | collective-permute-start | bytes 2359304 | tf_op jit(solution)/shard_map/ppermute | solution.py:245
  123.1 1.1 copy-start
  124.2 1.2 copy-start.2
  124.3 26.5 %collective-permute-start.8 = (bf16[512,1024]{1,0:T(8,128)(2,1)}, bf16[512,1024]{1,0:T(8,128)(2,1)}, u32[]{:S(2)}, u32[]{:S(2)}) collective-permute-start(bf16[512,1024]{1,0:T(8,128)(2,1)} %pack.9.refs_2_), channel_id=1, source_target_pairs={{0,4},{4,8},{8,12},{12,0},{1,5},{5,9},{9,13},{13,1},{2,6},{6,10},{... | collective-permute-start | bytes 3145736 | tf_op jit(solution)/shard_map/ppermute | solution.py:269
  125.5 47.5 %collective-permute-start.10 = (bf16[512,1024]{1,0:T(8,128)(2,1)S(1)}, bf16[512,1024]{1,0:T(8,128)(2,1)}, u32[]{:S(2)}, u32[]{:S(2)}) collective-permute-start(bf16[512,1024]{1,0:T(8,128)(2,1)S(1)} %copy-done.2), channel_id=1, source_target_pairs={{0,12},{4,0},{8,4},{12,8},{1,13},{5,1},{9,5},{13,9},{2,14},{6,2},{... | collective-permute-start | bytes 3145736 | tf_op jit(solution)/shard_map/ppermute | solution.py:269
  127.7 50.0 %collective-permute-start.7 = (bf16[512,1536]{1,0:T(8,128)(2,1)}, bf16[512,1536]{1,0:T(8,128)(2,1)S(1)}, u32[]{:S(2)}, u32[]{:S(2)}) collective-permute-start(bf16[512,1536]{1,0:T(8,128)(2,1)} %copy-done), channel_id=1, source_target_pairs={{0,16},{16,0},{1,17},{17,1},{2,18},{18,2},{3,19},{19,3},{4,20},{20... | collective-permute-start | bytes 4718600 | tf_op jit(solution)/shard_map/ppermute | solution.py:273
  150.8 36.9 %collective-permute-start.9 = (bf16[512,1024]{1,0:T(8,128)(2,1)}, bf16[512,1024]{1,0:T(8,128)(2,1)}, u32[]{:S(2)}, u32[]{:S(2)}) collective-permute-start(bf16[512,1024]{1,0:T(8,128)(2,1)} %collective-permute-done.8.refs_8_.refs_3_), channel_id=1, source_target_pairs={{0,16},{16,0},{1,17},{17,1},{2,18},{18,2},{3,19},{19,3},{4,20},{20... | collective-permute-start | bytes 3145736 | tf_op jit(solution)/shard_map/ppermute | solution.py:273
  172.9 37.3 %collective-permute-start.11 = (bf16[512,1024]{1,0:T(8,128)(2,1)}, bf16[512,1024]{1,0:T(8,128)(2,1)}, u32[]{:S(2)}, u32[]{:S(2)}) collective-permute-start(bf16[512,1024]{1,0:T(8,128)(2,1)} %collective-permute-done.10.refs_10_.refs_3_), channel_id=1, source_target_pairs={{0,16},{16,0},{1,17},{17,1},{2,18},{18,2},{3,19},{19,3},{4,20},{20... | collective-permute-start | bytes 3145736 | tf_op jit(solution)/shard_map/ppermute | solution.py:273
  175.5 17.0 %collective-permute-start.22 = (bf16[512,256]{1,0:T(8,128)(2,1)}, bf16[512,256]{1,0:T(8,128)(2,1)S(1)}, u32[]{:S(2)}, u32[]{:S(2)}) collective-permute-start(bf16[512,256]{1,0:T(8,128)(2,1)} %pack.11.refs_2_), channel_id=1, source_target_pairs={{0,8},{4,12},{8,0},{12,4},{1,9},{5,13},{9,1},{13,5},{2,10},{6,14},... | collective-permute-start | bytes 786440 | tf_op jit(solution)/shard_map/ppermute | solution.py:269
  177.7 1.2 copy-start.3
  180.8 33.6 %collective-permute-start.15 = (bf16[512,512]{1,0:T(8,128)(2,1)}, bf16[512,512]{1,0:T(8,128)(2,1)S(1)}, u32[]{:S(2)}, u32[]{:S(2)}) collective-permute-start(bf16[512,512]{1,0:T(8,128)(2,1)} %pack.12.refs_2_), channel_id=1, source_target_pairs={{0,4},{4,8},{8,12},{12,0},{1,5},{5,9},{9,13},{13,1},{2,6},{6,10},{... | collective-permute-start | bytes 1572872 | tf_op jit(solution)/shard_map/ppermute | solution.py:269
  189.7 31.4 %collective-permute-start.17 = (bf16[512,512]{1,0:T(8,128)(2,1)}, bf16[512,512]{1,0:T(8,128)(2,1)S(1)}, u32[]{:S(2)}, u32[]{:S(2)}) collective-permute-start(bf16[512,512]{1,0:T(8,128)(2,1)} %pack.13.refs_2_), channel_id=1, source_target_pairs={{0,12},{4,0},{8,4},{12,8},{1,13},{5,1},{9,5},{13,9},{2,14},{6,2},{... | collective-permute-start | bytes 1572872 | tf_op jit(solution)/shard_map/ppermute | solution.py:269
  192.5 17.8 %copy-start.8 = (bf16[512,256]{1,0:T(8,128)(2,1)}, bf16[512,256]{1,0:T(8,128)(2,1)S(1)}, u32[]{:S(2)}) copy-start(bf16[512,256]{1,0:T(8,128)(2,1)S(1)} %collective-permute-done.22.refs_3_.refs_6_) | copy-start | bytes 786436
  192.5 21.9 %collective-permute-start.23 = (bf16[512,256]{1,0:T(8,128)(2,1)S(1)}, bf16[512,256]{1,0:T(8,128)(2,1)S(1)}, u32[]{:S(2)}, u32[]{:S(2)}) collective-permute-start(bf16[512,256]{1,0:T(8,128)(2,1)S(1)} %collective-permute-done.22.refs_3_.refs_6_), channel_id=1, source_target_pairs={{0,16},{16,0},{1,17},{17,1},{2,18},{18,2},{3,19},{19,3},{4,20},{20... | collective-permute-start | bytes 786440 | tf_op jit(solution)/shard_map/ppermute | solution.py:273
  211.9 32.4 %collective-permute-start.24 = (bf16[512,256]{1,0:T(8,128)(2,1)}, bf16[512,256]{1,0:T(8,128)(2,1)S(1)}, u32[]{:S(2)}, u32[]{:S(2)}) collective-permute-start(bf16[512,256]{1,0:T(8,128)(2,1)} %pack.14.refs_2_), channel_id=1, source_target_pairs={{0,4},{4,8},{8,12},{12,0},{1,5},{5,9},{9,13},{13,1},{2,6},{6,10},{... | collective-permute-start | bytes 786440 | tf_op jit(solution)/shard_map/ppermute | solution.py:269
  214.4 0.7 copy-start.9
  215.1 0.8 copy-start.6
  217.6 29.4 %collective-permute-start.26 = (bf16[512,256]{1,0:T(8,128)(2,1)}, bf16[512,256]{1,0:T(8,128)(2,1)S(1)}, u32[]{:S(2)}, u32[]{:S(2)}) collective-permute-start(bf16[512,256]{1,0:T(8,128)(2,1)} %pack.15), channel_id=1, source_target_pairs={{0,12},{4,0},{8,4},{12,8},{1,13},{5,1},{9,5},{13,9},{2,14},{6,2},{... | collective-permute-start | bytes 786440 | tf_op jit(solution)/shard_map/ppermute | solution.py:269
  220.1 27.7 %collective-permute-start.16 = (bf16[512,512]{1,0:T(8,128)(2,1)}, bf16[512,512]{1,0:T(8,128)(2,1)S(1)}, u32[]{:S(2)}, u32[]{:S(2)}) collective-permute-start(bf16[512,512]{1,0:T(8,128)(2,1)} %copy-done.6), channel_id=1, source_target_pairs={{0,16},{16,0},{1,17},{17,1},{2,18},{18,2},{3,19},{19,3},{4,20},{20... | collective-permute-start | bytes 1572872 | tf_op jit(solution)/shard_map/ppermute | solution.py:273
  221.1 22.8 %copy-start.14 = (bf16[512,512]{1,0:T(8,128)(2,1)}, bf16[512,512]{1,0:T(8,128)(2,1)S(1)}, u32[]{:S(2)}) copy-start(bf16[512,512]{1,0:T(8,128)(2,1)S(1)} %collective-permute-done.17.refs_10_) | copy-start | bytes 1572868
  221.1 27.7 %collective-permute-start.18 = (bf16[512,512]{1,0:T(8,128)(2,1)S(1)}, bf16[512,512]{1,0:T(8,128)(2,1)S(1)}, u32[]{:S(2)}, u32[]{:S(2)}) collective-permute-start(bf16[512,512]{1,0:T(8,128)(2,1)S(1)} %collective-permute-done.17.refs_10_), channel_id=1, source_target_pairs={{0,16},{16,0},{1,17},{17,1},{2,18},{18,2},{3,19},{19,3},{4,20},{20... | collective-permute-start | bytes 1572872 | tf_op jit(solution)/shard_map/ppermute | solution.py:273
  243.9 21.3 %collective-permute-start.12 = (bf16[384,512]{1,0:T(8,128)(2,1)}, bf16[384,512]{1,0:T(8,128)(2,1)S(1)}, u32[]{:S(2)}, u32[]{:S(2)}) collective-permute-start(bf16[384,512]{1,0:T(8,128)(2,1)} %get-tuple-element.18), channel_id=1, source_target_pairs={{0,8},{4,12},{8,0},{12,4},{1,9},{5,13},{9,1},{13,5},{2,10},{6,14},... | collective-permute-start | bytes 1179656 | tf_op jit(solution)/shard_map/ppermute | solution.py:280
  244.3 2.8 copy-start.10
  244.3 56.0 %collective-permute-start.13 = (bf16[384,512]{1,0:T(8,128)(2,1)}, bf16[384,512]{1,0:T(8,128)(2,1)S(1)}, u32[]{:S(2)}, u32[]{:S(2)}) collective-permute-start(bf16[384,512]{1,0:T(8,128)(2,1)} %get-tuple-element.19), channel_id=1, source_target_pairs={{0,4},{4,8},{8,12},{12,0},{1,5},{5,9},{9,13},{13,1},{2,6},{6,10},{... | collective-permute-start | bytes 1179656 | tf_op jit(solution)/shard_map/ppermute | solution.py:280
  247.1 0.7 copy-start.11
  247.1 53.2 %collective-permute-start.14 = (bf16[384,512]{1,0:T(8,128)(2,1)}, bf16[384,512]{1,0:T(8,128)(2,1)S(1)}, u32[]{:S(2)}, u32[]{:S(2)}) collective-permute-start(bf16[384,512]{1,0:T(8,128)(2,1)} %get-tuple-element.20), channel_id=1, source_target_pairs={{0,12},{4,0},{8,4},{12,8},{1,13},{5,1},{9,5},{13,9},{2,14},{6,2},{... | collective-permute-start | bytes 1179656 | tf_op jit(solution)/shard_map/ppermute | solution.py:280
  247.8 2.0 copy-start.15
  247.8 13.9 %collective-permute-start.25 = (bf16[512,256]{1,0:T(8,128)(2,1)}, bf16[512,256]{1,0:T(8,128)(2,1)S(1)}, u32[]{:S(2)}, u32[]{:S(2)}) collective-permute-start(bf16[512,256]{1,0:T(8,128)(2,1)} %hold.6.refs_8_), channel_id=1, source_target_pairs={{0,16},{16,0},{1,17},{17,1},{2,18},{18,2},{3,19},{19,3},{4,20},{20... | collective-permute-start | bytes 786440 | tf_op jit(solution)/shard_map/ppermute | solution.py:273
  248.8 1.1 copy-start.16
  248.8 14.6 %collective-permute-start.27 = (bf16[512,256]{1,0:T(8,128)(2,1)}, bf16[512,256]{1,0:T(8,128)(2,1)S(1)}, u32[]{:S(2)}, u32[]{:S(2)}) collective-permute-start(bf16[512,256]{1,0:T(8,128)(2,1)} %hold.7.refs_10_), channel_id=1, source_target_pairs={{0,16},{16,0},{1,17},{17,1},{2,18},{18,2},{3,19},{19,3},{4,20},{20... | collective-permute-start | bytes 786440 | tf_op jit(solution)/shard_map/ppermute | solution.py:273
  261.7 15.6 %copy-start.19 = (bf16[512,256]{1,0:T(8,128)(2,1)}, bf16[512,256]{1,0:T(8,128)(2,1)S(1)}, u32[]{:S(2)}) copy-start(bf16[512,256]{1,0:T(8,128)(2,1)S(1)} %collective-permute-done.25.refs_9_) | copy-start | bytes 786436
  261.7 27.6 %collective-permute-start.19 = (bf16[384,256]{1,0:T(8,128)(2,1)}, bf16[384,256]{1,0:T(8,128)(2,1)S(1)}, u32[]{:S(2)}, u32[]{:S(2)}) collective-permute-start(bf16[384,256]{1,0:T(8,128)(2,1)} %get-tuple-element.22), channel_id=1, source_target_pairs={{0,8},{4,12},{8,0},{12,4},{1,9},{5,13},{9,1},{13,5},{2,10},{6,14},... | collective-permute-start | bytes 589832 | tf_op jit(solution)/shard_map/ppermute | solution.py:280
  263.4 14.0 %copy-start.20 = (bf16[512,256]{1,0:T(8,128)(2,1)}, bf16[512,256]{1,0:T(8,128)(2,1)S(1)}, u32[]{:S(2)}) copy-start(bf16[512,256]{1,0:T(8,128)(2,1)S(1)} %collective-permute-done.27.refs_11_) | copy-start | bytes 786436
  263.4 32.1 %collective-permute-start.20 = (bf16[384,256]{1,0:T(8,128)(2,1)}, bf16[384,256]{1,0:T(8,128)(2,1)S(1)}, u32[]{:S(2)}, u32[]{:S(2)}) collective-permute-start(bf16[384,256]{1,0:T(8,128)(2,1)} %get-tuple-element.23), channel_id=1, source_target_pairs={{0,4},{4,8},{8,12},{12,0},{1,5},{5,9},{9,13},{13,1},{2,6},{6,10},{... | collective-permute-start | bytes 589832 | tf_op jit(solution)/shard_map/ppermute | solution.py:280
  265.1 12.2 %copy-start.7 = (bf16[384,512]{1,0:T(8,128)(2,1)}, bf16[384,512]{1,0:T(8,128)(2,1)S(1)}, u32[]{:S(2)}) copy-start(bf16[384,512]{1,0:T(8,128)(2,1)S(1)} %collective-permute-done.12.refs_1_.refs_13_) | copy-start | bytes 1179652
  265.1 35.1 %collective-permute-start.21 = (bf16[384,256]{1,0:T(8,128)(2,1)}, bf16[384,256]{1,0:T(8,128)(2,1)S(1)}, u32[]{:S(2)}, u32[]{:S(2)}) collective-permute-start(bf16[384,256]{1,0:T(8,128)(2,1)} %get-tuple-element.24), channel_id=1, source_target_pairs={{0,12},{4,0},{8,4},{12,8},{1,13},{5,1},{9,5},{13,9},{2,14},{6,2},{... | collective-permute-start | bytes 589832 | tf_op jit(solution)/shard_map/ppermute | solution.py:280
  289.3 10.9 %copy-start.21 = (bf16[384,256]{1,0:T(8,128)(2,1)}, bf16[384,256]{1,0:T(8,128)(2,1)S(1)}, u32[]{:S(2)}) copy-start(bf16[384,256]{1,0:T(8,128)(2,1)S(1)} %collective-permute-done.19.refs_5_) | copy-start | bytes 589828
  289.3 15.0 %collective-permute-start.28 = (bf16[384,128]{1,0:T(8,128)(2,1)}, bf16[384,128]{1,0:T(8,128)(2,1)S(1)}, u32[]{:S(2)}, u32[]{:S(2)}) collective-permute-start(bf16[384,128]{1,0:T(8,128)(2,1)} %get-tuple-element.26), channel_id=1, source_target_pairs={{0,8},{4,12},{8,0},{12,4},{1,9},{5,13},{9,1},{13,5},{2,10},{6,14},... | collective-permute-start | bytes 294920 | tf_op jit(solution)/shard_map/ppermute | solution.py:280
  295.5 4.8 %copy-start.22 = (bf16[384,256]{1,0:T(8,128)(2,1)}, bf16[384,256]{1,0:T(8,128)(2,1)S(1)}, u32[]{:S(2)}) copy-start(bf16[384,256]{1,0:T(8,128)(2,1)S(1)} %collective-permute-done.20.refs_6_) | copy-start | bytes 589828
  295.5 8.8 %collective-permute-start.29 = (bf16[384,128]{1,0:T(8,128)(2,1)}, bf16[384,128]{1,0:T(8,128)(2,1)S(1)}, u32[]{:S(2)}, u32[]{:S(2)}) collective-permute-start(bf16[384,128]{1,0:T(8,128)(2,1)} %get-tuple-element.27), channel_id=1, source_target_pairs={{0,4},{4,8},{8,12},{12,0},{1,5},{5,9},{9,13},{13,1},{2,6},{6,10},{... | collective-permute-start | bytes 294920 | tf_op jit(solution)/shard_map/ppermute | solution.py:280
  300.2 0.7 copy-start.23
  300.2 4.8 %collective-permute-start.30 = (bf16[384,128]{1,0:T(8,128)(2,1)}, bf16[384,128]{1,0:T(8,128)(2,1)S(1)}, u32[]{:S(2)}, u32[]{:S(2)}) collective-permute-start(bf16[384,128]{1,0:T(8,128)(2,1)} %get-tuple-element.28), channel_id=1, source_target_pairs={{0,12},{4,0},{8,4},{12,8},{1,13},{5,1},{9,5},{13,9},{2,14},{6,2},{... | collective-permute-start | bytes 294920 | tf_op jit(solution)/shard_map/ppermute | solution.py:280
  300.2 0.8 copy-start.17
  301.0 0.7 copy-start.18
  304.3 0.7 copy-start.24
  304.3 0.7 copy-start.25
  305.1 0.6 copy-start.26
Sparse Core Ops, SparseCore 0:
  8.9 29.6 all-gather.4
  40.2 28.5 all-gather.6
  70.3 28.5 all-gather.8
  124.4 30.4 all-gather.10

commit v20 on v17

--- a/solution.py
+++ b/solution.py
@@ -293,10 +293,10 @@
     held = [[] for _ in spans]
     whole = []
     for step in plan:
-        if last and len(sent) == max(len(plan) - 2, 3):
+        if last and len(sent) == max(len(plan) - 3, 3):
             hidden_of(0, [])
         weights(*step)
-        if len(sent) == min(3, max(len(plan) - 2, 3)):
+        if len(sent) == min(3, max(len(plan) - 3, 3)):
             tokens_of()
     for n in range(min(last, 1), last + 1):
         hidden_of(n, done[-1:] + (returned[n - 2][:1] if n > 1 else []))

time: 299 us -> 296 us (0.990)
  waiting for transfers between devices: 155 us -> 148 us
  starting transfers between devices: 52.9 us -> 59.2 us
    ppermute x8, waiting for transfers between devices: 7.3 us -> 0.15 us  [weights(): swapped.append(lax.ppermute(came, 'parts', around(parts, -turn)))]
    ppermute x8, starting transfers between devices: 11.8 us -> 17.7 us  [weights(): arrived.append(lax.ppermute(sent[-1], 'row', around(rows, shift)))]
    ppermute x8, waiting for transfers between devices: 95.5 us -> 98.5 us  [weights(): arrived.append(lax.ppermute(sent[-1], 'row', around(rows, shift)))]
  transfers between devices with their start and end apart: 35 -> 35, of which waited for: 18 -> 15; matrix products, arithmetic and copies ran while one was open for 1% -> 1% of each run, Pallas kernels for 21% -> 21%
where the time goes in v20:
time: 296 us; the launch traced here: 295 us
  waiting for transfers between devices  148 us (50%)
  Pallas kernels  63.2 us (21%)
  starting transfers between devices  59.2 us (20%)
  between operations  13.5 us (5%)
  local copies, waits for them, and re-layouts  8.5 us (3%)
    ppermute x8, waiting for transfers between devices, weights(): arrived.append(lax.ppermute(sent[-1], 'row', around(rows, shift)))  98.5 us
    pallas_call x3, Pallas kernels, product(): pl.pallas_call(body, out_shape=[jax.ShapeDtypeStruct((mine, wide), jnp.bf...  40.2 us
    ppermute x3, waiting for transfers between devices, tokens_of(): lax.ppermute(upper[-1], 'row', [(i, i - 1) for i in range(1, rows - step...  35.7 us
    ppermute x8, starting transfers between devices, weights(): arrived.append(lax.ppermute(sent[-1], 'row', around(rows, shift)))  17.7 us
    pallas_call x8, Pallas kernels, pack(): pl.pallas_call(body, out_shape=jax.ShapeDtypeStruct((share, 2 * wide), ga...  16.7 us
    ppermute x9, starting transfers between devices, hidden_of(): lax.ppermute(outs[shift], 'row', around(rows, shift))  16.2 us
    ppermute x9, waiting for transfers between devices, hidden_of(): lax.ppermute(outs[shift], 'row', around(rows, shift))  9.62 us
    ppermute x3, starting transfers between devices, tokens_of(): lax.ppermute(lower[-1], 'row', [(i, i + 1) for i in range(step - 1, rows...  9.05 us
  transfers between devices with their start and end apart: 35, of which 15 were waited for; matrix products, arithmetic and copies ran while one was open for 1% of the time, Pallas kernels for 21%

profile of v20, /device:TPU:12, one launch (start us, length us, event | category | flops | bytes accessed | tf_op | source)
XLA Modules:
  0.0 294.5 jit_solution(17376281511426639312)
XLA Ops:
  6.5 0.7 all-gather.5.cloned.1.call-update
  7.3 2.4 collective-permute-start
  9.7 3.5 %collective-permute-start.1 = (bf16[384,1024]{1,0:T(8,128)(2,1)}, bf16[384,1024]{1,0:T(8,128)(2,1)S(1)}, u32[]{:S(2)}, u32[]{:S(2)}) collective-permute-start(bf16[384,1024]{1,0:T(8,128)(2,1)} %param.3), channel_id=1, source_target_pairs={{0,4},{4,8},{8,12},{1,5},{5,9},{9,13},{2,6},{6,10},{10,14},{3,7},{... | collective-permute-start | bytes 2359304 | tf_op jit(solution)/shard_map/ppermute | solution.py:245
  13.2 2.6 pack.8.refs_1_.refs_2_
  15.7 13.0 %collective-permute-done.refs_2_ = bf16[384,1024]{1,0:T(8,128)(2,1)S(1)} collective-permute-done((bf16[384,1024]{1,0:T(8,128)(2,1)}, bf16[384,1024]{1,0:T(8,128)(2,1)S(1)}, u32[]{:S(2)}, u32[]{:S(2)}) %collective-permute-start) | collective-permute-done | bytes 786464 | tf_op jit(solution)/shard_map/ppermute | solution.py:246
  28.7 2.1 collective-permute-done.1.refs_1_
  30.8 1.1 broadcast_select_fusion.1.refs_0_
  31.9 2.1 collective-permute-start.2
  34.0 4.0 %collective-permute-start.3 = (bf16[384,1024]{1,0:T(8,128)(2,1)S(1)}, bf16[384,1024]{1,0:T(8,128)(2,1)S(1)}, u32[]{:S(2)}, u32[]{:S(2)}) collective-permute-start(bf16[384,1024]{1,0:T(8,128)(2,1)S(1)} %collective-permute-done.1.refs_1_), channel_id=1, source_target_pairs={{4,8},{8,12},{5,9},{9,13},{6,10},{10,14},{7,11},{11,15},{20,24},{2... | collective-permute-start | bytes 2359304 | tf_op jit(solution)/shard_map/ppermute | solution.py:245
  38.0 14.1 %collective-permute-done.2 = bf16[384,1024]{1,0:T(8,128)(2,1)S(1)} collective-permute-done((bf16[384,1024]{1,0:T(8,128)(2,1)S(1)}, bf16[384,1024]{1,0:T(8,128)(2,1)S(1)}, u32[]{:S(2)}, u32[]{:S(2)}) %collective-permute-start.2) | collective-permute-done | bytes 786464 | tf_op jit(solution)/shard_map/ppermute | solution.py:246
  52.2 1.2 collective-permute-done.3
  53.4 0.9 copy-done.15
  54.3 1.0 broadcast_select_fusion
  55.3 2.3 collective-permute-start.6
  57.6 3.7 %collective-permute-start.4 = (bf16[384,1024]{1,0:T(8,128)(2,1)}, bf16[384,1024]{1,0:T(8,128)(2,1)S(1)}, u32[]{:S(2)}, u32[]{:S(2)}) collective-permute-start(bf16[384,1024]{1,0:T(8,128)(2,1)} %copy-done.14), channel_id=1, source_target_pairs={{4,0},{5,1},{6,2},{7,3},{20,16},{21,17},{22,18},{23,19}} | collective-permute-start | bytes 2359304 | tf_op jit(solution)/shard_map/ppermute | solution.py:246
  61.3 1.6 collective-permute-start.5
  62.9 2.2 pack.9.refs_2_
  65.1 2.2 pack.10.refs_3_.refs_2_
  67.2 8.6 %collective-permute-done.4.refs_0_ = bf16[384,1024]{1,0:T(8,128)(2,1)S(1)} collective-permute-done((bf16[384,1024]{1,0:T(8,128)(2,1)}, bf16[384,1024]{1,0:T(8,128)(2,1)S(1)}, u32[]{:S(2)}, u32[]{:S(2)}) %collective-permute-start.4) | collective-permute-done | bytes 786464 | tf_op jit(solution)/shard_map/ppermute | solution.py:246
  75.9 0.9 copy-done.16
  76.8 2.1 pick.1.refs_0_
  78.9 33.0 %collective-permute-done.6.refs_1_.refs_6_.refs_3_ = bf16[512,1280]{1,0:T(8,128)(2,1)S(1)} collective-permute-done((bf16[512,1280]{1,0:T(8,128)(2,1)S(1)}, bf16[512,1280]{1,0:T(8,128)(2,1)S(1)}, u32[]{:S(2)}, u32[]{:S(2)}) %collective-permute-start.6) | collective-permute-done | bytes 1310752 | tf_op jit(solution)/shard_map/ppermute | solution.py:269
  111.8 1.1 copy-done
  112.9 1.0 collective-permute-start.7
  114.3 1.9 collective-permute-start.10
  116.2 1.9 pack.11.refs_2_
  118.2 3.3 %collective-permute-start.22 = (bf16[512,512]{1,0:T(8,128)(2,1)}, bf16[512,512]{1,0:T(8,128)(2,1)S(1)}, u32[]{:S(2)}, u32[]{:S(2)}) collective-permute-start(bf16[512,512]{1,0:T(8,128)(2,1)} %pack.11.refs_2_), channel_id=1, source_target_pairs={{0,8},{4,12},{8,0},{12,4},{1,9},{5,13},{9,1},{13,5},{2,10},{6,14},... | collective-permute-start | bytes 1572872 | tf_op jit(solution)/shard_map/ppermute | solution.py:269
  121.5 13.2 %collective-permute-done.8.refs_8_.refs_3_ = bf16[512,768]{1,0:T(8,128)(2,1)} collective-permute-done((bf16[512,768]{1,0:T(8,128)(2,1)S(1)}, bf16[512,768]{1,0:T(8,128)(2,1)}, u32[]{:S(2)}, u32[]{:S(2)}) %collective-permute-start.8) | collective-permute-done | bytes 786464 | tf_op jit(solution)/shard_map/ppermute | solution.py:269
  134.7 1.0 collective-permute-start.9
  135.7 28.6 %collective-permute-done.10.refs_10_.refs_3_ = bf16[512,768]{1,0:T(8,128)(2,1)} collective-permute-done((bf16[512,768]{1,0:T(8,128)(2,1)S(1)}, bf16[512,768]{1,0:T(8,128)(2,1)}, u32[]{:S(2)}, u32[]{:S(2)}) %collective-permute-start.10) | collective-permute-done | bytes 786464 | tf_op jit(solution)/shard_map/ppermute | solution.py:269
  164.3 1.0 collective-permute-start.11
  165.3 5.4 %collective-permute-done.22.refs_3_.refs_6_ = bf16[512,512]{1,0:T(8,128)(2,1)S(1)} collective-permute-done((bf16[512,512]{1,0:T(8,128)(2,1)}, bf16[512,512]{1,0:T(8,128)(2,1)S(1)}, u32[]{:S(2)}, u32[]{:S(2)}) %collective-permute-start.22) | collective-permute-done | bytes 524320 | tf_op jit(solution)/shard_map/ppermute | solution.py:269
  170.7 1.0 collective-permute-start.23
  171.7 1.1 copy-done.4
  172.7 1.9 pack.12.refs_2_
  174.7 2.7 collective-permute-start.15
  177.3 2.0 pack.13.refs_2_
  179.3 1.9 collective-permute-start.17
  181.2 2.0 pack.14.refs_2_
  183.2 5.3 %collective-permute-start.24 = (bf16[512,512]{1,0:T(8,128)(2,1)}, bf16[512,512]{1,0:T(8,128)(2,1)S(1)}, u32[]{:S(2)}, u32[]{:S(2)}) collective-permute-start(bf16[512,512]{1,0:T(8,128)(2,1)} %pack.14.refs_2_), channel_id=1, source_target_pairs={{0,4},{4,8},{8,12},{12,0},{1,5},{5,9},{9,13},{13,1},{2,6},{6,10},{... | collective-permute-start | bytes 1572872 | tf_op jit(solution)/shard_map/ppermute | solution.py:269
  188.5 10.9 %collective-permute-done.15.refs_8_.refs_3_ = bf16[512,512]{1,0:T(8,128)(2,1)S(1)} collective-permute-done((bf16[512,512]{1,0:T(8,128)(2,1)}, bf16[512,512]{1,0:T(8,128)(2,1)S(1)}, u32[]{:S(2)}, u32[]{:S(2)}) %collective-permute-start.15) | collective-permute-done | bytes 524320 | tf_op jit(solution)/shard_map/ppermute | solution.py:269
  199.5 0.8 copy-done.9
  200.3 1.9 pack.15
  202.3 1.3 collective-permute-start.16
  203.5 16.5 %product.3 = (bf16[384,384]{1,0:T(8,128)(2,1)}, bf16[384,384]{1,0:T(8,128)(2,1)}, bf16[384,384]{1,0:T(8,128)(2,1)}, bf16[384,384]{1,0:T(8,128)(2,1)}) custom-call(bf16[384,4096]{1,0:T(8,128)(2,1)} %all-gather.5.cloned.1.call-done.refs_0_, bf16[384,4096]{1,0:T(8,128)(2,1)} %all-gather.7.cloned.1.call-done.refs_1_, ...), custom_call_target="tpu_custom_call" | custom-call | flops 9663676416 | bytes 20054016 | tf_op jit(solution)/shard_map/product/pallas_call | solution.py:138
  220.1 0.8 copy-done.12
  220.9 0.8 collective-permute-start.18
  221.7 4.3 %collective-permute-start.12 = (bf16[384,384]{1,0:T(8,128)(2,1)}, bf16[384,384]{1,0:T(8,128)(2,1)S(1)}, u32[]{:S(2)}, u32[]{:S(2)}) collective-permute-start(bf16[384,384]{1,0:T(8,128)(2,1)} %get-tuple-element.18), channel_id=1, source_target_pairs={{0,8},{4,12},{8,0},{12,4},{1,9},{5,13},{9,1},{13,5},{2,10},{6,14},... | collective-permute-start | bytes 884744 | tf_op jit(solution)/shard_map/ppermute | solution.py:280
  226.1 1.8 collective-permute-start.13
  227.9 7.4 %collective-permute-done.26.refs_0_ = bf16[512,512]{1,0:T(8,128)(2,1)S(1)} collective-permute-done((bf16[512,512]{1,0:T(8,128)(2,1)}, bf16[512,512]{1,0:T(8,128)(2,1)S(1)}, u32[]{:S(2)}, u32[]{:S(2)}) %collective-permute-start.26) | collective-permute-done | bytes 524320 | tf_op jit(solution)/shard_map/ppermute | solution.py:269
  235.2 0.8 copy-done.11
  236.1 2.0 collective-permute-start.27
  238.1 11.8 %product.4 = (bf16[384,256]{1,0:T(8,128)(2,1)}, bf16[384,256]{1,0:T(8,128)(2,1)}, bf16[384,256]{1,0:T(8,128)(2,1)}, bf16[384,256]{1,0:T(8,128)(2,1)}) custom-call(bf16[384,4096]{1,0:T(8,128)(2,1)} %all-gather.5.cloned.1.call-done.refs_0_, bf16[384,4096]{1,0:T(8,128)(2,1)} %all-gather.7.cloned.1.call-done.refs_1_, ...), custom_call_target="tpu_custom_call" | custom-call | flops 6442450944 | bytes 17563648 | tf_op jit(solution)/shard_map/product/pallas_call | solution.py:138
  249.9 2.3 collective-permute-start.19
  252.2 1.0 collective-permute-start.20
  253.3 3.8 %collective-permute-start.21 = (bf16[384,256]{1,0:T(8,128)(2,1)}, bf16[384,256]{1,0:T(8,128)(2,1)S(1)}, u32[]{:S(2)}, u32[]{:S(2)}) collective-permute-start(bf16[384,256]{1,0:T(8,128)(2,1)} %get-tuple-element.24), channel_id=1, source_target_pairs={{0,12},{4,0},{8,4},{12,8},{1,13},{5,1},{9,5},{13,9},{2,14},{6,2},{... | collective-permute-start | bytes 589832 | tf_op jit(solution)/shard_map/ppermute | solution.py:280
  257.1 11.8 %product.5 = (bf16[384,256]{1,0:T(8,128)(2,1)}, bf16[384,256]{1,0:T(8,128)(2,1)}, bf16[384,256]{1,0:T(8,128)(2,1)}, bf16[384,256]{1,0:T(8,128)(2,1)}) custom-call(bf16[384,4096]{1,0:T(8,128)(2,1)} %all-gather.5.cloned.1.call-done.refs_0_, bf16[384,4096]{1,0:T(8,128)(2,1)} %all-gather.7.cloned.1.call-done.refs_1_, ...), custom_call_target="tpu_custom_call" | custom-call | flops 6442450944 | bytes 17563648 | tf_op jit(solution)/shard_map/product/pallas_call | solution.py:138
  269.0 0.9 collective-permute-start.28
  269.9 2.1 collective-permute-start.29
  273.4 2.4 place.2.refs_0_
  275.7 5.3 %collective-permute-done.28.refs_2_ = bf16[384,256]{1,0:T(8,128)(2,1)S(1)} collective-permute-done((bf16[384,256]{1,0:T(8,128)(2,1)}, bf16[384,256]{1,0:T(8,128)(2,1)S(1)}, u32[]{:S(2)}, u32[]{:S(2)}) %collective-permute-start.28) | collective-permute-done | bytes 196640 | tf_op jit(solution)/shard_map/ppermute | solution.py:280
  281.1 2.1 collective-permute-done.29.refs_3_
  283.2 2.1 collective-permute-done.30.refs_4_
  286.0 2.0 place.3
  (89 shorter events, 2.9 us)
Async XLA Ops:
  6.5 197.0 %all-gather.5.cloned.1.call-start = ((), (), s32[]{:S(2)}) async-start(), calls=%async_computation | async-start | bytes 3932160 | tf_op jit(solution)/shard_map/all_gather | solution.py:264
  7.3 196.3 %all-gather.7.cloned.1.call-start = ((), (), s32[]{:S(2)}) async-start(), calls=%async_computation.1 | async-start | bytes 3932160 | tf_op jit(solution)/shard_map/all_gather | solution.py:264
  7.3 21.4 %collective-permute-start = (bf16[384,1024]{1,0:T(8,128)(2,1)}, bf16[384,1024]{1,0:T(8,128)(2,1)S(1)}, u32[]{:S(2)}, u32[]{:S(2)}) collective-permute-start(bf16[384,1024]{1,0:T(8,128)(2,1)} %param.3), channel_id=1, source_target_pairs={{4,0},{8,4},{12,8},{5,1},{9,5},{13,9},{6,2},{10,6},{14,10},{7,3},{... | collective-permute-start | bytes 2359304 | tf_op jit(solution)/shard_map/ppermute | solution.py:246
  9.7 21.1 %collective-permute-start.1 = (bf16[384,1024]{1,0:T(8,128)(2,1)}, bf16[384,1024]{1,0:T(8,128)(2,1)S(1)}, u32[]{:S(2)}, u32[]{:S(2)}) collective-permute-start(bf16[384,1024]{1,0:T(8,128)(2,1)} %param.3), channel_id=1, source_target_pairs={{0,4},{4,8},{8,12},{1,5},{5,9},{9,13},{2,6},{6,10},{10,14},{3,7},{... | collective-permute-start | bytes 2359304 | tf_op jit(solution)/shard_map/ppermute | solution.py:245
  28.7 26.6 %copy-start.5 = (bf16[384,1024]{1,0:T(8,128)(2,1)}, bf16[384,1024]{1,0:T(8,128)(2,1)S(1)}, u32[]{:S(2)}) copy-start(bf16[384,1024]{1,0:T(8,128)(2,1)S(1)} %collective-permute-done.refs_2_) | copy-start | bytes 2359300
  30.8 24.5 %copy-start.6 = (bf16[384,1024]{1,0:T(8,128)(2,1)}, bf16[384,1024]{1,0:T(8,128)(2,1)S(1)}, u32[]{:S(2)}) copy-start(bf16[384,1024]{1,0:T(8,128)(2,1)S(1)} %collective-permute-done.1.refs_1_) | copy-start | bytes 2359300
  31.9 23.5 %copy-start.1 = (bf16[512,1280]{1,0:T(8,128)(2,1)S(1)}, bf16[512,1280]{1,0:T(8,128)(2,1)}, u32[]{:S(2)}) copy-start(bf16[512,1280]{1,0:T(8,128)(2,1)} %pack.8.refs_1_.refs_2_) | copy-start | bytes 3932164
  31.9 171.6 %all-gather.9.cloned.1.call-start = ((), (), s32[]{:S(2)}) async-start(), calls=%async_computation.2 | async-start | bytes 3932160 | tf_op jit(solution)/shard_map/all_gather | solution.py:264
  31.9 20.2 %collective-permute-start.2 = (bf16[384,1024]{1,0:T(8,128)(2,1)S(1)}, bf16[384,1024]{1,0:T(8,128)(2,1)S(1)}, u32[]{:S(2)}, u32[]{:S(2)}) collective-permute-start(bf16[384,1024]{1,0:T(8,128)(2,1)S(1)} %collective-permute-done.refs_2_), channel_id=1, source_target_pairs={{4,0},{8,4},{5,1},{9,5},{6,2},{10,6},{7,3},{11,7},{20,16},{24,20},... | collective-permute-start | bytes 2359304 | tf_op jit(solution)/shard_map/ppermute | solution.py:246
  34.0 19.4 %collective-permute-start.3 = (bf16[384,1024]{1,0:T(8,128)(2,1)S(1)}, bf16[384,1024]{1,0:T(8,128)(2,1)S(1)}, u32[]{:S(2)}, u32[]{:S(2)}) collective-permute-start(bf16[384,1024]{1,0:T(8,128)(2,1)S(1)} %collective-permute-done.1.refs_1_), channel_id=1, source_target_pairs={{4,8},{8,12},{5,9},{9,13},{6,10},{10,14},{7,11},{11,15},{20,24},{2... | collective-permute-start | bytes 2359304 | tf_op jit(solution)/shard_map/ppermute | solution.py:245
  52.2 1.2 copy-start.14
  53.4 0.9 copy-start.15
  55.3 148.2 %all-gather.11.cloned.1.call-start = ((), (), s32[]{:S(2)}) async-start(), calls=%async_computation.3 | async-start | bytes 3932160 | tf_op jit(solution)/shard_map/all_gather | solution.py:264
  55.3 56.5 %collective-permute-start.6 = (bf16[512,1280]{1,0:T(8,128)(2,1)S(1)}, bf16[512,1280]{1,0:T(8,128)(2,1)S(1)}, u32[]{:S(2)}, u32[]{:S(2)}) collective-permute-start(bf16[512,1280]{1,0:T(8,128)(2,1)S(1)} %copy-done.1), channel_id=1, source_target_pairs={{0,8},{4,12},{8,0},{12,4},{1,9},{5,13},{9,1},{13,5},{2,10},{6,14},... | collective-permute-start | bytes 3932168 | tf_op jit(solution)/shard_map/ppermute | solution.py:269
  57.6 18.3 %collective-permute-start.4 = (bf16[384,1024]{1,0:T(8,128)(2,1)}, bf16[384,1024]{1,0:T(8,128)(2,1)S(1)}, u32[]{:S(2)}, u32[]{:S(2)}) collective-permute-start(bf16[384,1024]{1,0:T(8,128)(2,1)} %copy-done.14), channel_id=1, source_target_pairs={{4,0},{5,1},{6,2},{7,3},{20,16},{21,17},{22,18},{23,19}} | collective-permute-start | bytes 2359304 | tf_op jit(solution)/shard_map/ppermute | solution.py:246
  61.3 14.6 %collective-permute-start.5 = (bf16[384,1024]{1,0:T(8,128)(2,1)}, bf16[384,1024]{1,0:T(8,128)(2,1)}, u32[]{:S(2)}, u32[]{:S(2)}) collective-permute-start(bf16[384,1024]{1,0:T(8,128)(2,1)} %copy-done.15), channel_id=1, source_target_pairs={{8,12},{9,13},{10,14},{11,15},{24,28},{25,29},{26,30},{27,31}} | collective-permute-start | bytes 2359304 | tf_op jit(solution)/shard_map/ppermute | solution.py:245
  75.9 0.9 copy-start.16
  78.9 35.5 %copy-start.2 = (bf16[512,768]{1,0:T(8,128)(2,1)S(1)}, bf16[512,768]{1,0:T(8,128)(2,1)}, u32[]{:S(2)}) copy-start(bf16[512,768]{1,0:T(8,128)(2,1)} %pack.10.refs_3_.refs_2_) | copy-start | bytes 2359300
  111.8 1.1 copy-start
  112.9 1.1 copy-start.3
  112.9 58.7 %collective-permute-start.7 = (bf16[512,1280]{1,0:T(8,128)(2,1)}, bf16[512,1280]{1,0:T(8,128)(2,1)S(1)}, u32[]{:S(2)}, u32[]{:S(2)}) collective-permute-start(bf16[512,1280]{1,0:T(8,128)(2,1)} %copy-done), channel_id=1, source_target_pairs={{0,16},{16,0},{1,17},{17,1},{2,18},{18,2},{3,19},{19,3},{4,20},{20... | collective-permute-start | bytes 3932168 | tf_op jit(solution)/shard_map/ppermute | solution.py:273
  114.0 20.7 %collective-permute-start.8 = (bf16[512,768]{1,0:T(8,128)(2,1)S(1)}, bf16[512,768]{1,0:T(8,128)(2,1)}, u32[]{:S(2)}, u32[]{:S(2)}) collective-permute-start(bf16[512,768]{1,0:T(8,128)(2,1)S(1)} %copy-done.3), channel_id=1, source_target_pairs={{0,4},{4,8},{8,12},{12,0},{1,5},{5,9},{9,13},{13,1},{2,6},{6,10},{... | collective-permute-start | bytes 2359304 | tf_op jit(solution)/shard_map/ppermute | solution.py:269
  114.3 50.0 %collective-permute-start.10 = (bf16[512,768]{1,0:T(8,128)(2,1)S(1)}, bf16[512,768]{1,0:T(8,128)(2,1)}, u32[]{:S(2)}, u32[]{:S(2)}) collective-permute-start(bf16[512,768]{1,0:T(8,128)(2,1)S(1)} %copy-done.2), channel_id=1, source_target_pairs={{0,12},{4,0},{8,4},{12,8},{1,13},{5,1},{9,5},{13,9},{2,14},{6,2},{... | collective-permute-start | bytes 2359304 | tf_op jit(solution)/shard_map/ppermute | solution.py:269
  118.2 52.5 %collective-permute-start.22 = (bf16[512,512]{1,0:T(8,128)(2,1)}, bf16[512,512]{1,0:T(8,128)(2,1)S(1)}, u32[]{:S(2)}, u32[]{:S(2)}) collective-permute-start(bf16[512,512]{1,0:T(8,128)(2,1)} %pack.11.refs_2_), channel_id=1, source_target_pairs={{0,8},{4,12},{8,0},{12,4},{1,9},{5,13},{9,1},{13,5},{2,10},{6,14},... | collective-permute-start | bytes 1572872 | tf_op jit(solution)/shard_map/ppermute | solution.py:269
  134.7 42.6 %collective-permute-start.9 = (bf16[512,768]{1,0:T(8,128)(2,1)}, bf16[512,768]{1,0:T(8,128)(2,1)}, u32[]{:S(2)}, u32[]{:S(2)}) collective-permute-start(bf16[512,768]{1,0:T(8,128)(2,1)} %collective-permute-done.8.refs_8_.refs_3_), channel_id=1, source_target_pairs={{0,16},{16,0},{1,17},{17,1},{2,18},{18,2},{3,19},{19,3},{4,20},{20... | collective-permute-start | bytes 2359304 | tf_op jit(solution)/shard_map/ppermute | solution.py:273
  164.3 16.9 %collective-permute-start.11 = (bf16[512,768]{1,0:T(8,128)(2,1)}, bf16[512,768]{1,0:T(8,128)(2,1)}, u32[]{:S(2)}, u32[]{:S(2)}) collective-permute-start(bf16[512,768]{1,0:T(8,128)(2,1)} %collective-permute-done.10.refs_10_.refs_3_), channel_id=1, source_target_pairs={{0,16},{16,0},{1,17},{17,1},{2,18},{18,2},{3,19},{19,3},{4,20},{20... | collective-permute-start | bytes 2359304 | tf_op jit(solution)/shard_map/ppermute | solution.py:273
  170.7 8.6 %copy-start.7 = (bf16[512,512]{1,0:T(8,128)(2,1)}, bf16[512,512]{1,0:T(8,128)(2,1)S(1)}, u32[]{:S(2)}) copy-start(bf16[512,512]{1,0:T(8,128)(2,1)S(1)} %collective-permute-done.22.refs_3_.refs_6_) | copy-start | bytes 1572868
  170.7 17.8 %collective-permute-start.23 = (bf16[512,512]{1,0:T(8,128)(2,1)S(1)}, bf16[512,512]{1,0:T(8,128)(2,1)S(1)}, u32[]{:S(2)}, u32[]{:S(2)}) collective-permute-start(bf16[512,512]{1,0:T(8,128)(2,1)S(1)} %collective-permute-done.22.refs_3_.refs_6_), channel_id=1, source_target_pairs={{0,16},{16,0},{1,17},{17,1},{2,18},{18,2},{3,19},{19,3},{4,20},{20... | collective-permute-start | bytes 1572872 | tf_op jit(solution)/shard_map/ppermute | solution.py:273
  171.7 1.1 copy-start.4
  174.7 24.8 %collective-permute-start.15 = (bf16[512,512]{1,0:T(8,128)(2,1)}, bf16[512,512]{1,0:T(8,128)(2,1)S(1)}, u32[]{:S(2)}, u32[]{:S(2)}) collective-permute-start(bf16[512,512]{1,0:T(8,128)(2,1)} %pack.12.refs_2_), channel_id=1, source_target_pairs={{0,4},{4,8},{8,12},{12,0},{1,5},{5,9},{9,13},{13,1},{2,6},{6,10},{... | collective-permute-start | bytes 1572872 | tf_op jit(solution)/shard_map/ppermute | solution.py:269
  179.3 40.8 %collective-permute-start.17 = (bf16[512,512]{1,0:T(8,128)(2,1)}, bf16[512,512]{1,0:T(8,128)(2,1)S(1)}, u32[]{:S(2)}, u32[]{:S(2)}) collective-permute-start(bf16[512,512]{1,0:T(8,128)(2,1)} %pack.13.refs_2_), channel_id=1, source_target_pairs={{0,12},{4,0},{8,4},{12,8},{1,13},{5,1},{9,5},{13,9},{2,14},{6,2},{... | collective-permute-start | bytes 1572872 | tf_op jit(solution)/shard_map/ppermute | solution.py:269
  183.2 42.9 %collective-permute-start.24 = (bf16[512,512]{1,0:T(8,128)(2,1)}, bf16[512,512]{1,0:T(8,128)(2,1)S(1)}, u32[]{:S(2)}, u32[]{:S(2)}) collective-permute-start(bf16[512,512]{1,0:T(8,128)(2,1)} %pack.14.refs_2_), channel_id=1, source_target_pairs={{0,4},{4,8},{8,12},{12,0},{1,5},{5,9},{9,13},{13,1},{2,6},{6,10},{... | collective-permute-start | bytes 1572872 | tf_op jit(solution)/shard_map/ppermute | solution.py:269
  188.5 11.0 %copy-start.8 = (bf16[512,512]{1,0:T(8,128)(2,1)}, bf16[512,512]{1,0:T(8,128)(2,1)S(1)}, u32[]{:S(2)}) copy-start(bf16[512,512]{1,0:T(8,128)(2,1)S(1)} %collective-permute-done.23.refs_4_.refs_7_) | copy-start | bytes 1572868
  199.5 0.8 copy-start.9
  202.2 33.0 %collective-permute-start.26 = (bf16[512,512]{1,0:T(8,128)(2,1)}, bf16[512,512]{1,0:T(8,128)(2,1)S(1)}, u32[]{:S(2)}, u32[]{:S(2)}) collective-permute-start(bf16[512,512]{1,0:T(8,128)(2,1)} %pack.15), channel_id=1, source_target_pairs={{0,12},{4,0},{8,4},{12,8},{1,13},{5,1},{9,5},{13,9},{2,14},{6,2},{... | collective-permute-start | bytes 1572872 | tf_op jit(solution)/shard_map/ppermute | solution.py:269
  202.3 33.8 %collective-permute-start.16 = (bf16[512,512]{1,0:T(8,128)(2,1)}, bf16[512,512]{1,0:T(8,128)(2,1)S(1)}, u32[]{:S(2)}, u32[]{:S(2)}) collective-permute-start(bf16[512,512]{1,0:T(8,128)(2,1)} %copy-done.9), channel_id=1, source_target_pairs={{0,16},{16,0},{1,17},{17,1},{2,18},{18,2},{3,19},{19,3},{4,20},{20... | collective-permute-start | bytes 1572872 | tf_op jit(solution)/shard_map/ppermute | solution.py:273
  220.1 0.8 copy-start.12
  220.9 15.2 %collective-permute-start.18 = (bf16[512,512]{1,0:T(8,128)(2,1)}, bf16[512,512]{1,0:T(8,128)(2,1)S(1)}, u32[]{:S(2)}, u32[]{:S(2)}) collective-permute-start(bf16[512,512]{1,0:T(8,128)(2,1)} %hold.7.refs_10_), channel_id=1, source_target_pairs={{0,16},{16,0},{1,17},{17,1},{2,18},{18,2},{3,19},{19,3},{4,20},{20... | collective-permute-start | bytes 1572872 | tf_op jit(solution)/shard_map/ppermute | solution.py:273
  221.7 28.2 %collective-permute-start.12 = (bf16[384,384]{1,0:T(8,128)(2,1)}, bf16[384,384]{1,0:T(8,128)(2,1)S(1)}, u32[]{:S(2)}, u32[]{:S(2)}) collective-permute-start(bf16[384,384]{1,0:T(8,128)(2,1)} %get-tuple-element.18), channel_id=1, source_target_pairs={{0,8},{4,12},{8,0},{12,4},{1,9},{5,13},{9,1},{13,5},{2,10},{6,14},... | collective-permute-start | bytes 884744 | tf_op jit(solution)/shard_map/ppermute | solution.py:280
  226.1 1.8 copy-start.10
  226.1 42.9 %collective-permute-start.13 = (bf16[384,384]{1,0:T(8,128)(2,1)}, bf16[384,384]{1,0:T(8,128)(2,1)S(1)}, u32[]{:S(2)}, u32[]{:S(2)}) collective-permute-start(bf16[384,384]{1,0:T(8,128)(2,1)} %get-tuple-element.19), channel_id=1, source_target_pairs={{0,4},{4,8},{8,12},{12,0},{1,5},{5,9},{9,13},{13,1},{2,6},{6,10},{... | collective-permute-start | bytes 884744 | tf_op jit(solution)/shard_map/ppermute | solution.py:280
  235.2 0.8 copy-start.11
  235.2 34.6 %collective-permute-start.14 = (bf16[384,384]{1,0:T(8,128)(2,1)}, bf16[384,384]{1,0:T(8,128)(2,1)S(1)}, u32[]{:S(2)}, u32[]{:S(2)}) collective-permute-start(bf16[384,384]{1,0:T(8,128)(2,1)} %get-tuple-element.20), channel_id=1, source_target_pairs={{0,12},{4,0},{8,4},{12,8},{1,13},{5,1},{9,5},{13,9},{2,14},{6,2},{... | collective-permute-start | bytes 884744 | tf_op jit(solution)/shard_map/ppermute | solution.py:280
  236.0 2.0 copy-start.17
  236.0 16.1 %collective-permute-start.25 = (bf16[512,512]{1,0:T(8,128)(2,1)}, bf16[512,512]{1,0:T(8,128)(2,1)S(1)}, u32[]{:S(2)}, u32[]{:S(2)}) collective-permute-start(bf16[512,512]{1,0:T(8,128)(2,1)} %hold.8.refs_8_), channel_id=1, source_target_pairs={{0,16},{16,0},{1,17},{17,1},{2,18},{18,2},{3,19},{19,3},{4,20},{20... | collective-permute-start | bytes 1572872 | tf_op jit(solution)/shard_map/ppermute | solution.py:273
  236.1 2.0 copy-start.19
  236.1 17.2 %collective-permute-start.27 = (bf16[512,512]{1,0:T(8,128)(2,1)}, bf16[512,512]{1,0:T(8,128)(2,1)S(1)}, u32[]{:S(2)}, u32[]{:S(2)}) collective-permute-start(bf16[512,512]{1,0:T(8,128)(2,1)} %hold.9.refs_10_), channel_id=1, source_target_pairs={{0,16},{16,0},{1,17},{17,1},{2,18},{18,2},{3,19},{19,3},{4,20},{20... | collective-permute-start | bytes 1572872 | tf_op jit(solution)/shard_map/ppermute | solution.py:273
  249.9 7.2 %copy-start.13 = (bf16[384,384]{1,0:T(8,128)(2,1)}, bf16[384,384]{1,0:T(8,128)(2,1)S(1)}, u32[]{:S(2)}) copy-start(bf16[384,384]{1,0:T(8,128)(2,1)S(1)} %collective-permute-done.12.refs_1_.refs_13_) | copy-start | bytes 884740
  249.9 22.0 %collective-permute-start.19 = (bf16[384,256]{1,0:T(8,128)(2,1)}, bf16[384,256]{1,0:T(8,128)(2,1)S(1)}, u32[]{:S(2)}, u32[]{:S(2)}) collective-permute-start(bf16[384,256]{1,0:T(8,128)(2,1)} %get-tuple-element.22), channel_id=1, source_target_pairs={{0,8},{4,12},{8,0},{12,4},{1,9},{5,13},{9,1},{13,5},{2,10},{6,14},... | collective-permute-start | bytes 589832 | tf_op jit(solution)/shard_map/ppermute | solution.py:280
  252.2 4.9 %copy-start.18 = (bf16[512,512]{1,0:T(8,128)(2,1)}, bf16[512,512]{1,0:T(8,128)(2,1)S(1)}, u32[]{:S(2)}) copy-start(bf16[512,512]{1,0:T(8,128)(2,1)S(1)} %collective-permute-done.25.refs_9_) | copy-start | bytes 1572868
  252.2 19.8 %collective-permute-start.20 = (bf16[384,256]{1,0:T(8,128)(2,1)}, bf16[384,256]{1,0:T(8,128)(2,1)S(1)}, u32[]{:S(2)}, u32[]{:S(2)}) collective-permute-start(bf16[384,256]{1,0:T(8,128)(2,1)} %get-tuple-element.23), channel_id=1, source_target_pairs={{0,4},{4,8},{8,12},{12,0},{1,5},{5,9},{9,13},{13,1},{2,6},{6,10},{... | collective-permute-start | bytes 589832 | tf_op jit(solution)/shard_map/ppermute | solution.py:280
  253.3 3.8 %copy-start.20 = (bf16[512,512]{1,0:T(8,128)(2,1)}, bf16[512,512]{1,0:T(8,128)(2,1)S(1)}, u32[]{:S(2)}) copy-start(bf16[512,512]{1,0:T(8,128)(2,1)S(1)} %collective-permute-done.27.refs_11_) | copy-start | bytes 1572868
  253.3 18.7 %collective-permute-start.21 = (bf16[384,256]{1,0:T(8,128)(2,1)}, bf16[384,256]{1,0:T(8,128)(2,1)S(1)}, u32[]{:S(2)}, u32[]{:S(2)}) collective-permute-start(bf16[384,256]{1,0:T(8,128)(2,1)} %get-tuple-element.24), channel_id=1, source_target_pairs={{0,12},{4,0},{8,4},{12,8},{1,13},{5,1},{9,5},{13,9},{2,14},{6,2},{... | collective-permute-start | bytes 589832 | tf_op jit(solution)/shard_map/ppermute | solution.py:280
  269.0 3.0 %copy-start.21 = (bf16[384,384]{1,0:T(8,128)(2,1)}, bf16[384,384]{1,0:T(8,128)(2,1)S(1)}, u32[]{:S(2)}) copy-start(bf16[384,384]{1,0:T(8,128)(2,1)S(1)} %collective-permute-done.13.refs_2_) | copy-start | bytes 884740
  269.0 12.1 %collective-permute-start.28 = (bf16[384,256]{1,0:T(8,128)(2,1)}, bf16[384,256]{1,0:T(8,128)(2,1)S(1)}, u32[]{:S(2)}, u32[]{:S(2)}) collective-permute-start(bf16[384,256]{1,0:T(8,128)(2,1)} %get-tuple-element.26), channel_id=1, source_target_pairs={{0,8},{4,12},{8,0},{12,4},{1,9},{5,13},{9,1},{13,5},{2,10},{6,14},... | collective-permute-start | bytes 589832 | tf_op jit(solution)/shard_map/ppermute | solution.py:280
  269.9 2.1 copy-start.22
  269.9 13.3 %collective-permute-start.29 = (bf16[384,256]{1,0:T(8,128)(2,1)}, bf16[384,256]{1,0:T(8,128)(2,1)S(1)}, u32[]{:S(2)}, u32[]{:S(2)}) collective-permute-start(bf16[384,256]{1,0:T(8,128)(2,1)} %get-tuple-element.27), channel_id=1, source_target_pairs={{0,4},{4,8},{8,12},{12,0},{1,5},{5,9},{9,13},{13,1},{2,6},{6,10},{... | collective-permute-start | bytes 589832 | tf_op jit(solution)/shard_map/ppermute | solution.py:280
  272.0 0.7 copy-start.23
  272.0 13.4 %collective-permute-start.30 = (bf16[384,256]{1,0:T(8,128)(2,1)}, bf16[384,256]{1,0:T(8,128)(2,1)S(1)}, u32[]{:S(2)}, u32[]{:S(2)}) collective-permute-start(bf16[384,256]{1,0:T(8,128)(2,1)} %get-tuple-element.28), channel_id=1, source_target_pairs={{0,12},{4,0},{8,4},{12,8},{1,13},{5,1},{9,5},{13,9},{2,14},{6,2},{... | collective-permute-start | bytes 589832 | tf_op jit(solution)/shard_map/ppermute | solution.py:280
  272.0 0.7 copy-start.24
  272.7 0.7 copy-start.25
  281.1 4.3 %copy-start.26 = (bf16[384,256]{1,0:T(8,128)(2,1)}, bf16[384,256]{1,0:T(8,128)(2,1)S(1)}, u32[]{:S(2)}) copy-start(bf16[384,256]{1,0:T(8,128)(2,1)S(1)} %collective-permute-done.28.refs_2_) | copy-start | bytes 589828
  283.2 2.2 copy-start.27
  285.3 0.7 copy-start.28
Sparse Core Ops, SparseCore 0:
  8.9 29.6 all-gather.4
  40.2 28.5 all-gather.6
  70.3 28.5 all-gather.8
  113.0 30.4 all-gather.10
